TPU v7x, 32 devices: a whole 2x2x4 slice. The times are simulated.
32 devices in a mesh: dp: 2 (over core), seq: 16 (over z, y, x).
Axes of the slice: x: 2, y: 2, z: 4, core: 2. Of those that a mesh axis runs over, the one named last changes fastest.
Arguments:
- inputs: bfloat16 [2, 16384, 2048], P('dp', 'seq'), may hold values from -45 to 45, as said below
- upstream: bfloat16 [2, 16384, 2048], P('dp', 'seq'), may hold values from -1 to 1
- right_blocks: bfloat16 [128, 128, 128], P('seq'), may hold values from -0.5 to 0.5
- left_blocks: bfloat16 [128, 128, 128], P('seq'), may hold values from -0.5 to 0.5
- gain: float32 [2048], replicated, may hold values from 0.1 to 1.9
- mid_scale: float32 [2048], replicated, may hold values from 0.5 to 2.5
Outputs:
- output: bfloat16 [2, 16384, 2048], P('dp', 'seq')
- input_gradient: bfloat16 [2, 16384, 2048], P('dp', 'seq')
- grad_right: float32 [128, 128, 128], P('seq')
- grad_left: float32 [128, 128, 128], P('seq')
- gain_gradient: float32 [2048], replicated
- grad_mid: float32 [2048], replicated
Inputs may be any that keep to these rules, and one draw needn't show every extreme that they name: `inputs`: activations with independent scales per position and per channel.
All inputs are finite; a program needn't handle non-finite values.
Results may differ from a plain program's by a relative error of at most 0.0063.
Values may be sent and summed in bfloat16 or wider, within the bound.
No kernel may reach another device: no remote copies, remote signals or barrier semaphores. Data moves between devices by JAX's collectives and lax.ppermute only.
A program may use at most 128 MiB of HBM per device.

v0:
```python
import jax
import jax.numpy as jnp
from jax import lax
from jax.sharding import PartitionSpec as P


def from_partner(block, axis, bit):
    count = lax.axis_size(axis)
    route = []
    for low in range(count):
        high = low | 1 << bit
        if high != low and high < count:
            route += [(low, high), (high, low)]
    return lax.ppermute(block, axis, route)


def regroup(panels):
    count = lax.axis_size("seq")
    levels = count.bit_length() - 1
    device = lax.axis_index("seq")
    height, span, width = panels.shape
    piece = span // count
    current = panels
    for level in range(levels):
        mine = device >> level & 1
        other = 1 - mine
        view = current.reshape(height, count >> level + 1, 2, (1 << level) * piece, width)
        outgoing = lax.dynamic_index_in_dim(view, other, axis=2, keepdims=False)
        incoming = from_partner(outgoing, "seq", level)
        view = lax.dynamic_update_index_in_dim(view, incoming, other, axis=2)
        current = view.reshape(height, span, width)
    return current


def body(inputs, upstream, right_blocks, left_blocks, gain, mid_scale):
    count = lax.axis_size("seq")
    rows = inputs.shape[1]
    width = inputs.shape[2]
    order = right_blocks.shape[1]
    local = order // count
    input_float = inputs[0].astype(jnp.float32)
    inverse_norm = lax.rsqrt(jnp.mean(input_float * input_float, axis=-1, keepdims=True) + 1e-06)
    standardized_input = input_float * inverse_norm
    normalized_rows = (standardized_input * gain).astype(jnp.bfloat16)
    grid = normalized_rows.reshape(local, order, width)
    first = jnp.einsum("aij,ajd->aid", right_blocks, grid, preferred_element_type=jnp.float32)
    sig = jax.nn.sigmoid(first * mid_scale)
    gated = (first * sig).astype(jnp.bfloat16)
    arrived = regroup(gated).reshape(local, count, local, width)
    lefts = left_blocks.reshape(local, count, local, count, local)
    second = jnp.einsum("bpqrs,srbd->qpbd", lefts, arrived, preferred_element_type=jnp.float32)
    mixed = second.astype(jnp.bfloat16).reshape(local, order, width)
    back = regroup(mixed).reshape(rows, width)
    output = (input_float + back.astype(jnp.float32)).astype(jnp.bfloat16)
    upward = regroup(upstream[0].reshape(local, order, width)).reshape(local, count, local, width)
    grad_left = jnp.einsum("qpbd,srbd->bpqrs", upward, arrived, preferred_element_type=jnp.float32)
    grad_left = grad_left.reshape(local, order, order)
    returned = jnp.einsum("bpqrs,qpbd->srbd", lefts, upward, preferred_element_type=jnp.float32)
    returned = returned.astype(jnp.bfloat16).reshape(local, order, width)
    dgated = regroup(returned).astype(jnp.float32)
    slope = sig * (1.0 - sig)
    dfirst = (dgated * (sig + first * mid_scale * slope)).astype(jnp.bfloat16)
    mid_part = jnp.sum(dgated * first * first * slope, axis=(0, 1))
    grad_right = jnp.einsum("aid,ajd->aij", dfirst, grid, preferred_element_type=jnp.float32)
    normalized_gradient = jnp.einsum(
        "aij,aid->ajd", right_blocks, dfirst, preferred_element_type=jnp.float32
    ).reshape(rows, width)
    gain_slice = jnp.sum(normalized_gradient * standardized_input, axis=0)
    centered_gradient = normalized_gradient * gain
    input_gradient = upstream[0].astype(jnp.float32) + inverse_norm * (
        centered_gradient
        - standardized_input
        * jnp.mean(centered_gradient * standardized_input, axis=-1, keepdims=True)
    )
    input_gradient = input_gradient.astype(jnp.bfloat16)
    grad_right, grad_left = lax.psum((grad_right, grad_left), "dp")
    gain_gradient, grad_mid = lax.psum((gain_slice, mid_part), ("dp", "seq"))
    return (
        output.reshape(1, rows, width),
        input_gradient.reshape(1, rows, width),
        grad_right,
        grad_left,
        gain_gradient,
        grad_mid,
    )


def solution(mesh):
    in_specs = (
        P("dp", "seq", None),
        P("dp", "seq", None),
        P("seq", None, None),
        P("seq", None, None),
        P(),
        P(),
    )
    out_specs = (
        P("dp", "seq", None),
        P("dp", "seq", None),
        P("seq", None, None),
        P("seq", None, None),
        P(),
        P(),
    )
    return jax.shard_map(body, mesh=mesh, in_specs=in_specs, out_specs=out_specs, check_vma=False)
```

profile of v0, /device:TPU:0, one launch (start us, length us, event | category | flops | bytes accessed | tf_op | source)
XLA Modules:
  0.0 1081.1 jit_solution(15376470853901818490)
XLA Ops:
  13.4 4.8 copy.66
  18.2 41.0 %collective-permute-done.8 = bf16[8,8,8,2048]{3,2,1,0:T(8,128)(2,1)S(1)} collective-permute-done((bf16[8,8,8,2048]{3,2,1,0:T(8,128)(2,1)}, bf16[8,8,8,2048]{3,2,1,0:T(8,128)(2,1)S(1)}, u32[]{:S(2)}, u32[]{:S(2)}) %collective-permute-start.8) | collective-permute-done | bytes 2097184 | tf_op jit(solution)/shard_map/ppermute | solution.py:14
  65.6 45.3 %collective-permute-done.9 = bf16[8,4,16,2048]{3,2,1,0:T(8,128)(2,1)S(1)} collective-permute-done((bf16[8,4,16,2048]{3,2,1,0:T(8,128)(2,1)}, bf16[8,4,16,2048]{3,2,1,0:T(8,128)(2,1)S(1)}, u32[]{:S(2)}, u32[]{:S(2)}) %collective-permute-start.9) | collective-permute-done | bytes 2097184 | tf_op jit(solution)/shard_map/ppermute | solution.py:14
  117.0 44.6 %collective-permute-done.10 = bf16[8,2,32,2048]{3,2,1,0:T(8,128)(2,1)S(1)} collective-permute-done((bf16[8,2,32,2048]{3,2,1,0:T(8,128)(2,1)}, bf16[8,2,32,2048]{3,2,1,0:T(8,128)(2,1)S(1)}, u32[]{:S(2)}, u32[]{:S(2)}) %collective-permute-start.10) | collective-permute-done | bytes 2097184 | tf_op jit(solution)/shard_map/ppermute | solution.py:14
  168.4 5.7 reshape.151
  174.1 7.0 copy.21
  181.2 76.2 %collective-permute-done.11 = bf16[8,1,64,2048]{3,2,0,1:T(8,128)(2,1)} collective-permute-done((bf16[8,1,64,2048]{3,2,0,1:T(8,128)(2,1)}, bf16[8,1,64,2048]{3,2,0,1:T(8,128)(2,1)}, u32[]{:S(2)}, u32[]{:S(2)}) %collective-permute-start.11) | collective-permute-done | bytes 2097184 | tf_op jit(solution)/shard_map/ppermute | solution.py:14
  260.5 10.0 fusion.20
  270.5 7.8 reshape_reshape.61
  278.3 7.1 constant_dynamic-slice_fusion
  293.0 41.9 %collective-permute-done.12 = bf16[8,8,8,2048]{3,2,1,0:T(8,128)(2,1)S(1)} collective-permute-done((bf16[8,8,8,2048]{3,2,1,0:T(8,128)(2,1)S(1)}, bf16[8,8,8,2048]{3,2,1,0:T(8,128)(2,1)S(1)}, u32[]{:S(2)}, u32[]{:S(2)}) %collective-permute-start.12) | collective-permute-done | bytes 2097184 | tf_op jit(solution)/shard_map/ppermute | solution.py:14
  335.9 46.2 %collective-permute-done.13 = bf16[8,4,16,2048]{3,2,1,0:T(8,128)(2,1)S(1)} collective-permute-done((bf16[8,4,16,2048]{3,2,1,0:T(8,128)(2,1)S(1)}, bf16[8,4,16,2048]{3,2,1,0:T(8,128)(2,1)S(1)}, u32[]{:S(2)}, u32[]{:S(2)}) %collective-permute-start.13) | collective-permute-done | bytes 2097184 | tf_op jit(solution)/shard_map/ppermute | solution.py:14
  383.4 44.6 %collective-permute-done.14 = bf16[8,2,32,2048]{3,2,1,0:T(8,128)(2,1)S(1)} collective-permute-done((bf16[8,2,32,2048]{3,2,1,0:T(8,128)(2,1)S(1)}, bf16[8,2,32,2048]{3,2,1,0:T(8,128)(2,1)S(1)}, u32[]{:S(2)}, u32[]{:S(2)}) %collective-permute-start.14) | collective-permute-done | bytes 2097184 | tf_op jit(solution)/shard_map/ppermute | solution.py:14
  433.7 86.1 %collective-permute-done.15 = bf16[8,1,64,2048]{3,2,0,1:T(8,128)(2,1)S(1)} collective-permute-done((bf16[8,1,64,2048]{3,2,0,1:T(8,128)(2,1)S(1)}, bf16[8,1,64,2048]{3,2,0,1:T(8,128)(2,1)S(1)}, u32[]{:S(2)}, u32[]{:S(2)}) %collective-permute-start.15) | collective-permute-done | bytes 2097184 | tf_op jit(solution)/shard_map/ppermute | solution.py:14
  520.0 6.6 fusion.2
  528.3 45.1 %collective-permute-done = bf16[8,8,8,2048]{3,2,1,0:T(8,128)(2,1)S(1)} collective-permute-done((bf16[8,8,8,2048]{3,2,1,0:T(8,128)(2,1)S(1)}, bf16[8,8,8,2048]{3,2,1,0:T(8,128)(2,1)S(1)}, u32[]{:S(2)}, u32[]{:S(2)}) %collective-permute-start) | collective-permute-done | bytes 2097184 | tf_op jit(solution)/shard_map/ppermute | solution.py:14
  575.4 44.2 %collective-permute-done.1 = bf16[8,4,16,2048]{3,2,1,0:T(8,128)(2,1)S(1)} collective-permute-done((bf16[8,4,16,2048]{3,2,1,0:T(8,128)(2,1)S(1)}, bf16[8,4,16,2048]{3,2,1,0:T(8,128)(2,1)S(1)}, u32[]{:S(2)}, u32[]{:S(2)}) %collective-permute-start.1) | collective-permute-done | bytes 2097184 | tf_op jit(solution)/shard_map/ppermute | solution.py:14
  622.8 44.0 %collective-permute-done.2 = bf16[8,2,32,2048]{3,2,1,0:T(8,128)(2,1)S(1)} collective-permute-done((bf16[8,2,32,2048]{3,2,1,0:T(8,128)(2,1)S(1)}, bf16[8,2,32,2048]{3,2,1,0:T(8,128)(2,1)S(1)}, u32[]{:S(2)}, u32[]{:S(2)}) %collective-permute-start.2) | collective-permute-done | bytes 2097184 | tf_op jit(solution)/shard_map/ppermute | solution.py:14
  677.9 84.6 %collective-permute-done.3 = bf16[8,1,64,2048]{3,2,0,1:T(8,128)(2,1)} collective-permute-done((bf16[8,1,64,2048]{3,2,0,1:T(8,128)(2,1)}, bf16[8,1,64,2048]{3,2,0,1:T(8,128)(2,1)}, u32[]{:S(2)}, u32[]{:S(2)}) %collective-permute-start.3) | collective-permute-done | bytes 2097184 | tf_op jit(solution)/shard_map/ppermute | solution.py:14
  765.7 10.0 fusion.17
  775.7 7.8 reshape_reshape.53
  783.4 7.1 constant_dynamic-slice_fusion.1
  794.3 4.5 copy.18
  798.8 40.6 %collective-permute-done.4 = bf16[8,8,8,2048]{3,2,1,0:T(8,128)(2,1)S(1)} collective-permute-done((bf16[8,8,8,2048]{3,2,1,0:T(8,128)(2,1)S(1)}, bf16[8,8,8,2048]{3,2,1,0:T(8,128)(2,1)S(1)}, u32[]{:S(2)}, u32[]{:S(2)}) %collective-permute-start.4) | collective-permute-done | bytes 2097184 | tf_op jit(solution)/shard_map/ppermute | solution.py:14
  841.7 44.2 %collective-permute-done.5 = bf16[8,4,16,2048]{3,2,1,0:T(8,128)(2,1)S(1)} collective-permute-done((bf16[8,4,16,2048]{3,2,1,0:T(8,128)(2,1)S(1)}, bf16[8,4,16,2048]{3,2,1,0:T(8,128)(2,1)S(1)}, u32[]{:S(2)}, u32[]{:S(2)}) %collective-permute-start.5) | collective-permute-done | bytes 2097184 | tf_op jit(solution)/shard_map/ppermute | solution.py:14
  892.3 4.9 fusion.8
  897.1 62.8 %all-reduce = (f32[2048]{0:T(1024)}, f32[2048]{0:T(1024)}) all-reduce(f32[2048]{0:T(1024)S(1)} %get-tuple-element.6, f32[2048]{0:T(1024)S(1)} %get-tuple-element.12), channel_id=1, replica_groups=mesh['dp'=2,'seq'=16] {'dp','seq'}, use_global_device_ids=true, to_apply=%region_5.6 | all-reduce | flops 4096 | bytes 32768 | tf_op jit(solution)/shard_map/psum | solution.py:77
  968.8 12.8 %fusion.23 = f32[8,16,8,16,8]{1,3,2,4,0:T(8,128)} fusion(bf16[8,16,8,2048,1]{3,2,1,0,4:T(8,128)(2,1)S(1)} %bitcast.206, bf16[8,16,8,2048,1]{3,2,1,0,4:T(8,128)(2,1)S(1)} %bitcast.196), kind=kOutput, calls=%fused_computation.33 | convolution fusion | flops 536870912 | bytes 8912896 | tf_op jit(solution)/shard_map/qpbd,srbd->bpqrs/dot_general | solution.py:56
  981.6 9.1 copy.28
  990.7 7.1 reshape.153
  997.8 60.4 %collective-permute-done.7 = bf16[8,1,64,2048]{3,2,0,1:T(8,128)(2,1)S(1)} collective-permute-done((bf16[8,1,64,2048]{3,2,0,1:T(8,128)(2,1)}, bf16[8,1,64,2048]{3,2,0,1:T(8,128)(2,1)S(1)}, u32[]{:S(2)}, u32[]{:S(2)}) %collective-permute-start.7) | collective-permute-done | bytes 2097184 | tf_op jit(solution)/shard_map/ppermute | solution.py:14
  1059.7 10.5 fusion.6
  (93 shorter events, 92.1 us)
Async XLA Ops:
  7.2 425.1 %copy-start = (bf16[8,128,128]{2,1,0:T(8,128)(2,1)S(1)}, bf16[8,128,128]{2,1,0:T(8,128)(2,1)}, u32[]{:S(2)}) copy-start(bf16[8,128,128]{2,1,0:T(8,128)(2,1)} %param.8) | copy-start | bytes 786436
  7.2 1063.0 %all-reduce.4.cloned.1.call-start = ((), (), s32[]{:S(2)}) async-start(), calls=%async_computation | async-start | bytes 2097152 | tf_op jit(solution)/shard_map/psum | solution.py:76
  10.4 48.8 %collective-permute-start.8 = (bf16[8,8,8,2048]{3,2,1,0:T(8,128)(2,1)}, bf16[8,8,8,2048]{3,2,1,0:T(8,128)(2,1)S(1)}, u32[]{:S(2)}, u32[]{:S(2)}) collective-permute-start(bf16[8,8,8,2048]{3,2,1,0:T(8,128)(2,1)} %dynamic-slice_bitcast_fusion.6), channel_id=1, source_target_pairs={{0,1},{1,0},{2,3},{3,2},{4,5},{5,4},{6,7},{7,6},{8,9},{9,8},{10,11... | collective-permute-start | bytes 6291464 | tf_op jit(solution)/shard_map/ppermute | solution.py:14
  63.8 47.0 %collective-permute-start.9 = (bf16[8,4,16,2048]{3,2,1,0:T(8,128)(2,1)}, bf16[8,4,16,2048]{3,2,1,0:T(8,128)(2,1)S(1)}, u32[]{:S(2)}, u32[]{:S(2)}) collective-permute-start(bf16[8,4,16,2048]{3,2,1,0:T(8,128)(2,1)} %dynamic-slice_bitcast_fusion.5), channel_id=1, source_target_pairs={{0,2},{2,0},{1,3},{3,1},{4,6},{6,4},{5,7},{7,5},{8,10},{10,8},{9,1... | collective-permute-start | bytes 6291464 | tf_op jit(solution)/shard_map/ppermute | solution.py:14
  115.5 46.1 %collective-permute-start.10 = (bf16[8,2,32,2048]{3,2,1,0:T(8,128)(2,1)}, bf16[8,2,32,2048]{3,2,1,0:T(8,128)(2,1)S(1)}, u32[]{:S(2)}, u32[]{:S(2)}) collective-permute-start(bf16[8,2,32,2048]{3,2,1,0:T(8,128)(2,1)} %dynamic-slice_bitcast_fusion.4), channel_id=1, source_target_pairs={{0,4},{4,0},{1,5},{5,1},{2,6},{6,2},{3,7},{7,3},{8,12},{12,8},{9,1... | collective-permute-start | bytes 6291464 | tf_op jit(solution)/shard_map/ppermute | solution.py:14
  117.0 51.4 %copy-start.13 = (bf16[8,128,128]{2,1,0:T(8,128)(2,1)S(1)}, bf16[8,128,128]{2,1,0:T(8,128)(2,1)}, u32[]{:S(2)}) copy-start(bf16[8,128,128]{2,1,0:T(8,128)(2,1)} %param.9) | copy-start | bytes 786436
  166.2 91.1 %collective-permute-start.11 = (bf16[8,1,64,2048]{3,2,0,1:T(8,128)(2,1)}, bf16[8,1,64,2048]{3,2,0,1:T(8,128)(2,1)}, u32[]{:S(2)}, u32[]{:S(2)}) collective-permute-start(bf16[8,1,64,2048]{3,2,0,1:T(8,128)(2,1)} %dynamic-slice_bitcast_fusion.3), channel_id=1, source_target_pairs={{0,8},{8,0},{1,9},{9,1},{2,10},{10,2},{3,11},{11,3},{4,12},{12,4},... | collective-permute-start | bytes 6291464 | tf_op jit(solution)/shard_map/ppermute | solution.py:14
  285.4 3.1 copy-start.6
  287.7 47.2 %collective-permute-start.12 = (bf16[8,8,8,2048]{3,2,1,0:T(8,128)(2,1)S(1)}, bf16[8,8,8,2048]{3,2,1,0:T(8,128)(2,1)S(1)}, u32[]{:S(2)}, u32[]{:S(2)}) collective-permute-start(bf16[8,8,8,2048]{3,2,1,0:T(8,128)(2,1)S(1)} %bitcast.207), channel_id=1, source_target_pairs={{0,1},{1,0},{2,3},{3,2},{4,5},{5,4},{6,7},{7,6},{8,9},{9,8},{10,11... | collective-permute-start | bytes 6291464 | tf_op jit(solution)/shard_map/ppermute | solution.py:14
  335.7 46.3 %collective-permute-start.13 = (bf16[8,4,16,2048]{3,2,1,0:T(8,128)(2,1)S(1)}, bf16[8,4,16,2048]{3,2,1,0:T(8,128)(2,1)S(1)}, u32[]{:S(2)}, u32[]{:S(2)}) collective-permute-start(bf16[8,4,16,2048]{3,2,1,0:T(8,128)(2,1)S(1)} %dynamic-slice_bitcast_fusion.2), channel_id=1, source_target_pairs={{0,2},{2,0},{1,3},{3,1},{4,6},{6,4},{5,7},{7,5},{8,10},{10,8},{9,1... | collective-permute-start | bytes 6291464 | tf_op jit(solution)/shard_map/ppermute | solution.py:14
  382.5 48.9 %copy-start.2 = (bf16[1,1024,2048]{2,1,0:T(8,128)(2,1)S(1)}, bf16[1,1024,2048]{2,1,0:T(8,128)(2,1)}, u32[]{:S(2)}) copy-start(bf16[1,1024,2048]{2,1,0:T(8,128)(2,1)} %param.6) | copy-start | bytes 12582916
  382.5 45.4 %collective-permute-start.14 = (bf16[8,2,32,2048]{3,2,1,0:T(8,128)(2,1)S(1)}, bf16[8,2,32,2048]{3,2,1,0:T(8,128)(2,1)S(1)}, u32[]{:S(2)}, u32[]{:S(2)}) collective-permute-start(bf16[8,2,32,2048]{3,2,1,0:T(8,128)(2,1)S(1)} %dynamic-slice_bitcast_fusion.1), channel_id=1, source_target_pairs={{0,4},{4,0},{1,5},{5,1},{2,6},{6,2},{3,7},{7,3},{8,12},{12,8},{9,1... | collective-permute-start | bytes 6291464 | tf_op jit(solution)/shard_map/ppermute | solution.py:14
  428.2 4.1 copy-start.14
  428.5 91.3 %collective-permute-start.15 = (bf16[8,1,64,2048]{3,2,0,1:T(8,128)(2,1)S(1)}, bf16[8,1,64,2048]{3,2,0,1:T(8,128)(2,1)S(1)}, u32[]{:S(2)}, u32[]{:S(2)}) collective-permute-start(bf16[8,1,64,2048]{3,2,0,1:T(8,128)(2,1)S(1)} %dynamic-slice_bitcast_fusion), channel_id=1, source_target_pairs={{0,8},{8,0},{1,9},{9,1},{2,10},{10,2},{3,11},{11,3},{4,12},{12,4},... | collective-permute-start | bytes 6291464 | tf_op jit(solution)/shard_map/ppermute | solution.py:14
  433.7 86.3 %copy-start.15 = (f32[2048]{0:T(1024)S(1)}, f32[2048]{0:T(1024)}, u32[]{:S(2)}) copy-start(f32[2048]{0:T(1024)} %param.11) | copy-start | bytes 24580
  526.8 46.7 %collective-permute-start = (bf16[8,8,8,2048]{3,2,1,0:T(8,128)(2,1)S(1)}, bf16[8,8,8,2048]{3,2,1,0:T(8,128)(2,1)S(1)}, u32[]{:S(2)}, u32[]{:S(2)}) collective-permute-start(bf16[8,8,8,2048]{3,2,1,0:T(8,128)(2,1)S(1)} %dynamic-slice_bitcast_fusion.13), channel_id=1, source_target_pairs={{0,1},{1,0},{2,3},{3,2},{4,5},{5,4},{6,7},{7,6},{8,9},{9,8},{10,11... | collective-permute-start | bytes 6291464 | tf_op jit(solution)/shard_map/ppermute | solution.py:14
  573.8 45.7 %collective-permute-start.1 = (bf16[8,4,16,2048]{3,2,1,0:T(8,128)(2,1)S(1)}, bf16[8,4,16,2048]{3,2,1,0:T(8,128)(2,1)S(1)}, u32[]{:S(2)}, u32[]{:S(2)}) collective-permute-start(bf16[8,4,16,2048]{3,2,1,0:T(8,128)(2,1)S(1)} %dynamic-slice_bitcast_fusion.12), channel_id=1, source_target_pairs={{0,2},{2,0},{1,3},{3,1},{4,6},{6,4},{5,7},{7,5},{8,10},{10,8},{9,1... | collective-permute-start | bytes 6291464 | tf_op jit(solution)/shard_map/ppermute | solution.py:14
  620.0 46.8 %collective-permute-start.2 = (bf16[8,2,32,2048]{3,2,1,0:T(8,128)(2,1)S(1)}, bf16[8,2,32,2048]{3,2,1,0:T(8,128)(2,1)S(1)}, u32[]{:S(2)}, u32[]{:S(2)}) collective-permute-start(bf16[8,2,32,2048]{3,2,1,0:T(8,128)(2,1)S(1)} %dynamic-slice_bitcast_fusion.11), channel_id=1, source_target_pairs={{0,4},{4,0},{1,5},{5,1},{2,6},{6,2},{3,7},{7,3},{8,12},{12,8},{9,1... | collective-permute-start | bytes 6291464 | tf_op jit(solution)/shard_map/ppermute | solution.py:14
  670.5 92.0 %collective-permute-start.3 = (bf16[8,1,64,2048]{3,2,0,1:T(8,128)(2,1)}, bf16[8,1,64,2048]{3,2,0,1:T(8,128)(2,1)}, u32[]{:S(2)}, u32[]{:S(2)}) collective-permute-start(bf16[8,1,64,2048]{3,2,0,1:T(8,128)(2,1)} %dynamic-slice_bitcast_fusion.10), channel_id=1, source_target_pairs={{0,8},{8,0},{1,9},{9,1},{2,10},{10,2},{3,11},{11,3},{4,12},{12,4},... | collective-permute-start | bytes 6291464 | tf_op jit(solution)/shard_map/ppermute | solution.py:14
  790.5 3.8 copy-start.7
  792.8 46.7 %collective-permute-start.4 = (bf16[8,8,8,2048]{3,2,1,0:T(8,128)(2,1)S(1)}, bf16[8,8,8,2048]{3,2,1,0:T(8,128)(2,1)S(1)}, u32[]{:S(2)}, u32[]{:S(2)}) collective-permute-start(bf16[8,8,8,2048]{3,2,1,0:T(8,128)(2,1)S(1)} %bitcast.208), channel_id=1, source_target_pairs={{0,1},{1,0},{2,3},{3,2},{4,5},{5,4},{6,7},{7,6},{8,9},{9,8},{10,11... | collective-permute-start | bytes 6291464 | tf_op jit(solution)/shard_map/ppermute | solution.py:14
  840.1 52.2 %copy-start.3 = (bf16[1,1024,2048]{2,1,0:T(8,128)(2,1)S(1)}, bf16[1,1024,2048]{2,1,0:T(8,128)(2,1)}, u32[]{:S(2)}) copy-start(bf16[1,1024,2048]{2,1,0:T(8,128)(2,1)} %param.6) | copy-start | bytes 12582916
  840.1 52.2 %copy-start.11 = (bf16[8,128,2048]{2,1,0:T(8,128)(2,1)S(1)}, bf16[8,128,2048]{2,1,0:T(8,128)(2,1)}, u32[]{:S(2)}) copy-start(bf16[8,128,2048]{2,1,0:T(8,128)(2,1)} %get-tuple-element.13) | copy-start | bytes 12582916
  840.1 45.7 %collective-permute-start.5 = (bf16[8,4,16,2048]{3,2,1,0:T(8,128)(2,1)S(1)}, bf16[8,4,16,2048]{3,2,1,0:T(8,128)(2,1)S(1)}, u32[]{:S(2)}, u32[]{:S(2)}) collective-permute-start(bf16[8,4,16,2048]{3,2,1,0:T(8,128)(2,1)S(1)} %dynamic-slice_bitcast_fusion.9), channel_id=1, source_target_pairs={{0,2},{2,0},{1,3},{3,1},{4,6},{6,4},{5,7},{7,5},{8,10},{10,8},{9,1... | collective-permute-start | bytes 6291464 | tf_op jit(solution)/shard_map/ppermute | solution.py:14
  886.1 2.0 copy-start.1
  889.5 70.4 %collective-permute-start.6 = (bf16[8,2,32,2048]{3,2,1,0:T(8,128)(2,1)}, bf16[8,2,32,2048]{3,2,1,0:T(8,128)(2,1)S(1)}, u32[]{:S(2)}, u32[]{:S(2)}) collective-permute-start(bf16[8,2,32,2048]{3,2,1,0:T(8,128)(2,1)} %dynamic-slice_bitcast_fusion.8), channel_id=1, source_target_pairs={{0,4},{4,0},{1,5},{5,1},{2,6},{6,2},{3,7},{7,3},{8,12},{12,8},{9,1... | collective-permute-start | bytes 6291464 | tf_op jit(solution)/shard_map/ppermute | solution.py:14
  959.9 6.5 copy-start.4
  959.9 6.5 copy-start.12
  965.3 3.2 copy-start.9
  965.3 3.5 copy-start.10
  965.3 92.9 %collective-permute-start.7 = (bf16[8,1,64,2048]{3,2,0,1:T(8,128)(2,1)}, bf16[8,1,64,2048]{3,2,0,1:T(8,128)(2,1)S(1)}, u32[]{:S(2)}, u32[]{:S(2)}) collective-permute-start(bf16[8,1,64,2048]{3,2,0,1:T(8,128)(2,1)} %dynamic-slice_bitcast_fusion.7), channel_id=1, source_target_pairs={{0,8},{8,0},{1,9},{9,1},{2,10},{10,2},{3,11},{11,3},{4,12},{12,4},... | collective-permute-start | bytes 6291464 | tf_op jit(solution)/shard_map/ppermute | solution.py:14
  997.8 61.9 %copy-start.5 = (bf16[1,1024,2048]{2,1,0:T(8,128)(2,1)S(1)}, bf16[1,1024,2048]{2,1,0:T(8,128)(2,1)}, u32[]{:S(2)}) copy-start(bf16[1,1024,2048]{2,1,0:T(8,128)(2,1)} %param.6) | copy-start | bytes 12582916
  (1 other events, 2.0 us)
Sparse Core Ops, SparseCore 0:
  997.9 19.3 all-reduce.3
where the time goes:
time: 1090 us; the launch traced here: 1080 us
  waiting for transfers between devices  789 us (72%)
  local copies, waits for them, and re-layouts  126 us (12%)
  blocking collectives  62.8 us (6%)
  matrix products  41.1 us (4%)
  starting transfers between devices  29.4 us (3%)
  other arithmetic  18 us (2%)
  between operations  14.7 us (1%)
    ppermute x16, waiting for transfers between devices, from_partner(): return lax.ppermute(block, axis, route)  789 us
    psum x1, blocking collectives, body(): gain_gradient, grad_mid = lax.psum((gain_slice, mid_part), ('dp', 'seq'))  62.8 us
    ppermute x16, starting transfers between devices, from_partner(): return lax.ppermute(block, axis, route)  29.3 us
    another operation x4, local copies, waits for them, and re-layouts, regroup(): current.reshape(height, count >> level + 1, 2, (1 << level) * piece, width)  24.5 us
  transfers between devices with their start and end apart: 17, of which 15 were waited for; matrix products, arithmetic and copies ran while one was open for 7% of the time, Pallas kernels for 0%

commit v1 on v0

v1 whole, which is shorter than its diff:
```python
import jax
import jax.numpy as jnp
from jax import lax
from jax.sharding import PartitionSpec as P


def to_offsets(rows):
    return lax.all_to_all(rows, "seq", 1, 0, tiled=True)


def to_blocks(rows):
    return lax.all_to_all(rows, "seq", 0, 1, tiled=True)


def body(inputs, upstream, right_blocks, left_blocks, gain, mid_scale):
    count = lax.axis_size("seq")
    rows = inputs.shape[1]
    width = inputs.shape[2]
    order = right_blocks.shape[1]
    local = order // count
    f32 = jnp.float32
    bf16 = jnp.bfloat16
    upward = to_offsets(upstream[0].reshape(local, order, width))
    input_float = inputs[0].astype(f32)
    inverse_norm = lax.rsqrt(jnp.mean(input_float * input_float, axis=-1, keepdims=True) + 1e-06)
    standardized_input = input_float * inverse_norm
    normalized_rows = (standardized_input * gain).astype(bf16)
    grid = normalized_rows.reshape(local, order, width)
    first = jnp.einsum("aij,ajd->aid", right_blocks, grid, preferred_element_type=f32)
    sig = jax.nn.sigmoid(first * mid_scale)
    gated = (first * sig).astype(bf16)
    arrived = to_offsets(gated)
    returned = jnp.einsum("bij,ibd->jbd", left_blocks, upward, preferred_element_type=f32).astype(bf16)
    dgated = to_blocks(returned).astype(f32)
    mixed = jnp.einsum("bij,jbd->ibd", left_blocks, arrived, preferred_element_type=f32).astype(bf16)
    back = to_blocks(mixed).reshape(rows, width)
    grad_left = jnp.einsum("ibd,jbd->bij", upward, arrived, preferred_element_type=f32)
    output = (input_float + back.astype(f32)).astype(bf16)
    slope = sig * (1.0 - sig)
    dfirst = (dgated * (sig + first * mid_scale * slope)).astype(bf16)
    mid_part = jnp.sum(dgated * first * first * slope, axis=(0, 1))
    grad_right = jnp.einsum("aid,ajd->aij", dfirst, grid, preferred_element_type=f32)
    normalized_gradient = jnp.einsum(
        "aij,aid->ajd", right_blocks, dfirst, preferred_element_type=f32
    ).reshape(rows, width)
    gain_slice = jnp.sum(normalized_gradient * standardized_input, axis=0)
    centered_gradient = normalized_gradient * gain
    input_gradient = upstream[0].astype(f32) + inverse_norm * (
        centered_gradient
        - standardized_input
        * jnp.mean(centered_gradient * standardized_input, axis=-1, keepdims=True)
    )
    input_gradient = input_gradient.astype(bf16)
    grad_left = lax.psum(grad_left, "dp")
    grad_right = lax.psum(grad_right, "dp")
    gain_gradient, grad_mid = lax.psum((gain_slice, mid_part), ("dp", "seq"))
    return (
        output.reshape(1, rows, width),
        input_gradient.reshape(1, rows, width),
        grad_right,
        grad_left,
        gain_gradient,
        grad_mid,
    )


def solution(mesh):
    in_specs = (
        P("dp", "seq", None),
        P("dp", "seq", None),
        P("seq", None, None),
        P("seq", None, None),
        P(),
        P(),
    )
    out_specs = (
        P("dp", "seq", None),
        P("dp", "seq", None),
        P("seq", None, None),
        P("seq", None, None),
        P(),
        P(),
    )
    return jax.shard_map(body, mesh=mesh, in_specs=in_specs, out_specs=out_specs, check_vma=False)
```

time: 1090 us -> 508 us (0.47)
  waiting for transfers between devices: 789 us -> 75.2 us
  blocking collectives: 62.8 us -> 305 us
  local copies, waits for them, and re-layouts: 126 us -> 33.9 us
  starting transfers between devices: 29.4 us -> 9.88 us
    ppermute x16 -> x0, waiting for transfers between devices: 789 us -> none  [from_partner(): return lax.ppermute(block, axis, route)]
    all_to_all x0 -> x2, blocking collectives: none -> 213 us  [to_offsets(): return lax.all_to_all(rows, 'seq', 1, 0, tiled=True)]
    all_to_all x0 -> x2, waiting for transfers between devices: none -> 75.2 us  [to_blocks(): return lax.all_to_all(rows, 'seq', 0, 1, tiled=True)]
    ppermute x16 -> x0, starting transfers between devices: 29.3 us -> none  [from_partner(): return lax.ppermute(block, axis, route)]
    psum x1, blocking collectives: 62.8 us -> 91.3 us  [body(): gain_gradient, grad_mid = lax.psum((gain_slice, mid_part), ('dp', 'seq'))]
    reshape x4 -> x0, local copies, waits for them, and re-layouts: 23.9 us -> none  [the longest x3 16.8 us: body(): lefts = left_blocks.reshape(local, count, local, count, local)]
    squeeze x14 -> x0, local copies, waits for them, and re-layouts: 20.7 us -> none  [regroup(): outgoing = lax.dynamic_index_in_dim(view, other, axis=2, keepdims=False)]
    another operation x4 -> x1, local copies, waits for them, and re-layouts: 24.5 us -> 4.53 us  [body(): upward = to_offsets(upstream[0].reshape(local, order, width))]
  transfers between devices with their start and end apart: 17 -> 3, of which waited for: 15 -> 1; matrix products, arithmetic and copies ran while one was open for 7% -> 5% of each run, Pallas kernels for 0% -> 0%
where the time goes in v1:
time: 508 us; the launch traced here: 499 us
  blocking collectives  305 us (60%)
  waiting for transfers between devices  75.2 us (15%)
  matrix products  44.1 us (9%)
  local copies, waits for them, and re-layouts  33.9 us (7%)
  other arithmetic  16.6 us (3%)
  between operations  14.4 us (3%)
  starting transfers between devices  9.88 us (2%)
    all_to_all x2, blocking collectives, to_offsets(): return lax.all_to_all(rows, 'seq', 1, 0, tiled=True)  213 us
    psum x1, blocking collectives, body(): gain_gradient, grad_mid = lax.psum((gain_slice, mid_part), ('dp', 'seq'))  91.3 us
    all_to_all x2, waiting for transfers between devices, to_blocks(): return lax.all_to_all(rows, 'seq', 0, 1, tiled=True)  75.2 us
    convert_element_type x1, other arithmetic, body(): input_gradient = input_gradient.astype(bf16)  10.3 us
  transfers between devices with their start and end apart: 3, of which 1 were waited for; matrix products, arithmetic and copies ran while one was open for 5% of the time, Pallas kernels for 0%

profile of v1, /device:TPU:0, one launch (start us, length us, event | category | flops | bytes accessed | tf_op | source)
XLA Modules:
  0.0 498.9 jit_solution(11240432389978212156)
XLA Ops:
  7.2 0.0 copy-start
  7.2 4.5 copy.61
  11.7 101.9 %all_to_all.54 = bf16[8,128,2048]{2,0,1:T(8,128)(2,1)S(1)} all-to-all(bf16[8,128,2048]{2,0,1:T(8,128)(2,1)S(1)} %copy.61), channel_id=1, replica_groups=mesh['dp'=2,'seq'=16] {'seq'}, dimensions={1} | all-to-all | bytes 8388608 | tf_op jit(solution)/shard_map/all_to_all | solution.py:8
  113.6 2.8 copy.63
  116.4 1.9 copy-done.1
  118.4 6.8 %convert_bitcast_fusion.2 = bf16[128,8,2048]{0,2,1:T(8,128)(2,1)} fusion(bf16[8,128,128]{2,1,0:T(8,128)(2,1)S(1)} %copy-done.5, bf16[128,8,2048]{2,1,0:T(8,128)(2,1)S(1)} %bitcast.79), kind=kOutput, calls=%fused_computation.25 | convolution fusion | flops 538968064 | bytes 8650752 | tf_op jit(solution)/shard_map/bij,ibd->jbd/dot_general | solution.py:33
  125.1 6.7 %copy.65 = bf16[128,8,2048]{2,1,0:T(8,128)(2,1)} copy(bf16[128,8,2048]{0,2,1:T(8,128)(2,1)} %convert_bitcast_fusion.2) | data formatting | bytes 8388608 | tf_op jit(solution)/shard_map/convert_element_type | solution.py:33
  131.8 5.1 %all-to-all-start.3 = ((bf16[128,8,2048]{2,1,0:T(8,128)(2,1)}), bf16[128,8,2048]{2,1,0:T(8,128)(2,1)}, u32[]{:S(2)}, u32[]{:S(2)}) async-start(bf16[128,8,2048]{2,1,0:T(8,128)(2,1)} %copy.65), calls=%async_computation.3 | async-start | bytes 8388608 | tf_op jit(solution)/shard_map/all_to_all | solution.py:12
  136.9 0.0 copy-start.7
  136.9 0.0 copy-start.8
  136.9 3.1 multiply_reduce_fusion
  140.0 75.2 %all-to-all-done.3 = bf16[128,8,2048]{2,1,0:T(8,128)(2,1)} async-done(((bf16[128,8,2048]{2,1,0:T(8,128)(2,1)}), bf16[128,8,2048]{2,1,0:T(8,128)(2,1)}, u32[]{:S(2)}, u32[]{:S(2)}) %all-to-all-start.3) | async-done | bytes 4194336 | tf_op jit(solution)/shard_map/all_to_all | solution.py:12
  215.2 10.1 %fusion.1 = (f32[2048]{0:T(1024)S(1)}, bf16[8,128,2048]{2,1,0:T(8,128)(2,1)}, bf16[8,128,2048]{2,1,0:T(8,128)(2,1)S(1)}) fusion(f32[2048]{0:T(1024)S(1)} %copy-done.8, bf16[8,128,128]{2,1,0:T(8,128)(2,1)S(1)} %copy-done, f32[2048]{0:T(1024)S(1)} %copy-done.7, f32[8,128]{1,0:T(8,128)S(1)} %get-tuple-element.48, bf16[8,128,2048]{2,1,0:T(8,128)(2,1)} %bitcast.85, ...), kind=kOutput, calls=%fused_computation.3 | convolution fusion | flops 580909056 | bytes 17068032 | tf_op jit(solution)/shard_map/aij,ajd->aid/dot_general | solution.py:29
  225.3 2.3 copy.55
  227.6 111.6 %all_to_all.55 = bf16[8,128,2048]{2,0,1:T(8,128)(2,1)S(1)} all-to-all(bf16[8,128,2048]{2,0,1:T(8,128)(2,1)S(1)} %copy.55), channel_id=1, replica_groups=mesh['dp'=2,'seq'=16] {'seq'}, dimensions={1} | all-to-all | bytes 8388608 | tf_op jit(solution)/shard_map/all_to_all | solution.py:8
  339.2 2.8 copy.57
  342.0 2.0 copy-done.3
  344.0 6.8 %convert_bitcast_fusion.3 = bf16[128,8,2048]{0,2,1:T(8,128)(2,1)} fusion(bf16[8,128,128]{2,1,0:T(8,128)(2,1)S(1)} %copy-done.5, bf16[128,8,2048]{2,1,0:T(8,128)(2,1)S(1)} %bitcast.81), kind=kOutput, calls=%fused_computation.26 | convolution fusion | flops 538968064 | bytes 8650752 | tf_op jit(solution)/shard_map/bij,jbd->ibd/dot_general | solution.py:35
  350.7 6.7 %copy.59 = bf16[128,8,2048]{2,1,0:T(8,128)(2,1)} copy(bf16[128,8,2048]{0,2,1:T(8,128)(2,1)} %convert_bitcast_fusion.3) | data formatting | bytes 8388608 | tf_op jit(solution)/shard_map/convert_element_type | solution.py:35
  357.5 4.6 all-to-all-start.1
  362.0 0.3 all-reduce.4.cloned.1.call-start
  362.3 5.7 %fusion.21 = f32[8,128,128]{2,1,0:T(8,128)} fusion(bf16[8,128,2048]{2,1,0:T(8,128)(2,1)} %get-tuple-element.43, f32[2048]{0:T(1024)S(1)} %copy-done.7, f32[8,128]{1,0:T(8,128)S(1)} %get-tuple-element.48, bf16[8,128,2048]{2,1,0:T(8,128)(2,1)} %bitcast.86), kind=kOutput, calls=%fused_computation.33 | convolution fusion | flops 545259520 | bytes 8925184 | tf_op jit(solution)/shard_map/aid,ajd->aij/dot_general | solution.py:42
  368.1 0.2 copy-done.4
  368.2 5.2 %fusion.16 = f32[8,128,128]{1,2,0:T(8,128)} fusion(bf16[128,8,2048]{2,1,0:T(8,128)(2,1)S(1)} %bitcast.80, bf16[128,8,2048]{2,1,0:T(8,128)(2,1)S(1)} %bitcast.82), kind=kOutput, calls=%fused_computation.32 | convolution fusion | flops 536870912 | bytes 8912896 | tf_op jit(solution)/shard_map/ibd,jbd->bij/dot_general | solution.py:37
  373.5 0.0 all-reduce.4.cloned.1.call-update
  373.5 9.5 %fusion.6 = (f32[2048]{0:T(1024)S(1)}, f32[8,128]{1,0:T(8,128)S(1)}, f32[8,2048,128]{1,2,0:T(8,128)}) fusion(f32[8,128]{1,0:T(8,128)S(1)} %get-tuple-element.48, f32[2048]{0:T(1024)S(1)} %copy-done.7, bf16[8,128,2048]{2,1,0:T(8,128)(2,1)} %get-tuple-element.43, bf16[8,128,128]{2,1,0:T(8,128)(2,1)S(1)} %copy-done, bf16[8,128,2048]{2,1,0:T(8,128)(2,1)} %bitcast.87), kind=kOutput, calls=%fused_computation.13 | convolution fusion | flops 551547904 | bytes 17063936 | tf_op jit(solution)/shard_map/aij,aid->ajd/dot_general | solution.py:43
  383.0 91.3 %all-reduce = (f32[2048]{0:T(1024)}, f32[2048]{0:T(1024)}) all-reduce(f32[2048]{0:T(1024)S(1)} %get-tuple-element.36, f32[2048]{0:T(1024)S(1)} %get-tuple-element.42), channel_id=1, replica_groups=mesh['dp'=2,'seq'=16] {'dp','seq'}, use_global_device_ids=true, to_apply=%region_5.0 | all-reduce | flops 4096 | bytes 32768 | tf_op jit(solution)/shard_map/psum | solution.py:56
  474.3 2.0 copy.70
  476.3 3.2 convert_bitcast_fusion.1
  479.6 1.1 copy.60
  480.7 10.3 %fusion.5 = (bf16[1,1024,2048]{2,1,0:T(8,128)(2,1)}, bf16[1,1024,2048]{2,1,0:T(8,128)(2,1)}) fusion(f32[8,2048,128]{1,2,0:T(8,128)} %get-tuple-element.49, bf16[1,1024,2048]{2,1,0:T(8,128)(2,1)} %param.7, bf16[1,1024,2048]{2,1,0:T(8,128)(2,1)} %param.6, f32[1024]{0:T(1024)S(1)} %multiply_bitcast_fusion, f32[2048]{0:T(1024)S(1)} %copy-done.7, ...), kind=kLoop, calls=%fused_computation.8 | loop fusion | flops 23068672 | bytes 33570816 | tf_op jit(solution)/shard_map/convert_element_type | solution.py:53
  491.0 0.8 copy.90
  (16 shorter events, 0.0 us)
Async XLA Ops:
  7.2 208.0 %copy-start = (bf16[8,128,128]{2,1,0:T(8,128)(2,1)S(1)}, bf16[8,128,128]{2,1,0:T(8,128)(2,1)}, u32[]{:S(2)}) copy-start(bf16[8,128,128]{2,1,0:T(8,128)(2,1)} %param.8) | copy-start | bytes 786436
  113.6 4.7 copy-start.5
  116.4 1.9 copy-start.1
  131.8 83.4 %all-to-all-start.3 = ((bf16[128,8,2048]{2,1,0:T(8,128)(2,1)}), bf16[128,8,2048]{2,1,0:T(8,128)(2,1)}, u32[]{:S(2)}, u32[]{:S(2)}) async-start(bf16[128,8,2048]{2,1,0:T(8,128)(2,1)} %copy.65), calls=%async_computation.3 | async-start | bytes 8388608 | tf_op jit(solution)/shard_map/all_to_all | solution.py:12
  136.9 78.3 %copy-start.7 = (f32[2048]{0:T(1024)S(1)}, f32[2048]{0:T(1024)}, u32[]{:S(2)}) copy-start(f32[2048]{0:T(1024)} %param.10) | copy-start | bytes 24580
  136.9 78.3 %copy-start.8 = (f32[2048]{0:T(1024)S(1)}, f32[2048]{0:T(1024)}, u32[]{:S(2)}) copy-start(f32[2048]{0:T(1024)} %param.11) | copy-start | bytes 24580
  342.0 2.0 copy-start.3
  357.5 118.9 %all-to-all-start.1 = ((bf16[128,8,2048]{2,1,0:T(8,128)(2,1)}), bf16[128,8,2048]{2,1,0:T(8,128)(2,1)}, u32[]{:S(2)}, u32[]{:S(2)}) async-start(bf16[128,8,2048]{2,1,0:T(8,128)(2,1)} %copy.59), calls=%async_computation.1 | async-start | bytes 8388608 | tf_op jit(solution)/shard_map/all_to_all | solution.py:12
  362.0 112.3 %all-reduce.4.cloned.1.call-start = ((), (), s32[]{:S(2)}) async-start(), calls=%async_computation.4 | async-start | bytes 2097152 | tf_op jit(solution)/shard_map/psum | solution.py:55
  362.3 5.8 %copy-start.2 = (bf16[16,8,8,2048]{3,2,1,0:T(8,128)(2,1)S(1)}, bf16[16,8,8,2048]{3,2,1,0:T(8,128)(2,1)}, u32[]{:S(2)}) copy-start(bf16[16,8,8,2048]{3,2,1,0:T(8,128)(2,1)} %copy-done.1) | copy-start | bytes 12582916
  362.3 5.9 %copy-start.4 = (bf16[16,8,8,2048]{3,2,1,0:T(8,128)(2,1)S(1)}, bf16[16,8,8,2048]{3,2,1,0:T(8,128)(2,1)}, u32[]{:S(2)}) copy-start(bf16[16,8,8,2048]{3,2,1,0:T(8,128)(2,1)} %copy-done.3) | copy-start | bytes 12582916
  480.7 10.3 %copy-start.6 = (f32[8,128,128]{2,1,0:T(8,128)S(1)}, f32[8,128,128]{2,1,0:T(8,128)}, u32[]{:S(2)}) copy-start(f32[8,128,128]{2,1,0:T(8,128)} %get-tuple-element.52) | copy-start | bytes 1572868
Sparse Core Ops, SparseCore 0:
  373.6 20.8 all-reduce.3

commit v2 on v1

--- a/solution.py
+++ b/solution.py
@@ -5,11 +5,19 @@
 
 
 def to_offsets(rows):
-    return lax.all_to_all(rows, "seq", 1, 0, tiled=True)
+    count = lax.axis_size("seq")
+    height, span, width = rows.shape
+    parts = rows.reshape(height, count, span // count, width).swapaxes(0, 1)
+    parts = lax.all_to_all(parts, "seq", 0, 0, tiled=True)
+    return parts.reshape(count * height, span // count, width)
 
 
 def to_blocks(rows):
-    return lax.all_to_all(rows, "seq", 0, 1, tiled=True)
+    count = lax.axis_size("seq")
+    span, height, width = rows.shape
+    parts = rows.reshape(count, span // count, height, width)
+    parts = lax.all_to_all(parts, "seq", 0, 0, tiled=True)
+    return parts.swapaxes(0, 1).reshape(span // count, count * height, width)
 
 
 def body(inputs, upstream, right_blocks, left_blocks, gain, mid_scale):
@@ -29,13 +37,17 @@
     first = jnp.einsum("aij,ajd->aid", right_blocks, grid, preferred_element_type=f32)
     sig = jax.nn.sigmoid(first * mid_scale)
     gated = (first * sig).astype(bf16)
+    gated, upward = lax.optimization_barrier((gated, upward))
     arrived = to_offsets(gated)
     returned = jnp.einsum("bij,ibd->jbd", left_blocks, upward, preferred_element_type=f32).astype(bf16)
-    dgated = to_blocks(returned).astype(f32)
+    arrived, returned = lax.optimization_barrier((arrived, returned))
+    dgated = to_blocks(returned)
     mixed = jnp.einsum("bij,jbd->ibd", left_blocks, arrived, preferred_element_type=f32).astype(bf16)
+    grad_left = jnp.einsum("ibd,jbd->bij", upward, arrived, preferred_element_type=f32)
+    mixed, dgated, grad_left = lax.optimization_barrier((mixed, dgated, grad_left))
     back = to_blocks(mixed).reshape(rows, width)
-    grad_left = jnp.einsum("ibd,jbd->bij", upward, arrived, preferred_element_type=f32)
     output = (input_float + back.astype(f32)).astype(bf16)
+    dgated = dgated.astype(f32)
     slope = sig * (1.0 - sig)
     dfirst = (dgated * (sig + first * mid_scale * slope)).astype(bf16)
     mid_part = jnp.sum(dgated * first * first * slope, axis=(0, 1))
@@ -53,7 +65,8 @@
     input_gradient = input_gradient.astype(bf16)
     grad_left = lax.psum(grad_left, "dp")
     grad_right = lax.psum(grad_right, "dp")
-    gain_gradient, grad_mid = lax.psum((gain_slice, mid_part), ("dp", "seq"))
+    vectors = lax.all_gather(jnp.stack((gain_slice, mid_part)), ("dp", "seq"))
+    gain_gradient, grad_mid = jnp.sum(vectors, axis=0)
     return (
         output.reshape(1, rows, width),
         input_gradient.reshape(1, rows, width),

time: 508 us -> 514 us (1.012); the launches traced: 499 us -> 513 us
  blocking collectives: 305 us -> 127 us
  waiting for transfers between devices: 75.2 us -> 197 us
  starting transfers between devices: 9.88 us -> 67.4 us
  other arithmetic: 16.6 us -> 24.3 us
    all_to_all x2 -> x0, blocking collectives: 213 us -> none  [to_offsets(): return lax.all_to_all(rows, 'seq', 1, 0, tiled=True)]
    all_gather x0 -> x1, blocking collectives: none -> 127 us  [body(): vectors = lax.all_gather(jnp.stack((gain_slice, mid_part)), ('dp', 'seq'))]
    all_to_all x2 -> x4, waiting for transfers between devices: 75.2 us -> 197 us  [the longest x2 137 us: to_offsets(): parts = lax.all_to_all(parts, 'seq', 0, 0, tiled=True)]
    psum x1 -> x0, blocking collectives: 91.3 us -> none  [body(): gain_gradient, grad_mid = lax.psum((gain_slice, mid_part), ('dp', 'seq'))]
    all_to_all x2 -> x4, starting transfers between devices: 9.63 us -> 67.2 us  [the longest x2 38.6 us: to_blocks(): parts = lax.all_to_all(parts, 'seq', 0, 0, tiled=True)]
    convert_element_type x3 -> x0, local copies, waits for them, and re-layouts: 15.7 us -> none  [the longest x1 6.75 us: body(): jnp.einsum('bij,jbd->ibd', left_blocks, arrived, preferred_element_type=f32)]
    optimization_barrier x0 -> x2, local copies, waits for them, and re-layouts: none -> 13.4 us  [the longest x1 6.69 us: body(): arrived, returned = lax.optimization_barrier((arrived, returned))]
    transpose x0 -> x2, local copies, waits for them, and re-layouts: none -> 9.59 us  [to_offsets(): parts = rows.reshape(height, count, span // count, width).swapaxes(0, 1)]
  transfers between devices with their start and end apart: 3 -> 5, of which waited for: 1 -> 3; matrix products, arithmetic and copies ran while one was open for 5% -> 14% of each run, Pallas kernels for 0% -> 0%
where the time goes in v2:
time: 514 us; the launch traced here: 513 us
  waiting for transfers between devices  197 us (38%)
  blocking collectives  127 us (25%)
  starting transfers between devices  67.4 us (13%)
  matrix products  47.8 us (9%)
  local copies, waits for them, and re-layouts  35.3 us (7%)
  other arithmetic  24.3 us (5%)
  between operations  14.2 us (3%)
    all_to_all x2, waiting for transfers between devices, to_offsets(): parts = lax.all_to_all(parts, 'seq', 0, 0, tiled=True)  137 us
    all_gather x1, blocking collectives, body(): vectors = lax.all_gather(jnp.stack((gain_slice, mid_part)), ('dp', 'seq'))  127 us
    all_to_all x2, waiting for transfers between devices, to_blocks(): parts = lax.all_to_all(parts, 'seq', 0, 0, tiled=True)  60.8 us
    all_to_all x2, starting transfers between devices, to_blocks(): parts = lax.all_to_all(parts, 'seq', 0, 0, tiled=True)  38.6 us
    all_to_all x2, starting transfers between devices, to_offsets(): parts = lax.all_to_all(parts, 'seq', 0, 0, tiled=True)  28.6 us
  transfers between devices with their start and end apart: 5, of which 3 were waited for; matrix products, arithmetic and copies ran while one was open for 14% of the time, Pallas kernels for 0%

profile of v2, /device:TPU:0, one launch (start us, length us, event | category | flops | bytes accessed | tf_op | source)
XLA Modules:
  0.0 512.9 jit_solution(3204503987757993239)
XLA Ops:
  7.2 0.0 copy-start
  7.2 4.8 copy.46
  12.0 8.5 %all-to-all-start = ((bf16[16,8,8,2048]{3,2,1,0:T(8,128)(2,1)}), bf16[16,8,8,2048]{3,2,1,0:T(8,128)(2,1)}, u32[]{:S(2)}, u32[]{:S(2)}) async-start(bf16[16,8,8,2048]{3,2,1,0:T(8,128)(2,1)} %copy.46), calls=%async_computation | async-start | bytes 8388608 | tf_op jit(solution)/shard_map/all_to_all | solution.py:11
  20.5 3.1 multiply_reduce_fusion
  23.6 9.5 %fusion.10 = (bf16[8,128,2048]{2,1,0:T(8,128)(2,1)}, f32[8,2048,128]{1,2,0:T(8,128)}) fusion(f32[2048]{0:T(1024)S(1)} %copy-done.4, bf16[8,128,128]{2,1,0:T(8,128)(2,1)S(1)} %copy-done, f32[2048]{0:T(1024)S(1)} %copy-done.5, f32[8,128]{1,0:T(8,128)S(1)} %get-tuple-element.31, bf16[8,128,2048]{2,1,0:T(8,128)(2,1)} %bitcast.81), kind=kOutput, calls=%fused_computation.18 | convolution fusion | flops 557842432 | bytes 17059840 | tf_op jit(solution)/shard_map/aij,ajd->aid/dot_general | solution.py:37
  33.1 67.1 %all-to-all-done = bf16[16,8,8,2048]{3,2,1,0:T(8,128)(2,1)} async-done(((bf16[16,8,8,2048]{3,2,1,0:T(8,128)(2,1)}), bf16[16,8,8,2048]{3,2,1,0:T(8,128)(2,1)}, u32[]{:S(2)}, u32[]{:S(2)}) %all-to-all-start) | async-done | bytes 4194336 | tf_op jit(solution)/shard_map/all_to_all | solution.py:11
  100.2 4.8 copy_bitcast_fusion.1
  105.0 20.1 %all-to-all-start.1 = ((bf16[16,8,8,2048]{3,2,1,0:T(8,128)(2,1)}), bf16[16,8,8,2048]{3,2,1,0:T(8,128)(2,1)}, u32[]{:S(2)}, u32[]{:S(2)}) async-start(bf16[16,8,8,2048]{3,2,1,0:T(8,128)(2,1)} %copy_bitcast_fusion.1), calls=%async_computation.1 | async-start | bytes 8388608 | tf_op jit(solution)/shard_map/all_to_all | solution.py:11
  125.1 9.0 %convert_bitcast_fusion.2 = bf16[128,8,2048]{0,2,1:T(8,128)(2,1)} fusion(bf16[8,128,128]{2,1,0:T(8,128)(2,1)S(1)} %copy-done.3, bf16[128,8,2048]{2,1,0:T(8,128)(2,1)} %bitcast.5), kind=kOutput, calls=%fused_computation.27 | convolution fusion | flops 538968064 | bytes 8650752 | tf_op jit(solution)/shard_map/bij,ibd->jbd/dot_general | solution.py:42
  134.0 69.5 %all-to-all-done.1 = bf16[16,8,8,2048]{3,2,1,0:T(8,128)(2,1)} async-done(((bf16[16,8,8,2048]{3,2,1,0:T(8,128)(2,1)}), bf16[16,8,8,2048]{3,2,1,0:T(8,128)(2,1)}, u32[]{:S(2)}, u32[]{:S(2)}) %all-to-all-start.1) | async-done | bytes 4194336 | tf_op jit(solution)/shard_map/all_to_all | solution.py:11
  203.5 6.7 %copy.50 = bf16[128,8,2048]{2,1,0:T(8,128)(2,1)} copy(bf16[128,8,2048]{0,2,1:T(8,128)(2,1)} %convert_bitcast_fusion.2) | data formatting | bytes 8388608 | tf_op jit(solution)/shard_map/optimization_barrier | solution.py:43
  210.2 19.3 %all-to-all-start.2 = ((bf16[16,8,8,2048]{3,2,1,0:T(8,128)(2,1)}), bf16[16,8,8,2048]{3,2,1,0:T(8,128)(2,1)}, u32[]{:S(2)}, u32[]{:S(2)}) async-start(bf16[16,8,8,2048]{3,2,1,0:T(8,128)(2,1)} %bitcast.80), calls=%async_computation.2 | async-start | bytes 8388608 | tf_op jit(solution)/shard_map/all_to_all | solution.py:19
  229.5 8.9 %convert_bitcast_fusion.1 = bf16[128,8,2048]{0,2,1:T(8,128)(2,1)} fusion(bf16[8,128,128]{2,1,0:T(8,128)(2,1)S(1)} %copy-done.3, bf16[128,8,2048]{2,1,0:T(8,128)(2,1)} %bitcast.8), kind=kOutput, calls=%fused_computation.26 | convolution fusion | flops 538968064 | bytes 8650752 | tf_op jit(solution)/shard_map/bij,jbd->ibd/dot_general | solution.py:45
  238.5 8.7 %fusion.12 = f32[8,128,128]{2,1,0:T(8,128)} fusion(bf16[128,8,2048]{2,1,0:T(8,128)(2,1)} %bitcast.8, bf16[128,8,2048]{2,1,0:T(8,128)(2,1)} %bitcast.5), kind=kOutput, calls=%fused_computation.29 | convolution fusion | flops 536870912 | bytes 8912896 | tf_op jit(solution)/shard_map/ibd,jbd->bij/dot_general | solution.py:46
  247.2 60.8 %all-to-all-done.2 = bf16[16,8,8,2048]{3,2,1,0:T(8,128)(2,1)} async-done(((bf16[16,8,8,2048]{3,2,1,0:T(8,128)(2,1)}), bf16[16,8,8,2048]{3,2,1,0:T(8,128)(2,1)}, u32[]{:S(2)}, u32[]{:S(2)}) %all-to-all-start.2) | async-done | bytes 4194336 | tf_op jit(solution)/shard_map/all_to_all | solution.py:19
  308.0 4.8 copy_bitcast_fusion
  312.8 6.7 %copy.54 = bf16[128,8,2048]{2,1,0:T(8,128)(2,1)} copy(bf16[128,8,2048]{0,2,1:T(8,128)(2,1)} %convert_bitcast_fusion.1) | data formatting | bytes 8388608 | tf_op jit(solution)/shard_map/optimization_barrier | solution.py:47
  319.5 19.3 %all-to-all-start.3 = ((bf16[16,8,8,2048]{3,2,1,0:T(8,128)(2,1)}), bf16[16,8,8,2048]{3,2,1,0:T(8,128)(2,1)}, u32[]{:S(2)}, u32[]{:S(2)}) async-start(bf16[16,8,8,2048]{3,2,1,0:T(8,128)(2,1)} %bitcast.79), calls=%async_computation.3 | async-start | bytes 8388608 | tf_op jit(solution)/shard_map/all_to_all | solution.py:19
  338.8 0.3 all-reduce.3.cloned.1.call-start
  339.1 7.5 %fusion.2 = (f32[2048]{0:T(1024)S(1)}, bf16[8,128,2048]{2,1,0:T(8,128)(2,1)S(1)}) fusion(bf16[8,128,2048]{2,1,0:T(8,128)(2,1)} %copy_bitcast_fusion, f32[8,2048,128]{1,2,0:T(8,128)} %get-tuple-element.33, f32[2048]{0:T(1024)S(1)} %copy-done.4), kind=kLoop, calls=%fused_computation.5 | loop fusion | flops 31455232 | bytes 16793600 | tf_op jit(solution)/shard_map/reduce_sum | solution.py:53
  346.6 2.0 copy-done.2
  348.6 2.2 fusion.16
  350.8 0.0 all-reduce.3.cloned.1.call-update
  350.8 9.5 %fusion.7 = (f32[2048]{0:T(1024)S(1)}, f32[8,128]{1,0:T(8,128)S(1)}, f32[8,2048,128]{1,2,0:T(8,128)}) fusion(f32[8,128]{1,0:T(8,128)S(1)} %get-tuple-element.31, f32[2048]{0:T(1024)S(1)} %copy-done.5, bf16[8,128,2048]{2,1,0:T(8,128)(2,1)} %copy-done.2, bf16[8,128,128]{2,1,0:T(8,128)(2,1)S(1)} %copy-done, bf16[8,128,2048]{2,1,0:T(8,128)(2,1)} %bitcast.82), kind=kOutput, calls=%fused_computation.13 | convolution fusion | flops 551547904 | bytes 17063936 | tf_op jit(solution)/shard_map/aij,aid->ajd/dot_general | solution.py:55
  360.4 126.5 %all-gather.1 = f32[32,2,2048]{2,1,0:T(2,128)S(1)} all-gather(f32[1,2,2048]{2,1,0:T(2,128)S(1)} %maximum_bitcast_fusion), channel_id=2, replica_groups=mesh['dp'=2,'seq'=16] {'dp','seq'}, dimensions={0}, use_global_device_ids=true | all-gather | bytes 540672 | tf_op jit(solution)/shard_map/all_gather | solution.py:68
  486.9 0.2 reduce_sum.49
  487.1 0.6 fusion.19
  487.7 3.2 convert_bitcast_fusion
  490.9 1.1 copy.55
  492.0 10.2 %fusion.6 = (bf16[1,1024,2048]{2,1,0:T(8,128)(2,1)}, bf16[1,1024,2048]{2,1,0:T(8,128)(2,1)}) fusion(f32[8,2048,128]{1,2,0:T(8,128)} %get-tuple-element.34, bf16[1,1024,2048]{2,1,0:T(8,128)(2,1)} %param.7, bf16[1,1024,2048]{2,1,0:T(8,128)(2,1)} %param.6, f32[1024]{0:T(1024)S(1)} %multiply_bitcast_fusion, f32[2048]{0:T(1024)S(1)} %copy-done.5, ...), kind=kLoop, calls=%fused_computation.10 | loop fusion | flops 23068672 | bytes 33570816 | tf_op jit(solution)/shard_map/convert_element_type | solution.py:65
  502.3 1.9 copy.70
  504.2 1.9 copy.71
  (15 shorter events, 0.1 us)
Async XLA Ops:
  7.2 16.4 %copy-start = (bf16[8,128,128]{2,1,0:T(8,128)(2,1)S(1)}, bf16[8,128,128]{2,1,0:T(8,128)(2,1)}, u32[]{:S(2)}) copy-start(bf16[8,128,128]{2,1,0:T(8,128)(2,1)} %param.8) | copy-start | bytes 786436
  12.0 11.6 %copy-start.4 = (f32[2048]{0:T(1024)S(1)}, f32[2048]{0:T(1024)}, u32[]{:S(2)}) copy-start(f32[2048]{0:T(1024)} %param.11) | copy-start | bytes 24580
  12.0 11.6 %copy-start.5 = (f32[2048]{0:T(1024)S(1)}, f32[2048]{0:T(1024)}, u32[]{:S(2)}) copy-start(f32[2048]{0:T(1024)} %param.10) | copy-start | bytes 24580
  12.0 88.2 %all-to-all-start = ((bf16[16,8,8,2048]{3,2,1,0:T(8,128)(2,1)}), bf16[16,8,8,2048]{3,2,1,0:T(8,128)(2,1)}, u32[]{:S(2)}, u32[]{:S(2)}) async-start(bf16[16,8,8,2048]{3,2,1,0:T(8,128)(2,1)} %copy.46), calls=%async_computation | async-start | bytes 8388608 | tf_op jit(solution)/shard_map/all_to_all | solution.py:11
  100.2 24.8 %copy-start.3 = (bf16[8,128,128]{2,1,0:T(8,128)(2,1)S(1)}, bf16[8,128,128]{2,1,0:T(8,128)(2,1)}, u32[]{:S(2)}) copy-start(bf16[8,128,128]{2,1,0:T(8,128)(2,1)} %param.9) | copy-start | bytes 786436
  105.0 98.5 %all-to-all-start.1 = ((bf16[16,8,8,2048]{3,2,1,0:T(8,128)(2,1)}), bf16[16,8,8,2048]{3,2,1,0:T(8,128)(2,1)}, u32[]{:S(2)}, u32[]{:S(2)}) async-start(bf16[16,8,8,2048]{3,2,1,0:T(8,128)(2,1)} %copy_bitcast_fusion.1), calls=%async_computation.1 | async-start | bytes 8388608 | tf_op jit(solution)/shard_map/all_to_all | solution.py:11
  210.2 97.8 %all-to-all-start.2 = ((bf16[16,8,8,2048]{3,2,1,0:T(8,128)(2,1)}), bf16[16,8,8,2048]{3,2,1,0:T(8,128)(2,1)}, u32[]{:S(2)}, u32[]{:S(2)}) async-start(bf16[16,8,8,2048]{3,2,1,0:T(8,128)(2,1)} %bitcast.80), calls=%async_computation.2 | async-start | bytes 8388608 | tf_op jit(solution)/shard_map/all_to_all | solution.py:19
  319.5 168.2 %all-to-all-start.3 = ((bf16[16,8,8,2048]{3,2,1,0:T(8,128)(2,1)}), bf16[16,8,8,2048]{3,2,1,0:T(8,128)(2,1)}, u32[]{:S(2)}, u32[]{:S(2)}) async-start(bf16[16,8,8,2048]{3,2,1,0:T(8,128)(2,1)} %bitcast.79), calls=%async_computation.3 | async-start | bytes 8388608 | tf_op jit(solution)/shard_map/all_to_all | solution.py:19
  338.8 163.5 %all-reduce.3.cloned.1.call-start = ((), (), s32[]{:S(2)}) async-start(), calls=%async_computation.4 | async-start | bytes 2097152 | tf_op jit(solution)/shard_map/psum | solution.py:67
  339.0 9.6 %copy-start.1 = (bf16[1,1024,2048]{2,1,0:T(8,128)(2,1)S(1)}, bf16[1,1024,2048]{2,1,0:T(8,128)(2,1)}, u32[]{:S(2)}) copy-start(bf16[1,1024,2048]{2,1,0:T(8,128)(2,1)} %param.6) | copy-start | bytes 12582916
  346.6 2.0 copy-start.2
Sparse Core Ops, SparseCore 0:
  350.9 20.8 all-reduce.2

commit v3 on v1

v3 whole, which is shorter than its diff:
```python
import jax
import jax.numpy as jnp
from jax import lax
from jax.sharding import PartitionSpec as P


def from_partner(block, axis, distance):
    if distance == 0:
        return block
    count = lax.axis_size(axis)
    return lax.ppermute(block, axis, [(i, i ^ distance) for i in range(count)])


def tree_sum(terms):
    while len(terms) > 1:
        terms = [terms[i] + terms[i + 1] for i in range(0, len(terms), 2)]
    return terms[0]


def sum_over(value, axis, low, high):
    return tree_sum([from_partner(value, axis, k << low) for k in range(1 << high - low)])


def after(value, other):
    return lax.optimization_barrier((value, other))[0]


def body(inputs, upstream, right_blocks, left_blocks, gain, mid_scale):
    count = lax.axis_size("seq")
    levels = count.bit_length() - 1
    low = levels // 2
    near = 1 << low
    far = count // near
    dp_levels = lax.axis_size("dp").bit_length() - 1
    device = lax.axis_index("seq")
    device_near = device & near - 1
    device_far = device >> low
    rows = inputs.shape[1]
    width = inputs.shape[2]
    order = right_blocks.shape[1]
    local = order // count
    f32 = jnp.float32
    bf16 = jnp.bfloat16

    place = lax.broadcasted_iota(jnp.int32, (order, order), 0)
    swap = (place ^ device * local) == lax.broadcasted_iota(jnp.int32, (order, order), 1)
    swap_half = swap.astype(bf16)
    swap_full = swap.astype(f32)
    rights = jnp.einsum("ki,aij->akj", swap_half, right_blocks)
    lefts = jnp.einsum("aij,jl->ail", jnp.einsum("ki,aij->akj", swap_half, left_blocks), swap_half)

    up_view = upstream[0].reshape(local, far, near, local, width)
    up_parts = [lax.dynamic_index_in_dim(up_view, device_far ^ k, 1, keepdims=False) for k in range(far)]
    up_far = [from_partner(up_parts[k], "seq", k << low) for k in range(far)]
    inputs = after(inputs, up_parts)
    input_float = inputs[0].astype(f32)
    inverse_norm = lax.rsqrt(jnp.mean(input_float * input_float, axis=-1, keepdims=True) + 1e-06)
    standardized_input = input_float * inverse_norm
    normalized_rows = (standardized_input * gain).astype(bf16)
    grid = normalized_rows.reshape(local, order, width)
    first = jnp.einsum("aij,ajd->aid", rights, grid, preferred_element_type=f32)
    sig = jax.nn.sigmoid(first * mid_scale)
    gated = (first * sig).astype(bf16)

    gated_view = gated.reshape(local, far, near, local, width)
    gated_near = [from_partner(gated_view[:, :, k], "seq", k) for k in range(near)]
    gated_near = [jnp.stack([t[:, k] for t in gated_near]) for k in range(far)]
    gated_far = [from_partner(gated_near[k], "seq", k << low) for k in range(far)]
    up_far = after(up_far, gated_near)
    up_near = [
        from_partner(
            jnp.stack([lax.dynamic_index_in_dim(t, device_near ^ k, 1, keepdims=False) for t in up_far]), "seq", k
        )
        for k in range(near)
    ]
    upward = jnp.stack(up_near, axis=1).reshape(order, local, width)
    returned = jnp.einsum("bij,ibd->jbd", lefts, upward, preferred_element_type=f32).astype(bf16)
    returned = returned.reshape(far, near, local, local, width)
    back_far = [from_partner(returned[k], "seq", k << low) for k in range(far)]
    gated_far = after(gated_far, returned)
    arrived = jnp.stack(gated_far).reshape(order, local, width)
    mixed = jnp.einsum("bij,jbd->ibd", lefts, arrived, preferred_element_type=f32).astype(bf16)
    mixed = mixed.reshape(far, near, local, local, width)
    mixed_near = jnp.zeros((far, near, local, local, width), bf16)
    for k in range(near):
        mixed_near = lax.dynamic_update_index_in_dim(
            mixed_near, from_partner(mixed[:, k], "seq", k), device_near ^ k, 1
        )
    back_far = after(back_far, mixed_near)
    back_near = [from_partner(jnp.stack([t[k] for t in back_far]), "seq", k) for k in range(near)]
    dgated = jnp.stack(back_near, axis=1).transpose(2, 0, 1, 3, 4).reshape(local, order, width).astype(f32)

    upward, arrived = after((upward, arrived), mixed)
    grad_left = jnp.einsum("ibd,jbd->bij", upward, arrived, preferred_element_type=f32)
    grad_left = sum_over(grad_left, "dp", 0, dp_levels)
    grad_left = jnp.einsum("ki,aij->akj", swap_full, grad_left, precision=lax.Precision.HIGHEST)
    grad_left = jnp.einsum("aij,jl->ail", grad_left, swap_full, precision=lax.Precision.HIGHEST)

    slope = sig * (1.0 - sig)
    dfirst = (dgated * (sig + first * mid_scale * slope)).astype(bf16)
    mid_part = jnp.sum(dgated * first * first * slope, axis=(0, 1))
    grad_right = jnp.einsum("aid,ajd->aij", dfirst, grid, preferred_element_type=f32)
    grad_right = sum_over(grad_right, "dp", 0, dp_levels)
    grad_right = jnp.einsum("ki,aij->akj", swap_full, grad_right, precision=lax.Precision.HIGHEST)
    normalized_gradient = jnp.einsum(
        "aij,aid->ajd", rights, dfirst, preferred_element_type=f32
    ).reshape(rows, width)
    gain_slice = jnp.sum(normalized_gradient * standardized_input, axis=0)
    centered_gradient = normalized_gradient * gain
    input_gradient = upstream[0].astype(f32) + inverse_norm * (
        centered_gradient
        - standardized_input
        * jnp.mean(centered_gradient * standardized_input, axis=-1, keepdims=True)
    )
    input_gradient = input_gradient.astype(bf16)
    vectors = jnp.stack((gain_slice, mid_part))
    vectors = sum_over(vectors, "dp", 0, dp_levels)
    vectors = sum_over(vectors, "seq", 0, low)
    gain_gradient, grad_mid = sum_over(vectors, "seq", low, levels)
    output = jnp.zeros((local, far, near, local, width), bf16)
    input_view = inputs[0].reshape(local, far, near, local, width)
    mixed_far = [from_partner(mixed_near[k], "seq", k << low) for k in range(far)]
    mixed_far = after(mixed_far, (input_gradient, grad_right))
    for k in range(far):
        place = device_far ^ k
        part = mixed_far[k].swapaxes(0, 1)
        residual = lax.dynamic_index_in_dim(input_view, place, 1, keepdims=False).astype(f32)
        output = lax.dynamic_update_index_in_dim(output, (residual + part.astype(f32)).astype(bf16), place, 1)
    return (
        output.reshape(1, rows, width),
        input_gradient.reshape(1, rows, width),
        grad_right,
        grad_left,
        gain_gradient,
        grad_mid,
    )


def solution(mesh):
    in_specs = (
        P("dp", "seq", None),
        P("dp", "seq", None),
        P("seq", None, None),
        P("seq", None, None),
        P(),
        P(),
    )
    out_specs = (
        P("dp", "seq", None),
        P("dp", "seq", None),
        P("seq", None, None),
        P("seq", None, None),
        P(),
        P(),
    )
    return jax.shard_map(body, mesh=mesh, in_specs=in_specs, out_specs=out_specs, check_vma=False)
```

time: 508 us -> 443 us (0.87); the launches traced: 499 us -> 442 us
  blocking collectives: 305 us -> 0 us
  waiting for transfers between devices: 75.2 us -> 240 us
  starting transfers between devices: 9.88 us -> 127 us
  matrix products: 44.1 us -> 18 us
  between operations: 14.4 us -> 1.29 us
  other arithmetic: 16.6 us -> 24.7 us
    ppermute x0 -> x33, waiting for transfers between devices: none -> 240 us  [from_partner(): return lax.ppermute(block, axis, [(i, i ^ distance) for i in range(count)])]
    all_to_all x2 -> x0, blocking collectives: 213 us -> none  [to_offsets(): return lax.all_to_all(rows, 'seq', 1, 0, tiled=True)]
    ppermute x0 -> x33, starting transfers between devices: none -> 127 us  [from_partner(): return lax.ppermute(block, axis, [(i, i ^ distance) for i in range(count)])]
    psum x1 -> x0, blocking collectives: 91.3 us -> none  [body(): gain_gradient, grad_mid = lax.psum((gain_slice, mid_part), ('dp', 'seq'))]
    all_to_all x2 -> x0, waiting for transfers between devices: 75.2 us -> none  [to_blocks(): return lax.all_to_all(rows, 'seq', 0, 1, tiled=True)]
    dot_general x4 -> x9, matrix products: 33.1 us -> 15.3 us  [the longest x1 5.54 us: body(): first = jnp.einsum('aij,ajd->aid', rights, grid, preferred_element_type=f32)]
    convert_element_type x4 -> x0, local copies, waits for them, and re-layouts: 16.8 us -> none  [the longest x1 6.75 us: body(): jnp.einsum('bij,jbd->ibd', left_blocks, arrived, preferred_element_type=f32)]
    another operation x0 -> x15, other arithmetic: none -> 10.9 us  [the longest x2 3.38 us: body(): upward = jnp.stack(up_near, axis=1).reshape(order, local, width)]
  transfers between devices with their start and end apart: 3 -> 33, of which waited for: 1 -> 12; matrix products, arithmetic and copies ran while one was open for 5% -> 10% of each run, Pallas kernels for 0% -> 0%
where the time goes in v3:
time: 443 us; the launch traced here: 442 us
  waiting for transfers between devices  240 us (54%)
  starting transfers between devices  127 us (29%)
  local copies, waits for them, and re-layouts  31.6 us (7%)
  other arithmetic  24.7 us (6%)
  matrix products  18 us (4%)
    ppermute x33, waiting for transfers between devices, from_partner(): return lax.ppermute(block, axis, [(i, i ^ distance) for i in range(count)])  240 us
    ppermute x33, starting transfers between devices, from_partner(): return lax.ppermute(block, axis, [(i, i ^ distance) for i in range(count)])  127 us
  transfers between devices with their start and end apart: 33, of which 12 were waited for; matrix products, arithmetic and copies ran while one was open for 10% of the time, Pallas kernels for 0%

profile of v3, /device:TPU:0, one launch (start us, length us, event | category | flops | bytes accessed | tf_op | source)
XLA Modules:
  0.0 442.4 jit_solution(4127377515331129847)
XLA Ops:
  0.7 4.1 dynamic-slice_bitcast_fusion
  6.0 5.5 %multiply_convert_fusion = (bf16[8,128,2048]{2,1,0:T(8,128)(2,1)S(1)}, f32[8,128,2048]{2,1,0:T(8,128)}) fusion(f32[2048]{0:T(1024)S(1)} %copy-done.9, bf16[8,128,128]{1,2,0:T(8,128)(2,1)S(1)} %convolution_bitcast_fusion.3, f32[2048]{0:T(1024)S(1)} %copy-done.8, f32[8,128]{1,0:T(8,128)S(1)} %get-tuple-element.137, bf16[8,128,2048]{2,1,0:T(8,128)(2,1)S(1)} %bitcast.270), kind=kOutput, calls=%fused_computation.13 | convolution fusion | flops 557842432 | bytes 17059840 | tf_op jit(solution)/shard_map/aij,ajd->aid/dot_general | solution.py:61
  13.9 3.0 collective-permute-start.1
  19.5 3.6 collective-permute-start.14
  23.7 16.6 %collective-permute-done.1 = bf16[8,4,8,2048]{3,2,0,1:T(8,128)(2,1)} collective-permute-done((bf16[8,4,8,2048]{3,2,0,1:T(8,128)(2,1)}, bf16[8,4,8,2048]{3,2,0,1:T(8,128)(2,1)}, u32[]{:S(2)}, u32[]{:S(2)}) %collective-permute-start.1) | collective-permute-done | bytes 1048608 | tf_op jit(solution)/shard_map/ppermute | solution.py:11
  40.4 1.8 collective-permute-start.12
  44.4 20.7 %collective-permute-done.2 = bf16[8,4,8,2048]{3,2,1,0:T(8,128)(2,1)} collective-permute-done((bf16[8,4,8,2048]{3,2,1,0:T(8,128)(2,1)}, bf16[8,4,8,2048]{3,2,1,0:T(8,128)(2,1)}, u32[]{:S(2)}, u32[]{:S(2)}) %collective-permute-start.2) | collective-permute-done | bytes 1048608 | tf_op jit(solution)/shard_map/ppermute | solution.py:11
  66.5 2.9 collective-permute-start.4
  73.5 64.2 %collective-permute-done.13 = bf16[8,4,8,2048]{3,2,1,0:T(8,128)(2,1)} collective-permute-done((bf16[8,4,8,2048]{3,2,1,0:T(8,128)(2,1)}, bf16[8,4,8,2048]{3,2,1,0:T(8,128)(2,1)}, u32[]{:S(2)}, u32[]{:S(2)}) %collective-permute-start.13) | collective-permute-done | bytes 1048608 | tf_op jit(solution)/shard_map/ppermute | solution.py:11
  137.9 2.4 dynamic-slice_bitcast_fusion.16
  143.6 37.3 %collective-permute-done.4 = bf16[4,8,8,2048]{3,2,1,0:T(8,128)(2,1)S(1)} collective-permute-done((bf16[4,8,8,2048]{3,2,1,0:T(8,128)(2,1)S(1)}, bf16[4,8,8,2048]{3,2,1,0:T(8,128)(2,1)S(1)}, u32[]{:S(2)}, u32[]{:S(2)}) %collective-permute-start.4) | collective-permute-done | bytes 1048608 | tf_op jit(solution)/shard_map/ppermute | solution.py:11
  184.8 2.1 pad_maximum_fusion
  186.9 2.3 copy.83
  189.3 16.9 %collective-permute-done.17 = bf16[4,8,8,2048]{3,2,1,0:T(8,128)(2,1)} collective-permute-done((bf16[4,8,8,2048]{3,2,1,0:T(8,128)(2,1)}, bf16[4,8,8,2048]{3,2,1,0:T(8,128)(2,1)}, u32[]{:S(2)}, u32[]{:S(2)}) %collective-permute-start.17) | collective-permute-done | bytes 1048608 | tf_op jit(solution)/shard_map/ppermute | solution.py:11
  206.2 2.3 pad_maximum_fusion.1
  208.5 2.3 copy.88
  222.3 2.5 collective-permute-start.8
  225.4 15.8 %collective-permute-done.6 = bf16[4,8,8,2048]{3,1,0,2:T(8,128)(2,1)S(1)} collective-permute-done((bf16[4,8,8,2048]{3,1,0,2:T(8,128)(2,1)S(1)}, bf16[4,8,8,2048]{3,1,0,2:T(8,128)(2,1)S(1)}, u32[]{:S(2)}, u32[]{:S(2)}) %collective-permute-start.6) | collective-permute-done | bytes 1048608 | tf_op jit(solution)/shard_map/ppermute | solution.py:11
  243.7 24.4 %collective-permute-done.7 = bf16[4,8,8,2048]{3,1,0,2:T(8,128)(2,1)S(1)} collective-permute-done((bf16[4,8,8,2048]{3,1,0,2:T(8,128)(2,1)S(1)}, bf16[4,8,8,2048]{3,1,0,2:T(8,128)(2,1)S(1)}, u32[]{:S(2)}, u32[]{:S(2)}) %collective-permute-start.7) | collective-permute-done | bytes 1048608 | tf_op jit(solution)/shard_map/ppermute | solution.py:11
  269.6 21.9 %collective-permute-done.19 = bf16[4,8,8,2048]{3,2,0,1:T(8,128)(2,1)S(1)} collective-permute-done((bf16[4,8,8,2048]{3,2,0,1:T(8,128)(2,1)S(1)}, bf16[4,8,8,2048]{3,2,0,1:T(8,128)(2,1)S(1)}, u32[]{:S(2)}, u32[]{:S(2)}) %collective-permute-start.19) | collective-permute-done | bytes 1048608 | tf_op jit(solution)/shard_map/ppermute | solution.py:11
  297.9 1.8 slice_bitcast_fusion.4
  299.7 2.5 collective-permute-start.11
  302.2 43.4 %collective-permute-start.10 = (bf16[4,8,8,2048]{3,2,0,1:T(8,128)(2,1)}, bf16[4,8,8,2048]{3,2,0,1:T(8,128)(2,1)}, u32[]{:S(2)}, u32[]{:S(2)}) collective-permute-start(bf16[4,8,8,2048]{3,2,0,1:T(8,128)(2,1)} %get-tuple-element.71), channel_id=1, source_target_pairs={{0,8},{1,9},{2,10},{3,11},{4,12},{5,13},{6,14},{7,15},{8,0},{9,1},... | collective-permute-start | bytes 3145736 | tf_op jit(solution)/shard_map/ppermute | solution.py:11
  345.8 4.8 %fusion.1 = (f32[2048]{0:T(1024)S(1)}, bf16[8,128,2048]{2,1,0:T(8,128)(2,1)S(1)}) fusion(f32[8,128,2048]{2,1,0:T(8,128)S(1)} %bitcast.285, f32[2048]{0:T(1024)S(1)} %copy-done.9, bf16[4,1,8,8,2048]{4,3,1,0,2:T(8,128)(2,1)S(1)} %bitcast.292, bf16[4,1,8,8,2048]{4,3,1,0,2:T(8,128)(2,1)S(1)} %bitcast.291, bf16[4,1,8,8,2048]{4,3,1,0,2:T(8,128)(2,1)S(1)} %bitcast.290, ...), kind=kLoop, calls=%fused_computation.3 | loop fusion | flops 37746688 | bytes 16793600 | tf_op jit(solution)/shard_map/reduce_sum | solution.py:101
  350.7 2.9 multiply_reduce_fusion
  355.4 2.5 collective-permute-start.29
  358.4 3.9 fusion.6
  362.4 2.5 collective-permute-start.32
  365.0 38.3 %collective-permute-start.31 = (f32[2,2048]{1,0:T(2,128)S(1)}, f32[2,2048]{1,0:T(2,128)S(1)}, u32[]{:S(2)}, u32[]{:S(2)}) collective-permute-start(f32[2,2048]{1,0:T(2,128)S(1)} %add_add_fusion.1), channel_id=1, source_target_pairs={{0,8},{1,9},{2,10},{3,11},{4,12},{5,13},{6,14},{7,15},{8,0},{9,1},... | collective-permute-start | bytes 49160 | tf_op jit(solution)/shard_map/ppermute | solution.py:11
  404.8 9.0 %collective-permute-start.9 = (bf16[4,8,8,2048]{3,2,0,1:T(8,128)(2,1)}, bf16[4,8,8,2048]{3,2,0,1:T(8,128)(2,1)S(1)}, u32[]{:S(2)}, u32[]{:S(2)}) collective-permute-start(bf16[4,8,8,2048]{3,2,0,1:T(8,128)(2,1)} %get-tuple-element.72), channel_id=1, source_target_pairs={{0,4},{1,5},{2,6},{3,7},{4,0},{5,1},{6,2},{7,3},{8,12},{9,13},{10,... | collective-permute-start | bytes 3145736 | tf_op jit(solution)/shard_map/ppermute | solution.py:11
  417.4 18.3 %collective-permute-done.9 = bf16[4,8,8,2048]{3,2,0,1:T(8,128)(2,1)S(1)} collective-permute-done((bf16[4,8,8,2048]{3,2,0,1:T(8,128)(2,1)}, bf16[4,8,8,2048]{3,2,0,1:T(8,128)(2,1)S(1)}, u32[]{:S(2)}, u32[]{:S(2)}) %collective-permute-start.9) | collective-permute-done | bytes 1048608 | tf_op jit(solution)/shard_map/ppermute | solution.py:11
  440.3 2.0 copy-done.6
  (130 shorter events, 56.4 us)
Async XLA Ops:
  13.9 26.4 %collective-permute-start.1 = (bf16[8,4,8,2048]{3,2,0,1:T(8,128)(2,1)}, bf16[8,4,8,2048]{3,2,0,1:T(8,128)(2,1)}, u32[]{:S(2)}, u32[]{:S(2)}) collective-permute-start(bf16[8,4,8,2048]{3,2,0,1:T(8,128)(2,1)} %bitcast.266), channel_id=1, source_target_pairs={{0,2},{1,3},{2,0},{3,1},{4,6},{5,7},{6,4},{7,5},{8,10},{9,11},{10,... | collective-permute-start | bytes 3145736 | tf_op jit(solution)/shard_map/ppermute | solution.py:11
  18.0 26.3 %collective-permute-start = (bf16[8,4,8,2048]{3,2,0,1:T(8,128)(2,1)}, bf16[8,4,8,2048]{3,2,0,1:T(8,128)(2,1)S(1)}, u32[]{:S(2)}, u32[]{:S(2)}) collective-permute-start(bf16[8,4,8,2048]{3,2,0,1:T(8,128)(2,1)} %bitcast.267), channel_id=1, source_target_pairs={{0,1},{1,0},{2,3},{3,2},{4,5},{5,4},{6,7},{7,6},{8,9},{9,8},{10,11... | collective-permute-start | bytes 3145736 | tf_op jit(solution)/shard_map/ppermute | solution.py:11
  19.5 53.9 %collective-permute-start.14 = (bf16[8,4,8,2048]{3,2,1,0:T(8,128)(2,1)}, bf16[8,4,8,2048]{3,2,1,0:T(8,128)(2,1)}, u32[]{:S(2)}, u32[]{:S(2)}) collective-permute-start(bf16[8,4,8,2048]{3,2,1,0:T(8,128)(2,1)} %get-tuple-element.82), channel_id=1, source_target_pairs={{0,12},{1,13},{2,14},{3,15},{4,8},{5,9},{6,10},{7,11},{8,4},{9,5},... | collective-permute-start | bytes 3145736 | tf_op jit(solution)/shard_map/ppermute | solution.py:11
  23.1 114.6 %collective-permute-start.13 = (bf16[8,4,8,2048]{3,2,1,0:T(8,128)(2,1)}, bf16[8,4,8,2048]{3,2,1,0:T(8,128)(2,1)}, u32[]{:S(2)}, u32[]{:S(2)}) collective-permute-start(bf16[8,4,8,2048]{3,2,1,0:T(8,128)(2,1)} %get-tuple-element.83), channel_id=1, source_target_pairs={{0,8},{1,9},{2,10},{3,11},{4,12},{5,13},{6,14},{7,15},{8,0},{9,1},... | collective-permute-start | bytes 3145736 | tf_op jit(solution)/shard_map/ppermute | solution.py:11
  23.1 42.0 %collective-permute-start.2 = (bf16[8,4,8,2048]{3,2,1,0:T(8,128)(2,1)}, bf16[8,4,8,2048]{3,2,1,0:T(8,128)(2,1)}, u32[]{:S(2)}, u32[]{:S(2)}) collective-permute-start(bf16[8,4,8,2048]{3,2,1,0:T(8,128)(2,1)} %get-tuple-element.80), channel_id=1, source_target_pairs={{0,3},{1,2},{2,1},{3,0},{4,7},{5,6},{6,5},{7,4},{8,11},{9,10},{10,... | collective-permute-start | bytes 3145736 | tf_op jit(solution)/shard_map/ppermute | solution.py:11
  40.4 97.3 %collective-permute-start.12 = (bf16[8,4,8,2048]{3,2,1,0:T(8,128)(2,1)}, bf16[8,4,8,2048]{3,2,1,0:T(8,128)(2,1)S(1)}, u32[]{:S(2)}, u32[]{:S(2)}) collective-permute-start(bf16[8,4,8,2048]{3,2,1,0:T(8,128)(2,1)} %get-tuple-element.84), channel_id=1, source_target_pairs={{0,4},{1,5},{2,6},{3,7},{4,0},{5,1},{6,2},{7,3},{8,12},{9,13},{10,... | collective-permute-start | bytes 3145736 | tf_op jit(solution)/shard_map/ppermute | solution.py:11
  66.5 114.4 %collective-permute-start.4 = (bf16[4,8,8,2048]{3,2,1,0:T(8,128)(2,1)S(1)}, bf16[4,8,8,2048]{3,2,1,0:T(8,128)(2,1)S(1)}, u32[]{:S(2)}, u32[]{:S(2)}) collective-permute-start(bf16[4,8,8,2048]{3,2,1,0:T(8,128)(2,1)S(1)} %pad_maximum_fusion.5), channel_id=1, source_target_pairs={{0,8},{1,9},{2,10},{3,11},{4,12},{5,13},{6,14},{7,15},{8,0},{9,1},... | collective-permute-start | bytes 3145736 | tf_op jit(solution)/shard_map/ppermute | solution.py:11
  70.6 114.2 %collective-permute-start.3 = (bf16[4,8,8,2048]{3,2,1,0:T(8,128)(2,1)}, bf16[4,8,8,2048]{3,2,1,0:T(8,128)(2,1)}, u32[]{:S(2)}, u32[]{:S(2)}) collective-permute-start(bf16[4,8,8,2048]{3,2,1,0:T(8,128)(2,1)} %pad_maximum_fusion.4), channel_id=1, source_target_pairs={{0,4},{1,5},{2,6},{3,7},{4,0},{5,1},{6,2},{7,3},{8,12},{9,13},{10,... | collective-permute-start | bytes 3145736 | tf_op jit(solution)/shard_map/ppermute | solution.py:11
  73.4 111.4 %collective-permute-start.5 = (bf16[4,8,8,2048]{3,2,1,0:T(8,128)(2,1)}, bf16[4,8,8,2048]{3,2,1,0:T(8,128)(2,1)}, u32[]{:S(2)}, u32[]{:S(2)}) collective-permute-start(bf16[4,8,8,2048]{3,2,1,0:T(8,128)(2,1)} %pad_maximum_fusion.6), channel_id=1, source_target_pairs={{0,12},{1,13},{2,14},{3,15},{4,8},{5,9},{6,10},{7,11},{8,4},{9,5},... | collective-permute-start | bytes 3145736 | tf_op jit(solution)/shard_map/ppermute | solution.py:11
  140.5 48.8 %collective-permute-start.15 = (bf16[4,8,8,2048]{3,2,1,0:T(8,128)(2,1)S(1)}, bf16[4,8,8,2048]{3,2,1,0:T(8,128)(2,1)}, u32[]{:S(2)}, u32[]{:S(2)}) collective-permute-start(bf16[4,8,8,2048]{3,2,1,0:T(8,128)(2,1)S(1)} %pad_maximum_fusion.7), channel_id=1, source_target_pairs={{0,1},{1,0},{2,3},{3,2},{4,5},{5,4},{6,7},{7,6},{8,9},{9,8},{10,11... | collective-permute-start | bytes 3145736 | tf_op jit(solution)/shard_map/ppermute | solution.py:11
  142.2 47.1 %collective-permute-start.16 = (bf16[4,8,8,2048]{3,2,1,0:T(8,128)(2,1)}, bf16[4,8,8,2048]{3,2,1,0:T(8,128)(2,1)}, u32[]{:S(2)}, u32[]{:S(2)}) collective-permute-start(bf16[4,8,8,2048]{3,2,1,0:T(8,128)(2,1)} %pad_maximum_fusion.8), channel_id=1, source_target_pairs={{0,2},{1,3},{2,0},{3,1},{4,6},{5,7},{6,4},{7,5},{8,10},{9,11},{10,... | collective-permute-start | bytes 3145736 | tf_op jit(solution)/shard_map/ppermute | solution.py:11
  181.8 24.4 %collective-permute-start.17 = (bf16[4,8,8,2048]{3,2,1,0:T(8,128)(2,1)}, bf16[4,8,8,2048]{3,2,1,0:T(8,128)(2,1)}, u32[]{:S(2)}, u32[]{:S(2)}) collective-permute-start(bf16[4,8,8,2048]{3,2,1,0:T(8,128)(2,1)} %pad_maximum_fusion.9), channel_id=1, source_target_pairs={{0,3},{1,2},{2,1},{3,0},{4,7},{5,6},{6,5},{7,4},{8,11},{9,10},{10,... | collective-permute-start | bytes 3145736 | tf_op jit(solution)/shard_map/ppermute | solution.py:11
  215.2 7.1 %collective-permute-start.25 = (f32[8,128,128]{2,1,0:T(8,128)S(1)}, f32[8,128,128]{2,1,0:T(8,128)S(1)}, u32[]{:S(2)}, u32[]{:S(2)}) collective-permute-start(f32[8,128,128]{2,1,0:T(8,128)S(1)} %fusion.48), channel_id=1, source_target_pairs={{0,16},{16,0},{1,17},{17,1},{2,18},{18,2},{3,19},{19,3},{4,20},{20... | collective-permute-start | bytes 1572872 | tf_op jit(solution)/shard_map/ppermute | solution.py:11
  215.3 26.0 %collective-permute-start.6 = (bf16[4,8,8,2048]{3,1,0,2:T(8,128)(2,1)S(1)}, bf16[4,8,8,2048]{3,1,0,2:T(8,128)(2,1)S(1)}, u32[]{:S(2)}, u32[]{:S(2)}) collective-permute-start(bf16[4,8,8,2048]{3,1,0,2:T(8,128)(2,1)S(1)} %get-tuple-element.76), channel_id=1, source_target_pairs={{0,1},{1,0},{2,3},{3,2},{4,5},{5,4},{6,7},{7,6},{8,9},{9,8},{10,11... | collective-permute-start | bytes 3145736 | tf_op jit(solution)/shard_map/ppermute | solution.py:11
  218.2 51.3 %collective-permute-start.18 = (bf16[4,8,8,2048]{3,2,0,1:T(8,128)(2,1)S(1)}, bf16[4,8,8,2048]{3,2,0,1:T(8,128)(2,1)S(1)}, u32[]{:S(2)}, u32[]{:S(2)}) collective-permute-start(bf16[4,8,8,2048]{3,2,0,1:T(8,128)(2,1)S(1)} %copy.90), channel_id=1, source_target_pairs={{0,4},{1,5},{2,6},{3,7},{4,0},{5,1},{6,2},{7,3},{8,12},{9,13},{10,... | collective-permute-start | bytes 3145736 | tf_op jit(solution)/shard_map/ppermute | solution.py:11
  219.5 71.9 %collective-permute-start.19 = (bf16[4,8,8,2048]{3,2,0,1:T(8,128)(2,1)S(1)}, bf16[4,8,8,2048]{3,2,0,1:T(8,128)(2,1)S(1)}, u32[]{:S(2)}, u32[]{:S(2)}) collective-permute-start(bf16[4,8,8,2048]{3,2,0,1:T(8,128)(2,1)S(1)} %copy.91), channel_id=1, source_target_pairs={{0,8},{1,9},{2,10},{3,11},{4,12},{5,13},{6,14},{7,15},{8,0},{9,1},... | collective-permute-start | bytes 3145736 | tf_op jit(solution)/shard_map/ppermute | solution.py:11
  220.6 47.4 %collective-permute-start.7 = (bf16[4,8,8,2048]{3,1,0,2:T(8,128)(2,1)S(1)}, bf16[4,8,8,2048]{3,1,0,2:T(8,128)(2,1)S(1)}, u32[]{:S(2)}, u32[]{:S(2)}) collective-permute-start(bf16[4,8,8,2048]{3,1,0,2:T(8,128)(2,1)S(1)} %get-tuple-element.75), channel_id=1, source_target_pairs={{0,2},{1,3},{2,0},{3,1},{4,6},{5,7},{6,4},{7,5},{8,10},{9,11},{10,... | collective-permute-start | bytes 3145736 | tf_op jit(solution)/shard_map/ppermute | solution.py:11
  222.3 46.4 %collective-permute-start.8 = (bf16[4,8,8,2048]{3,1,0,2:T(8,128)(2,1)S(1)}, bf16[4,8,8,2048]{3,1,0,2:T(8,128)(2,1)S(1)}, u32[]{:S(2)}, u32[]{:S(2)}) collective-permute-start(bf16[4,8,8,2048]{3,1,0,2:T(8,128)(2,1)S(1)} %get-tuple-element.74), channel_id=1, source_target_pairs={{0,3},{1,2},{2,1},{3,0},{4,7},{5,6},{6,5},{7,4},{8,11},{9,10},{10,... | collective-permute-start | bytes 3145736 | tf_op jit(solution)/shard_map/ppermute | solution.py:11
  241.3 50.1 %collective-permute-start.20 = (bf16[4,8,8,2048]{3,2,0,1:T(8,128)(2,1)S(1)}, bf16[4,8,8,2048]{3,2,0,1:T(8,128)(2,1)S(1)}, u32[]{:S(2)}, u32[]{:S(2)}) collective-permute-start(bf16[4,8,8,2048]{3,2,0,1:T(8,128)(2,1)S(1)} %copy.92), channel_id=1, source_target_pairs={{0,12},{1,13},{2,14},{3,15},{4,8},{5,9},{6,10},{7,11},{8,4},{9,5},... | collective-permute-start | bytes 3145736 | tf_op jit(solution)/shard_map/ppermute | solution.py:11
  292.6 53.2 %collective-permute-start.21 = (bf16[4,8,8,2048]{3,2,0,1:T(8,128)(2,1)S(1)}, bf16[4,8,8,2048]{3,2,0,1:T(8,128)(2,1)S(1)}, u32[]{:S(2)}, u32[]{:S(2)}) collective-permute-start(bf16[4,8,8,2048]{3,2,0,1:T(8,128)(2,1)S(1)} %pad_maximum_fusion.10), channel_id=1, source_target_pairs={{0,1},{1,0},{2,3},{3,2},{4,5},{5,4},{6,7},{7,6},{8,9},{9,8},{10,11... | collective-permute-start | bytes 3145736 | tf_op jit(solution)/shard_map/ppermute | solution.py:11
  294.3 51.5 %collective-permute-start.22 = (bf16[4,8,8,2048]{3,2,0,1:T(8,128)(2,1)S(1)}, bf16[4,8,8,2048]{3,2,0,1:T(8,128)(2,1)S(1)}, u32[]{:S(2)}, u32[]{:S(2)}) collective-permute-start(bf16[4,8,8,2048]{3,2,0,1:T(8,128)(2,1)S(1)} %pad_maximum_fusion.11), channel_id=1, source_target_pairs={{0,2},{1,3},{2,0},{3,1},{4,6},{5,7},{6,4},{7,5},{8,10},{9,11},{10,... | collective-permute-start | bytes 3145736 | tf_op jit(solution)/shard_map/ppermute | solution.py:11
  295.0 50.8 %collective-permute-start.23 = (bf16[4,8,8,2048]{3,2,0,1:T(8,128)(2,1)S(1)}, bf16[4,8,8,2048]{3,2,0,1:T(8,128)(2,1)S(1)}, u32[]{:S(2)}, u32[]{:S(2)}) collective-permute-start(bf16[4,8,8,2048]{3,2,0,1:T(8,128)(2,1)S(1)} %pad_maximum_fusion.12), channel_id=1, source_target_pairs={{0,3},{1,2},{2,1},{3,0},{4,7},{5,6},{6,5},{7,4},{8,11},{9,10},{10,... | collective-permute-start | bytes 3145736 | tf_op jit(solution)/shard_map/ppermute | solution.py:11
  299.7 117.7 %collective-permute-start.11 = (bf16[4,8,8,2048]{3,2,0,1:T(8,128)(2,1)}, bf16[4,8,8,2048]{3,2,0,1:T(8,128)(2,1)}, u32[]{:S(2)}, u32[]{:S(2)}) collective-permute-start(bf16[4,8,8,2048]{3,2,0,1:T(8,128)(2,1)} %get-tuple-element.70), channel_id=1, source_target_pairs={{0,12},{1,13},{2,14},{3,15},{4,8},{5,9},{6,10},{7,11},{8,4},{9,5},... | collective-permute-start | bytes 3145736 | tf_op jit(solution)/shard_map/ppermute | solution.py:11
  302.2 115.2 %collective-permute-start.10 = (bf16[4,8,8,2048]{3,2,0,1:T(8,128)(2,1)}, bf16[4,8,8,2048]{3,2,0,1:T(8,128)(2,1)}, u32[]{:S(2)}, u32[]{:S(2)}) collective-permute-start(bf16[4,8,8,2048]{3,2,0,1:T(8,128)(2,1)} %get-tuple-element.71), channel_id=1, source_target_pairs={{0,8},{1,9},{2,10},{3,11},{4,12},{5,13},{6,14},{7,15},{8,0},{9,1},... | collective-permute-start | bytes 3145736 | tf_op jit(solution)/shard_map/ppermute | solution.py:11
  354.9 7.5 %collective-permute-start.28 = (f32[2,2048]{1,0:T(2,128)S(1)}, f32[2,2048]{1,0:T(2,128)S(1)}, u32[]{:S(2)}, u32[]{:S(2)}) collective-permute-start(f32[2,2048]{1,0:T(2,128)S(1)} %fusion.39), channel_id=1, source_target_pairs={{0,2},{1,3},{2,0},{3,1},{4,6},{5,7},{6,4},{7,5},{8,10},{9,11},{10,... | collective-permute-start | bytes 49160 | tf_op jit(solution)/shard_map/ppermute | solution.py:11
  355.4 6.9 %collective-permute-start.29 = (f32[2,2048]{1,0:T(2,128)S(1)}, f32[2,2048]{1,0:T(2,128)S(1)}, u32[]{:S(2)}, u32[]{:S(2)}) collective-permute-start(f32[2,2048]{1,0:T(2,128)S(1)} %fusion.39), channel_id=1, source_target_pairs={{0,3},{1,2},{2,1},{3,0},{4,7},{5,6},{6,5},{7,4},{8,11},{9,10},{10,... | collective-permute-start | bytes 49160 | tf_op jit(solution)/shard_map/ppermute | solution.py:11
  357.9 4.5 %collective-permute-start.27 = (f32[2,2048]{1,0:T(2,128)S(1)}, f32[2,2048]{1,0:T(2,128)S(1)}, u32[]{:S(2)}, u32[]{:S(2)}) collective-permute-start(f32[2,2048]{1,0:T(2,128)S(1)} %fusion.39), channel_id=1, source_target_pairs={{0,1},{1,0},{2,3},{3,2},{4,5},{5,4},{6,7},{7,6},{8,9},{9,8},{10,11... | collective-permute-start | bytes 49160 | tf_op jit(solution)/shard_map/ppermute | solution.py:11
  362.4 42.4 %collective-permute-start.32 = (f32[2,2048]{1,0:T(2,128)S(1)}, f32[2,2048]{1,0:T(2,128)S(1)}, u32[]{:S(2)}, u32[]{:S(2)}) collective-permute-start(f32[2,2048]{1,0:T(2,128)S(1)} %add_add_fusion.1), channel_id=1, source_target_pairs={{0,12},{1,13},{2,14},{3,15},{4,8},{5,9},{6,10},{7,11},{8,4},{9,5},... | collective-permute-start | bytes 49160 | tf_op jit(solution)/shard_map/ppermute | solution.py:11
  365.0 48.9 %collective-permute-start.31 = (f32[2,2048]{1,0:T(2,128)S(1)}, f32[2,2048]{1,0:T(2,128)S(1)}, u32[]{:S(2)}, u32[]{:S(2)}) collective-permute-start(f32[2,2048]{1,0:T(2,128)S(1)} %add_add_fusion.1), channel_id=1, source_target_pairs={{0,8},{1,9},{2,10},{3,11},{4,12},{5,13},{6,14},{7,15},{8,0},{9,1},... | collective-permute-start | bytes 49160 | tf_op jit(solution)/shard_map/ppermute | solution.py:11
  403.3 10.6 %collective-permute-start.30 = (f32[2,2048]{1,0:T(2,128)S(1)}, f32[2,2048]{1,0:T(2,128)S(1)}, u32[]{:S(2)}, u32[]{:S(2)}) collective-permute-start(f32[2,2048]{1,0:T(2,128)S(1)} %add_add_fusion.1), channel_id=1, source_target_pairs={{0,4},{1,5},{2,6},{3,7},{4,0},{5,1},{6,2},{7,3},{8,12},{9,13},{10,... | collective-permute-start | bytes 49160 | tf_op jit(solution)/shard_map/ppermute | solution.py:11
  404.8 31.0 %collective-permute-start.9 = (bf16[4,8,8,2048]{3,2,0,1:T(8,128)(2,1)}, bf16[4,8,8,2048]{3,2,0,1:T(8,128)(2,1)S(1)}, u32[]{:S(2)}, u32[]{:S(2)}) collective-permute-start(bf16[4,8,8,2048]{3,2,0,1:T(8,128)(2,1)} %get-tuple-element.72), channel_id=1, source_target_pairs={{0,4},{1,5},{2,6},{3,7},{4,0},{5,1},{6,2},{7,3},{8,12},{9,13},{10,... | collective-permute-start | bytes 3145736 | tf_op jit(solution)/shard_map/ppermute | solution.py:11
  413.8 1.9 collective-permute-start.24
  (13 other events, 152.9 us)

commit v4 on v3

--- a/solution.py
+++ b/solution.py
@@ -19,10 +19,6 @@
 
 def sum_over(value, axis, low, high):
     return tree_sum([from_partner(value, axis, k << low) for k in range(1 << high - low)])
-
-
-def after(value, other):
-    return lax.optimization_barrier((value, other))[0]
 
 
 def body(inputs, upstream, right_blocks, left_blocks, gain, mid_scale):
@@ -51,8 +47,8 @@
 
     up_view = upstream[0].reshape(local, far, near, local, width)
     up_parts = [lax.dynamic_index_in_dim(up_view, device_far ^ k, 1, keepdims=False) for k in range(far)]
-    up_far = [from_partner(up_parts[k], "seq", k << low) for k in range(far)]
-    inputs = after(inputs, up_parts)
+    up_far = [from_partner(up_parts[k], "seq", k << low) for k in range(1, far)]
+    inputs, up_here = lax.optimization_barrier((inputs, up_parts[0]))
     input_float = inputs[0].astype(f32)
     inverse_norm = lax.rsqrt(jnp.mean(input_float * input_float, axis=-1, keepdims=True) + 1e-06)
     standardized_input = input_float * inverse_norm
@@ -65,8 +61,9 @@
     gated_view = gated.reshape(local, far, near, local, width)
     gated_near = [from_partner(gated_view[:, :, k], "seq", k) for k in range(near)]
     gated_near = [jnp.stack([t[:, k] for t in gated_near]) for k in range(far)]
-    gated_far = [from_partner(gated_near[k], "seq", k << low) for k in range(far)]
-    up_far = after(up_far, gated_near)
+    gated_far = [from_partner(gated_near[k], "seq", k << low) for k in range(1, far)]
+    up_far, gated_here = lax.optimization_barrier((up_far, gated_near[0]))
+    up_far = [up_here] + up_far
     up_near = [
         from_partner(
             jnp.stack([lax.dynamic_index_in_dim(t, device_near ^ k, 1, keepdims=False) for t in up_far]), "seq", k
@@ -76,21 +73,23 @@
     upward = jnp.stack(up_near, axis=1).reshape(order, local, width)
     returned = jnp.einsum("bij,ibd->jbd", lefts, upward, preferred_element_type=f32).astype(bf16)
     returned = returned.reshape(far, near, local, local, width)
-    back_far = [from_partner(returned[k], "seq", k << low) for k in range(far)]
-    gated_far = after(gated_far, returned)
-    arrived = jnp.stack(gated_far).reshape(order, local, width)
+    back_far = [from_partner(returned[k], "seq", k << low) for k in range(1, far)]
+    gated_far, returned_here = lax.optimization_barrier((gated_far, returned[0]))
+    arrived = jnp.stack([gated_here] + gated_far).reshape(order, local, width)
     mixed = jnp.einsum("bij,jbd->ibd", lefts, arrived, preferred_element_type=f32).astype(bf16)
     mixed = mixed.reshape(far, near, local, local, width)
+    mixed_here = mixed[:, 0]
+    mixed_sent = [from_partner(mixed[:, k], "seq", k) for k in range(1, near)]
+    upward, arrived, mixed_here = lax.optimization_barrier((upward, arrived, mixed_here))
     mixed_near = jnp.zeros((far, near, local, local, width), bf16)
-    for k in range(near):
-        mixed_near = lax.dynamic_update_index_in_dim(
-            mixed_near, from_partner(mixed[:, k], "seq", k), device_near ^ k, 1
-        )
-    back_far = after(back_far, mixed_near)
+    for k, part in enumerate([mixed_here] + mixed_sent):
+        mixed_near = lax.dynamic_update_index_in_dim(mixed_near, part, device_near ^ k, 1)
+    mixed_far = [from_partner(mixed_near[k], "seq", k << low) for k in range(1, far)]
+    back_far, mixed_here = lax.optimization_barrier((back_far, mixed_near[0]))
+    back_far = [returned_here] + back_far
     back_near = [from_partner(jnp.stack([t[k] for t in back_far]), "seq", k) for k in range(near)]
     dgated = jnp.stack(back_near, axis=1).transpose(2, 0, 1, 3, 4).reshape(local, order, width).astype(f32)
 
-    upward, arrived = after((upward, arrived), mixed)
     grad_left = jnp.einsum("ibd,jbd->bij", upward, arrived, preferred_element_type=f32)
     grad_left = sum_over(grad_left, "dp", 0, dp_levels)
     grad_left = jnp.einsum("ki,aij->akj", swap_full, grad_left, precision=lax.Precision.HIGHEST)
@@ -119,8 +118,8 @@
     gain_gradient, grad_mid = sum_over(vectors, "seq", low, levels)
     output = jnp.zeros((local, far, near, local, width), bf16)
     input_view = inputs[0].reshape(local, far, near, local, width)
-    mixed_far = [from_partner(mixed_near[k], "seq", k << low) for k in range(far)]
-    mixed_far = after(mixed_far, (input_gradient, grad_right))
+    mixed_far, input_gradient = lax.optimization_barrier((mixed_far, input_gradient))
+    mixed_far = [mixed_here] + mixed_far
     for k in range(far):
         place = device_far ^ k
         part = mixed_far[k].swapaxes(0, 1)

time: 443 us -> 446 us (level)
  waiting for transfers between devices: 240 us -> 230 us
  starting transfers between devices: 127 us -> 133 us
    ppermute x33, waiting for transfers between devices: 240 us -> 230 us  [from_partner(): return lax.ppermute(block, axis, [(i, i ^ distance) for i in range(count)])]
    ppermute x33, starting transfers between devices: 127 us -> 133 us  [from_partner(): return lax.ppermute(block, axis, [(i, i ^ distance) for i in range(count)])]
  transfers between devices with their start and end apart: 33 -> 33, of which waited for: 12 -> 14; matrix products, arithmetic and copies ran while one was open for 10% -> 11% of each run, Pallas kernels for 0% -> 0%
where the time goes in v4:
time: 446 us; the launch traced here: 444 us
  waiting for transfers between devices  230 us (52%)
  starting transfers between devices  133 us (30%)
  local copies, waits for them, and re-layouts  34.8 us (8%)
  other arithmetic  23.1 us (5%)
  matrix products  21.3 us (5%)
    ppermute x33, waiting for transfers between devices, from_partner(): return lax.ppermute(block, axis, [(i, i ^ distance) for i in range(count)])  230 us
    ppermute x33, starting transfers between devices, from_partner(): return lax.ppermute(block, axis, [(i, i ^ distance) for i in range(count)])  133 us
  transfers between devices with their start and end apart: 33, of which 14 were waited for; matrix products, arithmetic and copies ran while one was open for 11% of the time, Pallas kernels for 0%

profile of v4, /device:TPU:0, one launch (start us, length us, event | category | flops | bytes accessed | tf_op | source)
XLA Modules:
  0.0 443.8 jit_solution(6204644810349949217)
XLA Ops:
  0.7 4.1 dynamic-slice_bitcast_fusion.3
  6.0 8.9 %multiply_convert_fusion = (bf16[8,128,2048]{2,1,0:T(8,128)(2,1)S(1)}, f32[8,128,2048]{2,1,0:T(8,128)}) fusion(f32[2048]{0:T(1024)S(1)} %copy-done.14, bf16[8,128,128]{1,2,0:T(8,128)(2,1)S(1)} %convolution_bitcast_fusion.3, f32[2048]{0:T(1024)S(1)} %copy-done.13, f32[8,128]{1,0:T(8,128)S(1)} %get-tuple-element.141, bf16[8,128,2048]{2,1,0:T(8,128)(2,1)} %bitcast.283), kind=kOutput, calls=%fused_computation.17 | convolution fusion | flops 557842432 | bytes 17059840 | tf_op jit(solution)/shard_map/aij,ajd->aid/dot_general | solution.py:57
  17.2 2.9 collective-permute-start.3
  24.8 2.6 collective-permute-start.1
  27.6 16.9 %collective-permute-done.3 = bf16[8,4,8,2048]{3,2,0,1:T(8,128)(2,1)} collective-permute-done((bf16[8,4,8,2048]{3,2,0,1:T(8,128)(2,1)}, bf16[8,4,8,2048]{3,2,0,1:T(8,128)(2,1)}, u32[]{:S(2)}, u32[]{:S(2)}) %collective-permute-start.3) | collective-permute-done | bytes 1048608 | tf_op jit(solution)/shard_map/ppermute | solution.py:11
  44.5 4.2 collective-permute-start.2
  50.7 17.9 %collective-permute-done.4 = bf16[8,4,8,2048]{3,2,0,1:T(8,128)(2,1)} collective-permute-done((bf16[8,4,8,2048]{3,2,0,1:T(8,128)(2,1)}, bf16[8,4,8,2048]{3,2,0,1:T(8,128)(2,1)}, u32[]{:S(2)}, u32[]{:S(2)}) %collective-permute-start.4) | collective-permute-done | bytes 1048608 | tf_op jit(solution)/shard_map/ppermute | solution.py:11
  71.8 25.2 %collective-permute-done.1 = bf16[8,4,8,2048]{3,2,1,0:T(8,128)(2,1)} collective-permute-done((bf16[8,4,8,2048]{3,2,1,0:T(8,128)(2,1)}, bf16[8,4,8,2048]{3,2,1,0:T(8,128)(2,1)}, u32[]{:S(2)}, u32[]{:S(2)}) %collective-permute-start.1) | collective-permute-done | bytes 1048608 | tf_op jit(solution)/shard_map/ppermute | solution.py:11
  99.3 2.2 dynamic-slice_bitcast_fusion.16
  110.2 2.5 collective-permute-start.14
  114.0 42.2 %collective-permute-start.13 = (bf16[4,8,8,2048]{3,2,1,0:T(8,128)(2,1)S(1)}, bf16[4,8,8,2048]{3,2,1,0:T(8,128)(2,1)S(1)}, u32[]{:S(2)}, u32[]{:S(2)}) collective-permute-start(bf16[4,8,8,2048]{3,2,1,0:T(8,128)(2,1)S(1)} %pad_maximum_fusion.8), channel_id=1, source_target_pairs={{0,8},{1,9},{2,10},{3,11},{4,12},{5,13},{6,14},{7,15},{8,0},{9,1},... | collective-permute-start | bytes 3145736 | tf_op jit(solution)/shard_map/ppermute | solution.py:11
  156.5 14.5 %collective-permute-start.12 = (bf16[4,8,8,2048]{3,2,1,0:T(8,128)(2,1)S(1)}, bf16[4,8,8,2048]{3,2,1,0:T(8,128)(2,1)S(1)}, u32[]{:S(2)}, u32[]{:S(2)}) collective-permute-start(bf16[4,8,8,2048]{3,2,1,0:T(8,128)(2,1)S(1)} %pad_maximum_fusion.7), channel_id=1, source_target_pairs={{0,4},{1,5},{2,6},{3,7},{4,0},{5,1},{6,2},{7,3},{8,12},{9,13},{10,... | collective-permute-start | bytes 3145736 | tf_op jit(solution)/shard_map/ppermute | solution.py:11
  171.0 2.4 pad_maximum_fusion
  173.4 2.3 copy.81
  177.6 42.2 %collective-permute-done.13 = bf16[4,8,8,2048]{3,2,1,0:T(8,128)(2,1)S(1)} collective-permute-done((bf16[4,8,8,2048]{3,2,1,0:T(8,128)(2,1)S(1)}, bf16[4,8,8,2048]{3,2,1,0:T(8,128)(2,1)S(1)}, u32[]{:S(2)}, u32[]{:S(2)}) %collective-permute-start.13) | collective-permute-done | bytes 1048608 | tf_op jit(solution)/shard_map/ppermute | solution.py:11
  220.4 2.3 copy.88
  229.3 2.5 collective-permute-start.11
  235.5 15.1 %collective-permute-done.15 = bf16[4,8,8,2048]{3,1,0,2:T(8,128)(2,1)S(1)} collective-permute-done((bf16[4,8,8,2048]{3,1,0,2:T(8,128)(2,1)S(1)}, bf16[4,8,8,2048]{3,1,0,2:T(8,128)(2,1)S(1)}, u32[]{:S(2)}, u32[]{:S(2)}) %collective-permute-start.15) | collective-permute-done | bytes 1048608 | tf_op jit(solution)/shard_map/ppermute | solution.py:11
  251.3 18.5 %collective-permute-done.16 = bf16[4,8,8,2048]{3,1,0,2:T(8,128)(2,1)S(1)} collective-permute-done((bf16[4,8,8,2048]{3,1,0,2:T(8,128)(2,1)S(1)}, bf16[4,8,8,2048]{3,1,0,2:T(8,128)(2,1)S(1)}, u32[]{:S(2)}, u32[]{:S(2)}) %collective-permute-start.16) | collective-permute-done | bytes 1048608 | tf_op jit(solution)/shard_map/ppermute | solution.py:11
  272.8 23.5 %collective-permute-done.10 = bf16[4,8,8,2048]{3,2,0,1:T(8,128)(2,1)S(1)} collective-permute-done((bf16[4,8,8,2048]{3,2,0,1:T(8,128)(2,1)S(1)}, bf16[4,8,8,2048]{3,2,0,1:T(8,128)(2,1)S(1)}, u32[]{:S(2)}, u32[]{:S(2)}) %collective-permute-start.10) | collective-permute-done | bytes 1048608 | tf_op jit(solution)/shard_map/ppermute | solution.py:11
  296.4 14.3 %collective-permute-done.9 = bf16[4,8,8,2048]{3,2,0,1:T(8,128)(2,1)S(1)} collective-permute-done((bf16[4,8,8,2048]{3,2,0,1:T(8,128)(2,1)S(1)}, bf16[4,8,8,2048]{3,2,0,1:T(8,128)(2,1)S(1)}, u32[]{:S(2)}, u32[]{:S(2)}) %collective-permute-start.9) | collective-permute-done | bytes 1048608 | tf_op jit(solution)/shard_map/ppermute | solution.py:11
  312.8 10.3 %collective-permute-start.22 = (bf16[4,8,8,2048]{3,2,0,1:T(8,128)(2,1)S(1)}, bf16[4,8,8,2048]{3,2,0,1:T(8,128)(2,1)S(1)}, u32[]{:S(2)}, u32[]{:S(2)}) collective-permute-start(bf16[4,8,8,2048]{3,2,0,1:T(8,128)(2,1)S(1)} %pad_maximum_fusion.11), channel_id=1, source_target_pairs={{0,2},{1,3},{2,0},{3,1},{4,6},{5,7},{6,4},{7,5},{8,10},{9,11},{10,... | collective-permute-start | bytes 3145736 | tf_op jit(solution)/shard_map/ppermute | solution.py:11
  325.9 7.6 %collective-permute-start.18 = (bf16[4,8,8,2048]{3,2,0,1:T(8,128)(2,1)}, bf16[4,8,8,2048]{3,2,0,1:T(8,128)(2,1)}, u32[]{:S(2)}, u32[]{:S(2)}) collective-permute-start(bf16[4,8,8,2048]{3,2,0,1:T(8,128)(2,1)} %get-tuple-element.72), channel_id=1, source_target_pairs={{0,4},{1,5},{2,6},{3,7},{4,0},{5,1},{6,2},{7,3},{8,12},{9,13},{10,... | collective-permute-start | bytes 3145736 | tf_op jit(solution)/shard_map/ppermute | solution.py:11
  334.5 2.8 collective-permute-done.21
  337.3 4.3 collective-permute-start.20
  341.6 20.9 %collective-permute-done.22 = bf16[4,8,8,2048]{3,2,0,1:T(8,128)(2,1)S(1)} collective-permute-done((bf16[4,8,8,2048]{3,2,0,1:T(8,128)(2,1)S(1)}, bf16[4,8,8,2048]{3,2,0,1:T(8,128)(2,1)S(1)}, u32[]{:S(2)}, u32[]{:S(2)}) %collective-permute-start.22) | collective-permute-done | bytes 1048608 | tf_op jit(solution)/shard_map/ppermute | solution.py:11
  362.5 4.8 %fusion.1 = (f32[2048]{0:T(1024)S(1)}, bf16[8,128,2048]{2,1,0:T(8,128)(2,1)S(1)}) fusion(f32[8,128,2048]{2,1,0:T(8,128)S(1)} %bitcast.297, f32[2048]{0:T(1024)S(1)} %copy-done.14, bf16[4,1,8,8,2048]{4,3,1,0,2:T(8,128)(2,1)S(1)} %bitcast.306, bf16[4,1,8,8,2048]{4,3,1,0,2:T(8,128)(2,1)S(1)} %bitcast.305, bf16[4,1,8,8,2048]{4,3,1,0,2:T(8,128)(2,1)S(1)} %bitcast.304, ...), kind=kLoop, calls=%fused_computation.3 | loop fusion | flops 37746688 | bytes 16793600 | tf_op jit(solution)/shard_map/reduce_sum | solution.py:100
  367.3 2.9 multiply_reduce_fusion
  372.4 4.5 %fusion.2 = bf16[1024,2048]{1,0:T(8,128)(2,1)} fusion(f32[8,128,2048]{2,1,0:T(8,128)S(1)} %get-tuple-element.144, bf16[1,1024,2048]{2,1,0:T(8,128)(2,1)S(1)} %copy-done.4, bf16[1,1024,2048]{2,1,0:T(8,128)(2,1)S(1)} %copy-done.3, f32[1024]{0:T(1024)S(1)} %multiply_bitcast_fusion, f32[2048]{0:T(1024)S(1)} %copy-done.13, f32[1024]{0:T(1024)S(1)} %get-tuple-element.140), kind=kLoop, calls=%fused_computation.5 | loop fusion | flops 18874368 | bytes 20987904 | tf_op jit(solution)/shard_map/convert_element_type | solution.py:114
  376.9 28.8 %collective-permute-done.19 = bf16[4,8,8,2048]{3,2,0,1:T(8,128)(2,1)} collective-permute-done((bf16[4,8,8,2048]{3,2,0,1:T(8,128)(2,1)}, bf16[4,8,8,2048]{3,2,0,1:T(8,128)(2,1)}, u32[]{:S(2)}, u32[]{:S(2)}) %collective-permute-start.19) | collective-permute-done | bytes 1048608 | tf_op jit(solution)/shard_map/ppermute | solution.py:11
  412.7 2.4 collective-permute-done.29
  415.1 19.8 %collective-permute-start.30 = (f32[2,2048]{1,0:T(2,128)S(1)}, f32[2,2048]{1,0:T(2,128)S(1)}, u32[]{:S(2)}, u32[]{:S(2)}) collective-permute-start(f32[2,2048]{1,0:T(2,128)S(1)} %add_add_fusion.1), channel_id=1, source_target_pairs={{0,4},{1,5},{2,6},{3,7},{4,0},{5,1},{6,2},{7,3},{8,12},{9,13},{10,... | collective-permute-start | bytes 49160 | tf_op jit(solution)/shard_map/ppermute | solution.py:11
  (140 shorter events, 66.0 us)
Async XLA Ops:
  17.2 27.2 %collective-permute-start.3 = (bf16[8,4,8,2048]{3,2,0,1:T(8,128)(2,1)}, bf16[8,4,8,2048]{3,2,0,1:T(8,128)(2,1)}, u32[]{:S(2)}, u32[]{:S(2)}) collective-permute-start(bf16[8,4,8,2048]{3,2,0,1:T(8,128)(2,1)} %bitcast.281), channel_id=1, source_target_pairs={{0,1},{1,0},{2,3},{3,2},{4,5},{5,4},{6,7},{7,6},{8,9},{9,8},{10,11... | collective-permute-start | bytes 3145736 | tf_op jit(solution)/shard_map/ppermute | solution.py:11
  21.3 47.4 %collective-permute-start.4 = (bf16[8,4,8,2048]{3,2,0,1:T(8,128)(2,1)}, bf16[8,4,8,2048]{3,2,0,1:T(8,128)(2,1)}, u32[]{:S(2)}, u32[]{:S(2)}) collective-permute-start(bf16[8,4,8,2048]{3,2,0,1:T(8,128)(2,1)} %bitcast.280), channel_id=1, source_target_pairs={{0,2},{1,3},{2,0},{3,1},{4,6},{5,7},{6,4},{7,5},{8,10},{9,11},{10,... | collective-permute-start | bytes 3145736 | tf_op jit(solution)/shard_map/ppermute | solution.py:11
  22.8 48.0 %collective-permute-start.5 = (bf16[8,4,8,2048]{3,2,1,0:T(8,128)(2,1)}, bf16[8,4,8,2048]{3,2,1,0:T(8,128)(2,1)S(1)}, u32[]{:S(2)}, u32[]{:S(2)}) collective-permute-start(bf16[8,4,8,2048]{3,2,1,0:T(8,128)(2,1)} %get-tuple-element.84), channel_id=1, source_target_pairs={{0,3},{1,2},{2,1},{3,0},{4,7},{5,6},{6,5},{7,4},{8,11},{9,10},{10,... | collective-permute-start | bytes 3145736 | tf_op jit(solution)/shard_map/ppermute | solution.py:11
  22.8 49.1 %collective-permute-start = (bf16[8,4,8,2048]{3,2,1,0:T(8,128)(2,1)}, bf16[8,4,8,2048]{3,2,1,0:T(8,128)(2,1)}, u32[]{:S(2)}, u32[]{:S(2)}) collective-permute-start(bf16[8,4,8,2048]{3,2,1,0:T(8,128)(2,1)} %get-tuple-element.89), channel_id=1, source_target_pairs={{0,4},{1,5},{2,6},{3,7},{4,0},{5,1},{6,2},{7,3},{8,12},{9,13},{10,... | collective-permute-start | bytes 3145736 | tf_op jit(solution)/shard_map/ppermute | solution.py:11
  24.8 72.3 %collective-permute-start.1 = (bf16[8,4,8,2048]{3,2,1,0:T(8,128)(2,1)}, bf16[8,4,8,2048]{3,2,1,0:T(8,128)(2,1)}, u32[]{:S(2)}, u32[]{:S(2)}) collective-permute-start(bf16[8,4,8,2048]{3,2,1,0:T(8,128)(2,1)} %get-tuple-element.88), channel_id=1, source_target_pairs={{0,8},{1,9},{2,10},{3,11},{4,12},{5,13},{6,14},{7,15},{8,0},{9,1},... | collective-permute-start | bytes 3145736 | tf_op jit(solution)/shard_map/ppermute | solution.py:11
  44.5 52.6 %collective-permute-start.2 = (bf16[8,4,8,2048]{3,2,1,0:T(8,128)(2,1)}, bf16[8,4,8,2048]{3,2,1,0:T(8,128)(2,1)S(1)}, u32[]{:S(2)}, u32[]{:S(2)}) collective-permute-start(bf16[8,4,8,2048]{3,2,1,0:T(8,128)(2,1)} %get-tuple-element.87), channel_id=1, source_target_pairs={{0,12},{1,13},{2,14},{3,15},{4,8},{5,9},{6,10},{7,11},{8,4},{9,5},... | collective-permute-start | bytes 3145736 | tf_op jit(solution)/shard_map/ppermute | solution.py:11
  101.6 54.9 %collective-permute-start.6 = (bf16[4,8,8,2048]{3,2,1,0:T(8,128)(2,1)S(1)}, bf16[4,8,8,2048]{3,2,1,0:T(8,128)(2,1)}, u32[]{:S(2)}, u32[]{:S(2)}) collective-permute-start(bf16[4,8,8,2048]{3,2,1,0:T(8,128)(2,1)S(1)} %pad_maximum_fusion.4), channel_id=1, source_target_pairs={{0,1},{1,0},{2,3},{3,2},{4,5},{5,4},{6,7},{7,6},{8,9},{9,8},{10,11... | collective-permute-start | bytes 3145736 | tf_op jit(solution)/shard_map/ppermute | solution.py:11
  104.3 66.7 %collective-permute-start.7 = (bf16[4,8,8,2048]{3,2,1,0:T(8,128)(2,1)}, bf16[4,8,8,2048]{3,2,1,0:T(8,128)(2,1)}, u32[]{:S(2)}, u32[]{:S(2)}) collective-permute-start(bf16[4,8,8,2048]{3,2,1,0:T(8,128)(2,1)} %pad_maximum_fusion.5), channel_id=1, source_target_pairs={{0,2},{1,3},{2,0},{3,1},{4,6},{5,7},{6,4},{7,5},{8,10},{9,11},{10,... | collective-permute-start | bytes 3145736 | tf_op jit(solution)/shard_map/ppermute | solution.py:11
  106.9 64.1 %collective-permute-start.8 = (bf16[4,8,8,2048]{3,2,1,0:T(8,128)(2,1)}, bf16[4,8,8,2048]{3,2,1,0:T(8,128)(2,1)}, u32[]{:S(2)}, u32[]{:S(2)}) collective-permute-start(bf16[4,8,8,2048]{3,2,1,0:T(8,128)(2,1)} %pad_maximum_fusion.6), channel_id=1, source_target_pairs={{0,3},{1,2},{2,1},{3,0},{4,7},{5,6},{6,5},{7,4},{8,11},{9,10},{10,... | collective-permute-start | bytes 3145736 | tf_op jit(solution)/shard_map/ppermute | solution.py:11
  110.2 67.4 %collective-permute-start.14 = (bf16[4,8,8,2048]{3,2,1,0:T(8,128)(2,1)S(1)}, bf16[4,8,8,2048]{3,2,1,0:T(8,128)(2,1)S(1)}, u32[]{:S(2)}, u32[]{:S(2)}) collective-permute-start(bf16[4,8,8,2048]{3,2,1,0:T(8,128)(2,1)S(1)} %pad_maximum_fusion.9), channel_id=1, source_target_pairs={{0,12},{1,13},{2,14},{3,15},{4,8},{5,9},{6,10},{7,11},{8,4},{9,5},... | collective-permute-start | bytes 3145736 | tf_op jit(solution)/shard_map/ppermute | solution.py:11
  114.0 105.8 %collective-permute-start.13 = (bf16[4,8,8,2048]{3,2,1,0:T(8,128)(2,1)S(1)}, bf16[4,8,8,2048]{3,2,1,0:T(8,128)(2,1)S(1)}, u32[]{:S(2)}, u32[]{:S(2)}) collective-permute-start(bf16[4,8,8,2048]{3,2,1,0:T(8,128)(2,1)S(1)} %pad_maximum_fusion.8), channel_id=1, source_target_pairs={{0,8},{1,9},{2,10},{3,11},{4,12},{5,13},{6,14},{7,15},{8,0},{9,1},... | collective-permute-start | bytes 3145736 | tf_op jit(solution)/shard_map/ppermute | solution.py:11
  156.5 63.3 %collective-permute-start.12 = (bf16[4,8,8,2048]{3,2,1,0:T(8,128)(2,1)S(1)}, bf16[4,8,8,2048]{3,2,1,0:T(8,128)(2,1)S(1)}, u32[]{:S(2)}, u32[]{:S(2)}) collective-permute-start(bf16[4,8,8,2048]{3,2,1,0:T(8,128)(2,1)S(1)} %pad_maximum_fusion.7), channel_id=1, source_target_pairs={{0,4},{1,5},{2,6},{3,7},{4,0},{5,1},{6,2},{7,3},{8,12},{9,13},{10,... | collective-permute-start | bytes 3145736 | tf_op jit(solution)/shard_map/ppermute | solution.py:11
  224.5 26.2 %collective-permute-start.15 = (bf16[4,8,8,2048]{3,1,0,2:T(8,128)(2,1)S(1)}, bf16[4,8,8,2048]{3,1,0,2:T(8,128)(2,1)S(1)}, u32[]{:S(2)}, u32[]{:S(2)}) collective-permute-start(bf16[4,8,8,2048]{3,1,0,2:T(8,128)(2,1)S(1)} %get-tuple-element.76), channel_id=1, source_target_pairs={{0,1},{1,0},{2,3},{3,2},{4,5},{5,4},{6,7},{7,6},{8,9},{9,8},{10,11... | collective-permute-start | bytes 3145736 | tf_op jit(solution)/shard_map/ppermute | solution.py:11
  226.0 43.7 %collective-permute-start.16 = (bf16[4,8,8,2048]{3,1,0,2:T(8,128)(2,1)S(1)}, bf16[4,8,8,2048]{3,1,0,2:T(8,128)(2,1)S(1)}, u32[]{:S(2)}, u32[]{:S(2)}) collective-permute-start(bf16[4,8,8,2048]{3,1,0,2:T(8,128)(2,1)S(1)} %get-tuple-element.75), channel_id=1, source_target_pairs={{0,2},{1,3},{2,0},{3,1},{4,6},{5,7},{6,4},{7,5},{8,10},{9,11},{10,... | collective-permute-start | bytes 3145736 | tf_op jit(solution)/shard_map/ppermute | solution.py:11
  227.5 42.8 %collective-permute-start.17 = (bf16[4,8,8,2048]{3,1,0,2:T(8,128)(2,1)S(1)}, bf16[4,8,8,2048]{3,1,0,2:T(8,128)(2,1)S(1)}, u32[]{:S(2)}, u32[]{:S(2)}) collective-permute-start(bf16[4,8,8,2048]{3,1,0,2:T(8,128)(2,1)S(1)} %get-tuple-element.74), channel_id=1, source_target_pairs={{0,3},{1,2},{2,1},{3,0},{4,7},{5,6},{6,5},{7,4},{8,11},{9,10},{10,... | collective-permute-start | bytes 3145736 | tf_op jit(solution)/shard_map/ppermute | solution.py:11
  228.6 67.8 %collective-permute-start.10 = (bf16[4,8,8,2048]{3,2,0,1:T(8,128)(2,1)S(1)}, bf16[4,8,8,2048]{3,2,0,1:T(8,128)(2,1)S(1)}, u32[]{:S(2)}, u32[]{:S(2)}) collective-permute-start(bf16[4,8,8,2048]{3,2,0,1:T(8,128)(2,1)S(1)} %copy.84), channel_id=1, source_target_pairs={{0,8},{1,9},{2,10},{3,11},{4,12},{5,13},{6,14},{7,15},{8,0},{9,1},... | collective-permute-start | bytes 3145736 | tf_op jit(solution)/shard_map/ppermute | solution.py:11
  229.3 67.1 %collective-permute-start.11 = (bf16[4,8,8,2048]{3,2,0,1:T(8,128)(2,1)S(1)}, bf16[4,8,8,2048]{3,2,0,1:T(8,128)(2,1)S(1)}, u32[]{:S(2)}, u32[]{:S(2)}) collective-permute-start(bf16[4,8,8,2048]{3,2,0,1:T(8,128)(2,1)S(1)} %copy.85), channel_id=1, source_target_pairs={{0,12},{1,13},{2,14},{3,15},{4,8},{5,9},{6,10},{7,11},{8,4},{9,5},... | collective-permute-start | bytes 3145736 | tf_op jit(solution)/shard_map/ppermute | solution.py:11
  250.6 60.1 %collective-permute-start.9 = (bf16[4,8,8,2048]{3,2,0,1:T(8,128)(2,1)S(1)}, bf16[4,8,8,2048]{3,2,0,1:T(8,128)(2,1)S(1)}, u32[]{:S(2)}, u32[]{:S(2)}) collective-permute-start(bf16[4,8,8,2048]{3,2,0,1:T(8,128)(2,1)S(1)} %copy.83), channel_id=1, source_target_pairs={{0,4},{1,5},{2,6},{3,7},{4,0},{5,1},{6,2},{7,3},{8,12},{9,13},{10,... | collective-permute-start | bytes 3145736 | tf_op jit(solution)/shard_map/ppermute | solution.py:11
  269.7 54.0 %collective-permute-start.25 = (f32[8,128,128]{2,1,0:T(8,128)S(1)}, f32[8,128,128]{2,1,0:T(8,128)S(1)}, u32[]{:S(2)}, u32[]{:S(2)}) collective-permute-start(f32[8,128,128]{2,1,0:T(8,128)S(1)} %fusion.49), channel_id=1, source_target_pairs={{0,16},{16,0},{1,17},{17,1},{2,18},{18,2},{3,19},{19,3},{4,20},{20... | collective-permute-start | bytes 1572872 | tf_op jit(solution)/shard_map/ppermute | solution.py:11
  311.1 26.2 %collective-permute-start.21 = (bf16[4,8,8,2048]{3,2,0,1:T(8,128)(2,1)S(1)}, bf16[4,8,8,2048]{3,2,0,1:T(8,128)(2,1)S(1)}, u32[]{:S(2)}, u32[]{:S(2)}) collective-permute-start(bf16[4,8,8,2048]{3,2,0,1:T(8,128)(2,1)S(1)} %pad_maximum_fusion.10), channel_id=1, source_target_pairs={{0,1},{1,0},{2,3},{3,2},{4,5},{5,4},{6,7},{7,6},{8,9},{9,8},{10,11... | collective-permute-start | bytes 3145736 | tf_op jit(solution)/shard_map/ppermute | solution.py:11
  312.8 49.6 %collective-permute-start.22 = (bf16[4,8,8,2048]{3,2,0,1:T(8,128)(2,1)S(1)}, bf16[4,8,8,2048]{3,2,0,1:T(8,128)(2,1)S(1)}, u32[]{:S(2)}, u32[]{:S(2)}) collective-permute-start(bf16[4,8,8,2048]{3,2,0,1:T(8,128)(2,1)S(1)} %pad_maximum_fusion.11), channel_id=1, source_target_pairs={{0,2},{1,3},{2,0},{3,1},{4,6},{5,7},{6,4},{7,5},{8,10},{9,11},{10,... | collective-permute-start | bytes 3145736 | tf_op jit(solution)/shard_map/ppermute | solution.py:11
  323.2 39.2 %collective-permute-start.23 = (bf16[4,8,8,2048]{3,2,0,1:T(8,128)(2,1)S(1)}, bf16[4,8,8,2048]{3,2,0,1:T(8,128)(2,1)S(1)}, u32[]{:S(2)}, u32[]{:S(2)}) collective-permute-start(bf16[4,8,8,2048]{3,2,0,1:T(8,128)(2,1)S(1)} %pad_maximum_fusion.12), channel_id=1, source_target_pairs={{0,3},{1,2},{2,1},{3,0},{4,7},{5,6},{6,5},{7,4},{8,11},{9,10},{10,... | collective-permute-start | bytes 3145736 | tf_op jit(solution)/shard_map/ppermute | solution.py:11
  325.9 51.0 %collective-permute-start.18 = (bf16[4,8,8,2048]{3,2,0,1:T(8,128)(2,1)}, bf16[4,8,8,2048]{3,2,0,1:T(8,128)(2,1)}, u32[]{:S(2)}, u32[]{:S(2)}) collective-permute-start(bf16[4,8,8,2048]{3,2,0,1:T(8,128)(2,1)} %get-tuple-element.72), channel_id=1, source_target_pairs={{0,4},{1,5},{2,6},{3,7},{4,0},{5,1},{6,2},{7,3},{8,12},{9,13},{10,... | collective-permute-start | bytes 3145736 | tf_op jit(solution)/shard_map/ppermute | solution.py:11
  333.4 72.3 %collective-permute-start.19 = (bf16[4,8,8,2048]{3,2,0,1:T(8,128)(2,1)}, bf16[4,8,8,2048]{3,2,0,1:T(8,128)(2,1)}, u32[]{:S(2)}, u32[]{:S(2)}) collective-permute-start(bf16[4,8,8,2048]{3,2,0,1:T(8,128)(2,1)} %get-tuple-element.71), channel_id=1, source_target_pairs={{0,8},{1,9},{2,10},{3,11},{4,12},{5,13},{6,14},{7,15},{8,0},{9,1},... | collective-permute-start | bytes 3145736 | tf_op jit(solution)/shard_map/ppermute | solution.py:11
  337.3 68.4 %collective-permute-start.20 = (bf16[4,8,8,2048]{3,2,0,1:T(8,128)(2,1)}, bf16[4,8,8,2048]{3,2,0,1:T(8,128)(2,1)S(1)}, u32[]{:S(2)}, u32[]{:S(2)}) collective-permute-start(bf16[4,8,8,2048]{3,2,0,1:T(8,128)(2,1)} %get-tuple-element.70), channel_id=1, source_target_pairs={{0,12},{1,13},{2,14},{3,15},{4,8},{5,9},{6,10},{7,11},{8,4},{9,5},... | collective-permute-start | bytes 3145736 | tf_op jit(solution)/shard_map/ppermute | solution.py:11
  371.6 35.7 %collective-permute-start.26 = (f32[2,2048]{1,0:T(2,128)S(1)}, f32[2,2048]{1,0:T(2,128)S(1)}, u32[]{:S(2)}, u32[]{:S(2)}) collective-permute-start(f32[2,2048]{1,0:T(2,128)S(1)} %pad_maximum_fusion.13), channel_id=1, source_target_pairs={{0,16},{16,0},{1,17},{17,1},{2,18},{18,2},{3,19},{19,3},{4,20},{20... | collective-permute-start | bytes 49160 | tf_op jit(solution)/shard_map/ppermute | solution.py:11
  371.7 70.3 %collective-permute-start.24 = (f32[8,128,128]{2,1,0:T(8,128)S(1)}, f32[8,128,128]{2,1,0:T(8,128)S(1)}, u32[]{:S(2)}, u32[]{:S(2)}) collective-permute-start(f32[8,128,128]{2,1,0:T(8,128)S(1)} %fusion.13), channel_id=1, source_target_pairs={{0,16},{16,0},{1,17},{17,1},{2,18},{18,2},{3,19},{19,3},{4,20},{20... | collective-permute-start | bytes 1572872 | tf_op jit(solution)/shard_map/ppermute | solution.py:11
  407.4 5.2 %collective-permute-start.27 = (f32[2,2048]{1,0:T(2,128)S(1)}, f32[2,2048]{1,0:T(2,128)S(1)}, u32[]{:S(2)}, u32[]{:S(2)}) collective-permute-start(f32[2,2048]{1,0:T(2,128)S(1)} %fusion.40), channel_id=1, source_target_pairs={{0,1},{1,0},{2,3},{3,2},{4,5},{5,4},{6,7},{7,6},{8,9},{9,8},{10,11... | collective-permute-start | bytes 49160 | tf_op jit(solution)/shard_map/ppermute | solution.py:11
  410.4 4.6 %collective-permute-start.29 = (f32[2,2048]{1,0:T(2,128)S(1)}, f32[2,2048]{1,0:T(2,128)S(1)}, u32[]{:S(2)}, u32[]{:S(2)}) collective-permute-start(f32[2,2048]{1,0:T(2,128)S(1)} %fusion.40), channel_id=1, source_target_pairs={{0,3},{1,2},{2,1},{3,0},{4,7},{5,6},{6,5},{7,4},{8,11},{9,10},{10,... | collective-permute-start | bytes 49160 | tf_op jit(solution)/shard_map/ppermute | solution.py:11
  415.1 24.7 %collective-permute-start.30 = (f32[2,2048]{1,0:T(2,128)S(1)}, f32[2,2048]{1,0:T(2,128)S(1)}, u32[]{:S(2)}, u32[]{:S(2)}) collective-permute-start(f32[2,2048]{1,0:T(2,128)S(1)} %add_add_fusion.1), channel_id=1, source_target_pairs={{0,4},{1,5},{2,6},{3,7},{4,0},{5,1},{6,2},{7,3},{8,12},{9,13},{10,... | collective-permute-start | bytes 49160 | tf_op jit(solution)/shard_map/ppermute | solution.py:11
  435.0 4.9 %collective-permute-start.31 = (f32[2,2048]{1,0:T(2,128)S(1)}, f32[2,2048]{1,0:T(2,128)S(1)}, u32[]{:S(2)}, u32[]{:S(2)}) collective-permute-start(f32[2,2048]{1,0:T(2,128)S(1)} %add_add_fusion.1), channel_id=1, source_target_pairs={{0,8},{1,9},{2,10},{3,11},{4,12},{5,13},{6,14},{7,15},{8,0},{9,1},... | collective-permute-start | bytes 49160 | tf_op jit(solution)/shard_map/ppermute | solution.py:11
  435.8 5.5 %collective-permute-start.32 = (f32[2,2048]{1,0:T(2,128)S(1)}, f32[2,2048]{1,0:T(2,128)S(1)}, u32[]{:S(2)}, u32[]{:S(2)}) collective-permute-start(f32[2,2048]{1,0:T(2,128)S(1)} %add_add_fusion.1), channel_id=1, source_target_pairs={{0,12},{1,13},{2,14},{3,15},{4,8},{5,9},{6,10},{7,11},{8,4},{9,5},... | collective-permute-start | bytes 49160 | tf_op jit(solution)/shard_map/ppermute | solution.py:11
  (18 other events, 488.5 us)

commit v5 on v4

--- a/solution.py
+++ b/solution.py
@@ -61,9 +61,10 @@
     gated_view = gated.reshape(local, far, near, local, width)
     gated_near = [from_partner(gated_view[:, :, k], "seq", k) for k in range(near)]
     gated_near = [jnp.stack([t[:, k] for t in gated_near]) for k in range(far)]
+    up_far, gated_near = lax.optimization_barrier((up_far, gated_near))
+    up_far = [up_here] + up_far
+    gated_here = gated_near[0]
     gated_far = [from_partner(gated_near[k], "seq", k << low) for k in range(1, far)]
-    up_far, gated_here = lax.optimization_barrier((up_far, gated_near[0]))
-    up_far = [up_here] + up_far
     up_near = [
         from_partner(
             jnp.stack([lax.dynamic_index_in_dim(t, device_near ^ k, 1, keepdims=False) for t in up_far]), "seq", k
@@ -73,8 +74,9 @@
     upward = jnp.stack(up_near, axis=1).reshape(order, local, width)
     returned = jnp.einsum("bij,ibd->jbd", lefts, upward, preferred_element_type=f32).astype(bf16)
     returned = returned.reshape(far, near, local, local, width)
+    gated_far, returned = lax.optimization_barrier((gated_far, returned))
+    returned_here = returned[0]
     back_far = [from_partner(returned[k], "seq", k << low) for k in range(1, far)]
-    gated_far, returned_here = lax.optimization_barrier((gated_far, returned[0]))
     arrived = jnp.stack([gated_here] + gated_far).reshape(order, local, width)
     mixed = jnp.einsum("bij,jbd->ibd", lefts, arrived, preferred_element_type=f32).astype(bf16)
     mixed = mixed.reshape(far, near, local, local, width)
@@ -84,9 +86,10 @@
     mixed_near = jnp.zeros((far, near, local, local, width), bf16)
     for k, part in enumerate([mixed_here] + mixed_sent):
         mixed_near = lax.dynamic_update_index_in_dim(mixed_near, part, device_near ^ k, 1)
+    back_far, mixed_near = lax.optimization_barrier((back_far, mixed_near))
+    back_far = [returned_here] + back_far
+    mixed_here = mixed_near[0]
     mixed_far = [from_partner(mixed_near[k], "seq", k << low) for k in range(1, far)]
-    back_far, mixed_here = lax.optimization_barrier((back_far, mixed_near[0]))
-    back_far = [returned_here] + back_far
     back_near = [from_partner(jnp.stack([t[k] for t in back_far]), "seq", k) for k in range(near)]
     dgated = jnp.stack(back_near, axis=1).transpose(2, 0, 1, 3, 4).reshape(local, order, width).astype(f32)
 
@@ -118,7 +121,9 @@
     gain_gradient, grad_mid = sum_over(vectors, "seq", low, levels)
     output = jnp.zeros((local, far, near, local, width), bf16)
     input_view = inputs[0].reshape(local, far, near, local, width)
-    mixed_far, input_gradient = lax.optimization_barrier((mixed_far, input_gradient))
+    mixed_far, input_gradient, gain_gradient, grad_mid = lax.optimization_barrier(
+        (mixed_far, input_gradient, gain_gradient, grad_mid)
+    )
     mixed_far = [mixed_here] + mixed_far
     for k in range(far):
         place = device_far ^ k

time: 446 us -> 446 us (level)
  starting transfers between devices: 133 us -> 123 us
  between operations: 1.46 us -> 9.86 us
    ppermute x33, starting transfers between devices: 133 us -> 123 us  [from_partner(): return lax.ppermute(block, axis, [(i, i ^ distance) for i in range(count)])]
    optimization_barrier x1 -> x2, local copies, waits for them, and re-layouts: 0.58 us -> 5.5 us  [body(): gated_far, returned = lax.optimization_barrier((gated_far, returned))]
  transfers between devices with their start and end apart: 33 -> 33, of which waited for: 14 -> 15; matrix products, arithmetic and copies ran while one was open for 11% -> 11% of each run, Pallas kernels for 0% -> 0%
where the time goes in v5:
time: 446 us; the launch traced here: 444 us
  waiting for transfers between devices  231 us (52%)
  starting transfers between devices  123 us (28%)
  local copies, waits for them, and re-layouts  37.3 us (8%)
  matrix products  21.4 us (5%)
  other arithmetic  21.1 us (5%)
  between operations  9.86 us (2%)
    ppermute x33, waiting for transfers between devices, from_partner(): return lax.ppermute(block, axis, [(i, i ^ distance) for i in range(count)])  231 us
    ppermute x33, starting transfers between devices, from_partner(): return lax.ppermute(block, axis, [(i, i ^ distance) for i in range(count)])  123 us
    dot_general x1, matrix products, body(): first = jnp.einsum('aij,ajd->aid', rights, grid, preferred_element_type=f32)  8.97 us
  transfers between devices with their start and end apart: 33, of which 15 were waited for; matrix products, arithmetic and copies ran while one was open for 11% of the time, Pallas kernels for 0%

profile of v5, /device:TPU:0, one launch (start us, length us, event | category | flops | bytes accessed | tf_op | source)
XLA Modules:
  0.0 443.9 jit_solution(14290324000701952734)
XLA Ops:
  0.7 4.1 dynamic-slice_bitcast_fusion.3
  6.1 9.0 %multiply_convert_fusion = (bf16[8,128,2048]{2,1,0:T(8,128)(2,1)S(1)}, f32[8,128,2048]{2,1,0:T(8,128)}) fusion(f32[2048]{0:T(1024)S(1)} %copy-done.9, bf16[8,128,128]{1,2,0:T(8,128)(2,1)S(1)} %convolution_bitcast_fusion.3, f32[2048]{0:T(1024)S(1)} %copy-done.8, f32[8,128]{1,0:T(8,128)S(1)} %get-tuple-element.149, bf16[8,128,2048]{2,1,0:T(8,128)(2,1)} %bitcast.295), kind=kOutput, calls=%fused_computation.17 | convolution fusion | flops 557842432 | bytes 17059840 | tf_op jit(solution)/shard_map/aij,ajd->aid/dot_general | solution.py:57
  17.4 2.9 collective-permute-start.3
  22.9 2.0 collective-permute-start
  25.0 2.6 collective-permute-start.1
  28.6 16.0 %collective-permute-done.3 = bf16[8,4,8,2048]{3,2,0,1:T(8,128)(2,1)} collective-permute-done((bf16[8,4,8,2048]{3,2,0,1:T(8,128)(2,1)}, bf16[8,4,8,2048]{3,2,0,1:T(8,128)(2,1)}, u32[]{:S(2)}, u32[]{:S(2)}) %collective-permute-start.3) | collective-permute-done | bytes 1048608 | tf_op jit(solution)/shard_map/ppermute | solution.py:11
  44.6 4.2 collective-permute-start.2
  50.1 18.8 %collective-permute-done.4 = bf16[8,4,8,2048]{3,2,0,1:T(8,128)(2,1)} collective-permute-done((bf16[8,4,8,2048]{3,2,0,1:T(8,128)(2,1)}, bf16[8,4,8,2048]{3,2,0,1:T(8,128)(2,1)}, u32[]{:S(2)}, u32[]{:S(2)}) %collective-permute-start.4) | collective-permute-done | bytes 1048608 | tf_op jit(solution)/shard_map/ppermute | solution.py:11
  74.2 23.1 %collective-permute-done.1 = bf16[8,4,8,2048]{3,2,1,0:T(8,128)(2,1)} collective-permute-done((bf16[8,4,8,2048]{3,2,1,0:T(8,128)(2,1)}, bf16[8,4,8,2048]{3,2,1,0:T(8,128)(2,1)}, u32[]{:S(2)}, u32[]{:S(2)}) %collective-permute-start.1) | collective-permute-done | bytes 1048608 | tf_op jit(solution)/shard_map/ppermute | solution.py:11
  108.4 20.7 %collective-permute-start.6 = (bf16[4,8,8,2048]{3,2,1,0:T(8,128)(2,1)}, bf16[4,8,8,2048]{3,2,1,0:T(8,128)(2,1)S(1)}, u32[]{:S(2)}, u32[]{:S(2)}) collective-permute-start(bf16[4,8,8,2048]{3,2,1,0:T(8,128)(2,1)} %get-tuple-element.33), channel_id=1, source_target_pairs={{0,4},{1,5},{2,6},{3,7},{4,0},{5,1},{6,2},{7,3},{8,12},{9,13},{10,... | collective-permute-start | bytes 3145736 | tf_op jit(solution)/shard_map/ppermute | solution.py:11
  133.3 14.4 %collective-permute-done.10 = bf16[4,8,8,2048]{3,2,1,0:T(8,128)(2,1)} collective-permute-done((bf16[4,8,8,2048]{3,2,1,0:T(8,128)(2,1)S(1)}, bf16[4,8,8,2048]{3,2,1,0:T(8,128)(2,1)}, u32[]{:S(2)}, u32[]{:S(2)}) %collective-permute-start.10) | collective-permute-done | bytes 1048608 | tf_op jit(solution)/shard_map/ppermute | solution.py:11
  147.7 2.4 pad_maximum_fusion
  150.0 2.3 copy.83
  153.6 16.3 %collective-permute-done.6 = bf16[4,8,8,2048]{3,2,1,0:T(8,128)(2,1)S(1)} collective-permute-done((bf16[4,8,8,2048]{3,2,1,0:T(8,128)(2,1)}, bf16[4,8,8,2048]{3,2,1,0:T(8,128)(2,1)S(1)}, u32[]{:S(2)}, u32[]{:S(2)}) %collective-permute-start.6) | collective-permute-done | bytes 1048608 | tf_op jit(solution)/shard_map/ppermute | solution.py:11
  169.9 31.3 %collective-permute-done.7 = bf16[4,8,8,2048]{3,2,1,0:T(8,128)(2,1)S(1)} collective-permute-done((bf16[4,8,8,2048]{3,2,1,0:T(8,128)(2,1)}, bf16[4,8,8,2048]{3,2,1,0:T(8,128)(2,1)S(1)}, u32[]{:S(2)}, u32[]{:S(2)}) %collective-permute-start.7) | collective-permute-done | bytes 1048608 | tf_op jit(solution)/shard_map/ppermute | solution.py:11
  201.8 2.3 copy.88
  210.9 2.3 copy.85
  213.4 18.8 %collective-permute-start.12 = (bf16[4,8,8,2048]{3,2,0,1:T(8,128)(2,1)S(1)}, bf16[4,8,8,2048]{3,2,0,1:T(8,128)(2,1)S(1)}, u32[]{:S(2)}, u32[]{:S(2)}) collective-permute-start(bf16[4,8,8,2048]{3,2,0,1:T(8,128)(2,1)S(1)} %get-tuple-element.93), channel_id=1, source_target_pairs={{0,4},{1,5},{2,6},{3,7},{4,0},{5,1},{6,2},{7,3},{8,12},{9,13},{10,... | collective-permute-start | bytes 3145736 | tf_op jit(solution)/shard_map/ppermute | solution.py:11
  233.4 3.2 copy.95
  249.0 7.5 %collective-permute-done.16 = bf16[4,8,8,2048]{3,1,0,2:T(8,128)(2,1)S(1)} collective-permute-done((bf16[4,8,8,2048]{3,1,0,2:T(8,128)(2,1)S(1)}, bf16[4,8,8,2048]{3,1,0,2:T(8,128)(2,1)S(1)}, u32[]{:S(2)}, u32[]{:S(2)}) %collective-permute-start.16) | collective-permute-done | bytes 1048608 | tf_op jit(solution)/shard_map/ppermute | solution.py:11
  257.8 6.7 %collective-permute-done.12 = bf16[4,8,8,2048]{3,2,0,1:T(8,128)(2,1)S(1)} collective-permute-done((bf16[4,8,8,2048]{3,2,0,1:T(8,128)(2,1)S(1)}, bf16[4,8,8,2048]{3,2,0,1:T(8,128)(2,1)S(1)}, u32[]{:S(2)}, u32[]{:S(2)}) %collective-permute-start.12) | collective-permute-done | bytes 1048608 | tf_op jit(solution)/shard_map/ppermute | solution.py:11
  264.5 52.6 %collective-permute-done.13 = bf16[4,8,8,2048]{3,2,0,1:T(8,128)(2,1)S(1)} collective-permute-done((bf16[4,8,8,2048]{3,2,0,1:T(8,128)(2,1)S(1)}, bf16[4,8,8,2048]{3,2,0,1:T(8,128)(2,1)S(1)}, u32[]{:S(2)}, u32[]{:S(2)}) %collective-permute-start.13) | collective-permute-done | bytes 1048608 | tf_op jit(solution)/shard_map/ppermute | solution.py:11
  324.7 21.4 %collective-permute-start.18 = (bf16[4,8,8,2048]{3,2,0,1:T(8,128)(2,1)}, bf16[4,8,8,2048]{3,2,0,1:T(8,128)(2,1)S(1)}, u32[]{:S(2)}, u32[]{:S(2)}) collective-permute-start(bf16[4,8,8,2048]{3,2,0,1:T(8,128)(2,1)} %get-tuple-element.86), channel_id=1, source_target_pairs={{0,4},{1,5},{2,6},{3,7},{4,0},{5,1},{6,2},{7,3},{8,12},{9,13},{10,... | collective-permute-start | bytes 3145736 | tf_op jit(solution)/shard_map/ppermute | solution.py:11
  347.2 16.2 %collective-permute-done.22 = bf16[4,8,8,2048]{3,2,0,1:T(8,128)(2,1)S(1)} collective-permute-done((bf16[4,8,8,2048]{3,2,0,1:T(8,128)(2,1)S(1)}, bf16[4,8,8,2048]{3,2,0,1:T(8,128)(2,1)S(1)}, u32[]{:S(2)}, u32[]{:S(2)}) %collective-permute-start.22) | collective-permute-done | bytes 1048608 | tf_op jit(solution)/shard_map/ppermute | solution.py:11
  363.4 4.8 %fusion.1 = (f32[2048]{0:T(1024)S(1)}, bf16[8,128,2048]{2,1,0:T(8,128)(2,1)S(1)}) fusion(f32[8,128,2048]{2,1,0:T(8,128)S(1)} %bitcast.311, f32[2048]{0:T(1024)S(1)} %copy-done.9, bf16[4,1,8,8,2048]{4,3,1,0,2:T(8,128)(2,1)S(1)} %bitcast.320, bf16[4,1,8,8,2048]{4,3,1,0,2:T(8,128)(2,1)S(1)} %bitcast.319, bf16[4,1,8,8,2048]{4,3,1,0,2:T(8,128)(2,1)S(1)} %bitcast.318, ...), kind=kLoop, calls=%fused_computation.3 | loop fusion | flops 37746688 | bytes 16793600 | tf_op jit(solution)/shard_map/reduce_sum | solution.py:103
  368.2 2.9 multiply_reduce_fusion
  376.2 2.5 collective-permute-start.20
  379.2 23.1 %collective-permute-start.28 = (f32[2,2048]{1,0:T(2,128)S(1)}, f32[2,2048]{1,0:T(2,128)S(1)}, u32[]{:S(2)}, u32[]{:S(2)}) collective-permute-start(f32[2,2048]{1,0:T(2,128)S(1)} %add_add_fusion.1), channel_id=1, source_target_pairs={{0,4},{1,5},{2,6},{3,7},{4,0},{5,1},{6,2},{7,3},{8,12},{9,13},{10,... | collective-permute-start | bytes 49160 | tf_op jit(solution)/shard_map/ppermute | solution.py:11
  402.3 4.8 %fusion.2 = bf16[1024,2048]{1,0:T(8,128)(2,1)} fusion(f32[8,128,2048]{2,1,0:T(8,128)S(1)} %get-tuple-element.152, bf16[1,1024,2048]{2,1,0:T(8,128)(2,1)S(1)} %copy-done.4, bf16[1,1024,2048]{2,1,0:T(8,128)(2,1)S(1)} %copy-done.3, f32[1024]{0:T(1024)S(1)} %multiply_bitcast_fusion, f32[2048]{0:T(1024)S(1)} %copy-done.8, f32[1024]{0:T(1024)S(1)} %get-tuple-element.148), kind=kLoop, calls=%fused_computation.5 | loop fusion | flops 18874368 | bytes 20987904 | tf_op jit(solution)/shard_map/convert_element_type | solution.py:117
  408.2 6.6 %collective-permute-done.28 = f32[2,2048]{1,0:T(2,128)S(1)} collective-permute-done((f32[2,2048]{1,0:T(2,128)S(1)}, f32[2,2048]{1,0:T(2,128)S(1)}, u32[]{:S(2)}, u32[]{:S(2)}) %collective-permute-start.28) | collective-permute-done | bytes 16416 | tf_op jit(solution)/shard_map/ppermute | solution.py:11
  417.7 20.5 %collective-permute-done.29 = f32[2,2048]{1,0:T(2,128)S(1)} collective-permute-done((f32[2,2048]{1,0:T(2,128)S(1)}, f32[2,2048]{1,0:T(2,128)S(1)}, u32[]{:S(2)}, u32[]{:S(2)}) %collective-permute-start.29) | collective-permute-done | bytes 16416 | tf_op jit(solution)/shard_map/ppermute | solution.py:11
  440.1 2.0 copy-done.5
  (128 shorter events, 65.9 us)
Async XLA Ops:
  17.4 27.2 %collective-permute-start.3 = (bf16[8,4,8,2048]{3,2,0,1:T(8,128)(2,1)}, bf16[8,4,8,2048]{3,2,0,1:T(8,128)(2,1)}, u32[]{:S(2)}, u32[]{:S(2)}) collective-permute-start(bf16[8,4,8,2048]{3,2,0,1:T(8,128)(2,1)} %bitcast.293), channel_id=1, source_target_pairs={{0,1},{1,0},{2,3},{3,2},{4,5},{5,4},{6,7},{7,6},{8,9},{9,8},{10,11... | collective-permute-start | bytes 3145736 | tf_op jit(solution)/shard_map/ppermute | solution.py:11
  21.4 47.4 %collective-permute-start.4 = (bf16[8,4,8,2048]{3,2,0,1:T(8,128)(2,1)}, bf16[8,4,8,2048]{3,2,0,1:T(8,128)(2,1)}, u32[]{:S(2)}, u32[]{:S(2)}) collective-permute-start(bf16[8,4,8,2048]{3,2,0,1:T(8,128)(2,1)} %bitcast.292), channel_id=1, source_target_pairs={{0,2},{1,3},{2,0},{3,1},{4,6},{5,7},{6,4},{7,5},{8,10},{9,11},{10,... | collective-permute-start | bytes 3145736 | tf_op jit(solution)/shard_map/ppermute | solution.py:11
  22.9 47.1 %collective-permute-start.5 = (bf16[8,4,8,2048]{3,2,1,0:T(8,128)(2,1)}, bf16[8,4,8,2048]{3,2,1,0:T(8,128)(2,1)}, u32[]{:S(2)}, u32[]{:S(2)}) collective-permute-start(bf16[8,4,8,2048]{3,2,1,0:T(8,128)(2,1)} %get-tuple-element.96), channel_id=1, source_target_pairs={{0,3},{1,2},{2,1},{3,0},{4,7},{5,6},{6,5},{7,4},{8,11},{9,10},{10,... | collective-permute-start | bytes 3145736 | tf_op jit(solution)/shard_map/ppermute | solution.py:11
  22.9 51.2 %collective-permute-start = (bf16[8,4,8,2048]{3,2,1,0:T(8,128)(2,1)}, bf16[8,4,8,2048]{3,2,1,0:T(8,128)(2,1)}, u32[]{:S(2)}, u32[]{:S(2)}) collective-permute-start(bf16[8,4,8,2048]{3,2,1,0:T(8,128)(2,1)} %get-tuple-element.101), channel_id=1, source_target_pairs={{0,4},{1,5},{2,6},{3,7},{4,0},{5,1},{6,2},{7,3},{8,12},{9,13},{10,... | collective-permute-start | bytes 3145736 | tf_op jit(solution)/shard_map/ppermute | solution.py:11
  25.0 72.3 %collective-permute-start.1 = (bf16[8,4,8,2048]{3,2,1,0:T(8,128)(2,1)}, bf16[8,4,8,2048]{3,2,1,0:T(8,128)(2,1)}, u32[]{:S(2)}, u32[]{:S(2)}) collective-permute-start(bf16[8,4,8,2048]{3,2,1,0:T(8,128)(2,1)} %get-tuple-element.100), channel_id=1, source_target_pairs={{0,8},{1,9},{2,10},{3,11},{4,12},{5,13},{6,14},{7,15},{8,0},{9,1},... | collective-permute-start | bytes 3145736 | tf_op jit(solution)/shard_map/ppermute | solution.py:11
  44.6 52.6 %collective-permute-start.2 = (bf16[8,4,8,2048]{3,2,1,0:T(8,128)(2,1)}, bf16[8,4,8,2048]{3,2,1,0:T(8,128)(2,1)S(1)}, u32[]{:S(2)}, u32[]{:S(2)}) collective-permute-start(bf16[8,4,8,2048]{3,2,1,0:T(8,128)(2,1)} %get-tuple-element.99), channel_id=1, source_target_pairs={{0,12},{1,13},{2,14},{3,15},{4,8},{5,9},{6,10},{7,11},{8,4},{9,5},... | collective-permute-start | bytes 3145736 | tf_op jit(solution)/shard_map/ppermute | solution.py:11
  103.1 27.1 %collective-permute-start.9 = (bf16[4,8,8,2048]{3,2,1,0:T(8,128)(2,1)}, bf16[4,8,8,2048]{3,2,1,0:T(8,128)(2,1)}, u32[]{:S(2)}, u32[]{:S(2)}) collective-permute-start(bf16[4,8,8,2048]{3,2,1,0:T(8,128)(2,1)} %pad_maximum_fusion.7), channel_id=1, source_target_pairs={{0,1},{1,0},{2,3},{3,2},{4,5},{5,4},{6,7},{7,6},{8,9},{9,8},{10,11... | collective-permute-start | bytes 3145736 | tf_op jit(solution)/shard_map/ppermute | solution.py:11
  104.7 42.9 %collective-permute-start.10 = (bf16[4,8,8,2048]{3,2,1,0:T(8,128)(2,1)S(1)}, bf16[4,8,8,2048]{3,2,1,0:T(8,128)(2,1)}, u32[]{:S(2)}, u32[]{:S(2)}) collective-permute-start(bf16[4,8,8,2048]{3,2,1,0:T(8,128)(2,1)S(1)} %pad_maximum_fusion.8), channel_id=1, source_target_pairs={{0,2},{1,3},{2,0},{3,1},{4,6},{5,7},{6,4},{7,5},{8,10},{9,11},{10,... | collective-permute-start | bytes 3145736 | tf_op jit(solution)/shard_map/ppermute | solution.py:11
  106.4 41.2 %collective-permute-start.11 = (bf16[4,8,8,2048]{3,2,1,0:T(8,128)(2,1)S(1)}, bf16[4,8,8,2048]{3,2,1,0:T(8,128)(2,1)}, u32[]{:S(2)}, u32[]{:S(2)}) collective-permute-start(bf16[4,8,8,2048]{3,2,1,0:T(8,128)(2,1)S(1)} %pad_maximum_fusion.9), channel_id=1, source_target_pairs={{0,3},{1,2},{2,1},{3,0},{4,7},{5,6},{6,5},{7,4},{8,11},{9,10},{10,... | collective-permute-start | bytes 3145736 | tf_op jit(solution)/shard_map/ppermute | solution.py:11
  108.4 61.5 %collective-permute-start.6 = (bf16[4,8,8,2048]{3,2,1,0:T(8,128)(2,1)}, bf16[4,8,8,2048]{3,2,1,0:T(8,128)(2,1)S(1)}, u32[]{:S(2)}, u32[]{:S(2)}) collective-permute-start(bf16[4,8,8,2048]{3,2,1,0:T(8,128)(2,1)} %get-tuple-element.33), channel_id=1, source_target_pairs={{0,4},{1,5},{2,6},{3,7},{4,0},{5,1},{6,2},{7,3},{8,12},{9,13},{10,... | collective-permute-start | bytes 3145736 | tf_op jit(solution)/shard_map/ppermute | solution.py:11
  129.1 72.1 %collective-permute-start.7 = (bf16[4,8,8,2048]{3,2,1,0:T(8,128)(2,1)}, bf16[4,8,8,2048]{3,2,1,0:T(8,128)(2,1)S(1)}, u32[]{:S(2)}, u32[]{:S(2)}) collective-permute-start(bf16[4,8,8,2048]{3,2,1,0:T(8,128)(2,1)} %get-tuple-element.34), channel_id=1, source_target_pairs={{0,8},{1,9},{2,10},{3,11},{4,12},{5,13},{6,14},{7,15},{8,0},{9,1},... | collective-permute-start | bytes 3145736 | tf_op jit(solution)/shard_map/ppermute | solution.py:11
  130.2 71.1 %collective-permute-start.8 = (bf16[4,8,8,2048]{3,2,1,0:T(8,128)(2,1)}, bf16[4,8,8,2048]{3,2,1,0:T(8,128)(2,1)S(1)}, u32[]{:S(2)}, u32[]{:S(2)}) collective-permute-start(bf16[4,8,8,2048]{3,2,1,0:T(8,128)(2,1)} %get-tuple-element.35), channel_id=1, source_target_pairs={{0,12},{1,13},{2,14},{3,15},{4,8},{5,9},{6,10},{7,11},{8,4},{9,5},... | collective-permute-start | bytes 3145736 | tf_op jit(solution)/shard_map/ppermute | solution.py:11
  207.2 37.9 %collective-permute-start.32 = (f32[8,128,128]{2,1,0:T(8,128)S(1)}, f32[8,128,128]{2,1,0:T(8,128)S(1)}, u32[]{:S(2)}, u32[]{:S(2)}) collective-permute-start(f32[8,128,128]{2,1,0:T(8,128)S(1)} %fusion.49), channel_id=1, source_target_pairs={{0,16},{16,0},{1,17},{17,1},{2,18},{18,2},{3,19},{19,3},{4,20},{20... | collective-permute-start | bytes 1572872 | tf_op jit(solution)/shard_map/ppermute | solution.py:11
  207.3 39.6 %collective-permute-start.15 = (bf16[4,8,8,2048]{3,1,0,2:T(8,128)(2,1)S(1)}, bf16[4,8,8,2048]{3,1,0,2:T(8,128)(2,1)S(1)}, u32[]{:S(2)}, u32[]{:S(2)}) collective-permute-start(bf16[4,8,8,2048]{3,1,0,2:T(8,128)(2,1)S(1)} %get-tuple-element.89), channel_id=1, source_target_pairs={{0,1},{1,0},{2,3},{3,2},{4,5},{5,4},{6,7},{7,6},{8,9},{9,8},{10,11... | collective-permute-start | bytes 3145736 | tf_op jit(solution)/shard_map/ppermute | solution.py:11
  208.9 47.7 %collective-permute-start.16 = (bf16[4,8,8,2048]{3,1,0,2:T(8,128)(2,1)S(1)}, bf16[4,8,8,2048]{3,1,0,2:T(8,128)(2,1)S(1)}, u32[]{:S(2)}, u32[]{:S(2)}) collective-permute-start(bf16[4,8,8,2048]{3,1,0,2:T(8,128)(2,1)S(1)} %get-tuple-element.88), channel_id=1, source_target_pairs={{0,2},{1,3},{2,0},{3,1},{4,6},{5,7},{6,4},{7,5},{8,10},{9,11},{10,... | collective-permute-start | bytes 3145736 | tf_op jit(solution)/shard_map/ppermute | solution.py:11
  210.4 46.8 %collective-permute-start.17 = (bf16[4,8,8,2048]{3,1,0,2:T(8,128)(2,1)S(1)}, bf16[4,8,8,2048]{3,1,0,2:T(8,128)(2,1)S(1)}, u32[]{:S(2)}, u32[]{:S(2)}) collective-permute-start(bf16[4,8,8,2048]{3,1,0,2:T(8,128)(2,1)S(1)} %get-tuple-element.87), channel_id=1, source_target_pairs={{0,3},{1,2},{2,1},{3,0},{4,7},{5,6},{6,5},{7,4},{8,11},{9,10},{10,... | collective-permute-start | bytes 3145736 | tf_op jit(solution)/shard_map/ppermute | solution.py:11
  213.4 51.1 %collective-permute-start.12 = (bf16[4,8,8,2048]{3,2,0,1:T(8,128)(2,1)S(1)}, bf16[4,8,8,2048]{3,2,0,1:T(8,128)(2,1)S(1)}, u32[]{:S(2)}, u32[]{:S(2)}) collective-permute-start(bf16[4,8,8,2048]{3,2,0,1:T(8,128)(2,1)S(1)} %get-tuple-element.93), channel_id=1, source_target_pairs={{0,4},{1,5},{2,6},{3,7},{4,0},{5,1},{6,2},{7,3},{8,12},{9,13},{10,... | collective-permute-start | bytes 3145736 | tf_op jit(solution)/shard_map/ppermute | solution.py:11
  245.1 72.0 %collective-permute-start.13 = (bf16[4,8,8,2048]{3,2,0,1:T(8,128)(2,1)S(1)}, bf16[4,8,8,2048]{3,2,0,1:T(8,128)(2,1)S(1)}, u32[]{:S(2)}, u32[]{:S(2)}) collective-permute-start(bf16[4,8,8,2048]{3,2,0,1:T(8,128)(2,1)S(1)} %get-tuple-element.92), channel_id=1, source_target_pairs={{0,8},{1,9},{2,10},{3,11},{4,12},{5,13},{6,14},{7,15},{8,0},{9,1},... | collective-permute-start | bytes 3145736 | tf_op jit(solution)/shard_map/ppermute | solution.py:11
  246.9 70.2 %collective-permute-start.14 = (bf16[4,8,8,2048]{3,2,0,1:T(8,128)(2,1)S(1)}, bf16[4,8,8,2048]{3,2,0,1:T(8,128)(2,1)S(1)}, u32[]{:S(2)}, u32[]{:S(2)}) collective-permute-start(bf16[4,8,8,2048]{3,2,0,1:T(8,128)(2,1)S(1)} %get-tuple-element.91), channel_id=1, source_target_pairs={{0,12},{1,13},{2,14},{3,15},{4,8},{5,9},{6,10},{7,11},{8,4},{9,5},... | collective-permute-start | bytes 3145736 | tf_op jit(solution)/shard_map/ppermute | solution.py:11
  317.6 29.6 %collective-permute-start.21 = (bf16[4,8,8,2048]{3,2,0,1:T(8,128)(2,1)S(1)}, bf16[4,8,8,2048]{3,2,0,1:T(8,128)(2,1)S(1)}, u32[]{:S(2)}, u32[]{:S(2)}) collective-permute-start(bf16[4,8,8,2048]{3,2,0,1:T(8,128)(2,1)S(1)} %pad_maximum_fusion.10), channel_id=1, source_target_pairs={{0,1},{1,0},{2,3},{3,2},{4,5},{5,4},{6,7},{7,6},{8,9},{9,8},{10,11... | collective-permute-start | bytes 3145736 | tf_op jit(solution)/shard_map/ppermute | solution.py:11
  319.3 44.1 %collective-permute-start.22 = (bf16[4,8,8,2048]{3,2,0,1:T(8,128)(2,1)S(1)}, bf16[4,8,8,2048]{3,2,0,1:T(8,128)(2,1)S(1)}, u32[]{:S(2)}, u32[]{:S(2)}) collective-permute-start(bf16[4,8,8,2048]{3,2,0,1:T(8,128)(2,1)S(1)} %pad_maximum_fusion.11), channel_id=1, source_target_pairs={{0,2},{1,3},{2,0},{3,1},{4,6},{5,7},{6,4},{7,5},{8,10},{9,11},{10,... | collective-permute-start | bytes 3145736 | tf_op jit(solution)/shard_map/ppermute | solution.py:11
  321.0 42.4 %collective-permute-start.23 = (bf16[4,8,8,2048]{3,2,0,1:T(8,128)(2,1)S(1)}, bf16[4,8,8,2048]{3,2,0,1:T(8,128)(2,1)S(1)}, u32[]{:S(2)}, u32[]{:S(2)}) collective-permute-start(bf16[4,8,8,2048]{3,2,0,1:T(8,128)(2,1)S(1)} %pad_maximum_fusion.12), channel_id=1, source_target_pairs={{0,3},{1,2},{2,1},{3,0},{4,7},{5,6},{6,5},{7,4},{8,11},{9,10},{10,... | collective-permute-start | bytes 3145736 | tf_op jit(solution)/shard_map/ppermute | solution.py:11
  324.7 114.1 %collective-permute-start.18 = (bf16[4,8,8,2048]{3,2,0,1:T(8,128)(2,1)}, bf16[4,8,8,2048]{3,2,0,1:T(8,128)(2,1)S(1)}, u32[]{:S(2)}, u32[]{:S(2)}) collective-permute-start(bf16[4,8,8,2048]{3,2,0,1:T(8,128)(2,1)} %get-tuple-element.86), channel_id=1, source_target_pairs={{0,4},{1,5},{2,6},{3,7},{4,0},{5,1},{6,2},{7,3},{8,12},{9,13},{10,... | collective-permute-start | bytes 3145736 | tf_op jit(solution)/shard_map/ppermute | solution.py:11
  346.0 92.8 %collective-permute-start.19 = (bf16[4,8,8,2048]{3,2,0,1:T(8,128)(2,1)}, bf16[4,8,8,2048]{3,2,0,1:T(8,128)(2,1)S(1)}, u32[]{:S(2)}, u32[]{:S(2)}) collective-permute-start(bf16[4,8,8,2048]{3,2,0,1:T(8,128)(2,1)} %get-tuple-element.85), channel_id=1, source_target_pairs={{0,8},{1,9},{2,10},{3,11},{4,12},{5,13},{6,14},{7,15},{8,0},{9,1},... | collective-permute-start | bytes 3145736 | tf_op jit(solution)/shard_map/ppermute | solution.py:11
  372.4 3.8 collective-permute-start.25
  373.5 5.2 %collective-permute-start.26 = (f32[2,2048]{1,0:T(2,128)S(1)}, f32[2,2048]{1,0:T(2,128)S(1)}, u32[]{:S(2)}, u32[]{:S(2)}) collective-permute-start(f32[2,2048]{1,0:T(2,128)S(1)} %fusion.41), channel_id=1, source_target_pairs={{0,2},{1,3},{2,0},{3,1},{4,6},{5,7},{6,4},{7,5},{8,10},{9,11},{10,... | collective-permute-start | bytes 49160 | tf_op jit(solution)/shard_map/ppermute | solution.py:11
  374.6 4.6 %collective-permute-start.27 = (f32[2,2048]{1,0:T(2,128)S(1)}, f32[2,2048]{1,0:T(2,128)S(1)}, u32[]{:S(2)}, u32[]{:S(2)}) collective-permute-start(f32[2,2048]{1,0:T(2,128)S(1)} %fusion.41), channel_id=1, source_target_pairs={{0,3},{1,2},{2,1},{3,0},{4,7},{5,6},{6,5},{7,4},{8,11},{9,10},{10,... | collective-permute-start | bytes 49160 | tf_op jit(solution)/shard_map/ppermute | solution.py:11
  376.2 62.5 %collective-permute-start.20 = (bf16[4,8,8,2048]{3,2,0,1:T(8,128)(2,1)}, bf16[4,8,8,2048]{3,2,0,1:T(8,128)(2,1)S(1)}, u32[]{:S(2)}, u32[]{:S(2)}) collective-permute-start(bf16[4,8,8,2048]{3,2,0,1:T(8,128)(2,1)} %get-tuple-element.84), channel_id=1, source_target_pairs={{0,12},{1,13},{2,14},{3,15},{4,8},{5,9},{6,10},{7,11},{8,4},{9,5},... | collective-permute-start | bytes 3145736 | tf_op jit(solution)/shard_map/ppermute | solution.py:11
  379.2 35.6 %collective-permute-start.28 = (f32[2,2048]{1,0:T(2,128)S(1)}, f32[2,2048]{1,0:T(2,128)S(1)}, u32[]{:S(2)}, u32[]{:S(2)}) collective-permute-start(f32[2,2048]{1,0:T(2,128)S(1)} %add_add_fusion.1), channel_id=1, source_target_pairs={{0,4},{1,5},{2,6},{3,7},{4,0},{5,1},{6,2},{7,3},{8,12},{9,13},{10,... | collective-permute-start | bytes 49160 | tf_op jit(solution)/shard_map/ppermute | solution.py:11
  407.1 31.0 %collective-permute-start.29 = (f32[2,2048]{1,0:T(2,128)S(1)}, f32[2,2048]{1,0:T(2,128)S(1)}, u32[]{:S(2)}, u32[]{:S(2)}) collective-permute-start(f32[2,2048]{1,0:T(2,128)S(1)} %add_add_fusion.1), channel_id=1, source_target_pairs={{0,8},{1,9},{2,10},{3,11},{4,12},{5,13},{6,14},{7,15},{8,0},{9,1},... | collective-permute-start | bytes 49160 | tf_op jit(solution)/shard_map/ppermute | solution.py:11
  414.9 23.3 %collective-permute-start.30 = (f32[2,2048]{1,0:T(2,128)S(1)}, f32[2,2048]{1,0:T(2,128)S(1)}, u32[]{:S(2)}, u32[]{:S(2)}) collective-permute-start(f32[2,2048]{1,0:T(2,128)S(1)} %add_add_fusion.1), channel_id=1, source_target_pairs={{0,12},{1,13},{2,14},{3,15},{4,8},{5,9},{6,10},{7,11},{8,4},{9,5},... | collective-permute-start | bytes 49160 | tf_op jit(solution)/shard_map/ppermute | solution.py:11
  438.1 3.9 collective-permute-start.31
  (13 other events, 156.2 us)

commit v6 on v3

--- a/solution.py
+++ b/solution.py
@@ -19,10 +19,6 @@
 
 def sum_over(value, axis, low, high):
     return tree_sum([from_partner(value, axis, k << low) for k in range(1 << high - low)])
-
-
-def after(value, other):
-    return lax.optimization_barrier((value, other))[0]
 
 
 def body(inputs, upstream, right_blocks, left_blocks, gain, mid_scale):
@@ -49,10 +45,13 @@
     rights = jnp.einsum("ki,aij->akj", swap_half, right_blocks)
     lefts = jnp.einsum("aij,jl->ail", jnp.einsum("ki,aij->akj", swap_half, left_blocks), swap_half)
 
+    half = far // 2
+    rest = [k for k in range(1, far) if k != half]
+
     up_view = upstream[0].reshape(local, far, near, local, width)
     up_parts = [lax.dynamic_index_in_dim(up_view, device_far ^ k, 1, keepdims=False) for k in range(far)]
     up_far = [from_partner(up_parts[k], "seq", k << low) for k in range(far)]
-    inputs = after(inputs, up_parts)
+    inputs, up_far[0] = lax.optimization_barrier((inputs, up_far[0]))
     input_float = inputs[0].astype(f32)
     inverse_norm = lax.rsqrt(jnp.mean(input_float * input_float, axis=-1, keepdims=True) + 1e-06)
     standardized_input = input_float * inverse_norm
@@ -64,33 +63,64 @@
 
     gated_view = gated.reshape(local, far, near, local, width)
     gated_near = [from_partner(gated_view[:, :, k], "seq", k) for k in range(near)]
-    gated_near = [jnp.stack([t[:, k] for t in gated_near]) for k in range(far)]
-    gated_far = [from_partner(gated_near[k], "seq", k << low) for k in range(far)]
-    up_far = after(up_far, gated_near)
-    up_near = [
-        from_partner(
-            jnp.stack([lax.dynamic_index_in_dim(t, device_near ^ k, 1, keepdims=False) for t in up_far]), "seq", k
-        )
-        for k in range(near)
-    ]
+
+    def sent_near(part):
+        return [lax.dynamic_index_in_dim(part, device_near ^ k, 1, keepdims=False) for k in range(near)]
+
+    up_half = sent_near(up_far[half])
+    up_half, gated_near = lax.optimization_barrier((up_half, gated_near))
+    gated_sent = [jnp.stack([t[:, k] for t in gated_near]) for k in range(far)]
+    up_rest, gated_rest = lax.optimization_barrier(([up_far[k] for k in rest], [gated_sent[k] for k in rest]))
+    for k, up_part, gated_part in zip(rest, up_rest, gated_rest):
+        up_far[k], gated_sent[k] = up_part, gated_part
+    gated_far = [from_partner(gated_sent[k], "seq", k << low) for k in range(far)]
+    up_sent = [up_half if k == half else sent_near(up_far[k]) for k in range(far)]
+    up_near = [from_partner(jnp.stack([t[k] for t in up_sent]), "seq", k) for k in range(near)]
+
+    gated_pair = jnp.stack([gated_far[0], gated_far[half]])
+    gated_pair, up_near = lax.optimization_barrier((gated_pair, up_near))
+    gated_far[0], gated_far[half] = gated_pair[0], gated_pair[1]
     upward = jnp.stack(up_near, axis=1).reshape(order, local, width)
     returned = jnp.einsum("bij,ibd->jbd", lefts, upward, preferred_element_type=f32).astype(bf16)
-    returned = returned.reshape(far, near, local, local, width)
+    returned = list(returned.reshape(far, near, local, local, width))
+    gated_rest, returned_rest = lax.optimization_barrier(
+        ([gated_far[k] for k in rest], [returned[k] for k in rest])
+    )
+    for k, gated_part, returned_part in zip(rest, gated_rest, returned_rest):
+        gated_far[k], returned[k] = gated_part, returned_part
     back_far = [from_partner(returned[k], "seq", k << low) for k in range(far)]
-    gated_far = after(gated_far, returned)
+
     arrived = jnp.stack(gated_far).reshape(order, local, width)
     mixed = jnp.einsum("bij,jbd->ibd", lefts, arrived, preferred_element_type=f32).astype(bf16)
     mixed = mixed.reshape(far, near, local, local, width)
+    mixed_parts = [from_partner(mixed[:, k], "seq", k) for k in range(near)]
+    upward, arrived, mixed_parts[0] = lax.optimization_barrier((upward, arrived, mixed_parts[0]))
+    back_pair = jnp.stack([back_far[0], back_far[half]])
+    back_pair, mixed_parts = lax.optimization_barrier((back_pair, mixed_parts))
+    back_far[0], back_far[half] = back_pair[0], back_pair[1]
     mixed_near = jnp.zeros((far, near, local, local, width), bf16)
-    for k in range(near):
-        mixed_near = lax.dynamic_update_index_in_dim(
-            mixed_near, from_partner(mixed[:, k], "seq", k), device_near ^ k, 1
-        )
-    back_far = after(back_far, mixed_near)
+    for k, part in enumerate(mixed_parts):
+        mixed_near = lax.dynamic_update_index_in_dim(mixed_near, part, device_near ^ k, 1)
+    mixed_sent = list(mixed_near)
+    back_rest, mixed_rest = lax.optimization_barrier(([back_far[k] for k in rest], [mixed_sent[k] for k in rest]))
+    for k, back_part, mixed_part in zip(rest, back_rest, mixed_rest):
+        back_far[k], mixed_sent[k] = back_part, mixed_part
+    mixed_far = [from_partner(mixed_sent[k], "seq", k << low) for k in range(far)]
     back_near = [from_partner(jnp.stack([t[k] for t in back_far]), "seq", k) for k in range(near)]
+
+    input_view = inputs[0].reshape(local, far, near, local, width)
+
+    def placed(output, part, k):
+        place = device_far ^ k
+        residual = lax.dynamic_index_in_dim(input_view, place, 1, keepdims=False).astype(f32)
+        block = (residual + part.swapaxes(0, 1).astype(f32)).astype(bf16)
+        return lax.dynamic_update_index_in_dim(output, block, place, 1)
+
+    output = jnp.zeros((local, far, near, local, width), bf16)
+    output = placed(placed(output, mixed_far[0], 0), mixed_far[half], half)
+    output, back_near = lax.optimization_barrier((output, back_near))
     dgated = jnp.stack(back_near, axis=1).transpose(2, 0, 1, 3, 4).reshape(local, order, width).astype(f32)
 
-    upward, arrived = after((upward, arrived), mixed)
     grad_left = jnp.einsum("ibd,jbd->bij", upward, arrived, preferred_element_type=f32)
     grad_left = sum_over(grad_left, "dp", 0, dp_levels)
     grad_left = jnp.einsum("ki,aij->akj", swap_full, grad_left, precision=lax.Precision.HIGHEST)
@@ -117,15 +147,11 @@
     vectors = sum_over(vectors, "dp", 0, dp_levels)
     vectors = sum_over(vectors, "seq", 0, low)
     gain_gradient, grad_mid = sum_over(vectors, "seq", low, levels)
-    output = jnp.zeros((local, far, near, local, width), bf16)
-    input_view = inputs[0].reshape(local, far, near, local, width)
-    mixed_far = [from_partner(mixed_near[k], "seq", k << low) for k in range(far)]
-    mixed_far = after(mixed_far, (input_gradient, grad_right))
-    for k in range(far):
-        place = device_far ^ k
-        part = mixed_far[k].swapaxes(0, 1)
-        residual = lax.dynamic_index_in_dim(input_view, place, 1, keepdims=False).astype(f32)
-        output = lax.dynamic_update_index_in_dim(output, (residual + part.astype(f32)).astype(bf16), place, 1)
+    mixed_rest, input_gradient, gain_gradient, grad_mid = lax.optimization_barrier(
+        ([mixed_far[k] for k in rest], input_gradient, gain_gradient, grad_mid)
+    )
+    for k, part in zip(rest, mixed_rest):
+        output = placed(output, part, k)
     return (
         output.reshape(1, rows, width),
         input_gradient.reshape(1, rows, width),

time: 443 us -> 400 us (0.903); the launches traced: 442 us -> 393 us
  starting transfers between devices: 127 us -> 82.3 us
  waiting for transfers between devices: 240 us -> 217 us
  other arithmetic: 24.7 us -> 35 us
  local copies, waits for them, and re-layouts: 31.6 us -> 36.1 us
    ppermute x33, starting transfers between devices: 127 us -> 82.3 us  [from_partner(): return lax.ppermute(block, axis, [(i, i ^ distance) for i in range(count)])]
    ppermute x33, waiting for transfers between devices: 240 us -> 217 us  [from_partner(): return lax.ppermute(block, axis, [(i, i ^ distance) for i in range(count)])]
    another operation x2 -> x1, other arithmetic: 3.38 us -> 13.8 us  [body(): upward = jnp.stack(up_near, axis=1).reshape(order, local, width)]
    another operation x6 -> x11, local copies, waits for them, and re-layouts: 5.33 us -> 12.2 us  [the longest x5 7.57 us: body(): gated_sent = [jnp.stack([t[:, k] for t in gated_near]) for k in range(far)]]
  transfers between devices with their start and end apart: 33 -> 33, of which waited for: 12 -> 11; matrix products, arithmetic and copies ran while one was open for 10% -> 19% of each run, Pallas kernels for 0% -> 0%
where the time goes in v6:
time: 400 us; the launch traced here: 393 us
  waiting for transfers between devices  217 us (54%)
  starting transfers between devices  82.3 us (21%)
  local copies, waits for them, and re-layouts  36.1 us (9%)
  other arithmetic  35 us (9%)
  matrix products  21.4 us (5%)
    ppermute x33, waiting for transfers between devices, from_partner(): return lax.ppermute(block, axis, [(i, i ^ distance) for i in range(count)])  217 us
    ppermute x33, starting transfers between devices, from_partner(): return lax.ppermute(block, axis, [(i, i ^ distance) for i in range(count)])  82.3 us
    another operation x1, other arithmetic, body(): upward = jnp.stack(up_near, axis=1).reshape(order, local, width)  13.8 us
    dot_general x1, matrix products, body(): first = jnp.einsum('aij,ajd->aid', rights, grid, preferred_element_type=f32)  8.98 us
  transfers between devices with their start and end apart: 33, of which 11 were waited for; matrix products, arithmetic and copies ran while one was open for 19% of the time, Pallas kernels for 0%

profile of v6, /device:TPU:0, one launch (start us, length us, event | category | flops | bytes accessed | tf_op | source)
XLA Modules:
  0.0 393.2 jit_solution(10106803348579838891)
XLA Ops:
  0.7 4.2 %dynamic-slice_bitcast_fusion = (bf16[8,4,8,2048]{3,2,1,0:T(8,128)(2,1)}, bf16[8,4,8,2048]{3,2,1,0:T(8,128)(2,1)}, bf16[8,4,8,2048]{3,2,1,0:T(8,128)(2,1)}, bf16[8,4,8,2048]{3,2,1,0:T(8,128)(2,1)S(1)}) fusion(bf16[8,4,4,8,2048]{4,3,2,1,0:T(8,128)(2,1)} %bitcast.328, s32[]{:T(128)S(6)} %select_n.59, s32[]{:T(128)S(6)} %select_n.58, s32[]{:T(128)S(6)} %select_n.53, ...), kind=kLoop, calls=%fused_computation.83 | loop fusion | bytes 8388624 | tf_op jit(solution)/shard_map/jit(dynamic_index_in_dim)/squeeze | solution.py:52
  4.9 4.0 %collective-permute-start = (bf16[8,4,8,2048]{3,2,1,0:T(8,128)(2,1)}, bf16[8,4,8,2048]{3,2,1,0:T(8,128)(2,1)}, u32[]{:S(2)}, u32[]{:S(2)}) collective-permute-start(bf16[8,4,8,2048]{3,2,1,0:T(8,128)(2,1)} %get-tuple-element.131), channel_id=1, source_target_pairs={{0,8},{1,9},{2,10},{3,11},{4,12},{5,13},{6,14},{7,15},{8,0},{9,1},... | collective-permute-start | bytes 3145736 | tf_op jit(solution)/shard_map/ppermute | solution.py:11
  10.1 9.0 %multiply_convert_fusion = (bf16[8,128,2048]{2,1,0:T(8,128)(2,1)S(1)}, f32[8,128,2048]{2,1,0:T(8,128)}) fusion(f32[2048]{0:T(1024)S(1)} %copy-done.9, bf16[8,128,128]{1,2,0:T(8,128)(2,1)S(1)} %convolution_bitcast_fusion.3, f32[2048]{0:T(1024)S(1)} %copy-done.8, f32[8,128]{1,0:T(8,128)S(1)} %get-tuple-element.189, bf16[8,128,2048]{2,1,0:T(8,128)(2,1)} %bitcast.316), kind=kOutput, calls=%fused_computation.17 | convolution fusion | flops 557842432 | bytes 17059840 | tf_op jit(solution)/shard_map/aij,ajd->aid/dot_general | solution.py:60
  28.6 26.4 %collective-permute-done = bf16[8,4,8,2048]{3,2,1,0:T(8,128)(2,1)} collective-permute-done((bf16[8,4,8,2048]{3,2,1,0:T(8,128)(2,1)}, bf16[8,4,8,2048]{3,2,1,0:T(8,128)(2,1)}, u32[]{:S(2)}, u32[]{:S(2)}) %collective-permute-start) | collective-permute-done | bytes 1048608 | tf_op jit(solution)/shard_map/ppermute | solution.py:11
  54.9 3.5 collective-permute-start.6
  58.5 2.0 dynamic-slice_bitcast_fusion.16
  60.5 10.7 %collective-permute-done.2 = bf16[8,4,8,2048]{3,2,0,1:T(8,128)(2,1)} collective-permute-done((bf16[8,4,8,2048]{3,2,0,1:T(8,128)(2,1)}, bf16[8,4,8,2048]{3,2,0,1:T(8,128)(2,1)}, u32[]{:S(2)}, u32[]{:S(2)}) %collective-permute-start.2) | collective-permute-done | bytes 1048608 | tf_op jit(solution)/shard_map/ppermute | solution.py:11
  72.0 2.0 slice_bitcast_fusion.28
  74.0 2.0 slice_bitcast_fusion.27
  79.1 14.9 %collective-permute-done.5 = bf16[8,4,8,2048]{3,2,1,0:T(8,128)(2,1)} collective-permute-done((bf16[8,4,8,2048]{3,2,1,0:T(8,128)(2,1)}, bf16[8,4,8,2048]{3,2,1,0:T(8,128)(2,1)}, u32[]{:S(2)}, u32[]{:S(2)}) %collective-permute-start.5) | collective-permute-done | bytes 1048608 | tf_op jit(solution)/shard_map/ppermute | solution.py:11
  93.9 2.2 dynamic-slice_bitcast_fusion.4
  96.2 2.6 collective-permute-start.9
  99.9 9.1 %collective-permute-start.4 = (bf16[4,8,8,2048]{3,2,1,0:T(8,128)(2,1)}, bf16[4,8,8,2048]{3,2,1,0:T(8,128)(2,1)}, u32[]{:S(2)}, u32[]{:S(2)}) collective-permute-start(bf16[4,8,8,2048]{3,2,1,0:T(8,128)(2,1)} %pad_maximum_fusion.5), channel_id=1, source_target_pairs={{0,8},{1,9},{2,10},{3,11},{4,12},{5,13},{6,14},{7,15},{8,0},{9,1},... | collective-permute-start | bytes 3145736 | tf_op jit(solution)/shard_map/ppermute | solution.py:11
  116.7 37.8 %collective-permute-done.4 = bf16[4,8,8,2048]{3,2,1,0:T(8,128)(2,1)} collective-permute-done((bf16[4,8,8,2048]{3,2,1,0:T(8,128)(2,1)}, bf16[4,8,8,2048]{3,2,1,0:T(8,128)(2,1)}, u32[]{:S(2)}, u32[]{:S(2)}) %collective-permute-start.4) | collective-permute-done | bytes 1048608 | tf_op jit(solution)/shard_map/ppermute | solution.py:11
  154.4 2.8 collective-permute-start.12
  158.7 13.8 %pad_maximum_fusion = bf16[4,4,8,8,2048]{4,3,2,0,1:T(8,128)(2,1)S(1)} fusion(bf16[4,1,8,8,2048]{4,3,2,0,1:T(8,128)(2,1)} %bitcast.58, bf16[4,1,8,8,2048]{4,3,2,0,1:T(8,128)(2,1)} %bitcast.57, bf16[4,1,8,8,2048]{4,3,2,0,1:T(8,128)(2,1)} %bitcast.56, bf16[4,1,8,8,2048]{4,3,2,0,1:T(8,128)(2,1)S(1)} %bitcast.336), kind=kLoop, calls=%fused_computation.20 | loop fusion | flops 6291456 | bytes 8388608 | tf_op jit(solution)/shard_map/stack | solution.py:83
  172.5 2.3 copy.91
  176.4 3.5 collective-permute-done.11
  180.7 2.3 copy.95
  185.3 20.7 %collective-permute-start.10 = (bf16[4,8,8,2048]{3,2,1,0:T(8,128)(2,1)S(1)}, bf16[4,8,8,2048]{3,2,1,0:T(8,128)(2,1)S(1)}, u32[]{:S(2)}, u32[]{:S(2)}) collective-permute-start(bf16[4,8,8,2048]{3,2,1,0:T(8,128)(2,1)S(1)} %copy.93), channel_id=1, source_target_pairs={{0,8},{1,9},{2,10},{3,11},{4,12},{5,13},{6,14},{7,15},{8,0},{9,1},... | collective-permute-start | bytes 3145736 | tf_op jit(solution)/shard_map/ppermute | solution.py:11
  208.5 2.4 collective-permute-start.15
  214.9 35.5 %collective-permute-done.10 = bf16[4,8,8,2048]{3,2,1,0:T(8,128)(2,1)S(1)} collective-permute-done((bf16[4,8,8,2048]{3,2,1,0:T(8,128)(2,1)S(1)}, bf16[4,8,8,2048]{3,2,1,0:T(8,128)(2,1)S(1)}, u32[]{:S(2)}, u32[]{:S(2)}) %collective-permute-start.10) | collective-permute-done | bytes 1048608 | tf_op jit(solution)/shard_map/ppermute | solution.py:11
  251.3 4.4 %collective-permute-done.14 = bf16[4,8,8,2048]{3,1,0,2:T(8,128)(2,1)S(1)} collective-permute-done((bf16[4,8,8,2048]{3,1,0,2:T(8,128)(2,1)S(1)}, bf16[4,8,8,2048]{3,1,0,2:T(8,128)(2,1)S(1)}, u32[]{:S(2)}, u32[]{:S(2)}) %collective-permute-start.14) | collective-permute-done | bytes 1048608 | tf_op jit(solution)/shard_map/ppermute | solution.py:11
  259.2 22.5 %collective-permute-done.17 = bf16[4,8,8,2048]{3,2,1,0:T(8,128)(2,1)S(1)} collective-permute-done((bf16[4,8,8,2048]{3,2,1,0:T(8,128)(2,1)S(1)}, bf16[4,8,8,2048]{3,2,1,0:T(8,128)(2,1)S(1)}, u32[]{:S(2)}, u32[]{:S(2)}) %collective-permute-start.17) | collective-permute-done | bytes 1048608 | tf_op jit(solution)/shard_map/ppermute | solution.py:11
  282.7 14.9 %collective-permute-start.16 = (bf16[4,8,8,2048]{3,2,0,1:T(8,128)(2,1)S(1)}, bf16[4,8,8,2048]{3,2,0,1:T(8,128)(2,1)S(1)}, u32[]{:S(2)}, u32[]{:S(2)}) collective-permute-start(bf16[4,8,8,2048]{3,2,0,1:T(8,128)(2,1)S(1)} %get-tuple-element.120), channel_id=1, source_target_pairs={{0,8},{1,9},{2,10},{3,11},{4,12},{5,13},{6,14},{7,15},{8,0},{9,1},... | collective-permute-start | bytes 3145736 | tf_op jit(solution)/shard_map/ppermute | solution.py:11
  302.1 39.9 %collective-permute-done.16 = bf16[4,8,8,2048]{3,2,0,1:T(8,128)(2,1)S(1)} collective-permute-done((bf16[4,8,8,2048]{3,2,0,1:T(8,128)(2,1)S(1)}, bf16[4,8,8,2048]{3,2,0,1:T(8,128)(2,1)S(1)}, u32[]{:S(2)}, u32[]{:S(2)}) %collective-permute-start.16) | collective-permute-done | bytes 1048608 | tf_op jit(solution)/shard_map/ppermute | solution.py:11
  344.3 4.8 %fusion.1 = (f32[2048]{0:T(1024)S(1)}, bf16[8,128,2048]{2,1,0:T(8,128)(2,1)S(1)}) fusion(f32[8,128,2048]{2,1,0:T(8,128)S(1)} %bitcast.330, f32[2048]{0:T(1024)S(1)} %copy-done.9, bf16[4,1,8,8,2048]{4,3,1,0,2:T(8,128)(2,1)S(1)} %bitcast.337, bf16[4,1,8,8,2048]{4,3,1,0,2:T(8,128)(2,1)S(1)} %bitcast.338, bf16[4,8,8,2048]{3,2,1,0:T(8,128)(2,1)S(1)} %pad_maximum_fusion.12, ...), kind=kLoop, calls=%fused_computation.3 | loop fusion | flops 46135296 | bytes 16793600 | tf_op jit(solution)/shard_map/reduce_sum | solution.py:131
  349.2 2.9 multiply_reduce_fusion
  356.9 4.7 %fusion.2 = bf16[1024,2048]{1,0:T(8,128)(2,1)} fusion(f32[8,128,2048]{2,1,0:T(8,128)S(1)} %get-tuple-element.192, bf16[1,1024,2048]{2,1,0:T(8,128)(2,1)S(1)} %copy-done.4, bf16[1,1024,2048]{2,1,0:T(8,128)(2,1)S(1)} %copy-done.3, f32[1024]{0:T(1024)S(1)} %multiply_bitcast_fusion, f32[2048]{0:T(1024)S(1)} %copy-done.8, f32[1024]{0:T(1024)S(1)} %get-tuple-element.188), kind=kLoop, calls=%fused_computation.5 | loop fusion | flops 18874368 | bytes 20987904 | tf_op jit(solution)/shard_map/convert_element_type | solution.py:145
  361.8 2.5 collective-permute-start.29
  367.7 20.0 %collective-permute-done.29 = f32[2,2048]{1,0:T(2,128)S(1)} collective-permute-done((f32[2,2048]{1,0:T(2,128)S(1)}, f32[2,2048]{1,0:T(2,128)S(1)}, u32[]{:S(2)}, u32[]{:S(2)}) %collective-permute-start.29) | collective-permute-done | bytes 16416 | tf_op jit(solution)/shard_map/ppermute | solution.py:11
  389.1 2.0 copy-done.5
  (135 shorter events, 59.3 us)
Async XLA Ops:
  4.9 50.1 %collective-permute-start = (bf16[8,4,8,2048]{3,2,1,0:T(8,128)(2,1)}, bf16[8,4,8,2048]{3,2,1,0:T(8,128)(2,1)}, u32[]{:S(2)}, u32[]{:S(2)}) collective-permute-start(bf16[8,4,8,2048]{3,2,1,0:T(8,128)(2,1)} %get-tuple-element.131), channel_id=1, source_target_pairs={{0,8},{1,9},{2,10},{3,11},{4,12},{5,13},{6,14},{7,15},{8,0},{9,1},... | collective-permute-start | bytes 3145736 | tf_op jit(solution)/shard_map/ppermute | solution.py:11
  21.5 39.0 %collective-permute-start.1 = (bf16[8,4,8,2048]{3,2,0,1:T(8,128)(2,1)}, bf16[8,4,8,2048]{3,2,0,1:T(8,128)(2,1)}, u32[]{:S(2)}, u32[]{:S(2)}) collective-permute-start(bf16[8,4,8,2048]{3,2,0,1:T(8,128)(2,1)} %bitcast.314), channel_id=1, source_target_pairs={{0,1},{1,0},{2,3},{3,2},{4,5},{5,4},{6,7},{7,6},{8,9},{9,8},{10,11... | collective-permute-start | bytes 3145736 | tf_op jit(solution)/shard_map/ppermute | solution.py:11
  24.1 47.1 %collective-permute-start.2 = (bf16[8,4,8,2048]{3,2,0,1:T(8,128)(2,1)}, bf16[8,4,8,2048]{3,2,0,1:T(8,128)(2,1)}, u32[]{:S(2)}, u32[]{:S(2)}) collective-permute-start(bf16[8,4,8,2048]{3,2,0,1:T(8,128)(2,1)} %bitcast.313), channel_id=1, source_target_pairs={{0,2},{1,3},{2,0},{3,1},{4,6},{5,7},{6,4},{7,5},{8,10},{9,11},{10,... | collective-permute-start | bytes 3145736 | tf_op jit(solution)/shard_map/ppermute | solution.py:11
  25.6 45.6 %collective-permute-start.3 = (bf16[8,4,8,2048]{3,2,1,0:T(8,128)(2,1)}, bf16[8,4,8,2048]{3,2,1,0:T(8,128)(2,1)}, u32[]{:S(2)}, u32[]{:S(2)}) collective-permute-start(bf16[8,4,8,2048]{3,2,1,0:T(8,128)(2,1)} %get-tuple-element.133), channel_id=1, source_target_pairs={{0,3},{1,2},{2,1},{3,0},{4,7},{5,6},{6,5},{7,4},{8,11},{9,10},{10,... | collective-permute-start | bytes 3145736 | tf_op jit(solution)/shard_map/ppermute | solution.py:11
  26.1 67.9 %collective-permute-start.5 = (bf16[8,4,8,2048]{3,2,1,0:T(8,128)(2,1)}, bf16[8,4,8,2048]{3,2,1,0:T(8,128)(2,1)}, u32[]{:S(2)}, u32[]{:S(2)}) collective-permute-start(bf16[8,4,8,2048]{3,2,1,0:T(8,128)(2,1)} %get-tuple-element.130), channel_id=1, source_target_pairs={{0,4},{1,5},{2,6},{3,7},{4,0},{5,1},{6,2},{7,3},{8,12},{9,13},{10,... | collective-permute-start | bytes 3145736 | tf_op jit(solution)/shard_map/ppermute | solution.py:11
  54.9 39.0 %collective-permute-start.6 = (bf16[8,4,8,2048]{3,2,1,0:T(8,128)(2,1)}, bf16[8,4,8,2048]{3,2,1,0:T(8,128)(2,1)S(1)}, u32[]{:S(2)}, u32[]{:S(2)}) collective-permute-start(bf16[8,4,8,2048]{3,2,1,0:T(8,128)(2,1)} %get-tuple-element.129), channel_id=1, source_target_pairs={{0,12},{1,13},{2,14},{3,15},{4,8},{5,9},{6,10},{7,11},{8,4},{9,5},... | collective-permute-start | bytes 3145736 | tf_op jit(solution)/shard_map/ppermute | solution.py:11
  96.2 62.4 %collective-permute-start.9 = (bf16[4,8,8,2048]{3,2,1,0:T(8,128)(2,1)S(1)}, bf16[4,8,8,2048]{3,2,1,0:T(8,128)(2,1)}, u32[]{:S(2)}, u32[]{:S(2)}) collective-permute-start(bf16[4,8,8,2048]{3,2,1,0:T(8,128)(2,1)S(1)} %pad_maximum_fusion.11), channel_id=1, source_target_pairs={{0,3},{1,2},{2,1},{3,0},{4,7},{5,6},{6,5},{7,4},{8,11},{9,10},{10,... | collective-permute-start | bytes 3145736 | tf_op jit(solution)/shard_map/ppermute | solution.py:11
  99.9 54.5 %collective-permute-start.4 = (bf16[4,8,8,2048]{3,2,1,0:T(8,128)(2,1)}, bf16[4,8,8,2048]{3,2,1,0:T(8,128)(2,1)}, u32[]{:S(2)}, u32[]{:S(2)}) collective-permute-start(bf16[4,8,8,2048]{3,2,1,0:T(8,128)(2,1)} %pad_maximum_fusion.5), channel_id=1, source_target_pairs={{0,8},{1,9},{2,10},{3,11},{4,12},{5,13},{6,14},{7,15},{8,0},{9,1},... | collective-permute-start | bytes 3145736 | tf_op jit(solution)/shard_map/ppermute | solution.py:11
  110.1 48.6 %collective-permute-start.8 = (bf16[4,8,8,2048]{3,2,1,0:T(8,128)(2,1)}, bf16[4,8,8,2048]{3,2,1,0:T(8,128)(2,1)}, u32[]{:S(2)}, u32[]{:S(2)}) collective-permute-start(bf16[4,8,8,2048]{3,2,1,0:T(8,128)(2,1)} %pad_maximum_fusion.10), channel_id=1, source_target_pairs={{0,2},{1,3},{2,0},{3,1},{4,6},{5,7},{6,4},{7,5},{8,10},{9,11},{10,... | collective-permute-start | bytes 3145736 | tf_op jit(solution)/shard_map/ppermute | solution.py:11
  111.7 47.0 %collective-permute-start.7 = (bf16[4,8,8,2048]{3,2,1,0:T(8,128)(2,1)}, bf16[4,8,8,2048]{3,2,1,0:T(8,128)(2,1)}, u32[]{:S(2)}, u32[]{:S(2)}) collective-permute-start(bf16[4,8,8,2048]{3,2,1,0:T(8,128)(2,1)} %pad_maximum_fusion.9), channel_id=1, source_target_pairs={{0,1},{1,0},{2,3},{3,2},{4,5},{5,4},{6,7},{7,6},{8,9},{9,8},{10,11... | collective-permute-start | bytes 3145736 | tf_op jit(solution)/shard_map/ppermute | solution.py:11
  113.7 66.3 %collective-permute-start.11 = (bf16[4,8,8,2048]{3,2,1,0:T(8,128)(2,1)S(1)}, bf16[4,8,8,2048]{3,2,1,0:T(8,128)(2,1)S(1)}, u32[]{:S(2)}, u32[]{:S(2)}) collective-permute-start(bf16[4,8,8,2048]{3,2,1,0:T(8,128)(2,1)S(1)} %pad_maximum_fusion.6), channel_id=1, source_target_pairs={{0,4},{1,5},{2,6},{3,7},{4,0},{5,1},{6,2},{7,3},{8,12},{9,13},{10,... | collective-permute-start | bytes 3145736 | tf_op jit(solution)/shard_map/ppermute | solution.py:11
  154.4 25.5 %collective-permute-start.12 = (bf16[4,8,8,2048]{3,2,1,0:T(8,128)(2,1)S(1)}, bf16[4,8,8,2048]{3,2,1,0:T(8,128)(2,1)S(1)}, u32[]{:S(2)}, u32[]{:S(2)}) collective-permute-start(bf16[4,8,8,2048]{3,2,1,0:T(8,128)(2,1)S(1)} %pad_maximum_fusion.7), channel_id=1, source_target_pairs={{0,12},{1,13},{2,14},{3,15},{4,8},{5,9},{6,10},{7,11},{8,4},{9,5},... | collective-permute-start | bytes 3145736 | tf_op jit(solution)/shard_map/ppermute | solution.py:11
  185.3 65.0 %collective-permute-start.10 = (bf16[4,8,8,2048]{3,2,1,0:T(8,128)(2,1)S(1)}, bf16[4,8,8,2048]{3,2,1,0:T(8,128)(2,1)S(1)}, u32[]{:S(2)}, u32[]{:S(2)}) collective-permute-start(bf16[4,8,8,2048]{3,2,1,0:T(8,128)(2,1)S(1)} %copy.93), channel_id=1, source_target_pairs={{0,8},{1,9},{2,10},{3,11},{4,12},{5,13},{6,14},{7,15},{8,0},{9,1},... | collective-permute-start | bytes 3145736 | tf_op jit(solution)/shard_map/ppermute | solution.py:11
  207.3 5.4 %collective-permute-start.32 = (f32[8,128,128]{2,1,0:T(8,128)S(1)}, f32[8,128,128]{2,1,0:T(8,128)S(1)}, u32[]{:S(2)}, u32[]{:S(2)}) collective-permute-start(f32[8,128,128]{2,1,0:T(8,128)S(1)} %fusion.48), channel_id=1, source_target_pairs={{0,16},{16,0},{1,17},{17,1},{2,18},{18,2},{3,19},{19,3},{4,20},{20... | collective-permute-start | bytes 1572872 | tf_op jit(solution)/shard_map/ppermute | solution.py:11
  207.4 43.9 %collective-permute-start.13 = (bf16[4,8,8,2048]{3,1,0,2:T(8,128)(2,1)S(1)}, bf16[4,8,8,2048]{3,1,0,2:T(8,128)(2,1)S(1)}, u32[]{:S(2)}, u32[]{:S(2)}) collective-permute-start(bf16[4,8,8,2048]{3,1,0,2:T(8,128)(2,1)S(1)} %get-tuple-element.123), channel_id=1, source_target_pairs={{0,1},{1,0},{2,3},{3,2},{4,5},{5,4},{6,7},{7,6},{8,9},{9,8},{10,11... | collective-permute-start | bytes 3145736 | tf_op jit(solution)/shard_map/ppermute | solution.py:11
  208.0 47.7 %collective-permute-start.14 = (bf16[4,8,8,2048]{3,1,0,2:T(8,128)(2,1)S(1)}, bf16[4,8,8,2048]{3,1,0,2:T(8,128)(2,1)S(1)}, u32[]{:S(2)}, u32[]{:S(2)}) collective-permute-start(bf16[4,8,8,2048]{3,1,0,2:T(8,128)(2,1)S(1)} %get-tuple-element.122), channel_id=1, source_target_pairs={{0,2},{1,3},{2,0},{3,1},{4,6},{5,7},{6,4},{7,5},{8,10},{9,11},{10,... | collective-permute-start | bytes 3145736 | tf_op jit(solution)/shard_map/ppermute | solution.py:11
  208.5 47.2 %collective-permute-start.15 = (bf16[4,8,8,2048]{3,1,0,2:T(8,128)(2,1)S(1)}, bf16[4,8,8,2048]{3,1,0,2:T(8,128)(2,1)S(1)}, u32[]{:S(2)}, u32[]{:S(2)}) collective-permute-start(bf16[4,8,8,2048]{3,1,0,2:T(8,128)(2,1)S(1)} %get-tuple-element.121), channel_id=1, source_target_pairs={{0,3},{1,2},{2,1},{3,0},{4,7},{5,6},{6,5},{7,4},{8,11},{9,10},{10,... | collective-permute-start | bytes 3145736 | tf_op jit(solution)/shard_map/ppermute | solution.py:11
  212.7 69.0 %collective-permute-start.17 = (bf16[4,8,8,2048]{3,2,1,0:T(8,128)(2,1)S(1)}, bf16[4,8,8,2048]{3,2,1,0:T(8,128)(2,1)S(1)}, u32[]{:S(2)}, u32[]{:S(2)}) collective-permute-start(bf16[4,8,8,2048]{3,2,1,0:T(8,128)(2,1)S(1)} %copy.103), channel_id=1, source_target_pairs={{0,4},{1,5},{2,6},{3,7},{4,0},{5,1},{6,2},{7,3},{8,12},{9,13},{10,... | collective-permute-start | bytes 3145736 | tf_op jit(solution)/shard_map/ppermute | solution.py:11
  250.4 31.3 %collective-permute-start.18 = (bf16[4,8,8,2048]{3,2,0,1:T(8,128)(2,1)S(1)}, bf16[4,8,8,2048]{3,2,0,1:T(8,128)(2,1)S(1)}, u32[]{:S(2)}, u32[]{:S(2)}) collective-permute-start(bf16[4,8,8,2048]{3,2,0,1:T(8,128)(2,1)S(1)} %copy.104), channel_id=1, source_target_pairs={{0,12},{1,13},{2,14},{3,15},{4,8},{5,9},{6,10},{7,11},{8,4},{9,5},... | collective-permute-start | bytes 3145736 | tf_op jit(solution)/shard_map/ppermute | solution.py:11
  282.2 62.1 %collective-permute-start.21 = (bf16[4,8,8,2048]{3,2,0,1:T(8,128)(2,1)S(1)}, bf16[4,8,8,2048]{3,2,0,1:T(8,128)(2,1)S(1)}, u32[]{:S(2)}, u32[]{:S(2)}) collective-permute-start(bf16[4,8,8,2048]{3,2,0,1:T(8,128)(2,1)S(1)} %pad_maximum_fusion.15), channel_id=1, source_target_pairs={{0,3},{1,2},{2,1},{3,0},{4,7},{5,6},{6,5},{7,4},{8,11},{9,10},{10,... | collective-permute-start | bytes 3145736 | tf_op jit(solution)/shard_map/ppermute | solution.py:11
  282.7 59.3 %collective-permute-start.16 = (bf16[4,8,8,2048]{3,2,0,1:T(8,128)(2,1)S(1)}, bf16[4,8,8,2048]{3,2,0,1:T(8,128)(2,1)S(1)}, u32[]{:S(2)}, u32[]{:S(2)}) collective-permute-start(bf16[4,8,8,2048]{3,2,0,1:T(8,128)(2,1)S(1)} %get-tuple-element.120), channel_id=1, source_target_pairs={{0,8},{1,9},{2,10},{3,11},{4,12},{5,13},{6,14},{7,15},{8,0},{9,1},... | collective-permute-start | bytes 3145736 | tf_op jit(solution)/shard_map/ppermute | solution.py:11
  297.7 46.5 %collective-permute-start.20 = (bf16[4,8,8,2048]{3,2,0,1:T(8,128)(2,1)S(1)}, bf16[4,8,8,2048]{3,2,0,1:T(8,128)(2,1)S(1)}, u32[]{:S(2)}, u32[]{:S(2)}) collective-permute-start(bf16[4,8,8,2048]{3,2,0,1:T(8,128)(2,1)S(1)} %pad_maximum_fusion.14), channel_id=1, source_target_pairs={{0,2},{1,3},{2,0},{3,1},{4,6},{5,7},{6,4},{7,5},{8,10},{9,11},{10,... | collective-permute-start | bytes 3145736 | tf_op jit(solution)/shard_map/ppermute | solution.py:11
  299.5 44.8 %collective-permute-start.19 = (bf16[4,8,8,2048]{3,2,1,0:T(8,128)(2,1)S(1)}, bf16[4,8,8,2048]{3,2,1,0:T(8,128)(2,1)S(1)}, u32[]{:S(2)}, u32[]{:S(2)}) collective-permute-start(bf16[4,8,8,2048]{3,2,1,0:T(8,128)(2,1)S(1)} %pad_maximum_fusion.13), channel_id=1, source_target_pairs={{0,1},{1,0},{2,3},{3,2},{4,5},{5,4},{6,7},{7,6},{8,9},{9,8},{10,11... | collective-permute-start | bytes 3145736 | tf_op jit(solution)/shard_map/ppermute | solution.py:11
  301.0 87.3 %collective-permute-start.22 = (bf16[4,8,8,2048]{3,2,0,1:T(8,128)(2,1)S(1)}, bf16[4,8,8,2048]{3,2,0,1:T(8,128)(2,1)S(1)}, u32[]{:S(2)}, u32[]{:S(2)}) collective-permute-start(bf16[4,8,8,2048]{3,2,0,1:T(8,128)(2,1)S(1)} %get-tuple-element.83), channel_id=1, source_target_pairs={{0,4},{1,5},{2,6},{3,7},{4,0},{5,1},{6,2},{7,3},{8,12},{9,13},{10,... | collective-permute-start | bytes 3145736 | tf_op jit(solution)/shard_map/ppermute | solution.py:11
  342.0 46.3 %collective-permute-start.23 = (bf16[4,8,8,2048]{3,2,0,1:T(8,128)(2,1)S(1)}, bf16[4,8,8,2048]{3,2,0,1:T(8,128)(2,1)S(1)}, u32[]{:S(2)}, u32[]{:S(2)}) collective-permute-start(bf16[4,8,8,2048]{3,2,0,1:T(8,128)(2,1)S(1)} %get-tuple-element.84), channel_id=1, source_target_pairs={{0,12},{1,13},{2,14},{3,15},{4,8},{5,9},{6,10},{7,11},{8,4},{9,5},... | collective-permute-start | bytes 3145736 | tf_op jit(solution)/shard_map/ppermute | solution.py:11
  353.3 8.3 %collective-permute-start.25 = (f32[2,2048]{1,0:T(2,128)S(1)}, f32[2,2048]{1,0:T(2,128)S(1)}, u32[]{:S(2)}, u32[]{:S(2)}) collective-permute-start(f32[2,2048]{1,0:T(2,128)S(1)} %fusion.41), channel_id=1, source_target_pairs={{0,1},{1,0},{2,3},{3,2},{4,5},{5,4},{6,7},{7,6},{8,9},{9,8},{10,11... | collective-permute-start | bytes 49160 | tf_op jit(solution)/shard_map/ppermute | solution.py:11
  354.9 6.8 %collective-permute-start.26 = (f32[2,2048]{1,0:T(2,128)S(1)}, f32[2,2048]{1,0:T(2,128)S(1)}, u32[]{:S(2)}, u32[]{:S(2)}) collective-permute-start(f32[2,2048]{1,0:T(2,128)S(1)} %fusion.41), channel_id=1, source_target_pairs={{0,2},{1,3},{2,0},{3,1},{4,6},{5,7},{6,4},{7,5},{8,10},{9,11},{10,... | collective-permute-start | bytes 49160 | tf_op jit(solution)/shard_map/ppermute | solution.py:11
  356.4 5.2 %collective-permute-start.27 = (f32[2,2048]{1,0:T(2,128)S(1)}, f32[2,2048]{1,0:T(2,128)S(1)}, u32[]{:S(2)}, u32[]{:S(2)}) collective-permute-start(f32[2,2048]{1,0:T(2,128)S(1)} %fusion.41), channel_id=1, source_target_pairs={{0,3},{1,2},{2,1},{3,0},{4,7},{5,6},{6,5},{7,4},{8,11},{9,10},{10,... | collective-permute-start | bytes 49160 | tf_op jit(solution)/shard_map/ppermute | solution.py:11
  361.7 5.8 %collective-permute-start.28 = (f32[2,2048]{1,0:T(2,128)S(1)}, f32[2,2048]{1,0:T(2,128)S(1)}, u32[]{:S(2)}, u32[]{:S(2)}) collective-permute-start(f32[2,2048]{1,0:T(2,128)S(1)} %add_add_fusion.1), channel_id=1, source_target_pairs={{0,4},{1,5},{2,6},{3,7},{4,0},{5,1},{6,2},{7,3},{8,12},{9,13},{10,... | collective-permute-start | bytes 49160 | tf_op jit(solution)/shard_map/ppermute | solution.py:11
  361.8 25.8 %collective-permute-start.29 = (f32[2,2048]{1,0:T(2,128)S(1)}, f32[2,2048]{1,0:T(2,128)S(1)}, u32[]{:S(2)}, u32[]{:S(2)}) collective-permute-start(f32[2,2048]{1,0:T(2,128)S(1)} %add_add_fusion.1), channel_id=1, source_target_pairs={{0,8},{1,9},{2,10},{3,11},{4,12},{5,13},{6,14},{7,15},{8,0},{9,1},... | collective-permute-start | bytes 49160 | tf_op jit(solution)/shard_map/ppermute | solution.py:11
  364.3 23.3 %collective-permute-start.30 = (f32[2,2048]{1,0:T(2,128)S(1)}, f32[2,2048]{1,0:T(2,128)S(1)}, u32[]{:S(2)}, u32[]{:S(2)}) collective-permute-start(f32[2,2048]{1,0:T(2,128)S(1)} %add_add_fusion.1), channel_id=1, source_target_pairs={{0,12},{1,13},{2,14},{3,15},{4,8},{5,9},{6,10},{7,11},{8,4},{9,5},... | collective-permute-start | bytes 49160 | tf_op jit(solution)/shard_map/ppermute | solution.py:11
  367.6 23.6 %collective-permute-start.31 = (f32[8,128,128]{2,1,0:T(8,128)S(1)}, f32[8,128,128]{2,1,0:T(8,128)S(1)}, u32[]{:S(2)}, u32[]{:S(2)}) collective-permute-start(f32[8,128,128]{2,1,0:T(8,128)S(1)} %fusion.14), channel_id=1, source_target_pairs={{0,16},{16,0},{1,17},{17,1},{2,18},{18,2},{3,19},{19,3},{4,20},{20... | collective-permute-start | bytes 1572872 | tf_op jit(solution)/shard_map/ppermute | solution.py:11
  (13 other events, 165.2 us)

commit v7 on v6

--- a/solution.py
+++ b/solution.py
@@ -46,7 +46,7 @@
     lefts = jnp.einsum("aij,jl->ail", jnp.einsum("ki,aij->akj", swap_half, left_blocks), swap_half)
 
     half = far // 2
-    rest = [k for k in range(1, far) if k != half]
+    early, rest = list(range(1, half)), list(range(half + 1, far))
 
     up_view = upstream[0].reshape(local, far, near, local, width)
     up_parts = [lax.dynamic_index_in_dim(up_view, device_far ^ k, 1, keepdims=False) for k in range(far)]
@@ -67,6 +67,8 @@
     def sent_near(part):
         return [lax.dynamic_index_in_dim(part, device_near ^ k, 1, keepdims=False) for k in range(near)]
 
+    up_early = [sent_near(up_far[k]) for k in early]
+    up_early, up_far[half] = lax.optimization_barrier((up_early, up_far[half]))
     up_half = sent_near(up_far[half])
     up_half, gated_near = lax.optimization_barrier((up_half, gated_near))
     gated_sent = [jnp.stack([t[:, k] for t in gated_near]) for k in range(far)]
@@ -74,12 +76,14 @@
     for k, up_part, gated_part in zip(rest, up_rest, gated_rest):
         up_far[k], gated_sent[k] = up_part, gated_part
     gated_far = [from_partner(gated_sent[k], "seq", k << low) for k in range(far)]
-    up_sent = [up_half if k == half else sent_near(up_far[k]) for k in range(far)]
+    up_sent = [sent_near(up_far[0])] + up_early + [up_half] + [sent_near(up_far[k]) for k in rest]
     up_near = [from_partner(jnp.stack([t[k] for t in up_sent]), "seq", k) for k in range(near)]
 
-    gated_pair = jnp.stack([gated_far[0], gated_far[half]])
-    gated_pair, up_near = lax.optimization_barrier((gated_pair, up_near))
-    gated_far[0], gated_far[half] = gated_pair[0], gated_pair[1]
+    gated_first = jnp.stack(gated_far[:half])
+    gated_first, gated_far[half] = lax.optimization_barrier((gated_first, gated_far[half]))
+    gated_first = jnp.concatenate([gated_first, gated_far[half][None]])
+    gated_first, up_near = lax.optimization_barrier((gated_first, up_near))
+    gated_far[: half + 1] = list(gated_first)
     upward = jnp.stack(up_near, axis=1).reshape(order, local, width)
     returned = jnp.einsum("bij,ibd->jbd", lefts, upward, preferred_element_type=f32).astype(bf16)
     returned = list(returned.reshape(far, near, local, local, width))
@@ -95,9 +99,11 @@
     mixed = mixed.reshape(far, near, local, local, width)
     mixed_parts = [from_partner(mixed[:, k], "seq", k) for k in range(near)]
     upward, arrived, mixed_parts[0] = lax.optimization_barrier((upward, arrived, mixed_parts[0]))
-    back_pair = jnp.stack([back_far[0], back_far[half]])
-    back_pair, mixed_parts = lax.optimization_barrier((back_pair, mixed_parts))
-    back_far[0], back_far[half] = back_pair[0], back_pair[1]
+    back_first = jnp.stack(back_far[:half])
+    back_first, back_far[half] = lax.optimization_barrier((back_first, back_far[half]))
+    back_first = jnp.concatenate([back_first, back_far[half][None]])
+    back_first, mixed_parts = lax.optimization_barrier((back_first, mixed_parts))
+    back_far[: half + 1] = list(back_first)
     mixed_near = jnp.zeros((far, near, local, local, width), bf16)
     for k, part in enumerate(mixed_parts):
         mixed_near = lax.dynamic_update_index_in_dim(mixed_near, part, device_near ^ k, 1)
@@ -117,7 +123,10 @@
         return lax.dynamic_update_index_in_dim(output, block, place, 1)
 
     output = jnp.zeros((local, far, near, local, width), bf16)
-    output = placed(placed(output, mixed_far[0], 0), mixed_far[half], half)
+    for k in range(half):
+        output = placed(output, mixed_far[k], k)
+    output, mixed_far[half] = lax.optimization_barrier((output, mixed_far[half]))
+    output = placed(output, mixed_far[half], half)
     output, back_near = lax.optimization_barrier((output, back_near))
     dgated = jnp.stack(back_near, axis=1).transpose(2, 0, 1, 3, 4).reshape(local, order, width).astype(f32)
 
@@ -147,8 +156,8 @@
     vectors = sum_over(vectors, "dp", 0, dp_levels)
     vectors = sum_over(vectors, "seq", 0, low)
     gain_gradient, grad_mid = sum_over(vectors, "seq", low, levels)
-    mixed_rest, input_gradient, gain_gradient, grad_mid = lax.optimization_barrier(
-        ([mixed_far[k] for k in rest], input_gradient, gain_gradient, grad_mid)
+    mixed_rest, input_gradient, grad_right, gain_gradient, grad_mid = lax.optimization_barrier(
+        ([mixed_far[k] for k in rest], input_gradient, grad_right, gain_gradient, grad_mid)
     )
     for k, part in zip(rest, mixed_rest):
         output = placed(output, part, k)

time: 400 us -> 413 us (1.032)
  waiting for transfers between devices: 217 us -> 240 us
  other arithmetic: 35 us -> 18 us
  starting transfers between devices: 82.3 us -> 97 us
  local copies, waits for them, and re-layouts: 36.1 us -> 28.2 us
    ppermute x33, waiting for transfers between devices: 217 us -> 240 us  [from_partner(): return lax.ppermute(block, axis, [(i, i ^ distance) for i in range(count)])]
    ppermute x33, starting transfers between devices: 82.3 us -> 97 us  [from_partner(): return lax.ppermute(block, axis, [(i, i ^ distance) for i in range(count)])]
    another operation x1, other arithmetic: 13.8 us -> 0.75 us  [body(): upward = jnp.stack(up_near, axis=1).reshape(order, local, width)]
  transfers between devices with their start and end apart: 33 -> 33, of which waited for: 11 -> 12; matrix products, arithmetic and copies ran while one was open for 19% -> 13% of each run, Pallas kernels for 0% -> 0%
where the time goes in v7:
time: 413 us; the launch traced here: 406 us
  waiting for transfers between devices  240 us (58%)
  starting transfers between devices  97 us (23%)
  local copies, waits for them, and re-layouts  28.2 us (7%)
  matrix products  21.4 us (5%)
  other arithmetic  18 us (4%)
    ppermute x33, waiting for transfers between devices, from_partner(): return lax.ppermute(block, axis, [(i, i ^ distance) for i in range(count)])  240 us
    ppermute x33, starting transfers between devices, from_partner(): return lax.ppermute(block, axis, [(i, i ^ distance) for i in range(count)])  97 us
    dot_general x1, matrix products, body(): first = jnp.einsum('aij,ajd->aid', rights, grid, preferred_element_type=f32)  8.97 us
  transfers between devices with their start and end apart: 33, of which 12 were waited for; matrix products, arithmetic and copies ran while one was open for 13% of the time, Pallas kernels for 0%

profile of v7, /device:TPU:0, one launch (start us, length us, event | category | flops | bytes accessed | tf_op | source)
XLA Modules:
  0.0 405.9 jit_solution(9505020497230687056)
XLA Ops:
  0.7 4.1 %dynamic-slice_bitcast_fusion = (bf16[8,4,8,2048]{3,2,1,0:T(8,128)(2,1)}, bf16[8,4,8,2048]{3,2,1,0:T(8,128)(2,1)}, bf16[8,4,8,2048]{3,2,1,0:T(8,128)(2,1)}, bf16[8,4,8,2048]{3,2,1,0:T(8,128)(2,1)S(1)}) fusion(bf16[8,4,4,8,2048]{4,3,2,1,0:T(8,128)(2,1)} %bitcast.341, s32[]{:T(128)S(6)} %select_n.59, s32[]{:T(128)S(6)} %select_n.58, s32[]{:T(128)S(6)} %select_n.53, ...), kind=kLoop, calls=%fused_computation.85 | loop fusion | bytes 8388624 | tf_op jit(solution)/shard_map/jit(dynamic_index_in_dim)/squeeze | solution.py:52
  4.8 3.0 collective-permute-start
  7.8 2.6 collective-permute-start.1
  11.6 9.0 %multiply_convert_fusion = (bf16[8,128,2048]{2,1,0:T(8,128)(2,1)S(1)}, f32[8,128,2048]{2,1,0:T(8,128)}) fusion(f32[2048]{0:T(1024)S(1)} %copy-done.9, bf16[8,128,128]{1,2,0:T(8,128)(2,1)S(1)} %convolution_bitcast_fusion.3, f32[2048]{0:T(1024)S(1)} %copy-done.8, f32[8,128]{1,0:T(8,128)S(1)} %get-tuple-element.197, bf16[8,128,2048]{2,1,0:T(8,128)(2,1)} %bitcast.329), kind=kOutput, calls=%fused_computation.17 | convolution fusion | flops 557842432 | bytes 17059840 | tf_op jit(solution)/shard_map/aij,ajd->aid/dot_general | solution.py:60
  29.1 24.5 %collective-permute-done = bf16[8,4,8,2048]{3,2,1,0:T(8,128)(2,1)} collective-permute-done((bf16[8,4,8,2048]{3,2,1,0:T(8,128)(2,1)}, bf16[8,4,8,2048]{3,2,1,0:T(8,128)(2,1)}, u32[]{:S(2)}, u32[]{:S(2)}) %collective-permute-start) | collective-permute-done | bytes 1048608 | tf_op jit(solution)/shard_map/ppermute | solution.py:11
  53.6 2.6 collective-permute-start.7
  58.9 13.5 %collective-permute-done.3 = bf16[8,4,8,2048]{3,2,0,1:T(8,128)(2,1)} collective-permute-done((bf16[8,4,8,2048]{3,2,0,1:T(8,128)(2,1)}, bf16[8,4,8,2048]{3,2,0,1:T(8,128)(2,1)}, u32[]{:S(2)}, u32[]{:S(2)}) %collective-permute-start.3) | collective-permute-done | bytes 1048608 | tf_op jit(solution)/shard_map/ppermute | solution.py:11
  72.4 1.7 slice_bitcast_fusion.29
  76.5 3.6 collective-permute-done.7
  80.3 2.4 collective-permute-start.10
  82.8 21.7 %collective-permute-start.5 = (bf16[4,8,8,2048]{3,2,1,0:T(8,128)(2,1)S(1)}, bf16[4,8,8,2048]{3,2,1,0:T(8,128)(2,1)S(1)}, u32[]{:S(2)}, u32[]{:S(2)}) collective-permute-start(bf16[4,8,8,2048]{3,2,1,0:T(8,128)(2,1)S(1)} %pad_maximum_fusion.7), channel_id=1, source_target_pairs={{0,4},{1,5},{2,6},{3,7},{4,0},{5,1},{6,2},{7,3},{8,12},{9,13},{10,... | collective-permute-start | bytes 3145736 | tf_op jit(solution)/shard_map/ppermute | solution.py:11
  107.5 41.2 %collective-permute-done.5 = bf16[4,8,8,2048]{3,2,1,0:T(8,128)(2,1)S(1)} collective-permute-done((bf16[4,8,8,2048]{3,2,1,0:T(8,128)(2,1)S(1)}, bf16[4,8,8,2048]{3,2,1,0:T(8,128)(2,1)S(1)}, u32[]{:S(2)}, u32[]{:S(2)}) %collective-permute-start.5) | collective-permute-done | bytes 1048608 | tf_op jit(solution)/shard_map/ppermute | solution.py:11
  148.6 2.0 collective-permute-start.13
  150.8 24.7 %collective-permute-done.6 = bf16[4,8,8,2048]{3,2,1,0:T(8,128)(2,1)S(1)} collective-permute-done((bf16[4,8,8,2048]{3,2,1,0:T(8,128)(2,1)S(1)}, bf16[4,8,8,2048]{3,2,1,0:T(8,128)(2,1)S(1)}, u32[]{:S(2)}, u32[]{:S(2)}) %collective-permute-start.6) | collective-permute-done | bytes 1048608 | tf_op jit(solution)/shard_map/ppermute | solution.py:11
  176.6 2.3 copy.91
  180.9 2.3 copy.96
  185.5 17.2 %collective-permute-start.11 = (bf16[4,8,8,2048]{3,2,1,0:T(8,128)(2,1)S(1)}, bf16[4,8,8,2048]{3,2,1,0:T(8,128)(2,1)S(1)}, u32[]{:S(2)}, u32[]{:S(2)}) collective-permute-start(bf16[4,8,8,2048]{3,2,1,0:T(8,128)(2,1)S(1)} %copy.93), channel_id=1, source_target_pairs={{0,4},{1,5},{2,6},{3,7},{4,0},{5,1},{6,2},{7,3},{8,12},{9,13},{10,... | collective-permute-start | bytes 3145736 | tf_op jit(solution)/shard_map/ppermute | solution.py:11
  207.6 2.5 collective-permute-start.16
  212.2 31.5 %collective-permute-done.11 = bf16[4,8,8,2048]{3,2,1,0:T(8,128)(2,1)S(1)} collective-permute-done((bf16[4,8,8,2048]{3,2,1,0:T(8,128)(2,1)S(1)}, bf16[4,8,8,2048]{3,2,1,0:T(8,128)(2,1)S(1)}, u32[]{:S(2)}, u32[]{:S(2)}) %collective-permute-start.11) | collective-permute-done | bytes 1048608 | tf_op jit(solution)/shard_map/ppermute | solution.py:11
  243.7 2.0 collective-permute-start.19
  245.8 30.8 %collective-permute-done.12 = bf16[4,8,8,2048]{3,2,1,0:T(8,128)(2,1)S(1)} collective-permute-done((bf16[4,8,8,2048]{3,2,1,0:T(8,128)(2,1)S(1)}, bf16[4,8,8,2048]{3,2,1,0:T(8,128)(2,1)S(1)}, u32[]{:S(2)}, u32[]{:S(2)}) %collective-permute-start.12) | collective-permute-done | bytes 1048608 | tf_op jit(solution)/shard_map/ppermute | solution.py:11
  281.6 19.0 %collective-permute-start.17 = (bf16[4,8,8,2048]{3,2,0,1:T(8,128)(2,1)S(1)}, bf16[4,8,8,2048]{3,2,0,1:T(8,128)(2,1)S(1)}, u32[]{:S(2)}, u32[]{:S(2)}) collective-permute-start(bf16[4,8,8,2048]{3,2,0,1:T(8,128)(2,1)S(1)} %get-tuple-element.130), channel_id=1, source_target_pairs={{0,4},{1,5},{2,6},{3,7},{4,0},{5,1},{6,2},{7,3},{8,12},{9,13},{10,... | collective-permute-start | bytes 3145736 | tf_op jit(solution)/shard_map/ppermute | solution.py:11
  305.2 37.0 %collective-permute-done.17 = bf16[4,8,8,2048]{3,2,0,1:T(8,128)(2,1)S(1)} collective-permute-done((bf16[4,8,8,2048]{3,2,0,1:T(8,128)(2,1)S(1)}, bf16[4,8,8,2048]{3,2,0,1:T(8,128)(2,1)S(1)}, u32[]{:S(2)}, u32[]{:S(2)}) %collective-permute-start.17) | collective-permute-done | bytes 1048608 | tf_op jit(solution)/shard_map/ppermute | solution.py:11
  342.2 2.0 collective-permute-start.23
  344.6 31.1 %collective-permute-done.18 = bf16[4,8,8,2048]{3,2,0,1:T(8,128)(2,1)S(1)} collective-permute-done((bf16[4,8,8,2048]{3,2,0,1:T(8,128)(2,1)S(1)}, bf16[4,8,8,2048]{3,2,0,1:T(8,128)(2,1)S(1)}, u32[]{:S(2)}, u32[]{:S(2)}) %collective-permute-start.18) | collective-permute-done | bytes 1048608 | tf_op jit(solution)/shard_map/ppermute | solution.py:11
  376.2 5.1 %fusion.1 = (f32[2048]{0:T(1024)S(1)}, bf16[8,128,2048]{2,1,0:T(8,128)(2,1)S(1)}) fusion(f32[8,128,2048]{2,1,0:T(8,128)S(1)} %bitcast.343, f32[2048]{0:T(1024)S(1)} %copy-done.9, bf16[4,1,8,8,2048]{4,3,1,0,2:T(8,128)(2,1)S(1)} %bitcast.350, bf16[4,1,8,8,2048]{4,3,1,0,2:T(8,128)(2,1)S(1)} %bitcast.351, bf16[4,8,8,2048]{3,2,1,0:T(8,128)(2,1)S(1)} %pad_maximum_fusion.14, ...), kind=kLoop, calls=%fused_computation.3 | loop fusion | flops 46135296 | bytes 16793600 | tf_op jit(solution)/shard_map/reduce_sum | solution.py:140
  381.3 2.9 multiply_reduce_fusion
  387.0 2.8 collective-permute-start.28
  391.7 2.4 collective-permute-start.30
  394.1 2.0 collective-permute-start.31
  396.1 4.5 %fusion.2 = bf16[1024,2048]{1,0:T(8,128)(2,1)} fusion(f32[8,128,2048]{2,1,0:T(8,128)S(1)} %get-tuple-element.200, bf16[1,1024,2048]{2,1,0:T(8,128)(2,1)S(1)} %copy-done.4, bf16[1,1024,2048]{2,1,0:T(8,128)(2,1)S(1)} %copy-done.3, f32[1024]{0:T(1024)S(1)} %multiply_bitcast_fusion, f32[2048]{0:T(1024)S(1)} %copy-done.8, f32[1024]{0:T(1024)S(1)} %get-tuple-element.196), kind=kLoop, calls=%fused_computation.5 | loop fusion | flops 18874368 | bytes 20987904 | tf_op jit(solution)/shard_map/convert_element_type | solution.py:154
  402.9 2.6 fusion.23
  (134 shorter events, 47.8 us)
Async XLA Ops:
  4.8 48.9 %collective-permute-start = (bf16[8,4,8,2048]{3,2,1,0:T(8,128)(2,1)}, bf16[8,4,8,2048]{3,2,1,0:T(8,128)(2,1)}, u32[]{:S(2)}, u32[]{:S(2)}) collective-permute-start(bf16[8,4,8,2048]{3,2,1,0:T(8,128)(2,1)} %get-tuple-element.141), channel_id=1, source_target_pairs={{0,4},{1,5},{2,6},{3,7},{4,0},{5,1},{6,2},{7,3},{8,12},{9,13},{10,... | collective-permute-start | bytes 3145736 | tf_op jit(solution)/shard_map/ppermute | solution.py:11
  7.8 49.8 %collective-permute-start.1 = (bf16[8,4,8,2048]{3,2,1,0:T(8,128)(2,1)}, bf16[8,4,8,2048]{3,2,1,0:T(8,128)(2,1)}, u32[]{:S(2)}, u32[]{:S(2)}) collective-permute-start(bf16[8,4,8,2048]{3,2,1,0:T(8,128)(2,1)} %get-tuple-element.140), channel_id=1, source_target_pairs={{0,8},{1,9},{2,10},{3,11},{4,12},{5,13},{6,14},{7,15},{8,0},{9,1},... | collective-permute-start | bytes 3145736 | tf_op jit(solution)/shard_map/ppermute | solution.py:11
  23.0 35.9 %collective-permute-start.2 = (bf16[8,4,8,2048]{3,2,0,1:T(8,128)(2,1)}, bf16[8,4,8,2048]{3,2,0,1:T(8,128)(2,1)}, u32[]{:S(2)}, u32[]{:S(2)}) collective-permute-start(bf16[8,4,8,2048]{3,2,0,1:T(8,128)(2,1)} %bitcast.327), channel_id=1, source_target_pairs={{0,1},{1,0},{2,3},{3,2},{4,5},{5,4},{6,7},{7,6},{8,9},{9,8},{10,11... | collective-permute-start | bytes 3145736 | tf_op jit(solution)/shard_map/ppermute | solution.py:11
  25.5 46.8 %collective-permute-start.3 = (bf16[8,4,8,2048]{3,2,0,1:T(8,128)(2,1)}, bf16[8,4,8,2048]{3,2,0,1:T(8,128)(2,1)}, u32[]{:S(2)}, u32[]{:S(2)}) collective-permute-start(bf16[8,4,8,2048]{3,2,0,1:T(8,128)(2,1)} %bitcast.326), channel_id=1, source_target_pairs={{0,2},{1,3},{2,0},{3,1},{4,6},{5,7},{6,4},{7,5},{8,10},{9,11},{10,... | collective-permute-start | bytes 3145736 | tf_op jit(solution)/shard_map/ppermute | solution.py:11
  27.0 45.3 %collective-permute-start.4 = (bf16[8,4,8,2048]{3,2,1,0:T(8,128)(2,1)}, bf16[8,4,8,2048]{3,2,1,0:T(8,128)(2,1)}, u32[]{:S(2)}, u32[]{:S(2)}) collective-permute-start(bf16[8,4,8,2048]{3,2,1,0:T(8,128)(2,1)} %get-tuple-element.143), channel_id=1, source_target_pairs={{0,3},{1,2},{2,1},{3,0},{4,7},{5,6},{6,5},{7,4},{8,11},{9,10},{10,... | collective-permute-start | bytes 3145736 | tf_op jit(solution)/shard_map/ppermute | solution.py:11
  53.6 26.5 %collective-permute-start.7 = (bf16[8,4,8,2048]{3,2,1,0:T(8,128)(2,1)}, bf16[8,4,8,2048]{3,2,1,0:T(8,128)(2,1)S(1)}, u32[]{:S(2)}, u32[]{:S(2)}) collective-permute-start(bf16[8,4,8,2048]{3,2,1,0:T(8,128)(2,1)} %get-tuple-element.139), channel_id=1, source_target_pairs={{0,12},{1,13},{2,14},{3,15},{4,8},{5,9},{6,10},{7,11},{8,4},{9,5},... | collective-permute-start | bytes 3145736 | tf_op jit(solution)/shard_map/ppermute | solution.py:11
  80.3 95.5 %collective-permute-start.10 = (bf16[4,8,8,2048]{3,2,1,0:T(8,128)(2,1)S(1)}, bf16[4,8,8,2048]{3,2,1,0:T(8,128)(2,1)S(1)}, u32[]{:S(2)}, u32[]{:S(2)}) collective-permute-start(bf16[4,8,8,2048]{3,2,1,0:T(8,128)(2,1)S(1)} %pad_maximum_fusion.13), channel_id=1, source_target_pairs={{0,3},{1,2},{2,1},{3,0},{4,7},{5,6},{6,5},{7,4},{8,11},{9,10},{10,... | collective-permute-start | bytes 3145736 | tf_op jit(solution)/shard_map/ppermute | solution.py:11
  82.8 65.8 %collective-permute-start.5 = (bf16[4,8,8,2048]{3,2,1,0:T(8,128)(2,1)S(1)}, bf16[4,8,8,2048]{3,2,1,0:T(8,128)(2,1)S(1)}, u32[]{:S(2)}, u32[]{:S(2)}) collective-permute-start(bf16[4,8,8,2048]{3,2,1,0:T(8,128)(2,1)S(1)} %pad_maximum_fusion.7), channel_id=1, source_target_pairs={{0,4},{1,5},{2,6},{3,7},{4,0},{5,1},{6,2},{7,3},{8,12},{9,13},{10,... | collective-permute-start | bytes 3145736 | tf_op jit(solution)/shard_map/ppermute | solution.py:11
  104.6 70.9 %collective-permute-start.6 = (bf16[4,8,8,2048]{3,2,1,0:T(8,128)(2,1)S(1)}, bf16[4,8,8,2048]{3,2,1,0:T(8,128)(2,1)S(1)}, u32[]{:S(2)}, u32[]{:S(2)}) collective-permute-start(bf16[4,8,8,2048]{3,2,1,0:T(8,128)(2,1)S(1)} %pad_maximum_fusion.8), channel_id=1, source_target_pairs={{0,8},{1,9},{2,10},{3,11},{4,12},{5,13},{6,14},{7,15},{8,0},{9,1},... | collective-permute-start | bytes 3145736 | tf_op jit(solution)/shard_map/ppermute | solution.py:11
  105.9 69.9 %collective-permute-start.9 = (bf16[4,8,8,2048]{3,2,1,0:T(8,128)(2,1)S(1)}, bf16[4,8,8,2048]{3,2,1,0:T(8,128)(2,1)S(1)}, u32[]{:S(2)}, u32[]{:S(2)}) collective-permute-start(bf16[4,8,8,2048]{3,2,1,0:T(8,128)(2,1)S(1)} %pad_maximum_fusion.12), channel_id=1, source_target_pairs={{0,2},{1,3},{2,0},{3,1},{4,6},{5,7},{6,4},{7,5},{8,10},{9,11},{10,... | collective-permute-start | bytes 3145736 | tf_op jit(solution)/shard_map/ppermute | solution.py:11
  106.6 69.2 %collective-permute-start.8 = (bf16[4,8,8,2048]{3,2,1,0:T(8,128)(2,1)S(1)}, bf16[4,8,8,2048]{3,2,1,0:T(8,128)(2,1)S(1)}, u32[]{:S(2)}, u32[]{:S(2)}) collective-permute-start(bf16[4,8,8,2048]{3,2,1,0:T(8,128)(2,1)S(1)} %pad_maximum_fusion.11), channel_id=1, source_target_pairs={{0,1},{1,0},{2,3},{3,2},{4,5},{5,4},{6,7},{7,6},{8,9},{9,8},{10,11... | collective-permute-start | bytes 3145736 | tf_op jit(solution)/shard_map/ppermute | solution.py:11
  148.6 31.9 %collective-permute-start.13 = (bf16[4,8,8,2048]{3,2,1,0:T(8,128)(2,1)S(1)}, bf16[4,8,8,2048]{3,2,1,0:T(8,128)(2,1)S(1)}, u32[]{:S(2)}, u32[]{:S(2)}) collective-permute-start(bf16[4,8,8,2048]{3,2,1,0:T(8,128)(2,1)S(1)} %pad_maximum_fusion.9), channel_id=1, source_target_pairs={{0,12},{1,13},{2,14},{3,15},{4,8},{5,9},{6,10},{7,11},{8,4},{9,5},... | collective-permute-start | bytes 3145736 | tf_op jit(solution)/shard_map/ppermute | solution.py:11
  185.5 58.1 %collective-permute-start.11 = (bf16[4,8,8,2048]{3,2,1,0:T(8,128)(2,1)S(1)}, bf16[4,8,8,2048]{3,2,1,0:T(8,128)(2,1)S(1)}, u32[]{:S(2)}, u32[]{:S(2)}) collective-permute-start(bf16[4,8,8,2048]{3,2,1,0:T(8,128)(2,1)S(1)} %copy.93), channel_id=1, source_target_pairs={{0,4},{1,5},{2,6},{3,7},{4,0},{5,1},{6,2},{7,3},{8,12},{9,13},{10,... | collective-permute-start | bytes 3145736 | tf_op jit(solution)/shard_map/ppermute | solution.py:11
  204.0 3.6 collective-permute-start.32
  204.7 71.9 %collective-permute-start.12 = (bf16[4,8,8,2048]{3,2,1,0:T(8,128)(2,1)S(1)}, bf16[4,8,8,2048]{3,2,1,0:T(8,128)(2,1)S(1)}, u32[]{:S(2)}, u32[]{:S(2)}) collective-permute-start(bf16[4,8,8,2048]{3,2,1,0:T(8,128)(2,1)S(1)} %copy.95), channel_id=1, source_target_pairs={{0,8},{1,9},{2,10},{3,11},{4,12},{5,13},{6,14},{7,15},{8,0},{9,1},... | collective-permute-start | bytes 3145736 | tf_op jit(solution)/shard_map/ppermute | solution.py:11
  205.2 71.7 %collective-permute-start.14 = (bf16[4,8,8,2048]{3,1,0,2:T(8,128)(2,1)S(1)}, bf16[4,8,8,2048]{3,1,0,2:T(8,128)(2,1)S(1)}, u32[]{:S(2)}, u32[]{:S(2)}) collective-permute-start(bf16[4,8,8,2048]{3,1,0,2:T(8,128)(2,1)S(1)} %get-tuple-element.133), channel_id=1, source_target_pairs={{0,1},{1,0},{2,3},{3,2},{4,5},{5,4},{6,7},{7,6},{8,9},{9,8},{10,11... | collective-permute-start | bytes 3145736 | tf_op jit(solution)/shard_map/ppermute | solution.py:11
  205.7 71.2 %collective-permute-start.15 = (bf16[4,8,8,2048]{3,1,0,2:T(8,128)(2,1)S(1)}, bf16[4,8,8,2048]{3,1,0,2:T(8,128)(2,1)S(1)}, u32[]{:S(2)}, u32[]{:S(2)}) collective-permute-start(bf16[4,8,8,2048]{3,1,0,2:T(8,128)(2,1)S(1)} %get-tuple-element.132), channel_id=1, source_target_pairs={{0,2},{1,3},{2,0},{3,1},{4,6},{5,7},{6,4},{7,5},{8,10},{9,11},{10,... | collective-permute-start | bytes 3145736 | tf_op jit(solution)/shard_map/ppermute | solution.py:11
  207.6 69.3 %collective-permute-start.16 = (bf16[4,8,8,2048]{3,1,0,2:T(8,128)(2,1)S(1)}, bf16[4,8,8,2048]{3,1,0,2:T(8,128)(2,1)S(1)}, u32[]{:S(2)}, u32[]{:S(2)}) collective-permute-start(bf16[4,8,8,2048]{3,1,0,2:T(8,128)(2,1)S(1)} %get-tuple-element.131), channel_id=1, source_target_pairs={{0,3},{1,2},{2,1},{3,0},{4,7},{5,6},{6,5},{7,4},{8,11},{9,10},{10,... | collective-permute-start | bytes 3145736 | tf_op jit(solution)/shard_map/ppermute | solution.py:11
  243.7 36.6 %collective-permute-start.19 = (bf16[4,8,8,2048]{3,2,0,1:T(8,128)(2,1)S(1)}, bf16[4,8,8,2048]{3,2,0,1:T(8,128)(2,1)S(1)}, u32[]{:S(2)}, u32[]{:S(2)}) collective-permute-start(bf16[4,8,8,2048]{3,2,0,1:T(8,128)(2,1)S(1)} %copy.106), channel_id=1, source_target_pairs={{0,12},{1,13},{2,14},{3,15},{4,8},{5,9},{6,10},{7,11},{8,4},{9,5},... | collective-permute-start | bytes 3145736 | tf_op jit(solution)/shard_map/ppermute | solution.py:11
  280.8 95.3 %collective-permute-start.22 = (bf16[4,8,8,2048]{3,2,0,1:T(8,128)(2,1)S(1)}, bf16[4,8,8,2048]{3,2,0,1:T(8,128)(2,1)S(1)}, u32[]{:S(2)}, u32[]{:S(2)}) collective-permute-start(bf16[4,8,8,2048]{3,2,0,1:T(8,128)(2,1)S(1)} %pad_maximum_fusion.17), channel_id=1, source_target_pairs={{0,3},{1,2},{2,1},{3,0},{4,7},{5,6},{6,5},{7,4},{8,11},{9,10},{10,... | collective-permute-start | bytes 3145736 | tf_op jit(solution)/shard_map/ppermute | solution.py:11
  281.6 60.6 %collective-permute-start.17 = (bf16[4,8,8,2048]{3,2,0,1:T(8,128)(2,1)S(1)}, bf16[4,8,8,2048]{3,2,0,1:T(8,128)(2,1)S(1)}, u32[]{:S(2)}, u32[]{:S(2)}) collective-permute-start(bf16[4,8,8,2048]{3,2,0,1:T(8,128)(2,1)S(1)} %get-tuple-element.130), channel_id=1, source_target_pairs={{0,4},{1,5},{2,6},{3,7},{4,0},{5,1},{6,2},{7,3},{8,12},{9,13},{10,... | collective-permute-start | bytes 3145736 | tf_op jit(solution)/shard_map/ppermute | solution.py:11
  300.7 75.4 %collective-permute-start.21 = (bf16[4,8,8,2048]{3,2,0,1:T(8,128)(2,1)S(1)}, bf16[4,8,8,2048]{3,2,0,1:T(8,128)(2,1)S(1)}, u32[]{:S(2)}, u32[]{:S(2)}) collective-permute-start(bf16[4,8,8,2048]{3,2,0,1:T(8,128)(2,1)S(1)} %pad_maximum_fusion.16), channel_id=1, source_target_pairs={{0,2},{1,3},{2,0},{3,1},{4,6},{5,7},{6,4},{7,5},{8,10},{9,11},{10,... | collective-permute-start | bytes 3145736 | tf_op jit(solution)/shard_map/ppermute | solution.py:11
  302.2 73.9 %collective-permute-start.20 = (bf16[4,8,8,2048]{3,2,1,0:T(8,128)(2,1)S(1)}, bf16[4,8,8,2048]{3,2,1,0:T(8,128)(2,1)S(1)}, u32[]{:S(2)}, u32[]{:S(2)}) collective-permute-start(bf16[4,8,8,2048]{3,2,1,0:T(8,128)(2,1)S(1)} %pad_maximum_fusion.15), channel_id=1, source_target_pairs={{0,1},{1,0},{2,3},{3,2},{4,5},{5,4},{6,7},{7,6},{8,9},{9,8},{10,11... | collective-permute-start | bytes 3145736 | tf_op jit(solution)/shard_map/ppermute | solution.py:11
  303.8 71.9 %collective-permute-start.18 = (bf16[4,8,8,2048]{3,2,0,1:T(8,128)(2,1)S(1)}, bf16[4,8,8,2048]{3,2,0,1:T(8,128)(2,1)S(1)}, u32[]{:S(2)}, u32[]{:S(2)}) collective-permute-start(bf16[4,8,8,2048]{3,2,0,1:T(8,128)(2,1)S(1)} %get-tuple-element.129), channel_id=1, source_target_pairs={{0,8},{1,9},{2,10},{3,11},{4,12},{5,13},{6,14},{7,15},{8,0},{9,1},... | collective-permute-start | bytes 3145736 | tf_op jit(solution)/shard_map/ppermute | solution.py:11
  342.2 59.7 %collective-permute-start.23 = (bf16[4,8,8,2048]{3,2,0,1:T(8,128)(2,1)S(1)}, bf16[4,8,8,2048]{3,2,0,1:T(8,128)(2,1)S(1)}, u32[]{:S(2)}, u32[]{:S(2)}) collective-permute-start(bf16[4,8,8,2048]{3,2,0,1:T(8,128)(2,1)S(1)} %get-tuple-element.94), channel_id=1, source_target_pairs={{0,12},{1,13},{2,14},{3,15},{4,8},{5,9},{6,10},{7,11},{8,4},{9,5},... | collective-permute-start | bytes 3145736 | tf_op jit(solution)/shard_map/ppermute | solution.py:11
  385.7 15.6 %collective-permute-start.24 = (f32[8,128,128]{2,1,0:T(8,128)S(1)}, f32[8,128,128]{2,1,0:T(8,128)S(1)}, u32[]{:S(2)}, u32[]{:S(2)}) collective-permute-start(f32[8,128,128]{2,1,0:T(8,128)S(1)} %fusion.14), channel_id=1, source_target_pairs={{0,16},{16,0},{1,17},{17,1},{2,18},{18,2},{3,19},{19,3},{4,20},{20... | collective-permute-start | bytes 1572872 | tf_op jit(solution)/shard_map/ppermute | solution.py:11
  386.3 3.8 collective-permute-start.26
  386.9 3.7 collective-permute-start.27
  387.0 4.6 %collective-permute-start.28 = (f32[2,2048]{1,0:T(2,128)S(1)}, f32[2,2048]{1,0:T(2,128)S(1)}, u32[]{:S(2)}, u32[]{:S(2)}) collective-permute-start(f32[2,2048]{1,0:T(2,128)S(1)} %fusion.41), channel_id=1, source_target_pairs={{0,3},{1,2},{2,1},{3,0},{4,7},{5,6},{6,5},{7,4},{8,11},{9,10},{10,... | collective-permute-start | bytes 49160 | tf_op jit(solution)/shard_map/ppermute | solution.py:11
  391.6 9.0 %collective-permute-start.29 = (f32[2,2048]{1,0:T(2,128)S(1)}, f32[2,2048]{1,0:T(2,128)S(1)}, u32[]{:S(2)}, u32[]{:S(2)}) collective-permute-start(f32[2,2048]{1,0:T(2,128)S(1)} %add_add_fusion.1), channel_id=1, source_target_pairs={{0,4},{1,5},{2,6},{3,7},{4,0},{5,1},{6,2},{7,3},{8,12},{9,13},{10,... | collective-permute-start | bytes 49160 | tf_op jit(solution)/shard_map/ppermute | solution.py:11
  391.7 8.9 %collective-permute-start.30 = (f32[2,2048]{1,0:T(2,128)S(1)}, f32[2,2048]{1,0:T(2,128)S(1)}, u32[]{:S(2)}, u32[]{:S(2)}) collective-permute-start(f32[2,2048]{1,0:T(2,128)S(1)} %add_add_fusion.1), channel_id=1, source_target_pairs={{0,8},{1,9},{2,10},{3,11},{4,12},{5,13},{6,14},{7,15},{8,0},{9,1},... | collective-permute-start | bytes 49160 | tf_op jit(solution)/shard_map/ppermute | solution.py:11
  394.1 6.5 %collective-permute-start.31 = (f32[2,2048]{1,0:T(2,128)S(1)}, f32[2,2048]{1,0:T(2,128)S(1)}, u32[]{:S(2)}, u32[]{:S(2)}) collective-permute-start(f32[2,2048]{1,0:T(2,128)S(1)} %add_add_fusion.1), channel_id=1, source_target_pairs={{0,12},{1,13},{2,14},{3,15},{4,8},{5,9},{6,10},{7,11},{8,4},{9,5},... | collective-permute-start | bytes 49160 | tf_op jit(solution)/shard_map/ppermute | solution.py:11
  (13 other events, 223.9 us)

commit v8 on v6

--- a/solution.py
+++ b/solution.py
@@ -49,7 +49,12 @@
     rest = [k for k in range(1, far) if k != half]
 
     up_view = upstream[0].reshape(local, far, near, local, width)
-    up_parts = [lax.dynamic_index_in_dim(up_view, device_far ^ k, 1, keepdims=False) for k in range(far)]
+    up_first = lax.dynamic_index_in_dim(up_view, device_far ^ half, 1, keepdims=False)
+    up_view, up_first = lax.optimization_barrier((up_view, up_first))
+    up_parts = [
+        up_first if k == half else lax.dynamic_index_in_dim(up_view, device_far ^ k, 1, keepdims=False)
+        for k in range(far)
+    ]
     up_far = [from_partner(up_parts[k], "seq", k << low) for k in range(far)]
     inputs, up_far[0] = lax.optimization_barrier((inputs, up_far[0]))
     input_float = inputs[0].astype(f32)
@@ -94,9 +99,13 @@
     mixed = jnp.einsum("bij,jbd->ibd", lefts, arrived, preferred_element_type=f32).astype(bf16)
     mixed = mixed.reshape(far, near, local, local, width)
     mixed_parts = [from_partner(mixed[:, k], "seq", k) for k in range(near)]
-    upward, arrived, mixed_parts[0] = lax.optimization_barrier((upward, arrived, mixed_parts[0]))
     back_pair = jnp.stack([back_far[0], back_far[half]])
-    back_pair, mixed_parts = lax.optimization_barrier((back_pair, mixed_parts))
+    upward, arrived, back_pair = lax.optimization_barrier((upward, arrived, back_pair))
+    grad_left = jnp.einsum("ibd,jbd->bij", upward, arrived, preferred_element_type=f32)
+    grad_left, mixed_parts = lax.optimization_barrier((grad_left, mixed_parts))
+    grad_left = sum_over(grad_left, "dp", 0, dp_levels)
+    grad_left = jnp.einsum("ki,aij->akj", swap_full, grad_left, precision=lax.Precision.HIGHEST)
+    grad_left = jnp.einsum("aij,jl->ail", grad_left, swap_full, precision=lax.Precision.HIGHEST)
     back_far[0], back_far[half] = back_pair[0], back_pair[1]
     mixed_near = jnp.zeros((far, near, local, local, width), bf16)
     for k, part in enumerate(mixed_parts):
@@ -121,11 +130,6 @@
     output, back_near = lax.optimization_barrier((output, back_near))
     dgated = jnp.stack(back_near, axis=1).transpose(2, 0, 1, 3, 4).reshape(local, order, width).astype(f32)
 
-    grad_left = jnp.einsum("ibd,jbd->bij", upward, arrived, preferred_element_type=f32)
-    grad_left = sum_over(grad_left, "dp", 0, dp_levels)
-    grad_left = jnp.einsum("ki,aij->akj", swap_full, grad_left, precision=lax.Precision.HIGHEST)
-    grad_left = jnp.einsum("aij,jl->ail", grad_left, swap_full, precision=lax.Precision.HIGHEST)
-
     slope = sig * (1.0 - sig)
     dfirst = (dgated * (sig + first * mid_scale * slope)).astype(bf16)
     mid_part = jnp.sum(dgated * first * first * slope, axis=(0, 1))
@@ -147,8 +151,8 @@
     vectors = sum_over(vectors, "dp", 0, dp_levels)
     vectors = sum_over(vectors, "seq", 0, low)
     gain_gradient, grad_mid = sum_over(vectors, "seq", low, levels)
-    mixed_rest, input_gradient, gain_gradient, grad_mid = lax.optimization_barrier(
-        ([mixed_far[k] for k in rest], input_gradient, gain_gradient, grad_mid)
+    mixed_rest, input_gradient, grad_right, gain_gradient, grad_mid = lax.optimization_barrier(
+        ([mixed_far[k] for k in rest], input_gradient, grad_right, gain_gradient, grad_mid)
     )
     for k, part in zip(rest, mixed_rest):
         output = placed(output, part, k)

time: 400 us -> 404 us (1.010)
  other arithmetic: 35 us -> 39.6 us
    dynamic_update_slice x4, other arithmetic: 1.56 us -> 5.95 us  [placed(): return lax.dynamic_update_index_in_dim(output, block, place, 1)]
  transfers between devices with their start and end apart: 33 -> 33, of which waited for: 11 -> 11; matrix products, arithmetic and copies ran while one was open for 19% -> 21% of each run, Pallas kernels for 0% -> 0%
where the time goes in v8:
time: 404 us; the launch traced here: 397 us
  waiting for transfers between devices  216 us (53%)
  starting transfers between devices  80.7 us (20%)
  other arithmetic  39.6 us (10%)
  local copies, waits for them, and re-layouts  37.8 us (9%)
  matrix products  21.4 us (5%)
    ppermute x33, waiting for transfers between devices, from_partner(): return lax.ppermute(block, axis, [(i, i ^ distance) for i in range(count)])  216 us
    ppermute x33, starting transfers between devices, from_partner(): return lax.ppermute(block, axis, [(i, i ^ distance) for i in range(count)])  80.7 us
    another operation x1, other arithmetic, body(): upward = jnp.stack(up_near, axis=1).reshape(order, local, width)  13.8 us
    dot_general x1, matrix products, body(): first = jnp.einsum('aij,ajd->aid', rights, grid, preferred_element_type=f32)  8.98 us
  transfers between devices with their start and end apart: 33, of which 11 were waited for; matrix products, arithmetic and copies ran while one was open for 21% of the time, Pallas kernels for 0%

profile of v8, /device:TPU:0, one launch (start us, length us, event | category | flops | bytes accessed | tf_op | source)
XLA Modules:
  0.0 397.3 jit_solution(12860305134169252138)
XLA Ops:
  0.7 2.4 dynamic-slice_bitcast_fusion.3
  3.0 4.0 %collective-permute-start = (bf16[8,4,8,2048]{3,2,1,0:T(8,128)(2,1)}, bf16[8,4,8,2048]{3,2,1,0:T(8,128)(2,1)}, u32[]{:S(2)}, u32[]{:S(2)}) collective-permute-start(bf16[8,4,8,2048]{3,2,1,0:T(8,128)(2,1)} %dynamic-slice_bitcast_fusion.3), channel_id=1, source_target_pairs={{0,8},{1,9},{2,10},{3,11},{4,12},{5,13},{6,14},{7,15},{8,0},{9,1},... | collective-permute-start | bytes 3145736 | tf_op jit(solution)/shard_map/ppermute | solution.py:11
  7.1 3.7 dynamic-slice_bitcast_fusion
  12.0 9.0 %multiply_convert_fusion = (bf16[8,128,2048]{2,1,0:T(8,128)(2,1)S(1)}, f32[8,128,2048]{2,1,0:T(8,128)}) fusion(f32[2048]{0:T(1024)S(1)} %copy-done.9, bf16[8,128,128]{1,2,0:T(8,128)(2,1)S(1)} %convolution_bitcast_fusion.3, f32[2048]{0:T(1024)S(1)} %copy-done.8, f32[8,128]{1,0:T(8,128)S(1)} %get-tuple-element.194, bf16[8,128,2048]{2,1,0:T(8,128)(2,1)} %bitcast.316), kind=kOutput, calls=%fused_computation.17 | convolution fusion | flops 557842432 | bytes 17059840 | tf_op jit(solution)/shard_map/aij,ajd->aid/dot_general | solution.py:65
  30.4 22.7 %collective-permute-done = bf16[8,4,8,2048]{3,2,1,0:T(8,128)(2,1)} collective-permute-done((bf16[8,4,8,2048]{3,2,1,0:T(8,128)(2,1)}, bf16[8,4,8,2048]{3,2,1,0:T(8,128)(2,1)}, u32[]{:S(2)}, u32[]{:S(2)}) %collective-permute-start) | collective-permute-done | bytes 1048608 | tf_op jit(solution)/shard_map/ppermute | solution.py:11
  53.1 3.5 collective-permute-start.6
  58.6 14.4 %collective-permute-done.2 = bf16[8,4,8,2048]{3,2,0,1:T(8,128)(2,1)} collective-permute-done((bf16[8,4,8,2048]{3,2,0,1:T(8,128)(2,1)}, bf16[8,4,8,2048]{3,2,0,1:T(8,128)(2,1)}, u32[]{:S(2)}, u32[]{:S(2)}) %collective-permute-start.2) | collective-permute-done | bytes 1048608 | tf_op jit(solution)/shard_map/ppermute | solution.py:11
  80.9 14.9 %collective-permute-done.5 = bf16[8,4,8,2048]{3,2,1,0:T(8,128)(2,1)} collective-permute-done((bf16[8,4,8,2048]{3,2,1,0:T(8,128)(2,1)}, bf16[8,4,8,2048]{3,2,1,0:T(8,128)(2,1)}, u32[]{:S(2)}, u32[]{:S(2)}) %collective-permute-start.5) | collective-permute-done | bytes 1048608 | tf_op jit(solution)/shard_map/ppermute | solution.py:11
  95.8 2.2 dynamic-slice_bitcast_fusion.4
  98.1 2.6 collective-permute-start.9
  101.8 5.4 %collective-permute-start.4 = (bf16[4,8,8,2048]{3,2,1,0:T(8,128)(2,1)}, bf16[4,8,8,2048]{3,2,1,0:T(8,128)(2,1)}, u32[]{:S(2)}, u32[]{:S(2)}) collective-permute-start(bf16[4,8,8,2048]{3,2,1,0:T(8,128)(2,1)} %pad_maximum_fusion.5), channel_id=1, source_target_pairs={{0,8},{1,9},{2,10},{3,11},{4,12},{5,13},{6,14},{7,15},{8,0},{9,1},... | collective-permute-start | bytes 3145736 | tf_op jit(solution)/shard_map/ppermute | solution.py:11
  114.8 37.8 %collective-permute-done.4 = bf16[4,8,8,2048]{3,2,1,0:T(8,128)(2,1)} collective-permute-done((bf16[4,8,8,2048]{3,2,1,0:T(8,128)(2,1)}, bf16[4,8,8,2048]{3,2,1,0:T(8,128)(2,1)}, u32[]{:S(2)}, u32[]{:S(2)}) %collective-permute-start.4) | collective-permute-done | bytes 1048608 | tf_op jit(solution)/shard_map/ppermute | solution.py:11
  152.6 2.8 collective-permute-start.11
  156.9 13.8 %pad_maximum_fusion = bf16[4,4,8,8,2048]{4,3,2,0,1:T(8,128)(2,1)S(1)} fusion(bf16[4,1,8,8,2048]{4,3,2,0,1:T(8,128)(2,1)} %bitcast.58, bf16[4,1,8,8,2048]{4,3,2,0,1:T(8,128)(2,1)} %bitcast.57, bf16[4,1,8,8,2048]{4,3,2,0,1:T(8,128)(2,1)} %bitcast.56, bf16[4,1,8,8,2048]{4,3,2,0,1:T(8,128)(2,1)S(1)} %bitcast.337), kind=kLoop, calls=%fused_computation.20 | loop fusion | flops 6291456 | bytes 8388608 | tf_op jit(solution)/shard_map/stack | solution.py:88
  170.7 2.3 copy.91
  174.6 3.5 collective-permute-done.10
  178.9 2.3 copy.93
  181.8 20.7 %collective-permute-start.12 = (bf16[4,8,8,2048]{3,2,1,0:T(8,128)(2,1)S(1)}, bf16[4,8,8,2048]{3,2,1,0:T(8,128)(2,1)S(1)}, u32[]{:S(2)}, u32[]{:S(2)}) collective-permute-start(bf16[4,8,8,2048]{3,2,1,0:T(8,128)(2,1)S(1)} %copy.94), channel_id=1, source_target_pairs={{0,8},{1,9},{2,10},{3,11},{4,12},{5,13},{6,14},{7,15},{8,0},{9,1},... | collective-permute-start | bytes 3145736 | tf_op jit(solution)/shard_map/ppermute | solution.py:11
  205.4 2.4 collective-permute-start.15
  209.7 37.1 %collective-permute-done.12 = bf16[4,8,8,2048]{3,2,1,0:T(8,128)(2,1)S(1)} collective-permute-done((bf16[4,8,8,2048]{3,2,1,0:T(8,128)(2,1)S(1)}, bf16[4,8,8,2048]{3,2,1,0:T(8,128)(2,1)S(1)}, u32[]{:S(2)}, u32[]{:S(2)}) %collective-permute-start.12) | collective-permute-done | bytes 1048608 | tf_op jit(solution)/shard_map/ppermute | solution.py:11
  253.5 22.0 %collective-permute-done.17 = bf16[4,8,8,2048]{3,2,1,0:T(8,128)(2,1)S(1)} collective-permute-done((bf16[4,8,8,2048]{3,2,1,0:T(8,128)(2,1)S(1)}, bf16[4,8,8,2048]{3,2,1,0:T(8,128)(2,1)S(1)}, u32[]{:S(2)}, u32[]{:S(2)}) %collective-permute-start.17) | collective-permute-done | bytes 1048608 | tf_op jit(solution)/shard_map/ppermute | solution.py:11
  280.2 17.5 %collective-permute-start.16 = (bf16[4,8,8,2048]{3,2,0,1:T(8,128)(2,1)S(1)}, bf16[4,8,8,2048]{3,2,0,1:T(8,128)(2,1)S(1)}, u32[]{:S(2)}, u32[]{:S(2)}) collective-permute-start(bf16[4,8,8,2048]{3,2,0,1:T(8,128)(2,1)S(1)} %get-tuple-element.126), channel_id=1, source_target_pairs={{0,8},{1,9},{2,10},{3,11},{4,12},{5,13},{6,14},{7,15},{8,0},{9,1},... | collective-permute-start | bytes 3145736 | tf_op jit(solution)/shard_map/ppermute | solution.py:11
  300.9 42.5 %collective-permute-done.16 = bf16[4,8,8,2048]{3,2,0,1:T(8,128)(2,1)S(1)} collective-permute-done((bf16[4,8,8,2048]{3,2,0,1:T(8,128)(2,1)S(1)}, bf16[4,8,8,2048]{3,2,0,1:T(8,128)(2,1)S(1)}, u32[]{:S(2)}, u32[]{:S(2)}) %collective-permute-start.16) | collective-permute-done | bytes 1048608 | tf_op jit(solution)/shard_map/ppermute | solution.py:11
  345.1 2.0 copy-done.5
  347.1 4.8 %fusion.1 = (f32[2048]{0:T(1024)S(1)}, bf16[8,128,2048]{2,1,0:T(8,128)(2,1)S(1)}) fusion(f32[8,128,2048]{2,1,0:T(8,128)S(1)} %bitcast.331, f32[2048]{0:T(1024)S(1)} %copy-done.9, bf16[4,1,8,8,2048]{4,3,1,0,2:T(8,128)(2,1)S(1)} %bitcast.338, bf16[4,1,8,8,2048]{4,3,1,0,2:T(8,128)(2,1)S(1)} %bitcast.339, bf16[4,8,8,2048]{3,2,1,0:T(8,128)(2,1)S(1)} %pad_maximum_fusion.12, ...), kind=kLoop, calls=%fused_computation.3 | loop fusion | flops 46135296 | bytes 16793600 | tf_op jit(solution)/shard_map/reduce_sum | solution.py:135
  352.0 2.9 multiply_reduce_fusion
  357.3 2.5 collective-permute-start.28
  359.7 4.7 %fusion.2 = bf16[1024,2048]{1,0:T(8,128)(2,1)} fusion(f32[8,128,2048]{2,1,0:T(8,128)S(1)} %get-tuple-element.197, bf16[1,1024,2048]{2,1,0:T(8,128)(2,1)S(1)} %copy-done.4, bf16[1,1024,2048]{2,1,0:T(8,128)(2,1)S(1)} %copy-done.3, f32[1024]{0:T(1024)S(1)} %multiply_bitcast_fusion, f32[2048]{0:T(1024)S(1)} %copy-done.8, f32[1024]{0:T(1024)S(1)} %get-tuple-element.193), kind=kLoop, calls=%fused_computation.5 | loop fusion | flops 18874368 | bytes 20987904 | tf_op jit(solution)/shard_map/convert_element_type | solution.py:149
  364.6 3.1 collective-permute-start.30
  370.5 18.9 %collective-permute-done.30 = f32[2,2048]{1,0:T(2,128)S(1)} collective-permute-done((f32[2,2048]{1,0:T(2,128)S(1)}, f32[2,2048]{1,0:T(2,128)S(1)}, u32[]{:S(2)}, u32[]{:S(2)}) %collective-permute-start.30) | collective-permute-done | bytes 16416 | tf_op jit(solution)/shard_map/ppermute | solution.py:11
  391.7 2.6 fusion.21
  394.3 2.6 fusion.23
  (136 shorter events, 62.0 us)
Async XLA Ops:
  3.0 50.1 %collective-permute-start = (bf16[8,4,8,2048]{3,2,1,0:T(8,128)(2,1)}, bf16[8,4,8,2048]{3,2,1,0:T(8,128)(2,1)}, u32[]{:S(2)}, u32[]{:S(2)}) collective-permute-start(bf16[8,4,8,2048]{3,2,1,0:T(8,128)(2,1)} %dynamic-slice_bitcast_fusion.3), channel_id=1, source_target_pairs={{0,8},{1,9},{2,10},{3,11},{4,12},{5,13},{6,14},{7,15},{8,0},{9,1},... | collective-permute-start | bytes 3145736 | tf_op jit(solution)/shard_map/ppermute | solution.py:11
  23.3 35.3 %collective-permute-start.1 = (bf16[8,4,8,2048]{3,2,0,1:T(8,128)(2,1)}, bf16[8,4,8,2048]{3,2,0,1:T(8,128)(2,1)}, u32[]{:S(2)}, u32[]{:S(2)}) collective-permute-start(bf16[8,4,8,2048]{3,2,0,1:T(8,128)(2,1)} %bitcast.314), channel_id=1, source_target_pairs={{0,1},{1,0},{2,3},{3,2},{4,5},{5,4},{6,7},{7,6},{8,9},{9,8},{10,11... | collective-permute-start | bytes 3145736 | tf_op jit(solution)/shard_map/ppermute | solution.py:11
  25.9 47.1 %collective-permute-start.2 = (bf16[8,4,8,2048]{3,2,0,1:T(8,128)(2,1)}, bf16[8,4,8,2048]{3,2,0,1:T(8,128)(2,1)}, u32[]{:S(2)}, u32[]{:S(2)}) collective-permute-start(bf16[8,4,8,2048]{3,2,0,1:T(8,128)(2,1)} %bitcast.313), channel_id=1, source_target_pairs={{0,2},{1,3},{2,0},{3,1},{4,6},{5,7},{6,4},{7,5},{8,10},{9,11},{10,... | collective-permute-start | bytes 3145736 | tf_op jit(solution)/shard_map/ppermute | solution.py:11
  27.4 45.6 %collective-permute-start.3 = (bf16[8,4,8,2048]{3,2,1,0:T(8,128)(2,1)}, bf16[8,4,8,2048]{3,2,1,0:T(8,128)(2,1)}, u32[]{:S(2)}, u32[]{:S(2)}) collective-permute-start(bf16[8,4,8,2048]{3,2,1,0:T(8,128)(2,1)} %get-tuple-element.138), channel_id=1, source_target_pairs={{0,3},{1,2},{2,1},{3,0},{4,7},{5,6},{6,5},{7,4},{8,11},{9,10},{10,... | collective-permute-start | bytes 3145736 | tf_op jit(solution)/shard_map/ppermute | solution.py:11
  27.9 67.9 %collective-permute-start.5 = (bf16[8,4,8,2048]{3,2,1,0:T(8,128)(2,1)}, bf16[8,4,8,2048]{3,2,1,0:T(8,128)(2,1)}, u32[]{:S(2)}, u32[]{:S(2)}) collective-permute-start(bf16[8,4,8,2048]{3,2,1,0:T(8,128)(2,1)} %get-tuple-element.136), channel_id=1, source_target_pairs={{0,4},{1,5},{2,6},{3,7},{4,0},{5,1},{6,2},{7,3},{8,12},{9,13},{10,... | collective-permute-start | bytes 3145736 | tf_op jit(solution)/shard_map/ppermute | solution.py:11
  53.1 42.7 %collective-permute-start.6 = (bf16[8,4,8,2048]{3,2,1,0:T(8,128)(2,1)}, bf16[8,4,8,2048]{3,2,1,0:T(8,128)(2,1)S(1)}, u32[]{:S(2)}, u32[]{:S(2)}) collective-permute-start(bf16[8,4,8,2048]{3,2,1,0:T(8,128)(2,1)} %get-tuple-element.135), channel_id=1, source_target_pairs={{0,12},{1,13},{2,14},{3,15},{4,8},{5,9},{6,10},{7,11},{8,4},{9,5},... | collective-permute-start | bytes 3145736 | tf_op jit(solution)/shard_map/ppermute | solution.py:11
  98.1 58.7 %collective-permute-start.9 = (bf16[4,8,8,2048]{3,2,1,0:T(8,128)(2,1)S(1)}, bf16[4,8,8,2048]{3,2,1,0:T(8,128)(2,1)}, u32[]{:S(2)}, u32[]{:S(2)}) collective-permute-start(bf16[4,8,8,2048]{3,2,1,0:T(8,128)(2,1)S(1)} %pad_maximum_fusion.11), channel_id=1, source_target_pairs={{0,3},{1,2},{2,1},{3,0},{4,7},{5,6},{6,5},{7,4},{8,11},{9,10},{10,... | collective-permute-start | bytes 3145736 | tf_op jit(solution)/shard_map/ppermute | solution.py:11
  101.8 50.8 %collective-permute-start.4 = (bf16[4,8,8,2048]{3,2,1,0:T(8,128)(2,1)}, bf16[4,8,8,2048]{3,2,1,0:T(8,128)(2,1)}, u32[]{:S(2)}, u32[]{:S(2)}) collective-permute-start(bf16[4,8,8,2048]{3,2,1,0:T(8,128)(2,1)} %pad_maximum_fusion.5), channel_id=1, source_target_pairs={{0,8},{1,9},{2,10},{3,11},{4,12},{5,13},{6,14},{7,15},{8,0},{9,1},... | collective-permute-start | bytes 3145736 | tf_op jit(solution)/shard_map/ppermute | solution.py:11
  108.3 48.6 %collective-permute-start.8 = (bf16[4,8,8,2048]{3,2,1,0:T(8,128)(2,1)}, bf16[4,8,8,2048]{3,2,1,0:T(8,128)(2,1)}, u32[]{:S(2)}, u32[]{:S(2)}) collective-permute-start(bf16[4,8,8,2048]{3,2,1,0:T(8,128)(2,1)} %pad_maximum_fusion.10), channel_id=1, source_target_pairs={{0,2},{1,3},{2,0},{3,1},{4,6},{5,7},{6,4},{7,5},{8,10},{9,11},{10,... | collective-permute-start | bytes 3145736 | tf_op jit(solution)/shard_map/ppermute | solution.py:11
  109.9 47.0 %collective-permute-start.7 = (bf16[4,8,8,2048]{3,2,1,0:T(8,128)(2,1)}, bf16[4,8,8,2048]{3,2,1,0:T(8,128)(2,1)}, u32[]{:S(2)}, u32[]{:S(2)}) collective-permute-start(bf16[4,8,8,2048]{3,2,1,0:T(8,128)(2,1)} %pad_maximum_fusion.9), channel_id=1, source_target_pairs={{0,1},{1,0},{2,3},{3,2},{4,5},{5,4},{6,7},{7,6},{8,9},{9,8},{10,11... | collective-permute-start | bytes 3145736 | tf_op jit(solution)/shard_map/ppermute | solution.py:11
  111.8 66.3 %collective-permute-start.10 = (bf16[4,8,8,2048]{3,2,1,0:T(8,128)(2,1)S(1)}, bf16[4,8,8,2048]{3,2,1,0:T(8,128)(2,1)S(1)}, u32[]{:S(2)}, u32[]{:S(2)}) collective-permute-start(bf16[4,8,8,2048]{3,2,1,0:T(8,128)(2,1)S(1)} %pad_maximum_fusion.6), channel_id=1, source_target_pairs={{0,4},{1,5},{2,6},{3,7},{4,0},{5,1},{6,2},{7,3},{8,12},{9,13},{10,... | collective-permute-start | bytes 3145736 | tf_op jit(solution)/shard_map/ppermute | solution.py:11
  152.6 25.5 %collective-permute-start.11 = (bf16[4,8,8,2048]{3,2,1,0:T(8,128)(2,1)S(1)}, bf16[4,8,8,2048]{3,2,1,0:T(8,128)(2,1)S(1)}, u32[]{:S(2)}, u32[]{:S(2)}) collective-permute-start(bf16[4,8,8,2048]{3,2,1,0:T(8,128)(2,1)S(1)} %pad_maximum_fusion.7), channel_id=1, source_target_pairs={{0,12},{1,13},{2,14},{3,15},{4,8},{5,9},{6,10},{7,11},{8,4},{9,5},... | collective-permute-start | bytes 3145736 | tf_op jit(solution)/shard_map/ppermute | solution.py:11
  181.8 65.0 %collective-permute-start.12 = (bf16[4,8,8,2048]{3,2,1,0:T(8,128)(2,1)S(1)}, bf16[4,8,8,2048]{3,2,1,0:T(8,128)(2,1)S(1)}, u32[]{:S(2)}, u32[]{:S(2)}) collective-permute-start(bf16[4,8,8,2048]{3,2,1,0:T(8,128)(2,1)S(1)} %copy.94), channel_id=1, source_target_pairs={{0,8},{1,9},{2,10},{3,11},{4,12},{5,13},{6,14},{7,15},{8,0},{9,1},... | collective-permute-start | bytes 3145736 | tf_op jit(solution)/shard_map/ppermute | solution.py:11
  204.3 44.7 %collective-permute-start.13 = (bf16[4,8,8,2048]{3,1,0,2:T(8,128)(2,1)S(1)}, bf16[4,8,8,2048]{3,1,0,2:T(8,128)(2,1)S(1)}, u32[]{:S(2)}, u32[]{:S(2)}) collective-permute-start(bf16[4,8,8,2048]{3,1,0,2:T(8,128)(2,1)S(1)} %get-tuple-element.129), channel_id=1, source_target_pairs={{0,1},{1,0},{2,3},{3,2},{4,5},{5,4},{6,7},{7,6},{8,9},{9,8},{10,11... | collective-permute-start | bytes 3145736 | tf_op jit(solution)/shard_map/ppermute | solution.py:11
  204.9 45.2 %collective-permute-start.14 = (bf16[4,8,8,2048]{3,1,0,2:T(8,128)(2,1)S(1)}, bf16[4,8,8,2048]{3,1,0,2:T(8,128)(2,1)S(1)}, u32[]{:S(2)}, u32[]{:S(2)}) collective-permute-start(bf16[4,8,8,2048]{3,1,0,2:T(8,128)(2,1)S(1)} %get-tuple-element.128), channel_id=1, source_target_pairs={{0,2},{1,3},{2,0},{3,1},{4,6},{5,7},{6,4},{7,5},{8,10},{9,11},{10,... | collective-permute-start | bytes 3145736 | tf_op jit(solution)/shard_map/ppermute | solution.py:11
  205.4 44.7 %collective-permute-start.15 = (bf16[4,8,8,2048]{3,1,0,2:T(8,128)(2,1)S(1)}, bf16[4,8,8,2048]{3,1,0,2:T(8,128)(2,1)S(1)}, u32[]{:S(2)}, u32[]{:S(2)}) collective-permute-start(bf16[4,8,8,2048]{3,1,0,2:T(8,128)(2,1)S(1)} %get-tuple-element.127), channel_id=1, source_target_pairs={{0,3},{1,2},{2,1},{3,0},{4,7},{5,6},{6,5},{7,4},{8,11},{9,10},{10,... | collective-permute-start | bytes 3145736 | tf_op jit(solution)/shard_map/ppermute | solution.py:11
  209.0 66.5 %collective-permute-start.17 = (bf16[4,8,8,2048]{3,2,1,0:T(8,128)(2,1)S(1)}, bf16[4,8,8,2048]{3,2,1,0:T(8,128)(2,1)S(1)}, u32[]{:S(2)}, u32[]{:S(2)}) collective-permute-start(bf16[4,8,8,2048]{3,2,1,0:T(8,128)(2,1)S(1)} %copy.103), channel_id=1, source_target_pairs={{0,4},{1,5},{2,6},{3,7},{4,0},{5,1},{6,2},{7,3},{8,12},{9,13},{10,... | collective-permute-start | bytes 3145736 | tf_op jit(solution)/shard_map/ppermute | solution.py:11
  246.8 28.7 %collective-permute-start.18 = (bf16[4,8,8,2048]{3,2,0,1:T(8,128)(2,1)S(1)}, bf16[4,8,8,2048]{3,2,0,1:T(8,128)(2,1)S(1)}, u32[]{:S(2)}, u32[]{:S(2)}) collective-permute-start(bf16[4,8,8,2048]{3,2,0,1:T(8,128)(2,1)S(1)} %copy.104), channel_id=1, source_target_pairs={{0,12},{1,13},{2,14},{3,15},{4,8},{5,9},{6,10},{7,11},{8,4},{9,5},... | collective-permute-start | bytes 3145736 | tf_op jit(solution)/shard_map/ppermute | solution.py:11
  275.6 23.2 %collective-permute-start.32 = (f32[8,128,128]{2,1,0:T(8,128)S(1)}, f32[8,128,128]{2,1,0:T(8,128)S(1)}, u32[]{:S(2)}, u32[]{:S(2)}) collective-permute-start(f32[8,128,128]{2,1,0:T(8,128)S(1)} %fusion.48), channel_id=1, source_target_pairs={{0,16},{16,0},{1,17},{17,1},{2,18},{18,2},{3,19},{19,3},{4,20},{20... | collective-permute-start | bytes 1572872 | tf_op jit(solution)/shard_map/ppermute | solution.py:11
  276.0 69.1 %collective-permute-start.21 = (bf16[4,8,8,2048]{3,2,0,1:T(8,128)(2,1)S(1)}, bf16[4,8,8,2048]{3,2,0,1:T(8,128)(2,1)S(1)}, u32[]{:S(2)}, u32[]{:S(2)}) collective-permute-start(bf16[4,8,8,2048]{3,2,0,1:T(8,128)(2,1)S(1)} %pad_maximum_fusion.15), channel_id=1, source_target_pairs={{0,3},{1,2},{2,1},{3,0},{4,7},{5,6},{6,5},{7,4},{8,11},{9,10},{10,... | collective-permute-start | bytes 3145736 | tf_op jit(solution)/shard_map/ppermute | solution.py:11
  276.9 68.2 %collective-permute-start.20 = (bf16[4,8,8,2048]{3,2,0,1:T(8,128)(2,1)S(1)}, bf16[4,8,8,2048]{3,2,0,1:T(8,128)(2,1)S(1)}, u32[]{:S(2)}, u32[]{:S(2)}) collective-permute-start(bf16[4,8,8,2048]{3,2,0,1:T(8,128)(2,1)S(1)} %pad_maximum_fusion.14), channel_id=1, source_target_pairs={{0,2},{1,3},{2,0},{3,1},{4,6},{5,7},{6,4},{7,5},{8,10},{9,11},{10,... | collective-permute-start | bytes 3145736 | tf_op jit(solution)/shard_map/ppermute | solution.py:11
  278.6 66.5 %collective-permute-start.19 = (bf16[4,8,8,2048]{3,2,1,0:T(8,128)(2,1)S(1)}, bf16[4,8,8,2048]{3,2,1,0:T(8,128)(2,1)S(1)}, u32[]{:S(2)}, u32[]{:S(2)}) collective-permute-start(bf16[4,8,8,2048]{3,2,1,0:T(8,128)(2,1)S(1)} %pad_maximum_fusion.13), channel_id=1, source_target_pairs={{0,1},{1,0},{2,3},{3,2},{4,5},{5,4},{6,7},{7,6},{8,9},{9,8},{10,11... | collective-permute-start | bytes 3145736 | tf_op jit(solution)/shard_map/ppermute | solution.py:11
  280.2 63.2 %collective-permute-start.16 = (bf16[4,8,8,2048]{3,2,0,1:T(8,128)(2,1)S(1)}, bf16[4,8,8,2048]{3,2,0,1:T(8,128)(2,1)S(1)}, u32[]{:S(2)}, u32[]{:S(2)}) collective-permute-start(bf16[4,8,8,2048]{3,2,0,1:T(8,128)(2,1)S(1)} %get-tuple-element.126), channel_id=1, source_target_pairs={{0,8},{1,9},{2,10},{3,11},{4,12},{5,13},{6,14},{7,15},{8,0},{9,1},... | collective-permute-start | bytes 3145736 | tf_op jit(solution)/shard_map/ppermute | solution.py:11
  298.8 91.9 %collective-permute-start.22 = (bf16[4,8,8,2048]{3,2,0,1:T(8,128)(2,1)S(1)}, bf16[4,8,8,2048]{3,2,0,1:T(8,128)(2,1)S(1)}, u32[]{:S(2)}, u32[]{:S(2)}) collective-permute-start(bf16[4,8,8,2048]{3,2,0,1:T(8,128)(2,1)S(1)} %get-tuple-element.89), channel_id=1, source_target_pairs={{0,4},{1,5},{2,6},{3,7},{4,0},{5,1},{6,2},{7,3},{8,12},{9,13},{10,... | collective-permute-start | bytes 3145736 | tf_op jit(solution)/shard_map/ppermute | solution.py:11
  343.4 47.3 %collective-permute-start.23 = (bf16[4,8,8,2048]{3,2,0,1:T(8,128)(2,1)S(1)}, bf16[4,8,8,2048]{3,2,0,1:T(8,128)(2,1)S(1)}, u32[]{:S(2)}, u32[]{:S(2)}) collective-permute-start(bf16[4,8,8,2048]{3,2,0,1:T(8,128)(2,1)S(1)} %get-tuple-element.90), channel_id=1, source_target_pairs={{0,12},{1,13},{2,14},{3,15},{4,8},{5,9},{6,10},{7,11},{8,4},{9,5},... | collective-permute-start | bytes 3145736 | tf_op jit(solution)/shard_map/ppermute | solution.py:11
  356.2 8.3 %collective-permute-start.26 = (f32[2,2048]{1,0:T(2,128)S(1)}, f32[2,2048]{1,0:T(2,128)S(1)}, u32[]{:S(2)}, u32[]{:S(2)}) collective-permute-start(f32[2,2048]{1,0:T(2,128)S(1)} %fusion.41), channel_id=1, source_target_pairs={{0,1},{1,0},{2,3},{3,2},{4,5},{5,4},{6,7},{7,6},{8,9},{9,8},{10,11... | collective-permute-start | bytes 49160 | tf_op jit(solution)/shard_map/ppermute | solution.py:11
  356.7 7.7 %collective-permute-start.27 = (f32[2,2048]{1,0:T(2,128)S(1)}, f32[2,2048]{1,0:T(2,128)S(1)}, u32[]{:S(2)}, u32[]{:S(2)}) collective-permute-start(f32[2,2048]{1,0:T(2,128)S(1)} %fusion.41), channel_id=1, source_target_pairs={{0,2},{1,3},{2,0},{3,1},{4,6},{5,7},{6,4},{7,5},{8,10},{9,11},{10,... | collective-permute-start | bytes 49160 | tf_op jit(solution)/shard_map/ppermute | solution.py:11
  357.3 7.2 %collective-permute-start.28 = (f32[2,2048]{1,0:T(2,128)S(1)}, f32[2,2048]{1,0:T(2,128)S(1)}, u32[]{:S(2)}, u32[]{:S(2)}) collective-permute-start(f32[2,2048]{1,0:T(2,128)S(1)} %fusion.41), channel_id=1, source_target_pairs={{0,3},{1,2},{2,1},{3,0},{4,7},{5,6},{6,5},{7,4},{8,11},{9,10},{10,... | collective-permute-start | bytes 49160 | tf_op jit(solution)/shard_map/ppermute | solution.py:11
  364.5 5.8 %collective-permute-start.29 = (f32[2,2048]{1,0:T(2,128)S(1)}, f32[2,2048]{1,0:T(2,128)S(1)}, u32[]{:S(2)}, u32[]{:S(2)}) collective-permute-start(f32[2,2048]{1,0:T(2,128)S(1)} %add_add_fusion.1), channel_id=1, source_target_pairs={{0,4},{1,5},{2,6},{3,7},{4,0},{5,1},{6,2},{7,3},{8,12},{9,13},{10,... | collective-permute-start | bytes 49160 | tf_op jit(solution)/shard_map/ppermute | solution.py:11
  364.6 24.7 %collective-permute-start.30 = (f32[2,2048]{1,0:T(2,128)S(1)}, f32[2,2048]{1,0:T(2,128)S(1)}, u32[]{:S(2)}, u32[]{:S(2)}) collective-permute-start(f32[2,2048]{1,0:T(2,128)S(1)} %add_add_fusion.1), channel_id=1, source_target_pairs={{0,8},{1,9},{2,10},{3,11},{4,12},{5,13},{6,14},{7,15},{8,0},{9,1},... | collective-permute-start | bytes 49160 | tf_op jit(solution)/shard_map/ppermute | solution.py:11
  367.7 21.7 %collective-permute-start.31 = (f32[2,2048]{1,0:T(2,128)S(1)}, f32[2,2048]{1,0:T(2,128)S(1)}, u32[]{:S(2)}, u32[]{:S(2)}) collective-permute-start(f32[2,2048]{1,0:T(2,128)S(1)} %add_add_fusion.1), channel_id=1, source_target_pairs={{0,12},{1,13},{2,14},{3,15},{4,8},{5,9},{6,10},{7,11},{8,4},{9,5},... | collective-permute-start | bytes 49160 | tf_op jit(solution)/shard_map/ppermute | solution.py:11
  370.4 19.6 %collective-permute-start.24 = (f32[8,128,128]{2,1,0:T(8,128)S(1)}, f32[8,128,128]{2,1,0:T(8,128)S(1)}, u32[]{:S(2)}, u32[]{:S(2)}) collective-permute-start(f32[8,128,128]{2,1,0:T(8,128)S(1)} %fusion.14), channel_id=1, source_target_pairs={{0,16},{16,0},{1,17},{17,1},{2,18},{18,2},{3,19},{19,3},{4,20},{20... | collective-permute-start | bytes 1572872 | tf_op jit(solution)/shard_map/ppermute | solution.py:11
  (13 other events, 176.4 us)

commit v9 on v8

--- a/solution.py
+++ b/solution.py
@@ -102,17 +102,17 @@
     back_pair = jnp.stack([back_far[0], back_far[half]])
     upward, arrived, back_pair = lax.optimization_barrier((upward, arrived, back_pair))
     grad_left = jnp.einsum("ibd,jbd->bij", upward, arrived, preferred_element_type=f32)
-    grad_left, mixed_parts = lax.optimization_barrier((grad_left, mixed_parts))
     grad_left = sum_over(grad_left, "dp", 0, dp_levels)
     grad_left = jnp.einsum("ki,aij->akj", swap_full, grad_left, precision=lax.Precision.HIGHEST)
     grad_left = jnp.einsum("aij,jl->ail", grad_left, swap_full, precision=lax.Precision.HIGHEST)
+    grad_left, mixed_parts = lax.optimization_barrier((grad_left, mixed_parts))
     back_far[0], back_far[half] = back_pair[0], back_pair[1]
     mixed_near = jnp.zeros((far, near, local, local, width), bf16)
     for k, part in enumerate(mixed_parts):
         mixed_near = lax.dynamic_update_index_in_dim(mixed_near, part, device_near ^ k, 1)
     mixed_sent = list(mixed_near)
-    back_rest, mixed_rest = lax.optimization_barrier(([back_far[k] for k in rest], [mixed_sent[k] for k in rest]))
-    for k, back_part, mixed_part in zip(rest, back_rest, mixed_rest):
+    back_rest, mixed_rest = lax.optimization_barrier(([back_far[k] for k in rest[::-1]], [mixed_sent[k] for k in rest[::-1]]))
+    for k, back_part, mixed_part in zip(rest[::-1], back_rest, mixed_rest):
         back_far[k], mixed_sent[k] = back_part, mixed_part
     mixed_far = [from_partner(mixed_sent[k], "seq", k << low) for k in range(far)]
     back_near = [from_partner(jnp.stack([t[k] for t in back_far]), "seq", k) for k in range(near)]

time: 404 us -> 406 us (level)
  waiting for transfers between devices: 216 us -> 245 us
  starting transfers between devices: 80.7 us -> 66.4 us
  other arithmetic: 39.6 us -> 27.8 us
    ppermute x33, waiting for transfers between devices: 216 us -> 245 us  [from_partner(): return lax.ppermute(block, axis, [(i, i ^ distance) for i in range(count)])]
    ppermute x33, starting transfers between devices: 80.7 us -> 66.4 us  [from_partner(): return lax.ppermute(block, axis, [(i, i ^ distance) for i in range(count)])]
    another operation x1, other arithmetic: 13.8 us -> 2.29 us  [body(): upward = jnp.stack(up_near, axis=1).reshape(order, local, width)]
  transfers between devices with their start and end apart: 33 -> 33, of which waited for: 11 -> 13; matrix products, arithmetic and copies ran while one was open for 21% -> 18% of each run, Pallas kernels for 0% -> 0%
where the time goes in v9:
time: 406 us; the launch traced here: 399 us
  waiting for transfers between devices  245 us (60%)
  starting transfers between devices  66.4 us (16%)
  local copies, waits for them, and re-layouts  36.5 us (9%)
  other arithmetic  27.8 us (7%)
  matrix products  21.4 us (5%)
    ppermute x33, waiting for transfers between devices, from_partner(): return lax.ppermute(block, axis, [(i, i ^ distance) for i in range(count)])  245 us
    ppermute x33, starting transfers between devices, from_partner(): return lax.ppermute(block, axis, [(i, i ^ distance) for i in range(count)])  66.4 us
    dot_general x1, matrix products, body(): first = jnp.einsum('aij,ajd->aid', rights, grid, preferred_element_type=f32)  8.98 us
  transfers between devices with their start and end apart: 33, of which 13 were waited for; matrix products, arithmetic and copies ran while one was open for 18% of the time, Pallas kernels for 0%

profile of v9, /device:TPU:0, one launch (start us, length us, event | category | flops | bytes accessed | tf_op | source)
XLA Modules:
  0.0 399.1 jit_solution(2983342335829161823)
XLA Ops:
  0.7 2.4 dynamic-slice_bitcast_fusion.3
  3.0 4.0 %collective-permute-start = (bf16[8,4,8,2048]{3,2,1,0:T(8,128)(2,1)}, bf16[8,4,8,2048]{3,2,1,0:T(8,128)(2,1)}, u32[]{:S(2)}, u32[]{:S(2)}) collective-permute-start(bf16[8,4,8,2048]{3,2,1,0:T(8,128)(2,1)} %dynamic-slice_bitcast_fusion.3), channel_id=1, source_target_pairs={{0,8},{1,9},{2,10},{3,11},{4,12},{5,13},{6,14},{7,15},{8,0},{9,1},... | collective-permute-start | bytes 3145736 | tf_op jit(solution)/shard_map/ppermute | solution.py:11
  7.1 3.7 dynamic-slice_bitcast_fusion
  12.0 9.0 %multiply_convert_fusion = (bf16[8,128,2048]{2,1,0:T(8,128)(2,1)S(1)}, f32[8,128,2048]{2,1,0:T(8,128)}) fusion(f32[2048]{0:T(1024)S(1)} %copy-done.9, bf16[8,128,128]{1,2,0:T(8,128)(2,1)S(1)} %convolution_bitcast_fusion.3, f32[2048]{0:T(1024)S(1)} %copy-done.8, f32[8,128]{1,0:T(8,128)S(1)} %get-tuple-element.194, bf16[8,128,2048]{2,1,0:T(8,128)(2,1)} %bitcast.316), kind=kOutput, calls=%fused_computation.17 | convolution fusion | flops 557842432 | bytes 17059840 | tf_op jit(solution)/shard_map/aij,ajd->aid/dot_general | solution.py:65
  30.4 22.7 %collective-permute-done = bf16[8,4,8,2048]{3,2,1,0:T(8,128)(2,1)} collective-permute-done((bf16[8,4,8,2048]{3,2,1,0:T(8,128)(2,1)}, bf16[8,4,8,2048]{3,2,1,0:T(8,128)(2,1)}, u32[]{:S(2)}, u32[]{:S(2)}) %collective-permute-start) | collective-permute-done | bytes 1048608 | tf_op jit(solution)/shard_map/ppermute | solution.py:11
  53.1 3.5 collective-permute-start.6
  58.6 14.4 %collective-permute-done.2 = bf16[8,4,8,2048]{3,2,0,1:T(8,128)(2,1)} collective-permute-done((bf16[8,4,8,2048]{3,2,0,1:T(8,128)(2,1)}, bf16[8,4,8,2048]{3,2,0,1:T(8,128)(2,1)}, u32[]{:S(2)}, u32[]{:S(2)}) %collective-permute-start.2) | collective-permute-done | bytes 1048608 | tf_op jit(solution)/shard_map/ppermute | solution.py:11
  73.8 2.0 slice_bitcast_fusion.28
  80.9 14.9 %collective-permute-done.5 = bf16[8,4,8,2048]{3,2,1,0:T(8,128)(2,1)} collective-permute-done((bf16[8,4,8,2048]{3,2,1,0:T(8,128)(2,1)}, bf16[8,4,8,2048]{3,2,1,0:T(8,128)(2,1)}, u32[]{:S(2)}, u32[]{:S(2)}) %collective-permute-start.5) | collective-permute-done | bytes 1048608 | tf_op jit(solution)/shard_map/ppermute | solution.py:11
  95.8 2.2 dynamic-slice_bitcast_fusion.4
  98.1 2.6 collective-permute-start.9
  101.8 5.4 %collective-permute-start.4 = (bf16[4,8,8,2048]{3,2,1,0:T(8,128)(2,1)}, bf16[4,8,8,2048]{3,2,1,0:T(8,128)(2,1)}, u32[]{:S(2)}, u32[]{:S(2)}) collective-permute-start(bf16[4,8,8,2048]{3,2,1,0:T(8,128)(2,1)} %pad_maximum_fusion.5), channel_id=1, source_target_pairs={{0,8},{1,9},{2,10},{3,11},{4,12},{5,13},{6,14},{7,15},{8,0},{9,1},... | collective-permute-start | bytes 3145736 | tf_op jit(solution)/shard_map/ppermute | solution.py:11
  114.8 37.8 %collective-permute-done.4 = bf16[4,8,8,2048]{3,2,1,0:T(8,128)(2,1)} collective-permute-done((bf16[4,8,8,2048]{3,2,1,0:T(8,128)(2,1)}, bf16[4,8,8,2048]{3,2,1,0:T(8,128)(2,1)}, u32[]{:S(2)}, u32[]{:S(2)}) %collective-permute-start.4) | collective-permute-done | bytes 1048608 | tf_op jit(solution)/shard_map/ppermute | solution.py:11
  152.6 2.8 collective-permute-start.11
  156.9 2.3 pad_maximum_fusion
  159.2 2.3 copy.91
  163.4 14.8 %collective-permute-done.10 = bf16[4,8,8,2048]{3,2,1,0:T(8,128)(2,1)S(1)} collective-permute-done((bf16[4,8,8,2048]{3,2,1,0:T(8,128)(2,1)S(1)}, bf16[4,8,8,2048]{3,2,1,0:T(8,128)(2,1)S(1)}, u32[]{:S(2)}, u32[]{:S(2)}) %collective-permute-start.10) | collective-permute-done | bytes 1048608 | tf_op jit(solution)/shard_map/ppermute | solution.py:11
  179.0 20.7 %collective-permute-start.12 = (bf16[4,8,8,2048]{3,2,1,0:T(8,128)(2,1)S(1)}, bf16[4,8,8,2048]{3,2,1,0:T(8,128)(2,1)S(1)}, u32[]{:S(2)}, u32[]{:S(2)}) collective-permute-start(bf16[4,8,8,2048]{3,2,1,0:T(8,128)(2,1)S(1)} %copy.94), channel_id=1, source_target_pairs={{0,8},{1,9},{2,10},{3,11},{4,12},{5,13},{6,14},{7,15},{8,0},{9,1},... | collective-permute-start | bytes 3145736 | tf_op jit(solution)/shard_map/ppermute | solution.py:11
  200.5 2.3 copy.93
  205.6 2.4 collective-permute-start.16
  208.7 35.1 %collective-permute-done.12 = bf16[4,8,8,2048]{3,2,1,0:T(8,128)(2,1)S(1)} collective-permute-done((bf16[4,8,8,2048]{3,2,1,0:T(8,128)(2,1)S(1)}, bf16[4,8,8,2048]{3,2,1,0:T(8,128)(2,1)S(1)}, u32[]{:S(2)}, u32[]{:S(2)}) %collective-permute-start.12) | collective-permute-done | bytes 1048608 | tf_op jit(solution)/shard_map/ppermute | solution.py:11
  253.9 19.8 %collective-permute-done.18 = bf16[4,8,8,2048]{3,2,0,1:T(8,128)(2,1)S(1)} collective-permute-done((bf16[4,8,8,2048]{3,2,0,1:T(8,128)(2,1)S(1)}, bf16[4,8,8,2048]{3,2,0,1:T(8,128)(2,1)S(1)}, u32[]{:S(2)}, u32[]{:S(2)}) %collective-permute-start.18) | collective-permute-done | bytes 1048608 | tf_op jit(solution)/shard_map/ppermute | solution.py:11
  273.8 21.7 %collective-permute-done.19 = bf16[4,8,8,2048]{3,2,1,0:T(8,128)(2,1)S(1)} collective-permute-done((bf16[4,8,8,2048]{3,2,1,0:T(8,128)(2,1)S(1)}, bf16[4,8,8,2048]{3,2,1,0:T(8,128)(2,1)S(1)}, u32[]{:S(2)}, u32[]{:S(2)}) %collective-permute-start.19) | collective-permute-done | bytes 1048608 | tf_op jit(solution)/shard_map/ppermute | solution.py:11
  302.7 40.7 %collective-permute-done.17 = bf16[4,8,8,2048]{3,2,0,1:T(8,128)(2,1)S(1)} collective-permute-done((bf16[4,8,8,2048]{3,2,0,1:T(8,128)(2,1)S(1)}, bf16[4,8,8,2048]{3,2,0,1:T(8,128)(2,1)S(1)}, u32[]{:S(2)}, u32[]{:S(2)}) %collective-permute-start.17) | collective-permute-done | bytes 1048608 | tf_op jit(solution)/shard_map/ppermute | solution.py:11
  343.4 2.6 collective-permute-start.24
  346.5 4.8 %fusion.1 = (f32[2048]{0:T(1024)S(1)}, bf16[8,128,2048]{2,1,0:T(8,128)(2,1)S(1)}) fusion(f32[8,128,2048]{2,1,0:T(8,128)S(1)} %bitcast.331, f32[2048]{0:T(1024)S(1)} %copy-done.9, bf16[4,1,8,8,2048]{4,3,1,0,2:T(8,128)(2,1)S(1)} %bitcast.338, bf16[4,1,8,8,2048]{4,3,1,0,2:T(8,128)(2,1)S(1)} %bitcast.339, bf16[4,8,8,2048]{3,2,1,0:T(8,128)(2,1)S(1)} %pad_maximum_fusion.12, ...), kind=kLoop, calls=%fused_computation.3 | loop fusion | flops 46135296 | bytes 16793600 | tf_op jit(solution)/shard_map/reduce_sum | solution.py:135
  351.3 2.9 multiply_reduce_fusion
  359.1 4.5 %fusion.2 = bf16[1024,2048]{1,0:T(8,128)(2,1)} fusion(f32[8,128,2048]{2,1,0:T(8,128)S(1)} %get-tuple-element.197, bf16[1,1024,2048]{2,1,0:T(8,128)(2,1)S(1)} %copy-done.4, bf16[1,1024,2048]{2,1,0:T(8,128)(2,1)S(1)} %copy-done.3, f32[1024]{0:T(1024)S(1)} %multiply_bitcast_fusion, f32[2048]{0:T(1024)S(1)} %copy-done.8, f32[1024]{0:T(1024)S(1)} %get-tuple-element.193), kind=kLoop, calls=%fused_computation.5 | loop fusion | flops 18874368 | bytes 20987904 | tf_op jit(solution)/shard_map/convert_element_type | solution.py:149
  365.5 2.6 collective-permute-start.32
  370.0 21.1 %collective-permute-done.31 = f32[2,2048]{1,0:T(2,128)S(1)} collective-permute-done((f32[2,2048]{1,0:T(2,128)S(1)}, f32[2,2048]{1,0:T(2,128)S(1)}, u32[]{:S(2)}, u32[]{:S(2)}) %collective-permute-start.31) | collective-permute-done | bytes 16416 | tf_op jit(solution)/shard_map/ppermute | solution.py:11
  393.5 2.6 fusion.21
  396.0 2.6 fusion.23
  (136 shorter events, 64.2 us)
Async XLA Ops:
  3.0 50.1 %collective-permute-start = (bf16[8,4,8,2048]{3,2,1,0:T(8,128)(2,1)}, bf16[8,4,8,2048]{3,2,1,0:T(8,128)(2,1)}, u32[]{:S(2)}, u32[]{:S(2)}) collective-permute-start(bf16[8,4,8,2048]{3,2,1,0:T(8,128)(2,1)} %dynamic-slice_bitcast_fusion.3), channel_id=1, source_target_pairs={{0,8},{1,9},{2,10},{3,11},{4,12},{5,13},{6,14},{7,15},{8,0},{9,1},... | collective-permute-start | bytes 3145736 | tf_op jit(solution)/shard_map/ppermute | solution.py:11
  23.3 35.3 %collective-permute-start.1 = (bf16[8,4,8,2048]{3,2,0,1:T(8,128)(2,1)}, bf16[8,4,8,2048]{3,2,0,1:T(8,128)(2,1)}, u32[]{:S(2)}, u32[]{:S(2)}) collective-permute-start(bf16[8,4,8,2048]{3,2,0,1:T(8,128)(2,1)} %bitcast.314), channel_id=1, source_target_pairs={{0,1},{1,0},{2,3},{3,2},{4,5},{5,4},{6,7},{7,6},{8,9},{9,8},{10,11... | collective-permute-start | bytes 3145736 | tf_op jit(solution)/shard_map/ppermute | solution.py:11
  25.9 47.1 %collective-permute-start.2 = (bf16[8,4,8,2048]{3,2,0,1:T(8,128)(2,1)}, bf16[8,4,8,2048]{3,2,0,1:T(8,128)(2,1)}, u32[]{:S(2)}, u32[]{:S(2)}) collective-permute-start(bf16[8,4,8,2048]{3,2,0,1:T(8,128)(2,1)} %bitcast.313), channel_id=1, source_target_pairs={{0,2},{1,3},{2,0},{3,1},{4,6},{5,7},{6,4},{7,5},{8,10},{9,11},{10,... | collective-permute-start | bytes 3145736 | tf_op jit(solution)/shard_map/ppermute | solution.py:11
  27.4 45.6 %collective-permute-start.3 = (bf16[8,4,8,2048]{3,2,1,0:T(8,128)(2,1)}, bf16[8,4,8,2048]{3,2,1,0:T(8,128)(2,1)}, u32[]{:S(2)}, u32[]{:S(2)}) collective-permute-start(bf16[8,4,8,2048]{3,2,1,0:T(8,128)(2,1)} %get-tuple-element.138), channel_id=1, source_target_pairs={{0,3},{1,2},{2,1},{3,0},{4,7},{5,6},{6,5},{7,4},{8,11},{9,10},{10,... | collective-permute-start | bytes 3145736 | tf_op jit(solution)/shard_map/ppermute | solution.py:11
  27.9 67.9 %collective-permute-start.5 = (bf16[8,4,8,2048]{3,2,1,0:T(8,128)(2,1)}, bf16[8,4,8,2048]{3,2,1,0:T(8,128)(2,1)}, u32[]{:S(2)}, u32[]{:S(2)}) collective-permute-start(bf16[8,4,8,2048]{3,2,1,0:T(8,128)(2,1)} %get-tuple-element.136), channel_id=1, source_target_pairs={{0,4},{1,5},{2,6},{3,7},{4,0},{5,1},{6,2},{7,3},{8,12},{9,13},{10,... | collective-permute-start | bytes 3145736 | tf_op jit(solution)/shard_map/ppermute | solution.py:11
  53.1 42.7 %collective-permute-start.6 = (bf16[8,4,8,2048]{3,2,1,0:T(8,128)(2,1)}, bf16[8,4,8,2048]{3,2,1,0:T(8,128)(2,1)S(1)}, u32[]{:S(2)}, u32[]{:S(2)}) collective-permute-start(bf16[8,4,8,2048]{3,2,1,0:T(8,128)(2,1)} %get-tuple-element.135), channel_id=1, source_target_pairs={{0,12},{1,13},{2,14},{3,15},{4,8},{5,9},{6,10},{7,11},{8,4},{9,5},... | collective-permute-start | bytes 3145736 | tf_op jit(solution)/shard_map/ppermute | solution.py:11
  98.1 58.7 %collective-permute-start.9 = (bf16[4,8,8,2048]{3,2,1,0:T(8,128)(2,1)S(1)}, bf16[4,8,8,2048]{3,2,1,0:T(8,128)(2,1)}, u32[]{:S(2)}, u32[]{:S(2)}) collective-permute-start(bf16[4,8,8,2048]{3,2,1,0:T(8,128)(2,1)S(1)} %pad_maximum_fusion.11), channel_id=1, source_target_pairs={{0,3},{1,2},{2,1},{3,0},{4,7},{5,6},{6,5},{7,4},{8,11},{9,10},{10,... | collective-permute-start | bytes 3145736 | tf_op jit(solution)/shard_map/ppermute | solution.py:11
  101.8 50.8 %collective-permute-start.4 = (bf16[4,8,8,2048]{3,2,1,0:T(8,128)(2,1)}, bf16[4,8,8,2048]{3,2,1,0:T(8,128)(2,1)}, u32[]{:S(2)}, u32[]{:S(2)}) collective-permute-start(bf16[4,8,8,2048]{3,2,1,0:T(8,128)(2,1)} %pad_maximum_fusion.5), channel_id=1, source_target_pairs={{0,8},{1,9},{2,10},{3,11},{4,12},{5,13},{6,14},{7,15},{8,0},{9,1},... | collective-permute-start | bytes 3145736 | tf_op jit(solution)/shard_map/ppermute | solution.py:11
  108.3 48.6 %collective-permute-start.8 = (bf16[4,8,8,2048]{3,2,1,0:T(8,128)(2,1)}, bf16[4,8,8,2048]{3,2,1,0:T(8,128)(2,1)}, u32[]{:S(2)}, u32[]{:S(2)}) collective-permute-start(bf16[4,8,8,2048]{3,2,1,0:T(8,128)(2,1)} %pad_maximum_fusion.10), channel_id=1, source_target_pairs={{0,2},{1,3},{2,0},{3,1},{4,6},{5,7},{6,4},{7,5},{8,10},{9,11},{10,... | collective-permute-start | bytes 3145736 | tf_op jit(solution)/shard_map/ppermute | solution.py:11
  109.9 47.0 %collective-permute-start.7 = (bf16[4,8,8,2048]{3,2,1,0:T(8,128)(2,1)}, bf16[4,8,8,2048]{3,2,1,0:T(8,128)(2,1)}, u32[]{:S(2)}, u32[]{:S(2)}) collective-permute-start(bf16[4,8,8,2048]{3,2,1,0:T(8,128)(2,1)} %pad_maximum_fusion.9), channel_id=1, source_target_pairs={{0,1},{1,0},{2,3},{3,2},{4,5},{5,4},{6,7},{7,6},{8,9},{9,8},{10,11... | collective-permute-start | bytes 3145736 | tf_op jit(solution)/shard_map/ppermute | solution.py:11
  111.8 66.3 %collective-permute-start.10 = (bf16[4,8,8,2048]{3,2,1,0:T(8,128)(2,1)S(1)}, bf16[4,8,8,2048]{3,2,1,0:T(8,128)(2,1)S(1)}, u32[]{:S(2)}, u32[]{:S(2)}) collective-permute-start(bf16[4,8,8,2048]{3,2,1,0:T(8,128)(2,1)S(1)} %pad_maximum_fusion.6), channel_id=1, source_target_pairs={{0,4},{1,5},{2,6},{3,7},{4,0},{5,1},{6,2},{7,3},{8,12},{9,13},{10,... | collective-permute-start | bytes 3145736 | tf_op jit(solution)/shard_map/ppermute | solution.py:11
  152.6 25.5 %collective-permute-start.11 = (bf16[4,8,8,2048]{3,2,1,0:T(8,128)(2,1)S(1)}, bf16[4,8,8,2048]{3,2,1,0:T(8,128)(2,1)S(1)}, u32[]{:S(2)}, u32[]{:S(2)}) collective-permute-start(bf16[4,8,8,2048]{3,2,1,0:T(8,128)(2,1)S(1)} %pad_maximum_fusion.7), channel_id=1, source_target_pairs={{0,12},{1,13},{2,14},{3,15},{4,8},{5,9},{6,10},{7,11},{8,4},{9,5},... | collective-permute-start | bytes 3145736 | tf_op jit(solution)/shard_map/ppermute | solution.py:11
  179.0 64.8 %collective-permute-start.12 = (bf16[4,8,8,2048]{3,2,1,0:T(8,128)(2,1)S(1)}, bf16[4,8,8,2048]{3,2,1,0:T(8,128)(2,1)S(1)}, u32[]{:S(2)}, u32[]{:S(2)}) collective-permute-start(bf16[4,8,8,2048]{3,2,1,0:T(8,128)(2,1)S(1)} %copy.94), channel_id=1, source_target_pairs={{0,8},{1,9},{2,10},{3,11},{4,12},{5,13},{6,14},{7,15},{8,0},{9,1},... | collective-permute-start | bytes 3145736 | tf_op jit(solution)/shard_map/ppermute | solution.py:11
  204.5 45.3 %collective-permute-start.14 = (bf16[4,8,8,2048]{3,1,0,2:T(8,128)(2,1)S(1)}, bf16[4,8,8,2048]{3,1,0,2:T(8,128)(2,1)S(1)}, u32[]{:S(2)}, u32[]{:S(2)}) collective-permute-start(bf16[4,8,8,2048]{3,1,0,2:T(8,128)(2,1)S(1)} %get-tuple-element.129), channel_id=1, source_target_pairs={{0,1},{1,0},{2,3},{3,2},{4,5},{5,4},{6,7},{7,6},{8,9},{9,8},{10,11... | collective-permute-start | bytes 3145736 | tf_op jit(solution)/shard_map/ppermute | solution.py:11
  205.1 45.2 %collective-permute-start.15 = (bf16[4,8,8,2048]{3,1,0,2:T(8,128)(2,1)S(1)}, bf16[4,8,8,2048]{3,1,0,2:T(8,128)(2,1)S(1)}, u32[]{:S(2)}, u32[]{:S(2)}) collective-permute-start(bf16[4,8,8,2048]{3,1,0,2:T(8,128)(2,1)S(1)} %get-tuple-element.128), channel_id=1, source_target_pairs={{0,2},{1,3},{2,0},{3,1},{4,6},{5,7},{6,4},{7,5},{8,10},{9,11},{10,... | collective-permute-start | bytes 3145736 | tf_op jit(solution)/shard_map/ppermute | solution.py:11
  205.6 44.7 %collective-permute-start.16 = (bf16[4,8,8,2048]{3,1,0,2:T(8,128)(2,1)S(1)}, bf16[4,8,8,2048]{3,1,0,2:T(8,128)(2,1)S(1)}, u32[]{:S(2)}, u32[]{:S(2)}) collective-permute-start(bf16[4,8,8,2048]{3,1,0,2:T(8,128)(2,1)S(1)} %get-tuple-element.127), channel_id=1, source_target_pairs={{0,3},{1,2},{2,1},{3,0},{4,7},{5,6},{6,5},{7,4},{8,11},{9,10},{10,... | collective-permute-start | bytes 3145736 | tf_op jit(solution)/shard_map/ppermute | solution.py:11
  245.2 2.4 collective-permute-start.13
  245.9 27.9 %collective-permute-start.18 = (bf16[4,8,8,2048]{3,2,0,1:T(8,128)(2,1)S(1)}, bf16[4,8,8,2048]{3,2,0,1:T(8,128)(2,1)S(1)}, u32[]{:S(2)}, u32[]{:S(2)}) collective-permute-start(bf16[4,8,8,2048]{3,2,0,1:T(8,128)(2,1)S(1)} %copy.105), channel_id=1, source_target_pairs={{0,12},{1,13},{2,14},{3,15},{4,8},{5,9},{6,10},{7,11},{8,4},{9,5},... | collective-permute-start | bytes 3145736 | tf_op jit(solution)/shard_map/ppermute | solution.py:11
  247.7 47.8 %collective-permute-start.19 = (bf16[4,8,8,2048]{3,2,1,0:T(8,128)(2,1)S(1)}, bf16[4,8,8,2048]{3,2,1,0:T(8,128)(2,1)S(1)}, u32[]{:S(2)}, u32[]{:S(2)}) collective-permute-start(bf16[4,8,8,2048]{3,2,1,0:T(8,128)(2,1)S(1)} %copy.106), channel_id=1, source_target_pairs={{0,4},{1,5},{2,6},{3,7},{4,0},{5,1},{6,2},{7,3},{8,12},{9,13},{10,... | collective-permute-start | bytes 3145736 | tf_op jit(solution)/shard_map/ppermute | solution.py:11
  295.8 50.6 %collective-permute-start.22 = (bf16[4,8,8,2048]{3,2,0,1:T(8,128)(2,1)S(1)}, bf16[4,8,8,2048]{3,2,0,1:T(8,128)(2,1)S(1)}, u32[]{:S(2)}, u32[]{:S(2)}) collective-permute-start(bf16[4,8,8,2048]{3,2,0,1:T(8,128)(2,1)S(1)} %pad_maximum_fusion.15), channel_id=1, source_target_pairs={{0,3},{1,2},{2,1},{3,0},{4,7},{5,6},{6,5},{7,4},{8,11},{9,10},{10,... | collective-permute-start | bytes 3145736 | tf_op jit(solution)/shard_map/ppermute | solution.py:11
  296.4 47.0 %collective-permute-start.17 = (bf16[4,8,8,2048]{3,2,0,1:T(8,128)(2,1)S(1)}, bf16[4,8,8,2048]{3,2,0,1:T(8,128)(2,1)S(1)}, u32[]{:S(2)}, u32[]{:S(2)}) collective-permute-start(bf16[4,8,8,2048]{3,2,0,1:T(8,128)(2,1)S(1)} %get-tuple-element.126), channel_id=1, source_target_pairs={{0,8},{1,9},{2,10},{3,11},{4,12},{5,13},{6,14},{7,15},{8,0},{9,1},... | collective-permute-start | bytes 3145736 | tf_op jit(solution)/shard_map/ppermute | solution.py:11
  297.4 49.0 %collective-permute-start.21 = (bf16[4,8,8,2048]{3,2,0,1:T(8,128)(2,1)S(1)}, bf16[4,8,8,2048]{3,2,0,1:T(8,128)(2,1)S(1)}, u32[]{:S(2)}, u32[]{:S(2)}) collective-permute-start(bf16[4,8,8,2048]{3,2,0,1:T(8,128)(2,1)S(1)} %pad_maximum_fusion.14), channel_id=1, source_target_pairs={{0,2},{1,3},{2,0},{3,1},{4,6},{5,7},{6,4},{7,5},{8,10},{9,11},{10,... | collective-permute-start | bytes 3145736 | tf_op jit(solution)/shard_map/ppermute | solution.py:11
  299.1 47.3 %collective-permute-start.20 = (bf16[4,8,8,2048]{3,2,1,0:T(8,128)(2,1)S(1)}, bf16[4,8,8,2048]{3,2,1,0:T(8,128)(2,1)S(1)}, u32[]{:S(2)}, u32[]{:S(2)}) collective-permute-start(bf16[4,8,8,2048]{3,2,1,0:T(8,128)(2,1)S(1)} %pad_maximum_fusion.13), channel_id=1, source_target_pairs={{0,1},{1,0},{2,3},{3,2},{4,5},{5,4},{6,7},{7,6},{8,9},{9,8},{10,11... | collective-permute-start | bytes 3145736 | tf_op jit(solution)/shard_map/ppermute | solution.py:11
  300.7 91.8 %collective-permute-start.23 = (bf16[4,8,8,2048]{3,2,0,1:T(8,128)(2,1)S(1)}, bf16[4,8,8,2048]{3,2,0,1:T(8,128)(2,1)S(1)}, u32[]{:S(2)}, u32[]{:S(2)}) collective-permute-start(bf16[4,8,8,2048]{3,2,0,1:T(8,128)(2,1)S(1)} %get-tuple-element.89), channel_id=1, source_target_pairs={{0,4},{1,5},{2,6},{3,7},{4,0},{5,1},{6,2},{7,3},{8,12},{9,13},{10,... | collective-permute-start | bytes 3145736 | tf_op jit(solution)/shard_map/ppermute | solution.py:11
  343.4 49.1 %collective-permute-start.24 = (bf16[4,8,8,2048]{3,2,0,1:T(8,128)(2,1)S(1)}, bf16[4,8,8,2048]{3,2,0,1:T(8,128)(2,1)S(1)}, u32[]{:S(2)}, u32[]{:S(2)}) collective-permute-start(bf16[4,8,8,2048]{3,2,0,1:T(8,128)(2,1)S(1)} %get-tuple-element.90), channel_id=1, source_target_pairs={{0,12},{1,13},{2,14},{3,15},{4,8},{5,9},{6,10},{7,11},{8,4},{9,5},... | collective-permute-start | bytes 3145736 | tf_op jit(solution)/shard_map/ppermute | solution.py:11
  355.5 8.1 %collective-permute-start.27 = (f32[2,2048]{1,0:T(2,128)S(1)}, f32[2,2048]{1,0:T(2,128)S(1)}, u32[]{:S(2)}, u32[]{:S(2)}) collective-permute-start(f32[2,2048]{1,0:T(2,128)S(1)} %fusion.41), channel_id=1, source_target_pairs={{0,1},{1,0},{2,3},{3,2},{4,5},{5,4},{6,7},{7,6},{8,9},{9,8},{10,11... | collective-permute-start | bytes 49160 | tf_op jit(solution)/shard_map/ppermute | solution.py:11
  357.1 6.5 %collective-permute-start.28 = (f32[2,2048]{1,0:T(2,128)S(1)}, f32[2,2048]{1,0:T(2,128)S(1)}, u32[]{:S(2)}, u32[]{:S(2)}) collective-permute-start(f32[2,2048]{1,0:T(2,128)S(1)} %fusion.41), channel_id=1, source_target_pairs={{0,2},{1,3},{2,0},{3,1},{4,6},{5,7},{6,4},{7,5},{8,10},{9,11},{10,... | collective-permute-start | bytes 49160 | tf_op jit(solution)/shard_map/ppermute | solution.py:11
  358.6 5.0 %collective-permute-start.29 = (f32[2,2048]{1,0:T(2,128)S(1)}, f32[2,2048]{1,0:T(2,128)S(1)}, u32[]{:S(2)}, u32[]{:S(2)}) collective-permute-start(f32[2,2048]{1,0:T(2,128)S(1)} %fusion.41), channel_id=1, source_target_pairs={{0,3},{1,2},{2,1},{3,0},{4,7},{5,6},{6,5},{7,4},{8,11},{9,10},{10,... | collective-permute-start | bytes 49160 | tf_op jit(solution)/shard_map/ppermute | solution.py:11
  363.6 6.4 %collective-permute-start.30 = (f32[2,2048]{1,0:T(2,128)S(1)}, f32[2,2048]{1,0:T(2,128)S(1)}, u32[]{:S(2)}, u32[]{:S(2)}) collective-permute-start(f32[2,2048]{1,0:T(2,128)S(1)} %add_add_fusion.1), channel_id=1, source_target_pairs={{0,4},{1,5},{2,6},{3,7},{4,0},{5,1},{6,2},{7,3},{8,12},{9,13},{10,... | collective-permute-start | bytes 49160 | tf_op jit(solution)/shard_map/ppermute | solution.py:11
  363.7 27.4 %collective-permute-start.31 = (f32[2,2048]{1,0:T(2,128)S(1)}, f32[2,2048]{1,0:T(2,128)S(1)}, u32[]{:S(2)}, u32[]{:S(2)}) collective-permute-start(f32[2,2048]{1,0:T(2,128)S(1)} %add_add_fusion.1), channel_id=1, source_target_pairs={{0,8},{1,9},{2,10},{3,11},{4,12},{5,13},{6,14},{7,15},{8,0},{9,1},... | collective-permute-start | bytes 49160 | tf_op jit(solution)/shard_map/ppermute | solution.py:11
  365.5 25.7 %collective-permute-start.32 = (f32[2,2048]{1,0:T(2,128)S(1)}, f32[2,2048]{1,0:T(2,128)S(1)}, u32[]{:S(2)}, u32[]{:S(2)}) collective-permute-start(f32[2,2048]{1,0:T(2,128)S(1)} %add_add_fusion.1), channel_id=1, source_target_pairs={{0,12},{1,13},{2,14},{3,15},{4,8},{5,9},{6,10},{7,11},{8,4},{9,5},... | collective-permute-start | bytes 49160 | tf_op jit(solution)/shard_map/ppermute | solution.py:11
  370.0 21.8 %collective-permute-start.25 = (f32[8,128,128]{2,1,0:T(8,128)S(1)}, f32[8,128,128]{2,1,0:T(8,128)S(1)}, u32[]{:S(2)}, u32[]{:S(2)}) collective-permute-start(f32[8,128,128]{2,1,0:T(8,128)S(1)} %fusion.14), channel_id=1, source_target_pairs={{0,16},{16,0},{1,17},{17,1},{2,18},{18,2},{3,19},{19,3},{4,20},{20... | collective-permute-start | bytes 1572872 | tf_op jit(solution)/shard_map/ppermute | solution.py:11
  (13 other events, 161.5 us)

commit v10 on v6

--- a/solution.py
+++ b/solution.py
@@ -49,7 +49,12 @@
     rest = [k for k in range(1, far) if k != half]
 
     up_view = upstream[0].reshape(local, far, near, local, width)
-    up_parts = [lax.dynamic_index_in_dim(up_view, device_far ^ k, 1, keepdims=False) for k in range(far)]
+    up_first = lax.dynamic_index_in_dim(up_view, device_far ^ half, 1, keepdims=False)
+    up_view, up_first = lax.optimization_barrier((up_view, up_first))
+    up_parts = [
+        up_first if k == half else lax.dynamic_index_in_dim(up_view, device_far ^ k, 1, keepdims=False)
+        for k in range(far)
+    ]
     up_far = [from_partner(up_parts[k], "seq", k << low) for k in range(far)]
     inputs, up_far[0] = lax.optimization_barrier((inputs, up_far[0]))
     input_float = inputs[0].astype(f32)
@@ -70,9 +75,9 @@
     up_half = sent_near(up_far[half])
     up_half, gated_near = lax.optimization_barrier((up_half, gated_near))
     gated_sent = [jnp.stack([t[:, k] for t in gated_near]) for k in range(far)]
-    up_rest, gated_rest = lax.optimization_barrier(([up_far[k] for k in rest], [gated_sent[k] for k in rest]))
-    for k, up_part, gated_part in zip(rest, up_rest, gated_rest):
-        up_far[k], gated_sent[k] = up_part, gated_part
+    up_rest, gated_sent = lax.optimization_barrier(([up_far[k] for k in rest], gated_sent))
+    for k, up_part in zip(rest, up_rest):
+        up_far[k] = up_part
     gated_far = [from_partner(gated_sent[k], "seq", k << low) for k in range(far)]
     up_sent = [up_half if k == half else sent_near(up_far[k]) for k in range(far)]
     up_near = [from_partner(jnp.stack([t[k] for t in up_sent]), "seq", k) for k in range(near)]

time: 400 us -> 398 us (level)
  no operation moved by 1% of the time
where the time goes in v10:
time: 398 us; the launch traced here: 391 us
  waiting for transfers between devices  220 us (55%)
  starting transfers between devices  78.6 us (20%)
  local copies, waits for them, and re-layouts  35.1 us (9%)
  other arithmetic  34.8 us (9%)
  matrix products  21.4 us (5%)
    ppermute x33, waiting for transfers between devices, from_partner(): return lax.ppermute(block, axis, [(i, i ^ distance) for i in range(count)])  220 us
    ppermute x33, starting transfers between devices, from_partner(): return lax.ppermute(block, axis, [(i, i ^ distance) for i in range(count)])  78.6 us
    another operation x1, other arithmetic, body(): upward = jnp.stack(up_near, axis=1).reshape(order, local, width)  13.8 us
    dot_general x1, matrix products, body(): first = jnp.einsum('aij,ajd->aid', rights, grid, preferred_element_type=f32)  8.98 us
  transfers between devices with their start and end apart: 33, of which 11 were waited for; matrix products, arithmetic and copies ran while one was open for 19% of the time, Pallas kernels for 0%

profile of v10, /device:TPU:0, one launch (start us, length us, event | category | flops | bytes accessed | tf_op | source)
XLA Modules:
  0.0 391.2 jit_solution(6715291325019751752)
XLA Ops:
  0.7 2.4 dynamic-slice_bitcast_fusion.3
  3.0 4.0 %collective-permute-start.2 = (bf16[8,4,8,2048]{3,2,1,0:T(8,128)(2,1)}, bf16[8,4,8,2048]{3,2,1,0:T(8,128)(2,1)}, u32[]{:S(2)}, u32[]{:S(2)}) collective-permute-start(bf16[8,4,8,2048]{3,2,1,0:T(8,128)(2,1)} %dynamic-slice_bitcast_fusion.3), channel_id=1, source_target_pairs={{0,8},{1,9},{2,10},{3,11},{4,12},{5,13},{6,14},{7,15},{8,0},{9,1},... | collective-permute-start | bytes 3145736 | tf_op jit(solution)/shard_map/ppermute | solution.py:11
  7.1 3.7 dynamic-slice_bitcast_fusion.2
  12.0 9.0 %multiply_convert_fusion = (bf16[8,128,2048]{2,1,0:T(8,128)(2,1)S(1)}, f32[8,128,2048]{2,1,0:T(8,128)}) fusion(f32[2048]{0:T(1024)S(1)} %copy-done.9, bf16[8,128,128]{1,2,0:T(8,128)(2,1)S(1)} %convolution_bitcast_fusion.3, f32[2048]{0:T(1024)S(1)} %copy-done.8, f32[8,128]{1,0:T(8,128)S(1)} %get-tuple-element.196, bf16[8,128,2048]{2,1,0:T(8,128)(2,1)} %bitcast.315), kind=kOutput, calls=%fused_computation.17 | convolution fusion | flops 557842432 | bytes 17059840 | tf_op jit(solution)/shard_map/aij,ajd->aid/dot_general | solution.py:65
  30.4 22.7 %collective-permute-done.2 = bf16[8,4,8,2048]{3,2,1,0:T(8,128)(2,1)} collective-permute-done((bf16[8,4,8,2048]{3,2,1,0:T(8,128)(2,1)}, bf16[8,4,8,2048]{3,2,1,0:T(8,128)(2,1)}, u32[]{:S(2)}, u32[]{:S(2)}) %collective-permute-start.2) | collective-permute-done | bytes 1048608 | tf_op jit(solution)/shard_map/ppermute | solution.py:11
  53.1 3.5 collective-permute-start.1
  56.6 2.0 dynamic-slice_bitcast_fusion.16
  58.6 14.4 %collective-permute-done.4 = bf16[8,4,8,2048]{3,2,0,1:T(8,128)(2,1)} collective-permute-done((bf16[8,4,8,2048]{3,2,0,1:T(8,128)(2,1)}, bf16[8,4,8,2048]{3,2,0,1:T(8,128)(2,1)}, u32[]{:S(2)}, u32[]{:S(2)}) %collective-permute-start.4) | collective-permute-done | bytes 1048608 | tf_op jit(solution)/shard_map/ppermute | solution.py:11
  79.3 16.4 %collective-permute-done = bf16[8,4,8,2048]{3,2,1,0:T(8,128)(2,1)} collective-permute-done((bf16[8,4,8,2048]{3,2,1,0:T(8,128)(2,1)}, bf16[8,4,8,2048]{3,2,1,0:T(8,128)(2,1)}, u32[]{:S(2)}, u32[]{:S(2)}) %collective-permute-start) | collective-permute-done | bytes 1048608 | tf_op jit(solution)/shard_map/ppermute | solution.py:11
  95.7 2.2 dynamic-slice_bitcast_fusion.4
  99.0 2.5 collective-permute-start.9
  101.5 5.4 %collective-permute-start.6 = (bf16[4,8,8,2048]{3,2,1,0:T(8,128)(2,1)}, bf16[4,8,8,2048]{3,2,1,0:T(8,128)(2,1)}, u32[]{:S(2)}, u32[]{:S(2)}) collective-permute-start(bf16[4,8,8,2048]{3,2,1,0:T(8,128)(2,1)} %pad_maximum_fusion.7), channel_id=1, source_target_pairs={{0,8},{1,9},{2,10},{3,11},{4,12},{5,13},{6,14},{7,15},{8,0},{9,1},... | collective-permute-start | bytes 3145736 | tf_op jit(solution)/shard_map/ppermute | solution.py:11
  113.3 39.1 %collective-permute-done.6 = bf16[4,8,8,2048]{3,2,1,0:T(8,128)(2,1)} collective-permute-done((bf16[4,8,8,2048]{3,2,1,0:T(8,128)(2,1)}, bf16[4,8,8,2048]{3,2,1,0:T(8,128)(2,1)}, u32[]{:S(2)}, u32[]{:S(2)}) %collective-permute-start.6) | collective-permute-done | bytes 1048608 | tf_op jit(solution)/shard_map/ppermute | solution.py:11
  152.4 2.8 collective-permute-start.12
  156.6 13.8 %pad_maximum_fusion = bf16[4,4,8,8,2048]{4,3,2,0,1:T(8,128)(2,1)S(1)} fusion(bf16[4,1,8,8,2048]{4,3,2,0,1:T(8,128)(2,1)} %bitcast.58, bf16[4,1,8,8,2048]{4,3,2,0,1:T(8,128)(2,1)} %bitcast.57, bf16[4,1,8,8,2048]{4,3,2,0,1:T(8,128)(2,1)} %bitcast.56, bf16[4,1,8,8,2048]{4,3,2,0,1:T(8,128)(2,1)S(1)} %bitcast.337), kind=kLoop, calls=%fused_computation.20 | loop fusion | flops 6291456 | bytes 8388608 | tf_op jit(solution)/shard_map/stack | solution.py:88
  170.5 2.3 copy.91
  174.4 3.5 collective-permute-done.11
  178.6 2.3 copy.95
  183.3 20.7 %collective-permute-start.10 = (bf16[4,8,8,2048]{3,2,1,0:T(8,128)(2,1)S(1)}, bf16[4,8,8,2048]{3,2,1,0:T(8,128)(2,1)S(1)}, u32[]{:S(2)}, u32[]{:S(2)}) collective-permute-start(bf16[4,8,8,2048]{3,2,1,0:T(8,128)(2,1)S(1)} %copy.93), channel_id=1, source_target_pairs={{0,8},{1,9},{2,10},{3,11},{4,12},{5,13},{6,14},{7,15},{8,0},{9,1},... | collective-permute-start | bytes 3145736 | tf_op jit(solution)/shard_map/ppermute | solution.py:11
  206.5 2.4 collective-permute-start.15
  212.8 35.5 %collective-permute-done.10 = bf16[4,8,8,2048]{3,2,1,0:T(8,128)(2,1)S(1)} collective-permute-done((bf16[4,8,8,2048]{3,2,1,0:T(8,128)(2,1)S(1)}, bf16[4,8,8,2048]{3,2,1,0:T(8,128)(2,1)S(1)}, u32[]{:S(2)}, u32[]{:S(2)}) %collective-permute-start.10) | collective-permute-done | bytes 1048608 | tf_op jit(solution)/shard_map/ppermute | solution.py:11
  249.3 4.4 %collective-permute-done.14 = bf16[4,8,8,2048]{3,1,0,2:T(8,128)(2,1)S(1)} collective-permute-done((bf16[4,8,8,2048]{3,1,0,2:T(8,128)(2,1)S(1)}, bf16[4,8,8,2048]{3,1,0,2:T(8,128)(2,1)S(1)}, u32[]{:S(2)}, u32[]{:S(2)}) %collective-permute-start.14) | collective-permute-done | bytes 1048608 | tf_op jit(solution)/shard_map/ppermute | solution.py:11
  257.2 22.5 %collective-permute-done.17 = bf16[4,8,8,2048]{3,2,1,0:T(8,128)(2,1)S(1)} collective-permute-done((bf16[4,8,8,2048]{3,2,1,0:T(8,128)(2,1)S(1)}, bf16[4,8,8,2048]{3,2,1,0:T(8,128)(2,1)S(1)}, u32[]{:S(2)}, u32[]{:S(2)}) %collective-permute-start.17) | collective-permute-done | bytes 1048608 | tf_op jit(solution)/shard_map/ppermute | solution.py:11
  280.7 14.9 %collective-permute-start.16 = (bf16[4,8,8,2048]{3,2,0,1:T(8,128)(2,1)S(1)}, bf16[4,8,8,2048]{3,2,0,1:T(8,128)(2,1)S(1)}, u32[]{:S(2)}, u32[]{:S(2)}) collective-permute-start(bf16[4,8,8,2048]{3,2,0,1:T(8,128)(2,1)S(1)} %get-tuple-element.128), channel_id=1, source_target_pairs={{0,8},{1,9},{2,10},{3,11},{4,12},{5,13},{6,14},{7,15},{8,0},{9,1},... | collective-permute-start | bytes 3145736 | tf_op jit(solution)/shard_map/ppermute | solution.py:11
  300.0 39.9 %collective-permute-done.16 = bf16[4,8,8,2048]{3,2,0,1:T(8,128)(2,1)S(1)} collective-permute-done((bf16[4,8,8,2048]{3,2,0,1:T(8,128)(2,1)S(1)}, bf16[4,8,8,2048]{3,2,0,1:T(8,128)(2,1)S(1)}, u32[]{:S(2)}, u32[]{:S(2)}) %collective-permute-start.16) | collective-permute-done | bytes 1048608 | tf_op jit(solution)/shard_map/ppermute | solution.py:11
  342.3 4.8 %fusion.1 = (f32[2048]{0:T(1024)S(1)}, bf16[8,128,2048]{2,1,0:T(8,128)(2,1)S(1)}) fusion(f32[8,128,2048]{2,1,0:T(8,128)S(1)} %bitcast.330, f32[2048]{0:T(1024)S(1)} %copy-done.9, bf16[4,1,8,8,2048]{4,3,1,0,2:T(8,128)(2,1)S(1)} %bitcast.338, bf16[4,1,8,8,2048]{4,3,1,0,2:T(8,128)(2,1)S(1)} %bitcast.339, bf16[4,8,8,2048]{3,2,1,0:T(8,128)(2,1)S(1)} %pad_maximum_fusion.13, ...), kind=kLoop, calls=%fused_computation.3 | loop fusion | flops 46135296 | bytes 16793600 | tf_op jit(solution)/shard_map/reduce_sum | solution.py:136
  347.1 2.9 multiply_reduce_fusion
  354.9 4.7 %fusion.2 = bf16[1024,2048]{1,0:T(8,128)(2,1)} fusion(f32[8,128,2048]{2,1,0:T(8,128)S(1)} %get-tuple-element.199, bf16[1,1024,2048]{2,1,0:T(8,128)(2,1)S(1)} %copy-done.4, bf16[1,1024,2048]{2,1,0:T(8,128)(2,1)S(1)} %copy-done.3, f32[1024]{0:T(1024)S(1)} %multiply_bitcast_fusion, f32[2048]{0:T(1024)S(1)} %copy-done.8, f32[1024]{0:T(1024)S(1)} %get-tuple-element.195), kind=kLoop, calls=%fused_computation.5 | loop fusion | flops 18874368 | bytes 20987904 | tf_op jit(solution)/shard_map/convert_element_type | solution.py:150
  359.8 2.5 collective-permute-start.29
  362.3 1.9 collective-permute-start.30
  365.6 20.0 %collective-permute-done.29 = f32[2,2048]{1,0:T(2,128)S(1)} collective-permute-done((f32[2,2048]{1,0:T(2,128)S(1)}, f32[2,2048]{1,0:T(2,128)S(1)}, u32[]{:S(2)}, u32[]{:S(2)}) %collective-permute-start.29) | collective-permute-done | bytes 16416 | tf_op jit(solution)/shard_map/ppermute | solution.py:11
  387.1 2.0 copy-done.5
  (136 shorter events, 58.3 us)
Async XLA Ops:
  3.0 50.1 %collective-permute-start.2 = (bf16[8,4,8,2048]{3,2,1,0:T(8,128)(2,1)}, bf16[8,4,8,2048]{3,2,1,0:T(8,128)(2,1)}, u32[]{:S(2)}, u32[]{:S(2)}) collective-permute-start(bf16[8,4,8,2048]{3,2,1,0:T(8,128)(2,1)} %dynamic-slice_bitcast_fusion.3), channel_id=1, source_target_pairs={{0,8},{1,9},{2,10},{3,11},{4,12},{5,13},{6,14},{7,15},{8,0},{9,1},... | collective-permute-start | bytes 3145736 | tf_op jit(solution)/shard_map/ppermute | solution.py:11
  23.3 35.3 %collective-permute-start.3 = (bf16[8,4,8,2048]{3,2,0,1:T(8,128)(2,1)}, bf16[8,4,8,2048]{3,2,0,1:T(8,128)(2,1)}, u32[]{:S(2)}, u32[]{:S(2)}) collective-permute-start(bf16[8,4,8,2048]{3,2,0,1:T(8,128)(2,1)} %bitcast.313), channel_id=1, source_target_pairs={{0,1},{1,0},{2,3},{3,2},{4,5},{5,4},{6,7},{7,6},{8,9},{9,8},{10,11... | collective-permute-start | bytes 3145736 | tf_op jit(solution)/shard_map/ppermute | solution.py:11
  25.9 47.1 %collective-permute-start.4 = (bf16[8,4,8,2048]{3,2,0,1:T(8,128)(2,1)}, bf16[8,4,8,2048]{3,2,0,1:T(8,128)(2,1)}, u32[]{:S(2)}, u32[]{:S(2)}) collective-permute-start(bf16[8,4,8,2048]{3,2,0,1:T(8,128)(2,1)} %bitcast.312), channel_id=1, source_target_pairs={{0,2},{1,3},{2,0},{3,1},{4,6},{5,7},{6,4},{7,5},{8,10},{9,11},{10,... | collective-permute-start | bytes 3145736 | tf_op jit(solution)/shard_map/ppermute | solution.py:11
  27.4 45.6 %collective-permute-start.5 = (bf16[8,4,8,2048]{3,2,1,0:T(8,128)(2,1)}, bf16[8,4,8,2048]{3,2,1,0:T(8,128)(2,1)}, u32[]{:S(2)}, u32[]{:S(2)}) collective-permute-start(bf16[8,4,8,2048]{3,2,1,0:T(8,128)(2,1)} %get-tuple-element.137), channel_id=1, source_target_pairs={{0,3},{1,2},{2,1},{3,0},{4,7},{5,6},{6,5},{7,4},{8,11},{9,10},{10,... | collective-permute-start | bytes 3145736 | tf_op jit(solution)/shard_map/ppermute | solution.py:11
  27.9 67.9 %collective-permute-start = (bf16[8,4,8,2048]{3,2,1,0:T(8,128)(2,1)}, bf16[8,4,8,2048]{3,2,1,0:T(8,128)(2,1)}, u32[]{:S(2)}, u32[]{:S(2)}) collective-permute-start(bf16[8,4,8,2048]{3,2,1,0:T(8,128)(2,1)} %get-tuple-element.143), channel_id=1, source_target_pairs={{0,4},{1,5},{2,6},{3,7},{4,0},{5,1},{6,2},{7,3},{8,12},{9,13},{10,... | collective-permute-start | bytes 3145736 | tf_op jit(solution)/shard_map/ppermute | solution.py:11
  53.1 42.6 %collective-permute-start.1 = (bf16[8,4,8,2048]{3,2,1,0:T(8,128)(2,1)}, bf16[8,4,8,2048]{3,2,1,0:T(8,128)(2,1)S(1)}, u32[]{:S(2)}, u32[]{:S(2)}) collective-permute-start(bf16[8,4,8,2048]{3,2,1,0:T(8,128)(2,1)} %get-tuple-element.142), channel_id=1, source_target_pairs={{0,12},{1,13},{2,14},{3,15},{4,8},{5,9},{6,10},{7,11},{8,4},{9,5},... | collective-permute-start | bytes 3145736 | tf_op jit(solution)/shard_map/ppermute | solution.py:11
  99.0 57.6 %collective-permute-start.9 = (bf16[4,8,8,2048]{3,2,1,0:T(8,128)(2,1)}, bf16[4,8,8,2048]{3,2,1,0:T(8,128)(2,1)}, u32[]{:S(2)}, u32[]{:S(2)}) collective-permute-start(bf16[4,8,8,2048]{3,2,1,0:T(8,128)(2,1)} %pad_maximum_fusion.12), channel_id=1, source_target_pairs={{0,3},{1,2},{2,1},{3,0},{4,7},{5,6},{6,5},{7,4},{8,11},{9,10},{10,... | collective-permute-start | bytes 3145736 | tf_op jit(solution)/shard_map/ppermute | solution.py:11
  101.5 50.9 %collective-permute-start.6 = (bf16[4,8,8,2048]{3,2,1,0:T(8,128)(2,1)}, bf16[4,8,8,2048]{3,2,1,0:T(8,128)(2,1)}, u32[]{:S(2)}, u32[]{:S(2)}) collective-permute-start(bf16[4,8,8,2048]{3,2,1,0:T(8,128)(2,1)} %pad_maximum_fusion.7), channel_id=1, source_target_pairs={{0,8},{1,9},{2,10},{3,11},{4,12},{5,13},{6,14},{7,15},{8,0},{9,1},... | collective-permute-start | bytes 3145736 | tf_op jit(solution)/shard_map/ppermute | solution.py:11
  108.1 48.5 %collective-permute-start.8 = (bf16[4,8,8,2048]{3,2,1,0:T(8,128)(2,1)}, bf16[4,8,8,2048]{3,2,1,0:T(8,128)(2,1)}, u32[]{:S(2)}, u32[]{:S(2)}) collective-permute-start(bf16[4,8,8,2048]{3,2,1,0:T(8,128)(2,1)} %pad_maximum_fusion.11), channel_id=1, source_target_pairs={{0,2},{1,3},{2,0},{3,1},{4,6},{5,7},{6,4},{7,5},{8,10},{9,11},{10,... | collective-permute-start | bytes 3145736 | tf_op jit(solution)/shard_map/ppermute | solution.py:11
  109.7 46.9 %collective-permute-start.7 = (bf16[4,8,8,2048]{3,2,1,0:T(8,128)(2,1)}, bf16[4,8,8,2048]{3,2,1,0:T(8,128)(2,1)}, u32[]{:S(2)}, u32[]{:S(2)}) collective-permute-start(bf16[4,8,8,2048]{3,2,1,0:T(8,128)(2,1)} %pad_maximum_fusion.10), channel_id=1, source_target_pairs={{0,1},{1,0},{2,3},{3,2},{4,5},{5,4},{6,7},{7,6},{8,9},{9,8},{10,11... | collective-permute-start | bytes 3145736 | tf_op jit(solution)/shard_map/ppermute | solution.py:11
  111.6 66.3 %collective-permute-start.11 = (bf16[4,8,8,2048]{3,2,1,0:T(8,128)(2,1)S(1)}, bf16[4,8,8,2048]{3,2,1,0:T(8,128)(2,1)S(1)}, u32[]{:S(2)}, u32[]{:S(2)}) collective-permute-start(bf16[4,8,8,2048]{3,2,1,0:T(8,128)(2,1)S(1)} %pad_maximum_fusion.6), channel_id=1, source_target_pairs={{0,4},{1,5},{2,6},{3,7},{4,0},{5,1},{6,2},{7,3},{8,12},{9,13},{10,... | collective-permute-start | bytes 3145736 | tf_op jit(solution)/shard_map/ppermute | solution.py:11
  152.4 25.5 %collective-permute-start.12 = (bf16[4,8,8,2048]{3,2,1,0:T(8,128)(2,1)S(1)}, bf16[4,8,8,2048]{3,2,1,0:T(8,128)(2,1)S(1)}, u32[]{:S(2)}, u32[]{:S(2)}) collective-permute-start(bf16[4,8,8,2048]{3,2,1,0:T(8,128)(2,1)S(1)} %pad_maximum_fusion.8), channel_id=1, source_target_pairs={{0,12},{1,13},{2,14},{3,15},{4,8},{5,9},{6,10},{7,11},{8,4},{9,5},... | collective-permute-start | bytes 3145736 | tf_op jit(solution)/shard_map/ppermute | solution.py:11
  183.3 65.0 %collective-permute-start.10 = (bf16[4,8,8,2048]{3,2,1,0:T(8,128)(2,1)S(1)}, bf16[4,8,8,2048]{3,2,1,0:T(8,128)(2,1)S(1)}, u32[]{:S(2)}, u32[]{:S(2)}) collective-permute-start(bf16[4,8,8,2048]{3,2,1,0:T(8,128)(2,1)S(1)} %copy.93), channel_id=1, source_target_pairs={{0,8},{1,9},{2,10},{3,11},{4,12},{5,13},{6,14},{7,15},{8,0},{9,1},... | collective-permute-start | bytes 3145736 | tf_op jit(solution)/shard_map/ppermute | solution.py:11
  205.3 5.4 %collective-permute-start.32 = (f32[8,128,128]{2,1,0:T(8,128)S(1)}, f32[8,128,128]{2,1,0:T(8,128)S(1)}, u32[]{:S(2)}, u32[]{:S(2)}) collective-permute-start(f32[8,128,128]{2,1,0:T(8,128)S(1)} %fusion.48), channel_id=1, source_target_pairs={{0,16},{16,0},{1,17},{17,1},{2,18},{18,2},{3,19},{19,3},{4,20},{20... | collective-permute-start | bytes 1572872 | tf_op jit(solution)/shard_map/ppermute | solution.py:11
  205.4 43.9 %collective-permute-start.13 = (bf16[4,8,8,2048]{3,1,0,2:T(8,128)(2,1)S(1)}, bf16[4,8,8,2048]{3,1,0,2:T(8,128)(2,1)S(1)}, u32[]{:S(2)}, u32[]{:S(2)}) collective-permute-start(bf16[4,8,8,2048]{3,1,0,2:T(8,128)(2,1)S(1)} %get-tuple-element.131), channel_id=1, source_target_pairs={{0,1},{1,0},{2,3},{3,2},{4,5},{5,4},{6,7},{7,6},{8,9},{9,8},{10,11... | collective-permute-start | bytes 3145736 | tf_op jit(solution)/shard_map/ppermute | solution.py:11
  206.0 47.7 %collective-permute-start.14 = (bf16[4,8,8,2048]{3,1,0,2:T(8,128)(2,1)S(1)}, bf16[4,8,8,2048]{3,1,0,2:T(8,128)(2,1)S(1)}, u32[]{:S(2)}, u32[]{:S(2)}) collective-permute-start(bf16[4,8,8,2048]{3,1,0,2:T(8,128)(2,1)S(1)} %get-tuple-element.130), channel_id=1, source_target_pairs={{0,2},{1,3},{2,0},{3,1},{4,6},{5,7},{6,4},{7,5},{8,10},{9,11},{10,... | collective-permute-start | bytes 3145736 | tf_op jit(solution)/shard_map/ppermute | solution.py:11
  206.5 47.2 %collective-permute-start.15 = (bf16[4,8,8,2048]{3,1,0,2:T(8,128)(2,1)S(1)}, bf16[4,8,8,2048]{3,1,0,2:T(8,128)(2,1)S(1)}, u32[]{:S(2)}, u32[]{:S(2)}) collective-permute-start(bf16[4,8,8,2048]{3,1,0,2:T(8,128)(2,1)S(1)} %get-tuple-element.129), channel_id=1, source_target_pairs={{0,3},{1,2},{2,1},{3,0},{4,7},{5,6},{6,5},{7,4},{8,11},{9,10},{10,... | collective-permute-start | bytes 3145736 | tf_op jit(solution)/shard_map/ppermute | solution.py:11
  210.7 69.0 %collective-permute-start.17 = (bf16[4,8,8,2048]{3,2,1,0:T(8,128)(2,1)S(1)}, bf16[4,8,8,2048]{3,2,1,0:T(8,128)(2,1)S(1)}, u32[]{:S(2)}, u32[]{:S(2)}) collective-permute-start(bf16[4,8,8,2048]{3,2,1,0:T(8,128)(2,1)S(1)} %copy.103), channel_id=1, source_target_pairs={{0,4},{1,5},{2,6},{3,7},{4,0},{5,1},{6,2},{7,3},{8,12},{9,13},{10,... | collective-permute-start | bytes 3145736 | tf_op jit(solution)/shard_map/ppermute | solution.py:11
  248.3 31.3 %collective-permute-start.18 = (bf16[4,8,8,2048]{3,2,0,1:T(8,128)(2,1)S(1)}, bf16[4,8,8,2048]{3,2,0,1:T(8,128)(2,1)S(1)}, u32[]{:S(2)}, u32[]{:S(2)}) collective-permute-start(bf16[4,8,8,2048]{3,2,0,1:T(8,128)(2,1)S(1)} %copy.104), channel_id=1, source_target_pairs={{0,12},{1,13},{2,14},{3,15},{4,8},{5,9},{6,10},{7,11},{8,4},{9,5},... | collective-permute-start | bytes 3145736 | tf_op jit(solution)/shard_map/ppermute | solution.py:11
  280.1 62.1 %collective-permute-start.21 = (bf16[4,8,8,2048]{3,2,0,1:T(8,128)(2,1)S(1)}, bf16[4,8,8,2048]{3,2,0,1:T(8,128)(2,1)S(1)}, u32[]{:S(2)}, u32[]{:S(2)}) collective-permute-start(bf16[4,8,8,2048]{3,2,0,1:T(8,128)(2,1)S(1)} %pad_maximum_fusion.16), channel_id=1, source_target_pairs={{0,3},{1,2},{2,1},{3,0},{4,7},{5,6},{6,5},{7,4},{8,11},{9,10},{10,... | collective-permute-start | bytes 3145736 | tf_op jit(solution)/shard_map/ppermute | solution.py:11
  280.7 59.3 %collective-permute-start.16 = (bf16[4,8,8,2048]{3,2,0,1:T(8,128)(2,1)S(1)}, bf16[4,8,8,2048]{3,2,0,1:T(8,128)(2,1)S(1)}, u32[]{:S(2)}, u32[]{:S(2)}) collective-permute-start(bf16[4,8,8,2048]{3,2,0,1:T(8,128)(2,1)S(1)} %get-tuple-element.128), channel_id=1, source_target_pairs={{0,8},{1,9},{2,10},{3,11},{4,12},{5,13},{6,14},{7,15},{8,0},{9,1},... | collective-permute-start | bytes 3145736 | tf_op jit(solution)/shard_map/ppermute | solution.py:11
  295.7 46.5 %collective-permute-start.20 = (bf16[4,8,8,2048]{3,2,0,1:T(8,128)(2,1)S(1)}, bf16[4,8,8,2048]{3,2,0,1:T(8,128)(2,1)S(1)}, u32[]{:S(2)}, u32[]{:S(2)}) collective-permute-start(bf16[4,8,8,2048]{3,2,0,1:T(8,128)(2,1)S(1)} %pad_maximum_fusion.15), channel_id=1, source_target_pairs={{0,2},{1,3},{2,0},{3,1},{4,6},{5,7},{6,4},{7,5},{8,10},{9,11},{10,... | collective-permute-start | bytes 3145736 | tf_op jit(solution)/shard_map/ppermute | solution.py:11
  297.5 44.8 %collective-permute-start.19 = (bf16[4,8,8,2048]{3,2,1,0:T(8,128)(2,1)S(1)}, bf16[4,8,8,2048]{3,2,1,0:T(8,128)(2,1)S(1)}, u32[]{:S(2)}, u32[]{:S(2)}) collective-permute-start(bf16[4,8,8,2048]{3,2,1,0:T(8,128)(2,1)S(1)} %pad_maximum_fusion.14), channel_id=1, source_target_pairs={{0,1},{1,0},{2,3},{3,2},{4,5},{5,4},{6,7},{7,6},{8,9},{9,8},{10,11... | collective-permute-start | bytes 3145736 | tf_op jit(solution)/shard_map/ppermute | solution.py:11
  299.0 87.3 %collective-permute-start.22 = (bf16[4,8,8,2048]{3,2,0,1:T(8,128)(2,1)S(1)}, bf16[4,8,8,2048]{3,2,0,1:T(8,128)(2,1)S(1)}, u32[]{:S(2)}, u32[]{:S(2)}) collective-permute-start(bf16[4,8,8,2048]{3,2,0,1:T(8,128)(2,1)S(1)} %get-tuple-element.91), channel_id=1, source_target_pairs={{0,4},{1,5},{2,6},{3,7},{4,0},{5,1},{6,2},{7,3},{8,12},{9,13},{10,... | collective-permute-start | bytes 3145736 | tf_op jit(solution)/shard_map/ppermute | solution.py:11
  339.9 46.3 %collective-permute-start.23 = (bf16[4,8,8,2048]{3,2,0,1:T(8,128)(2,1)S(1)}, bf16[4,8,8,2048]{3,2,0,1:T(8,128)(2,1)S(1)}, u32[]{:S(2)}, u32[]{:S(2)}) collective-permute-start(bf16[4,8,8,2048]{3,2,0,1:T(8,128)(2,1)S(1)} %get-tuple-element.92), channel_id=1, source_target_pairs={{0,12},{1,13},{2,14},{3,15},{4,8},{5,9},{6,10},{7,11},{8,4},{9,5},... | collective-permute-start | bytes 3145736 | tf_op jit(solution)/shard_map/ppermute | solution.py:11
  351.3 8.3 %collective-permute-start.25 = (f32[2,2048]{1,0:T(2,128)S(1)}, f32[2,2048]{1,0:T(2,128)S(1)}, u32[]{:S(2)}, u32[]{:S(2)}) collective-permute-start(f32[2,2048]{1,0:T(2,128)S(1)} %fusion.41), channel_id=1, source_target_pairs={{0,1},{1,0},{2,3},{3,2},{4,5},{5,4},{6,7},{7,6},{8,9},{9,8},{10,11... | collective-permute-start | bytes 49160 | tf_op jit(solution)/shard_map/ppermute | solution.py:11
  352.9 6.8 %collective-permute-start.26 = (f32[2,2048]{1,0:T(2,128)S(1)}, f32[2,2048]{1,0:T(2,128)S(1)}, u32[]{:S(2)}, u32[]{:S(2)}) collective-permute-start(f32[2,2048]{1,0:T(2,128)S(1)} %fusion.41), channel_id=1, source_target_pairs={{0,2},{1,3},{2,0},{3,1},{4,6},{5,7},{6,4},{7,5},{8,10},{9,11},{10,... | collective-permute-start | bytes 49160 | tf_op jit(solution)/shard_map/ppermute | solution.py:11
  354.4 5.3 %collective-permute-start.27 = (f32[2,2048]{1,0:T(2,128)S(1)}, f32[2,2048]{1,0:T(2,128)S(1)}, u32[]{:S(2)}, u32[]{:S(2)}) collective-permute-start(f32[2,2048]{1,0:T(2,128)S(1)} %fusion.41), channel_id=1, source_target_pairs={{0,3},{1,2},{2,1},{3,0},{4,7},{5,6},{6,5},{7,4},{8,11},{9,10},{10,... | collective-permute-start | bytes 49160 | tf_op jit(solution)/shard_map/ppermute | solution.py:11
  359.7 5.8 %collective-permute-start.28 = (f32[2,2048]{1,0:T(2,128)S(1)}, f32[2,2048]{1,0:T(2,128)S(1)}, u32[]{:S(2)}, u32[]{:S(2)}) collective-permute-start(f32[2,2048]{1,0:T(2,128)S(1)} %add_add_fusion.1), channel_id=1, source_target_pairs={{0,4},{1,5},{2,6},{3,7},{4,0},{5,1},{6,2},{7,3},{8,12},{9,13},{10,... | collective-permute-start | bytes 49160 | tf_op jit(solution)/shard_map/ppermute | solution.py:11
  359.8 25.8 %collective-permute-start.29 = (f32[2,2048]{1,0:T(2,128)S(1)}, f32[2,2048]{1,0:T(2,128)S(1)}, u32[]{:S(2)}, u32[]{:S(2)}) collective-permute-start(f32[2,2048]{1,0:T(2,128)S(1)} %add_add_fusion.1), channel_id=1, source_target_pairs={{0,8},{1,9},{2,10},{3,11},{4,12},{5,13},{6,14},{7,15},{8,0},{9,1},... | collective-permute-start | bytes 49160 | tf_op jit(solution)/shard_map/ppermute | solution.py:11
  362.3 23.3 %collective-permute-start.30 = (f32[2,2048]{1,0:T(2,128)S(1)}, f32[2,2048]{1,0:T(2,128)S(1)}, u32[]{:S(2)}, u32[]{:S(2)}) collective-permute-start(f32[2,2048]{1,0:T(2,128)S(1)} %add_add_fusion.1), channel_id=1, source_target_pairs={{0,12},{1,13},{2,14},{3,15},{4,8},{5,9},{6,10},{7,11},{8,4},{9,5},... | collective-permute-start | bytes 49160 | tf_op jit(solution)/shard_map/ppermute | solution.py:11
  365.6 23.5 %collective-permute-start.31 = (f32[8,128,128]{2,1,0:T(8,128)S(1)}, f32[8,128,128]{2,1,0:T(8,128)S(1)}, u32[]{:S(2)}, u32[]{:S(2)}) collective-permute-start(f32[8,128,128]{2,1,0:T(8,128)S(1)} %fusion.14), channel_id=1, source_target_pairs={{0,16},{16,0},{1,17},{17,1},{2,18},{18,2},{3,19},{19,3},{4,20},{20... | collective-permute-start | bytes 1572872 | tf_op jit(solution)/shard_map/ppermute | solution.py:11
  (13 other events, 161.9 us)

commit v11 on v10

--- a/solution.py
+++ b/solution.py
@@ -151,6 +151,7 @@
     vectors = jnp.stack((gain_slice, mid_part))
     vectors = sum_over(vectors, "dp", 0, dp_levels)
     vectors = sum_over(vectors, "seq", 0, low)
+    vectors, grad_right = lax.optimization_barrier((vectors, grad_right))
     gain_gradient, grad_mid = sum_over(vectors, "seq", low, levels)
     mixed_rest, input_gradient, gain_gradient, grad_mid = lax.optimization_barrier(
         ([mixed_far[k] for k in rest], input_gradient, gain_gradient, grad_mid)

time: 398 us -> 415 us (1.043)
  waiting for transfers between devices: 220 us -> 236 us
  local copies, waits for them, and re-layouts: 35.1 us -> 43.1 us
  other arithmetic: 34.8 us -> 27.5 us
    ppermute x33, waiting for transfers between devices: 220 us -> 236 us  [from_partner(): return lax.ppermute(block, axis, [(i, i ^ distance) for i in range(count)])]
    another operation x1, other arithmetic: 13.8 us -> 2.38 us  [body(): upward = jnp.stack(up_near, axis=1).reshape(order, local, width)]
    dynamic_update_slice x4, local copies, waits for them, and re-layouts: 2.74 us -> 11.4 us  [body(): lax.dynamic_update_index_in_dim(mixed_near, part, device_near ^ k, 1)]
    dynamic_update_slice x4, other arithmetic: 1.56 us -> 5.94 us  [placed(): return lax.dynamic_update_index_in_dim(output, block, place, 1)]
  transfers between devices with their start and end apart: 33 -> 33, of which waited for: 11 -> 13; matrix products, arithmetic and copies ran while one was open for 19% -> 18% of each run, Pallas kernels for 0% -> 0%
where the time goes in v11:
time: 415 us; the launch traced here: 408 us
  waiting for transfers between devices  236 us (57%)
  starting transfers between devices  79.1 us (19%)
  local copies, waits for them, and re-layouts  43.1 us (10%)
  other arithmetic  27.5 us (7%)
  matrix products  21.4 us (5%)
    ppermute x33, waiting for transfers between devices, from_partner(): return lax.ppermute(block, axis, [(i, i ^ distance) for i in range(count)])  236 us
    ppermute x33, starting transfers between devices, from_partner(): return lax.ppermute(block, axis, [(i, i ^ distance) for i in range(count)])  79.1 us
    dynamic_update_slice x4, local copies, waits for them, and re-layouts, body(): lax.dynamic_update_index_in_dim(mixed_near, part, device_near ^ k, 1)  11.4 us
    dot_general x1, matrix products, body(): first = jnp.einsum('aij,ajd->aid', rights, grid, preferred_element_type=f32)  8.97 us
  transfers between devices with their start and end apart: 33, of which 13 were waited for; matrix products, arithmetic and copies ran while one was open for 18% of the time, Pallas kernels for 0%

profile of v11, /device:TPU:0, one launch (start us, length us, event | category | flops | bytes accessed | tf_op | source)
XLA Modules:
  0.0 408.0 jit_solution(7293343694725708006)
XLA Ops:
  0.7 2.4 dynamic-slice_bitcast_fusion.3
  3.0 4.0 collective-permute-start.2
  7.1 3.7 dynamic-slice_bitcast_fusion.2
  12.0 9.0 %multiply_convert_fusion = (bf16[8,128,2048]{2,1,0:T(8,128)(2,1)S(1)}, f32[8,128,2048]{2,1,0:T(8,128)}) fusion(f32[2048]{0:T(1024)S(1)} %copy-done.9, bf16[8,128,128]{1,2,0:T(8,128)(2,1)S(1)} %convolution_bitcast_fusion.3, f32[2048]{0:T(1024)S(1)} %copy-done.8, f32[8,128]{1,0:T(8,128)S(1)} %get-tuple-element.200, bf16[8,128,2048]{2,1,0:T(8,128)(2,1)} %bitcast.315), kind=kOutput, calls=%fused_computation.17 | convolution fusion | flops 557842432 | bytes 17059840 | tf_op jit(solution)/shard_map/aij,ajd->aid/dot_general | solution.py:65
  30.4 22.7 %collective-permute-done.2 = bf16[8,4,8,2048]{3,2,1,0:T(8,128)(2,1)} collective-permute-done((bf16[8,4,8,2048]{3,2,1,0:T(8,128)(2,1)}, bf16[8,4,8,2048]{3,2,1,0:T(8,128)(2,1)}, u32[]{:S(2)}, u32[]{:S(2)}) %collective-permute-start.2) | collective-permute-done | bytes 1048608 | tf_op jit(solution)/shard_map/ppermute | solution.py:11
  53.1 3.5 collective-permute-start.1
  58.6 14.4 %collective-permute-done.4 = bf16[8,4,8,2048]{3,2,0,1:T(8,128)(2,1)} collective-permute-done((bf16[8,4,8,2048]{3,2,0,1:T(8,128)(2,1)}, bf16[8,4,8,2048]{3,2,0,1:T(8,128)(2,1)}, u32[]{:S(2)}, u32[]{:S(2)}) %collective-permute-start.4) | collective-permute-done | bytes 1048608 | tf_op jit(solution)/shard_map/ppermute | solution.py:11
  79.3 16.4 %collective-permute-done = bf16[8,4,8,2048]{3,2,1,0:T(8,128)(2,1)} collective-permute-done((bf16[8,4,8,2048]{3,2,1,0:T(8,128)(2,1)}, bf16[8,4,8,2048]{3,2,1,0:T(8,128)(2,1)}, u32[]{:S(2)}, u32[]{:S(2)}) %collective-permute-start) | collective-permute-done | bytes 1048608 | tf_op jit(solution)/shard_map/ppermute | solution.py:11
  99.0 2.5 collective-permute-start.9
  101.5 5.4 %collective-permute-start.6 = (bf16[4,8,8,2048]{3,2,1,0:T(8,128)(2,1)}, bf16[4,8,8,2048]{3,2,1,0:T(8,128)(2,1)}, u32[]{:S(2)}, u32[]{:S(2)}) collective-permute-start(bf16[4,8,8,2048]{3,2,1,0:T(8,128)(2,1)} %pad_maximum_fusion.7), channel_id=1, source_target_pairs={{0,8},{1,9},{2,10},{3,11},{4,12},{5,13},{6,14},{7,15},{8,0},{9,1},... | collective-permute-start | bytes 3145736 | tf_op jit(solution)/shard_map/ppermute | solution.py:11
  113.3 39.1 %collective-permute-done.6 = bf16[4,8,8,2048]{3,2,1,0:T(8,128)(2,1)} collective-permute-done((bf16[4,8,8,2048]{3,2,1,0:T(8,128)(2,1)}, bf16[4,8,8,2048]{3,2,1,0:T(8,128)(2,1)}, u32[]{:S(2)}, u32[]{:S(2)}) %collective-permute-start.6) | collective-permute-done | bytes 1048608 | tf_op jit(solution)/shard_map/ppermute | solution.py:11
  152.4 2.8 collective-permute-start.12
  156.6 2.4 pad_maximum_fusion
  159.0 2.3 copy.91
  163.0 15.0 %collective-permute-done.11 = bf16[4,8,8,2048]{3,2,1,0:T(8,128)(2,1)S(1)} collective-permute-done((bf16[4,8,8,2048]{3,2,1,0:T(8,128)(2,1)S(1)}, bf16[4,8,8,2048]{3,2,1,0:T(8,128)(2,1)S(1)}, u32[]{:S(2)}, u32[]{:S(2)}) %collective-permute-start.11) | collective-permute-done | bytes 1048608 | tf_op jit(solution)/shard_map/ppermute | solution.py:11
  178.6 2.3 copy.95
  183.3 20.7 %collective-permute-start.10 = (bf16[4,8,8,2048]{3,2,1,0:T(8,128)(2,1)S(1)}, bf16[4,8,8,2048]{3,2,1,0:T(8,128)(2,1)S(1)}, u32[]{:S(2)}, u32[]{:S(2)}) collective-permute-start(bf16[4,8,8,2048]{3,2,1,0:T(8,128)(2,1)S(1)} %copy.93), channel_id=1, source_target_pairs={{0,8},{1,9},{2,10},{3,11},{4,12},{5,13},{6,14},{7,15},{8,0},{9,1},... | collective-permute-start | bytes 3145736 | tf_op jit(solution)/shard_map/ppermute | solution.py:11
  206.5 2.4 collective-permute-start.15
  212.8 35.5 %collective-permute-done.10 = bf16[4,8,8,2048]{3,2,1,0:T(8,128)(2,1)S(1)} collective-permute-done((bf16[4,8,8,2048]{3,2,1,0:T(8,128)(2,1)S(1)}, bf16[4,8,8,2048]{3,2,1,0:T(8,128)(2,1)S(1)}, u32[]{:S(2)}, u32[]{:S(2)}) %collective-permute-start.10) | collective-permute-done | bytes 1048608 | tf_op jit(solution)/shard_map/ppermute | solution.py:11
  249.3 4.4 %collective-permute-done.14 = bf16[4,8,8,2048]{3,1,0,2:T(8,128)(2,1)S(1)} collective-permute-done((bf16[4,8,8,2048]{3,1,0,2:T(8,128)(2,1)S(1)}, bf16[4,8,8,2048]{3,1,0,2:T(8,128)(2,1)S(1)}, u32[]{:S(2)}, u32[]{:S(2)}) %collective-permute-start.14) | collective-permute-done | bytes 1048608 | tf_op jit(solution)/shard_map/ppermute | solution.py:11
  256.1 9.4 %copy_dynamic-update-slice_fusion = bf16[4,4,8,8,2048]{4,3,1,2,0:T(8,128)(2,1)S(1)} fusion(bf16[4,4,8,8,2048]{4,3,1,2,0:T(8,128)(2,1)S(1)} %copy_dynamic-update-slice_fusion.1, s32[]{:T(128)S(6)} %select_n.59, bf16[4,1,8,8,2048]{4,2,0,3,1:T(8,128)(2,1)S(1)} %bitcast.342), kind=kLoop, calls=%fused_computation.79 | loop fusion | bytes 2097156 | tf_op jit(solution)/shard_map/jit(dynamic_update_index_in_dim)/dynamic_update_slice | solution.py:108
  267.1 12.5 %collective-permute-done.17 = bf16[4,8,8,2048]{3,2,1,0:T(8,128)(2,1)S(1)} collective-permute-done((bf16[4,8,8,2048]{3,2,1,0:T(8,128)(2,1)S(1)}, bf16[4,8,8,2048]{3,2,1,0:T(8,128)(2,1)S(1)}, u32[]{:S(2)}, u32[]{:S(2)}) %collective-permute-start.17) | collective-permute-done | bytes 1048608 | tf_op jit(solution)/shard_map/ppermute | solution.py:11
  280.8 14.9 %collective-permute-start.16 = (bf16[4,8,8,2048]{3,2,0,1:T(8,128)(2,1)S(1)}, bf16[4,8,8,2048]{3,2,0,1:T(8,128)(2,1)S(1)}, u32[]{:S(2)}, u32[]{:S(2)}) collective-permute-start(bf16[4,8,8,2048]{3,2,0,1:T(8,128)(2,1)S(1)} %get-tuple-element.132), channel_id=1, source_target_pairs={{0,8},{1,9},{2,10},{3,11},{4,12},{5,13},{6,14},{7,15},{8,0},{9,1},... | collective-permute-start | bytes 3145736 | tf_op jit(solution)/shard_map/ppermute | solution.py:11
  300.1 39.5 %collective-permute-done.16 = bf16[4,8,8,2048]{3,2,0,1:T(8,128)(2,1)S(1)} collective-permute-done((bf16[4,8,8,2048]{3,2,0,1:T(8,128)(2,1)S(1)}, bf16[4,8,8,2048]{3,2,0,1:T(8,128)(2,1)S(1)}, u32[]{:S(2)}, u32[]{:S(2)}) %collective-permute-start.16) | collective-permute-done | bytes 1048608 | tf_op jit(solution)/shard_map/ppermute | solution.py:11
  340.0 4.8 %fusion.1 = (f32[2048]{0:T(1024)S(1)}, bf16[8,128,2048]{2,1,0:T(8,128)(2,1)S(1)}) fusion(f32[8,128,2048]{2,1,0:T(8,128)S(1)} %bitcast.330, f32[2048]{0:T(1024)S(1)} %copy-done.9, bf16[4,1,8,8,2048]{4,3,1,0,2:T(8,128)(2,1)S(1)} %bitcast.338, bf16[4,1,8,8,2048]{4,3,1,0,2:T(8,128)(2,1)S(1)} %bitcast.339, bf16[4,8,8,2048]{3,2,1,0:T(8,128)(2,1)S(1)} %pad_maximum_fusion.13, ...), kind=kLoop, calls=%fused_computation.3 | loop fusion | flops 46135296 | bytes 16793600 | tf_op jit(solution)/shard_map/reduce_sum | solution.py:136
  344.9 2.9 multiply_reduce_fusion
  358.3 2.5 collective-permute-start.30
  362.7 4.5 %fusion.2 = bf16[1024,2048]{1,0:T(8,128)(2,1)} fusion(f32[8,128,2048]{2,1,0:T(8,128)S(1)} %get-tuple-element.203, bf16[1,1024,2048]{2,1,0:T(8,128)(2,1)S(1)} %copy-done.4, bf16[1,1024,2048]{2,1,0:T(8,128)(2,1)S(1)} %copy-done.3, f32[1024]{0:T(1024)S(1)} %multiply_bitcast_fusion, f32[2048]{0:T(1024)S(1)} %copy-done.8, f32[1024]{0:T(1024)S(1)} %get-tuple-element.199), kind=kLoop, calls=%fused_computation.5 | loop fusion | flops 18874368 | bytes 20987904 | tf_op jit(solution)/shard_map/convert_element_type | solution.py:150
  368.2 10.2 %collective-permute-done.29 = f32[2,2048]{1,0:T(2,128)S(1)} collective-permute-done((f32[2,2048]{1,0:T(2,128)S(1)}, f32[2,2048]{1,0:T(2,128)S(1)}, u32[]{:S(2)}, u32[]{:S(2)}) %collective-permute-start.29) | collective-permute-done | bytes 16416 | tf_op jit(solution)/shard_map/ppermute | solution.py:11
  378.4 23.6 %collective-permute-done.30 = f32[2,2048]{1,0:T(2,128)S(1)} collective-permute-done((f32[2,2048]{1,0:T(2,128)S(1)}, f32[2,2048]{1,0:T(2,128)S(1)}, u32[]{:S(2)}, u32[]{:S(2)}) %collective-permute-start.30) | collective-permute-done | bytes 16416 | tf_op jit(solution)/shard_map/ppermute | solution.py:11
  402.6 2.6 fusion.21
  405.2 2.6 fusion.23
  (136 shorter events, 65.7 us)
Async XLA Ops:
  3.0 50.1 %collective-permute-start.2 = (bf16[8,4,8,2048]{3,2,1,0:T(8,128)(2,1)}, bf16[8,4,8,2048]{3,2,1,0:T(8,128)(2,1)}, u32[]{:S(2)}, u32[]{:S(2)}) collective-permute-start(bf16[8,4,8,2048]{3,2,1,0:T(8,128)(2,1)} %dynamic-slice_bitcast_fusion.3), channel_id=1, source_target_pairs={{0,8},{1,9},{2,10},{3,11},{4,12},{5,13},{6,14},{7,15},{8,0},{9,1},... | collective-permute-start | bytes 3145736 | tf_op jit(solution)/shard_map/ppermute | solution.py:11
  23.3 35.3 %collective-permute-start.3 = (bf16[8,4,8,2048]{3,2,0,1:T(8,128)(2,1)}, bf16[8,4,8,2048]{3,2,0,1:T(8,128)(2,1)}, u32[]{:S(2)}, u32[]{:S(2)}) collective-permute-start(bf16[8,4,8,2048]{3,2,0,1:T(8,128)(2,1)} %bitcast.313), channel_id=1, source_target_pairs={{0,1},{1,0},{2,3},{3,2},{4,5},{5,4},{6,7},{7,6},{8,9},{9,8},{10,11... | collective-permute-start | bytes 3145736 | tf_op jit(solution)/shard_map/ppermute | solution.py:11
  25.9 47.1 %collective-permute-start.4 = (bf16[8,4,8,2048]{3,2,0,1:T(8,128)(2,1)}, bf16[8,4,8,2048]{3,2,0,1:T(8,128)(2,1)}, u32[]{:S(2)}, u32[]{:S(2)}) collective-permute-start(bf16[8,4,8,2048]{3,2,0,1:T(8,128)(2,1)} %bitcast.312), channel_id=1, source_target_pairs={{0,2},{1,3},{2,0},{3,1},{4,6},{5,7},{6,4},{7,5},{8,10},{9,11},{10,... | collective-permute-start | bytes 3145736 | tf_op jit(solution)/shard_map/ppermute | solution.py:11
  27.4 45.6 %collective-permute-start.5 = (bf16[8,4,8,2048]{3,2,1,0:T(8,128)(2,1)}, bf16[8,4,8,2048]{3,2,1,0:T(8,128)(2,1)}, u32[]{:S(2)}, u32[]{:S(2)}) collective-permute-start(bf16[8,4,8,2048]{3,2,1,0:T(8,128)(2,1)} %get-tuple-element.141), channel_id=1, source_target_pairs={{0,3},{1,2},{2,1},{3,0},{4,7},{5,6},{6,5},{7,4},{8,11},{9,10},{10,... | collective-permute-start | bytes 3145736 | tf_op jit(solution)/shard_map/ppermute | solution.py:11
  27.9 67.9 %collective-permute-start = (bf16[8,4,8,2048]{3,2,1,0:T(8,128)(2,1)}, bf16[8,4,8,2048]{3,2,1,0:T(8,128)(2,1)}, u32[]{:S(2)}, u32[]{:S(2)}) collective-permute-start(bf16[8,4,8,2048]{3,2,1,0:T(8,128)(2,1)} %get-tuple-element.147), channel_id=1, source_target_pairs={{0,4},{1,5},{2,6},{3,7},{4,0},{5,1},{6,2},{7,3},{8,12},{9,13},{10,... | collective-permute-start | bytes 3145736 | tf_op jit(solution)/shard_map/ppermute | solution.py:11
  53.1 42.6 %collective-permute-start.1 = (bf16[8,4,8,2048]{3,2,1,0:T(8,128)(2,1)}, bf16[8,4,8,2048]{3,2,1,0:T(8,128)(2,1)S(1)}, u32[]{:S(2)}, u32[]{:S(2)}) collective-permute-start(bf16[8,4,8,2048]{3,2,1,0:T(8,128)(2,1)} %get-tuple-element.146), channel_id=1, source_target_pairs={{0,12},{1,13},{2,14},{3,15},{4,8},{5,9},{6,10},{7,11},{8,4},{9,5},... | collective-permute-start | bytes 3145736 | tf_op jit(solution)/shard_map/ppermute | solution.py:11
  99.0 57.6 %collective-permute-start.9 = (bf16[4,8,8,2048]{3,2,1,0:T(8,128)(2,1)}, bf16[4,8,8,2048]{3,2,1,0:T(8,128)(2,1)}, u32[]{:S(2)}, u32[]{:S(2)}) collective-permute-start(bf16[4,8,8,2048]{3,2,1,0:T(8,128)(2,1)} %pad_maximum_fusion.12), channel_id=1, source_target_pairs={{0,3},{1,2},{2,1},{3,0},{4,7},{5,6},{6,5},{7,4},{8,11},{9,10},{10,... | collective-permute-start | bytes 3145736 | tf_op jit(solution)/shard_map/ppermute | solution.py:11
  101.5 50.9 %collective-permute-start.6 = (bf16[4,8,8,2048]{3,2,1,0:T(8,128)(2,1)}, bf16[4,8,8,2048]{3,2,1,0:T(8,128)(2,1)}, u32[]{:S(2)}, u32[]{:S(2)}) collective-permute-start(bf16[4,8,8,2048]{3,2,1,0:T(8,128)(2,1)} %pad_maximum_fusion.7), channel_id=1, source_target_pairs={{0,8},{1,9},{2,10},{3,11},{4,12},{5,13},{6,14},{7,15},{8,0},{9,1},... | collective-permute-start | bytes 3145736 | tf_op jit(solution)/shard_map/ppermute | solution.py:11
  108.1 48.6 %collective-permute-start.8 = (bf16[4,8,8,2048]{3,2,1,0:T(8,128)(2,1)}, bf16[4,8,8,2048]{3,2,1,0:T(8,128)(2,1)}, u32[]{:S(2)}, u32[]{:S(2)}) collective-permute-start(bf16[4,8,8,2048]{3,2,1,0:T(8,128)(2,1)} %pad_maximum_fusion.11), channel_id=1, source_target_pairs={{0,2},{1,3},{2,0},{3,1},{4,6},{5,7},{6,4},{7,5},{8,10},{9,11},{10,... | collective-permute-start | bytes 3145736 | tf_op jit(solution)/shard_map/ppermute | solution.py:11
  109.7 47.0 %collective-permute-start.7 = (bf16[4,8,8,2048]{3,2,1,0:T(8,128)(2,1)}, bf16[4,8,8,2048]{3,2,1,0:T(8,128)(2,1)}, u32[]{:S(2)}, u32[]{:S(2)}) collective-permute-start(bf16[4,8,8,2048]{3,2,1,0:T(8,128)(2,1)} %pad_maximum_fusion.10), channel_id=1, source_target_pairs={{0,1},{1,0},{2,3},{3,2},{4,5},{5,4},{6,7},{7,6},{8,9},{9,8},{10,11... | collective-permute-start | bytes 3145736 | tf_op jit(solution)/shard_map/ppermute | solution.py:11
  111.6 66.3 %collective-permute-start.11 = (bf16[4,8,8,2048]{3,2,1,0:T(8,128)(2,1)S(1)}, bf16[4,8,8,2048]{3,2,1,0:T(8,128)(2,1)S(1)}, u32[]{:S(2)}, u32[]{:S(2)}) collective-permute-start(bf16[4,8,8,2048]{3,2,1,0:T(8,128)(2,1)S(1)} %pad_maximum_fusion.6), channel_id=1, source_target_pairs={{0,4},{1,5},{2,6},{3,7},{4,0},{5,1},{6,2},{7,3},{8,12},{9,13},{10,... | collective-permute-start | bytes 3145736 | tf_op jit(solution)/shard_map/ppermute | solution.py:11
  152.4 25.5 %collective-permute-start.12 = (bf16[4,8,8,2048]{3,2,1,0:T(8,128)(2,1)S(1)}, bf16[4,8,8,2048]{3,2,1,0:T(8,128)(2,1)S(1)}, u32[]{:S(2)}, u32[]{:S(2)}) collective-permute-start(bf16[4,8,8,2048]{3,2,1,0:T(8,128)(2,1)S(1)} %pad_maximum_fusion.8), channel_id=1, source_target_pairs={{0,12},{1,13},{2,14},{3,15},{4,8},{5,9},{6,10},{7,11},{8,4},{9,5},... | collective-permute-start | bytes 3145736 | tf_op jit(solution)/shard_map/ppermute | solution.py:11
  183.3 65.0 %collective-permute-start.10 = (bf16[4,8,8,2048]{3,2,1,0:T(8,128)(2,1)S(1)}, bf16[4,8,8,2048]{3,2,1,0:T(8,128)(2,1)S(1)}, u32[]{:S(2)}, u32[]{:S(2)}) collective-permute-start(bf16[4,8,8,2048]{3,2,1,0:T(8,128)(2,1)S(1)} %copy.93), channel_id=1, source_target_pairs={{0,8},{1,9},{2,10},{3,11},{4,12},{5,13},{6,14},{7,15},{8,0},{9,1},... | collective-permute-start | bytes 3145736 | tf_op jit(solution)/shard_map/ppermute | solution.py:11
  205.3 5.4 %collective-permute-start.32 = (f32[8,128,128]{2,1,0:T(8,128)S(1)}, f32[8,128,128]{2,1,0:T(8,128)S(1)}, u32[]{:S(2)}, u32[]{:S(2)}) collective-permute-start(f32[8,128,128]{2,1,0:T(8,128)S(1)} %fusion.48), channel_id=1, source_target_pairs={{0,16},{16,0},{1,17},{17,1},{2,18},{18,2},{3,19},{19,3},{4,20},{20... | collective-permute-start | bytes 1572872 | tf_op jit(solution)/shard_map/ppermute | solution.py:11
  205.4 43.9 %collective-permute-start.13 = (bf16[4,8,8,2048]{3,1,0,2:T(8,128)(2,1)S(1)}, bf16[4,8,8,2048]{3,1,0,2:T(8,128)(2,1)S(1)}, u32[]{:S(2)}, u32[]{:S(2)}) collective-permute-start(bf16[4,8,8,2048]{3,1,0,2:T(8,128)(2,1)S(1)} %get-tuple-element.135), channel_id=1, source_target_pairs={{0,1},{1,0},{2,3},{3,2},{4,5},{5,4},{6,7},{7,6},{8,9},{9,8},{10,11... | collective-permute-start | bytes 3145736 | tf_op jit(solution)/shard_map/ppermute | solution.py:11
  206.0 47.7 %collective-permute-start.14 = (bf16[4,8,8,2048]{3,1,0,2:T(8,128)(2,1)S(1)}, bf16[4,8,8,2048]{3,1,0,2:T(8,128)(2,1)S(1)}, u32[]{:S(2)}, u32[]{:S(2)}) collective-permute-start(bf16[4,8,8,2048]{3,1,0,2:T(8,128)(2,1)S(1)} %get-tuple-element.134), channel_id=1, source_target_pairs={{0,2},{1,3},{2,0},{3,1},{4,6},{5,7},{6,4},{7,5},{8,10},{9,11},{10,... | collective-permute-start | bytes 3145736 | tf_op jit(solution)/shard_map/ppermute | solution.py:11
  206.5 47.2 %collective-permute-start.15 = (bf16[4,8,8,2048]{3,1,0,2:T(8,128)(2,1)S(1)}, bf16[4,8,8,2048]{3,1,0,2:T(8,128)(2,1)S(1)}, u32[]{:S(2)}, u32[]{:S(2)}) collective-permute-start(bf16[4,8,8,2048]{3,1,0,2:T(8,128)(2,1)S(1)} %get-tuple-element.133), channel_id=1, source_target_pairs={{0,3},{1,2},{2,1},{3,0},{4,7},{5,6},{6,5},{7,4},{8,11},{9,10},{10,... | collective-permute-start | bytes 3145736 | tf_op jit(solution)/shard_map/ppermute | solution.py:11
  210.7 69.0 %collective-permute-start.17 = (bf16[4,8,8,2048]{3,2,1,0:T(8,128)(2,1)S(1)}, bf16[4,8,8,2048]{3,2,1,0:T(8,128)(2,1)S(1)}, u32[]{:S(2)}, u32[]{:S(2)}) collective-permute-start(bf16[4,8,8,2048]{3,2,1,0:T(8,128)(2,1)S(1)} %copy.103), channel_id=1, source_target_pairs={{0,4},{1,5},{2,6},{3,7},{4,0},{5,1},{6,2},{7,3},{8,12},{9,13},{10,... | collective-permute-start | bytes 3145736 | tf_op jit(solution)/shard_map/ppermute | solution.py:11
  248.3 31.3 %collective-permute-start.18 = (bf16[4,8,8,2048]{3,2,0,1:T(8,128)(2,1)S(1)}, bf16[4,8,8,2048]{3,2,0,1:T(8,128)(2,1)S(1)}, u32[]{:S(2)}, u32[]{:S(2)}) collective-permute-start(bf16[4,8,8,2048]{3,2,0,1:T(8,128)(2,1)S(1)} %copy.104), channel_id=1, source_target_pairs={{0,12},{1,13},{2,14},{3,15},{4,8},{5,9},{6,10},{7,11},{8,4},{9,5},... | collective-permute-start | bytes 3145736 | tf_op jit(solution)/shard_map/ppermute | solution.py:11
  280.2 59.8 %collective-permute-start.21 = (bf16[4,8,8,2048]{3,2,0,1:T(8,128)(2,1)S(1)}, bf16[4,8,8,2048]{3,2,0,1:T(8,128)(2,1)S(1)}, u32[]{:S(2)}, u32[]{:S(2)}) collective-permute-start(bf16[4,8,8,2048]{3,2,0,1:T(8,128)(2,1)S(1)} %pad_maximum_fusion.16), channel_id=1, source_target_pairs={{0,3},{1,2},{2,1},{3,0},{4,7},{5,6},{6,5},{7,4},{8,11},{9,10},{10,... | collective-permute-start | bytes 3145736 | tf_op jit(solution)/shard_map/ppermute | solution.py:11
  280.8 58.8 %collective-permute-start.16 = (bf16[4,8,8,2048]{3,2,0,1:T(8,128)(2,1)S(1)}, bf16[4,8,8,2048]{3,2,0,1:T(8,128)(2,1)S(1)}, u32[]{:S(2)}, u32[]{:S(2)}) collective-permute-start(bf16[4,8,8,2048]{3,2,0,1:T(8,128)(2,1)S(1)} %get-tuple-element.132), channel_id=1, source_target_pairs={{0,8},{1,9},{2,10},{3,11},{4,12},{5,13},{6,14},{7,15},{8,0},{9,1},... | collective-permute-start | bytes 3145736 | tf_op jit(solution)/shard_map/ppermute | solution.py:11
  295.8 44.2 %collective-permute-start.20 = (bf16[4,8,8,2048]{3,2,0,1:T(8,128)(2,1)S(1)}, bf16[4,8,8,2048]{3,2,0,1:T(8,128)(2,1)S(1)}, u32[]{:S(2)}, u32[]{:S(2)}) collective-permute-start(bf16[4,8,8,2048]{3,2,0,1:T(8,128)(2,1)S(1)} %pad_maximum_fusion.15), channel_id=1, source_target_pairs={{0,2},{1,3},{2,0},{3,1},{4,6},{5,7},{6,4},{7,5},{8,10},{9,11},{10,... | collective-permute-start | bytes 3145736 | tf_op jit(solution)/shard_map/ppermute | solution.py:11
  297.5 42.5 %collective-permute-start.19 = (bf16[4,8,8,2048]{3,2,1,0:T(8,128)(2,1)S(1)}, bf16[4,8,8,2048]{3,2,1,0:T(8,128)(2,1)S(1)}, u32[]{:S(2)}, u32[]{:S(2)}) collective-permute-start(bf16[4,8,8,2048]{3,2,1,0:T(8,128)(2,1)S(1)} %pad_maximum_fusion.14), channel_id=1, source_target_pairs={{0,1},{1,0},{2,3},{3,2},{4,5},{5,4},{6,7},{7,6},{8,9},{9,8},{10,11... | collective-permute-start | bytes 3145736 | tf_op jit(solution)/shard_map/ppermute | solution.py:11
  299.0 103.6 %collective-permute-start.22 = (bf16[4,8,8,2048]{3,2,0,1:T(8,128)(2,1)}, bf16[4,8,8,2048]{3,2,0,1:T(8,128)(2,1)S(1)}, u32[]{:S(2)}, u32[]{:S(2)}) collective-permute-start(bf16[4,8,8,2048]{3,2,0,1:T(8,128)(2,1)} %get-tuple-element.93), channel_id=1, source_target_pairs={{0,4},{1,5},{2,6},{3,7},{4,0},{5,1},{6,2},{7,3},{8,12},{9,13},{10,... | collective-permute-start | bytes 3145736 | tf_op jit(solution)/shard_map/ppermute | solution.py:11
  349.3 8.3 %collective-permute-start.28 = (f32[8,128,128]{2,1,0:T(8,128)S(1)}, f32[8,128,128]{2,1,0:T(8,128)S(1)}, u32[]{:S(2)}, u32[]{:S(2)}) collective-permute-start(f32[8,128,128]{2,1,0:T(8,128)S(1)} %fusion.14), channel_id=1, source_target_pairs={{0,16},{16,0},{1,17},{17,1},{2,18},{18,2},{3,19},{19,3},{4,20},{20... | collective-permute-start | bytes 1572872 | tf_op jit(solution)/shard_map/ppermute | solution.py:11
  349.9 3.8 collective-permute-start.25
  351.4 4.2 %collective-permute-start.26 = (f32[2,2048]{1,0:T(2,128)S(1)}, f32[2,2048]{1,0:T(2,128)S(1)}, u32[]{:S(2)}, u32[]{:S(2)}) collective-permute-start(f32[2,2048]{1,0:T(2,128)S(1)} %fusion.41), channel_id=1, source_target_pairs={{0,2},{1,3},{2,0},{3,1},{4,6},{5,7},{6,4},{7,5},{8,10},{9,11},{10,... | collective-permute-start | bytes 49160 | tf_op jit(solution)/shard_map/ppermute | solution.py:11
  352.9 4.6 %collective-permute-start.27 = (f32[2,2048]{1,0:T(2,128)S(1)}, f32[2,2048]{1,0:T(2,128)S(1)}, u32[]{:S(2)}, u32[]{:S(2)}) collective-permute-start(f32[2,2048]{1,0:T(2,128)S(1)} %fusion.41), channel_id=1, source_target_pairs={{0,3},{1,2},{2,1},{3,0},{4,7},{5,6},{6,5},{7,4},{8,11},{9,10},{10,... | collective-permute-start | bytes 49160 | tf_op jit(solution)/shard_map/ppermute | solution.py:11
  353.7 48.9 %collective-permute-start.23 = (bf16[4,8,8,2048]{3,2,0,1:T(8,128)(2,1)}, bf16[4,8,8,2048]{3,2,0,1:T(8,128)(2,1)S(1)}, u32[]{:S(2)}, u32[]{:S(2)}) collective-permute-start(bf16[4,8,8,2048]{3,2,0,1:T(8,128)(2,1)} %get-tuple-element.94), channel_id=1, source_target_pairs={{0,12},{1,13},{2,14},{3,15},{4,8},{5,9},{6,10},{7,11},{8,4},{9,5},... | collective-permute-start | bytes 3145736 | tf_op jit(solution)/shard_map/ppermute | solution.py:11
  358.2 20.2 %collective-permute-start.29 = (f32[2,2048]{1,0:T(2,128)S(1)}, f32[2,2048]{1,0:T(2,128)S(1)}, u32[]{:S(2)}, u32[]{:S(2)}) collective-permute-start(f32[2,2048]{1,0:T(2,128)S(1)} %add_add_fusion.1), channel_id=1, source_target_pairs={{0,4},{1,5},{2,6},{3,7},{4,0},{5,1},{6,2},{7,3},{8,12},{9,13},{10,... | collective-permute-start | bytes 49160 | tf_op jit(solution)/shard_map/ppermute | solution.py:11
  358.3 43.6 %collective-permute-start.30 = (f32[2,2048]{1,0:T(2,128)S(1)}, f32[2,2048]{1,0:T(2,128)S(1)}, u32[]{:S(2)}, u32[]{:S(2)}) collective-permute-start(f32[2,2048]{1,0:T(2,128)S(1)} %add_add_fusion.1), channel_id=1, source_target_pairs={{0,8},{1,9},{2,10},{3,11},{4,12},{5,13},{6,14},{7,15},{8,0},{9,1},... | collective-permute-start | bytes 49160 | tf_op jit(solution)/shard_map/ppermute | solution.py:11
  360.8 41.2 %collective-permute-start.31 = (f32[2,2048]{1,0:T(2,128)S(1)}, f32[2,2048]{1,0:T(2,128)S(1)}, u32[]{:S(2)}, u32[]{:S(2)}) collective-permute-start(f32[2,2048]{1,0:T(2,128)S(1)} %add_add_fusion.1), channel_id=1, source_target_pairs={{0,12},{1,13},{2,14},{3,15},{4,8},{5,9},{6,10},{7,11},{8,4},{9,5},... | collective-permute-start | bytes 49160 | tf_op jit(solution)/shard_map/ppermute | solution.py:11
  (13 other events, 208.8 us)
